TPU v7x, 32 devices: a whole 2x2x4 slice. The times are simulated.
32 devices in a mesh: row: 4 (over z), wide: 8 (over y, x, core).
Axes of the slice: x: 2, y: 2, z: 4, core: 2. Of those that a mesh axis runs over, the one named last changes fastest.
Arguments:
- eigvec_t: float32 [2048, 32768], P(('row', 'wide')), may hold values from -6 to 6
- householder: float32 [16, 32, 32768], P('row', None, 'wide'), may hold values from -0.0625 to 0.0625
- wy_factor: float32 [6, 32, 32], replicated, may hold values from -0.5 to 0.5, as said below
- block_place: int32 [6], replicated, may hold values from 0 to 15, as said below
- offsets: int32 [6], replicated, may hold values from 0 to 16383, as said below
Outputs:
- vectors: float32 [2048, 32768], P('row', 'wide')
Inputs may be any that keep to these rules, and one draw needn't show every extreme that they name: wy_factor[s] is upper triangular. `offsets`: some step has offset 0 and some step has offset 32768 // 2 - 1. `block_place`: no stack position appears twice; positions 0 and 15 both appear.
All inputs are finite; a program needn't handle non-finite values.
Results may differ from a plain program's by a relative error of at most 0.0003.
Values sent between devices are 32-bit elements; how exact they have to be, the bound alone decides.
No kernel may reach another device: no remote copies, remote signals or barrier semaphores. Data moves between devices by JAX's collectives and lax.ppermute only.
A program may use at most 64 MiB of HBM per device.

v0:
```python
import functools

import jax
import jax.numpy as jnp
from jax import lax
from jax.experimental import pallas as pl
from jax.experimental.pallas import tpu as pltpu
from jax.sharding import PartitionSpec as P

HIGHEST = lax.Precision.HIGHEST
SMALL_LIMIT = 44 * 1024 * 1024
VMEM_LIMIT = 52 * 1024 * 1024
LARGE_LIMIT = 58 * 1024 * 1024
TAIL = 16
TAIL_TURN = (4, 1)
SPLITS = 2


def dot_t(a, b):
    return lax.dot_general(a, b, (((1,), (1,)), ((), ())), precision=HIGHEST, preferred_element_type=jnp.float32)


def dot(a, b):
    return lax.dot_general(a, b, (((1,), (0,)), ((), ())), precision=HIGHEST, preferred_element_type=jnp.float32)


def halves(x):
    high = x.astype(jnp.bfloat16)
    return high, (x - high.astype(jnp.float32)).astype(jnp.bfloat16)


def dot3(a, b, dims):
    rows = a[0].shape[0]
    both = lax.dot_general(jnp.concatenate(a, axis=0), b[0], (dims, ((), ())), preferred_element_type=jnp.float32)
    last = lax.dot_general(a[0], b[1], (dims, ((), ())), preferred_element_type=jnp.float32)
    return both[:rows] + (both[rows:] + last)


def after(x, *tokens):
    return lax.optimization_barrier((x, *tokens))[0]


def params(dims=0, limit=VMEM_LIMIT):
    semantics = ("arbitrary",) * dims if dims else None
    return pltpu.CompilerParams(dimension_semantics=semantics, vmem_limit_bytes=limit)


def cost(flops, nbytes):
    return pl.CostEstimate(flops=flops, bytes_accessed=nbytes, transcendentals=0)


SMEM = pl.BlockSpec(memory_space=pltpu.SMEM)
ANY = pl.BlockSpec(memory_space=pl.ANY)
VMEM = pl.BlockSpec(memory_space=pltpu.VMEM)


def pack(here, x, first, rows, n_wide, apart):
    ncols = x.shape[1] // n_wide

    def kernel(here_ref, x_ref, *refs):
        outs, (held, in_sems, out_sems) = refs[:-3], refs[-3:]
        into, out_of = [], []
        for k in range(n_wide):
            start = pl.multiple_of((here_ref[1] ^ k) * ncols, ncols) if apart else k * ncols
            source = x_ref.at[pl.ds(first, rows), pl.ds(start, ncols)]
            into.append(pltpu.make_async_copy(source, held.at[k], in_sems.at[k]))
            out_of.append(pltpu.make_async_copy(held.at[k], outs[k] if apart else outs[0].at[k], out_sems.at[k]))
        for copy in into:
            copy.start()
        for k in range(n_wide):
            into[k].wait()
            out_of[k].start()
        for copy in out_of:
            copy.wait()

    shapes = [(rows, ncols)] * n_wide if apart else [(n_wide, rows, ncols)]
    return pl.pallas_call(
        kernel,
        out_shape=[jax.ShapeDtypeStruct(shape, jnp.float32) for shape in shapes],
        in_specs=[SMEM, ANY],
        out_specs=[ANY] * len(shapes),
        scratch_shapes=[
            pltpu.VMEM((n_wide, rows, ncols), jnp.float32),
            pltpu.SemaphoreType.DMA((n_wide,)),
            pltpu.SemaphoreType.DMA((n_wide,)),
        ],
        compiler_params=params(limit=LARGE_LIMIT),
        cost_estimate=cost(0, 8 * rows * x.shape[1]),
        name="pack",
    )(here, x)


def plan(place_ref, slots, n_rows):
    places = [place_ref[s] for s in range(place_ref.shape[0])]
    roots = [lax.div(p, slots) for p in places]
    slot = [lax.rem(p, slots) for p in places]
    ranks = [sum([(roots[i] == roots[s]).astype(jnp.int32) for i in range(s)], jnp.int32(0)) for s in range(len(places))]
    counts = [sum([(r == i).astype(jnp.int32) for r in roots], jnp.int32(0)) for i in range(n_rows)]
    return roots, slot, ranks, counts


def feed(here, place, stack, evens, odds, n_rows, part, cols):
    slots, width, _ = stack.shape
    turn = len(evens)

    def kernel(here_ref, place_ref, stack_ref, *refs):
        arrived, (out_even, out_odd, sems) = refs[:-3], refs[-3:]
        roots, slot, ranks, _ = plan(place_ref, slots, n_rows)
        me = here_ref[0]
        mine = [r == me for r in roots]
        count = sum([m.astype(jnp.int32) for m in mine], jnp.int32(0))
        own = sum([jnp.where(m & (k == turn), s, 0) for m, k, s in zip(mine, ranks, slot)], jnp.int32(0))
        older = turn - jnp.maximum(count, 1)
        stored = stack_ref.at[own, :, pl.ds(part * cols, cols)]
        for side, out in ((0, out_even), (1, out_odd)):
            @pl.when((older < 0) | (count > turn))
            def _():
                pltpu.make_async_copy(stored, out, sems.at[side]).start()

            for i in range(turn):
                @pl.when((older == i) & (count <= turn))
                def _():
                    pltpu.make_async_copy(arrived[(1 - side) * turn + i], out, sems.at[side]).start()
        for side, out in ((0, out_even), (1, out_odd)):
            pltpu.make_async_copy(stored, out, sems.at[side]).wait()

    return pl.pallas_call(
        kernel,
        out_shape=[jax.ShapeDtypeStruct((width, cols), jnp.float32)] * 2,
        in_specs=[SMEM, SMEM, ANY] + [ANY] * (2 * turn),
        out_specs=[VMEM] * 2,
        scratch_shapes=[pltpu.SemaphoreType.DMA((2,))],
        compiler_params=params(limit=SMALL_LIMIT),
        cost_estimate=cost(0, 16 * width * cols),
        name="feed",
    )(here, place, stack, *evens, *odds)


def packed_width(steps, width):
    return -(-(width * steps * (steps - 1) // 2) // 128) * 128


def assemble(here, place, offsets, stack, evens, odds, n_rows):
    slots, width, ncols = stack.shape
    steps = place.shape[0]
    height = steps * width
    turns, splits = len(evens), len(evens[0])
    cols = ncols // splits

    def kernel(here_ref, place_ref, offset_ref, stack_ref, *refs):
        arrived, (high_ref, low_ref, gram_ref, held, sems) = refs[:-5], refs[-5:]
        even, odd = arrived[:turns * splits], arrived[turns * splits:]
        roots, slot, ranks, counts = plan(place_ref, slots, n_rows)
        me = here_ref[0]
        me_odd = lax.rem(me, 2) == 1
        for s in range(steps):
            root = roots[s]
            low, high = jnp.minimum(root, me), jnp.maximum(root, me)
            between = [jnp.where((i > low) & (i < high), jnp.maximum(counts[i], 1), 0) for i in range(n_rows)]
            turn = sum(between, ranks[s])
            target = held.at[pl.ds(s * width, width)]
            below, above = root < me, root > me

            @pl.when(root == me)
            def _():
                pltpu.make_async_copy(stack_ref.at[slot[s]], target, sems.at[s]).start()

            for side, came in (((below & me_odd) | (above & ~me_odd), even), ((below & ~me_odd) | (above & me_odd), odd)):
                for i in range(turns):
                    @pl.when(side & (turn == i))
                    def _():
                        for p in range(splits):
                            piece = held.at[pl.ds(s * width, width), pl.ds(p * cols, cols)]
                            pltpu.make_async_copy(came[i * splits + p], piece, sems.at[s]).start()
        columns = here_ref[1] * ncols + lax.broadcasted_iota(jnp.int32, (width, ncols), 1)
        for s in range(steps):
            rows = pl.ds(s * width, width)
            pltpu.make_async_copy(stack_ref.at[0], held.at[rows], sems.at[s]).wait()
            masked = jnp.where(columns >= offset_ref[s], held[rows, :], 0.0)
            held[rows, :] = masked
            high, low = halves(masked)
            high_ref[rows, :] = high
            low_ref[rows, :] = low
        gram = dot_t(held[...], held[...])
        gram_ref[...] = jnp.zeros_like(gram_ref)
        first = 0
        for s in range(1, steps):
            gram_ref[:, first:first + s * width] = gram[s * width:(s + 1) * width, :s * width]
            first += s * width

    return pl.pallas_call(
        kernel,
        out_shape=[
            jax.ShapeDtypeStruct((height, ncols), jnp.bfloat16),
            jax.ShapeDtypeStruct((height, ncols), jnp.bfloat16),
            jax.ShapeDtypeStruct((width, packed_width(steps, width)), jnp.float32),
        ],
        in_specs=[SMEM, SMEM, SMEM, ANY] + [ANY] * (2 * turns * splits),
        out_specs=[VMEM] * 3,
        scratch_shapes=[pltpu.VMEM((height, ncols), jnp.float32), pltpu.SemaphoreType.DMA((steps,))],
        compiler_params=params(limit=SMALL_LIMIT),
        cost_estimate=cost(12 * height * height * ncols, 8 * height * ncols),
        name="assemble",
    )(here, place, offsets, stack, *[p for turn in evens for p in turn], *[p for turn in odds for p in turn])


def merge(cross, factors, vecs):
    steps, width, _ = factors.shape
    height, ncols = vecs[0].shape

    def kernel(*refs):
        cross_refs, (factor_ref, v_high, v_low, p_high, p_low, total, m_ref) = refs[:-7], refs[-7:]
        total[...] = sum([ref[...] for ref in cross_refs[1:]], cross_refs[0][...])
        first = 0
        for k in range(steps):
            own = lax.broadcasted_iota(jnp.int32, (width, height), 0) + k * width
            rest = (own == lax.broadcasted_iota(jnp.int32, (width, height), 1)).astype(jnp.float32)
            if k:
                rest = rest - dot(total[:, first:first + k * width], m_ref[:k * width, :])
                first += k * width
            m_ref[k * width:(k + 1) * width, :] = dot(factor_ref[k], rest)
        product = dot3(halves(m_ref[...].T), (v_high[...], v_low[...]), ((1,), (0,)))
        p_high[...], p_low[...] = halves(product)

    return pl.pallas_call(
        kernel,
        out_shape=[jax.ShapeDtypeStruct((height, ncols), jnp.bfloat16)] * 2,
        out_specs=[VMEM] * 2,
        in_specs=[VMEM] * (len(cross) + 3),
        scratch_shapes=[pltpu.VMEM(cross[0].shape, jnp.float32), pltpu.VMEM((height, height), jnp.float32)],
        compiler_params=params(),
        cost_estimate=cost(6 * height * height * ncols, 8 * height * ncols),
        name="merge",
    )(*cross, factors, *vecs)


def column_block(rows, ncols):
    return 1024 if rows > 128 and ncols % 1024 == 0 else ncols


def fold(w):
    half = w.shape[0] // 2
    return jnp.concatenate([w[:half], w[half:]], axis=1)


def unfold(w):
    height = w.shape[1] // 2
    return jnp.concatenate([w[:, :height], w[:, height:]], axis=0)


def inner_products(here, x, vecs, split):
    apart = isinstance(x, list)
    pieces = x if apart else [x]
    lead = len(pieces) if apart else x.shape[0]
    rows, ncols = pieces[0].shape[-2:]
    height = vecs[0].shape[0]
    cols = column_block(lead * rows, ncols)
    blocks = ncols // cols
    parts = 2 if split else 1
    half = lead * rows // parts

    def kernel(here_ref, *refs):
        x_refs, (high_ref, low_ref), outs, total = refs[:len(pieces)], refs[len(pieces):len(pieces) + 2], refs[-1 - parts:-1], refs[-1]
        block = pl.program_id(0)
        here_cols = pl.ds(pl.multiple_of(block * cols, cols), cols) if blocks > 1 else slice(None)
        values = jnp.concatenate([ref[...] for ref in x_refs], axis=0).reshape(lead * rows, cols)
        part = dot3(halves(values), (high_ref[:, here_cols], low_ref[:, here_cols]), ((1,), (1,)))

        @pl.when(block == 0)
        def _():
            total[...] = part

        @pl.when(block > 0)
        def _():
            total[...] += part

        @pl.when(block == blocks - 1)
        def _():
            if apart:
                value = total[...]
                for k in range(lead):
                    total[pl.ds(pl.multiple_of((here_ref[1] ^ k) * rows, 8), rows), :] = value[k * rows:(k + 1) * rows]
            core = lax.rem(here_ref[1], 2)
            for i, out in enumerate(outs):
                start = pl.multiple_of((core ^ i) * half, 8) if split else 0
                out[...] = fold(total[pl.ds(start, half), :])

    block_shape, index = ((rows, cols), lambda c: (0, c)) if apart else ((lead, rows, cols), lambda c: (0, 0, c))
    return pl.pallas_call(
        kernel,
        out_shape=[jax.ShapeDtypeStruct((half // 2, 2 * height), jnp.float32)] * parts,
        grid=(blocks,),
        in_specs=[SMEM] + [pl.BlockSpec(block_shape, index)] * len(pieces) + [VMEM, VMEM],
        out_specs=[pl.BlockSpec((half // 2, 2 * height), lambda c: (0, 0))] * parts,
        scratch_shapes=[pltpu.VMEM((lead * rows, height), jnp.float32)],
        compiler_params=params(1),
        cost_estimate=cost(6 * lead * rows * ncols * height, 4 * lead * rows * ncols),
        name="inner_products",
    )(here, *pieces, *vecs)


def update(here, x, sums, other, changes, out, first, total):
    apart = isinstance(x, list)
    pieces = x if apart else [x]
    lead = len(pieces) if apart else x.shape[0]
    rows, ncols = pieces[0].shape[-2:]
    n_sums = len(sums)
    height = changes[0].shape[0]
    cols = column_block(lead * rows, ncols)
    blocks = ncols // cols
    half = lead * rows // 2

    def kernel(here_ref, *refs):
        sum_refs, x_refs = refs[:n_sums], refs[n_sums:n_sums + len(pieces)]
        high_ref, low_ref, *more = refs[n_sums + len(pieces):-4]
        out_ref, w_ref, w_high, w_low = refs[-4:]
        block = pl.program_id(0)

        @pl.when(block == 0)
        def _():
            w = unfold(sum([ref[...] for ref in sum_refs[1:]], sum_refs[0][...]))
            if other is not None:
                core = lax.rem(here_ref[1], 2)
                w_ref[pl.ds(pl.multiple_of(core * half, 8), half), :] = w
                w_ref[pl.ds(pl.multiple_of((1 - core) * half, 8), half), :] = unfold(more[0][...])
                w = w_ref[...]
            if apart:
                w_ref[...] = w
                w = jnp.concatenate(
                    [w_ref[pl.ds(pl.multiple_of((here_ref[1] ^ k) * rows, 8), rows), :] for k in range(lead)], axis=0
                )
            w_high[...], w_low[...] = halves(w)

        here_cols = pl.ds(pl.multiple_of(block * cols, cols), cols) if blocks > 1 else slice(None)
        change = dot3((w_high[...], w_low[...]), (high_ref[:, here_cols], low_ref[:, here_cols]), ((1,), (0,)))
        if apart:
            for k in range(lead):
                out_ref[pl.ds(here_ref[1] ^ k, 1)] = (x_refs[k][...] - change[k * rows:(k + 1) * rows])[None]
        else:
            out_ref[...] = (x_refs[0][...].reshape(lead * rows, cols) - change).reshape(lead, rows, cols)

    block_shape, index = ((rows, cols), lambda c: (0, c)) if apart else ((lead, rows, cols), lambda c: (0, 0, c))
    operands = [here] + list(sums) + pieces + list(changes)
    in_specs = [SMEM] + [VMEM] * n_sums + [pl.BlockSpec(block_shape, index)] * len(pieces) + [VMEM, VMEM]
    if other is not None:
        operands.append(other)
        in_specs.append(VMEM)
    aliases = {}
    if out is not None:
        aliases = {len(operands): 0}
        operands.append(out)
        in_specs.append(ANY)
    return pl.pallas_call(
        kernel,
        out_shape=jax.ShapeDtypeStruct((lead, total, ncols), jnp.float32),
        grid=(blocks,),
        in_specs=in_specs,
        out_specs=pl.BlockSpec((pl.Element(lead), pl.Element(rows), pl.Element(cols)), lambda c: (0, first, c * cols)),
        scratch_shapes=[pltpu.VMEM((lead * rows, height), jnp.float32)]
        + [pltpu.VMEM((lead * rows, height), jnp.bfloat16)] * 2,
        input_output_aliases=aliases,
        compiler_params=params(1),
        cost_estimate=cost(6 * lead * rows * ncols * height, 8 * lead * rows * ncols),
        name="update",
    )(*operands)


def swap(array, k, size):
    return lax.ppermute(array, "wide", [(i, i ^ k) for i in range(size)])


def spread(pair, size):
    return [pair] + [swap(pair, k, size) for k in range(2, size, 2)]


def body(n_row, n_wide, eigvec_t, householder, wy_factor, block_place, offsets):
    rows, order = eigvec_t.shape
    steps, width, _ = wy_factor.shape
    slots = householder.shape[0]
    ncols = order // n_wide
    here = jnp.stack([lax.axis_index("row"), lax.axis_index("wide")]).astype(jnp.int32)

    turns = max(z + min(steps - 1, slots * (n_row - 1 - z)) for z in range(n_row - 1))
    cols = ncols // SPLITS
    streams = [([], []) for _ in range(SPLITS)]

    def exchange(array, odd):
        pairs = []
        for z in range(n_row):
            mate = ((z + odd) ^ 1) - odd
            for w in range(n_wide):
                target = mate * n_wide + w if 0 <= mate < n_row else z * n_wide + (w ^ 1)
                pairs.append((z * n_wide + w, target))
        return lax.ppermute(array, ("row", "wide"), pairs)

    tail = TAIL if rows % 8 == 0 and rows > TAIL else 0
    bulk = rows - tail
    if tail:
        piece, = pack(here, eigvec_t, 0, bulk, n_wide, False)
        early = lax.all_to_all(piece, "wide", split_axis=0, concat_axis=0, tiled=True)
        pieces = pack(here, after(eigvec_t, piece), bulk, tail, n_wide, True)
    else:
        piece = here
        early = lax.all_to_all(eigvec_t, "wide", split_axis=1, concat_axis=0, tiled=True)[None]
        pieces = []

    tokens = [piece]
    for turn in range(turns):
        for part in range(SPLITS):
            evens, odds = streams[part]
            to_even, to_odd = feed(after(here, *tokens), block_place, householder, evens, odds, n_row, part, cols)
            tokens = [to_odd]
            streams[part] = (evens + [exchange(to_even, 0)], odds + [exchange(to_odd, 1)])
            if (turn, part) == (0, 1):
                tokens += pieces
            if (turn, part) == TAIL_TURN and tail:
                late = [pieces[0]] + [swap(after(pieces[k], to_odd), k, n_wide) for k in range(1, n_wide)]
    evens = list(zip(*[stream[0] for stream in streams]))
    odds = list(zip(*[stream[1] for stream in streams]))
    high, low, gram = assemble(here, block_place, offsets, householder, evens, odds, n_row)
    cross = spread(gram + swap(gram, 1, n_wide), n_wide)
    changes = merge(cross, wy_factor, (high, low))

    mine, theirs = inner_products(here, early, (high, low), True)
    mine = functools.reduce(jnp.add, spread(mine + swap(theirs, 1, n_wide), n_wide))
    total = rows if tail else rows * n_wide
    out = update(here, early, [mine], swap(mine, 1, n_wide), changes, None, 0, total)
    if tail:
        part, = inner_products(here, late, (high, low), False)
        out = update(here, late, spread(part + swap(part, 1, n_wide), n_wide), None, changes, out, bulk, total)
    return out.reshape(n_wide * rows, ncols)


def solution(mesh):
    return jax.shard_map(
        functools.partial(body, mesh.shape["row"], mesh.shape["wide"]),
        mesh=mesh,
        in_specs=(P(("row", "wide"), None), P("row", None, "wide"), P(), P(), P()),
        out_specs=P("row", "wide"),
        check_vma=False,
    )
```

profile of v0, /device:TPU:0, one launch (start us, length us, event | category | flops | bytes accessed | tf_op | source)
XLA Modules:
  0.0 161.4 jit_solution(11863211508640317342)
XLA Ops:
  0.6 6.2 %pack.2 = f32[8,48,4096]{2,1,0:T(8,128)} custom-call(s32[2]{0:T(128)} %pad_add_fusion.here_ref, f32[64,32768]{1,0:T(8,128)} %x_ref.2), custom_call_target="tpu_custom_call" | custom-call | bytes 12582912 | tf_op jit(solution)/shard_map/pack/pallas_call | solution.py:77
  6.8 5.3 %all-to-all-start = ((f32[8,48,4096]{2,1,0:T(8,128)}), f32[8,48,4096]{2,1,0:T(8,128)}, u32[]{:S(2)}, u32[]{:S(2)}) async-start(f32[8,48,4096]{2,1,0:T(8,128)} %pack.2), calls=%async_computation | async-start | bytes 12582912 | tf_op jit(solution)/shard_map/all_to_all | solution.py:400
  12.8 2.8 %collective-permute-start = (f32[32,2048]{1,0:T(8,128)S(1)}, f32[32,2048]{1,0:T(8,128)S(1)}, u32[]{:S(2)}, u32[]{:S(2)}) collective-permute-start(f32[32,2048]{1,0:T(8,128)S(1)} %get-tuple-element.78), channel_id=1, source_target_pairs={{0,8},{1,9},{2,10},{3,11},{4,12},{5,13},{6,14},{7,15},{8,0},{9,1},... | collective-permute-start | bytes 786440 | tf_op jit(solution)/shard_map/ppermute | solution.py:394
  16.2 3.1 %collective-permute-start.2 = (f32[32,2048]{1,0:T(8,128)S(1)}, f32[32,2048]{1,0:T(8,128)S(1)}, u32[]{:S(2)}, u32[]{:S(2)}) collective-permute-start(f32[32,2048]{1,0:T(8,128)S(1)} %get-tuple-element.81), channel_id=1, source_target_pairs={{0,8},{1,9},{2,10},{3,11},{4,12},{5,13},{6,14},{7,15},{8,0},{9,1},... | collective-permute-start | bytes 786440 | tf_op jit(solution)/shard_map/ppermute | solution.py:394
  19.4 3.1 %pack.3 = (f32[16,4096]{1,0:T(8,128)}, f32[16,4096]{1,0:T(8,128)}, f32[16,4096]{1,0:T(8,128)}, f32[16,4096]{1,0:T(8,128)}, f32[16,4096]{1,0:T(8,128)}, /*index=5...) custom-call(s32[2]{0:T(128)} %pad_add_fusion.here_ref, f32[64,32768]{1,0:T(8,128)} %x_ref.2), custom_call_target="tpu_custom_call" | custom-call | bytes 4194304 | tf_op jit(solution)/shard_map/pack/pallas_call | solution.py:77
  23.3 3.2 %collective-permute-start.4 = (f32[32,2048]{1,0:T(8,128)S(1)}, f32[32,2048]{1,0:T(8,128)S(1)}, u32[]{:S(2)}, u32[]{:S(2)}) collective-permute-start(f32[32,2048]{1,0:T(8,128)S(1)} %get-tuple-element.84), channel_id=1, source_target_pairs={{0,8},{1,9},{2,10},{3,11},{4,12},{5,13},{6,14},{7,15},{8,0},{9,1},... | collective-permute-start | bytes 786440 | tf_op jit(solution)/shard_map/ppermute | solution.py:394
  29.0 3.2 %collective-permute-start.6 = (f32[32,2048]{1,0:T(8,128)S(1)}, f32[32,2048]{1,0:T(8,128)S(1)}, u32[]{:S(2)}, u32[]{:S(2)}) collective-permute-start(f32[32,2048]{1,0:T(8,128)S(1)} %get-tuple-element.87), channel_id=1, source_target_pairs={{0,8},{1,9},{2,10},{3,11},{4,12},{5,13},{6,14},{7,15},{8,0},{9,1},... | collective-permute-start | bytes 786440 | tf_op jit(solution)/shard_map/ppermute | solution.py:394
  34.6 3.2 %collective-permute-start.8 = (f32[32,2048]{1,0:T(8,128)S(1)}, f32[32,2048]{1,0:T(8,128)S(1)}, u32[]{:S(2)}, u32[]{:S(2)}) collective-permute-start(f32[32,2048]{1,0:T(8,128)S(1)} %get-tuple-element.90), channel_id=1, source_target_pairs={{0,8},{1,9},{2,10},{3,11},{4,12},{5,13},{6,14},{7,15},{8,0},{9,1},... | collective-permute-start | bytes 786440 | tf_op jit(solution)/shard_map/ppermute | solution.py:394
  40.2 3.2 %collective-permute-start.10 = (f32[32,2048]{1,0:T(8,128)S(1)}, f32[32,2048]{1,0:T(8,128)S(1)}, u32[]{:S(2)}, u32[]{:S(2)}) collective-permute-start(f32[32,2048]{1,0:T(8,128)S(1)} %get-tuple-element.93), channel_id=1, source_target_pairs={{0,8},{1,9},{2,10},{3,11},{4,12},{5,13},{6,14},{7,15},{8,0},{9,1},... | collective-permute-start | bytes 786440 | tf_op jit(solution)/shard_map/ppermute | solution.py:394
  45.8 3.2 %collective-permute-start.12 = (f32[32,2048]{1,0:T(8,128)S(1)}, f32[32,2048]{1,0:T(8,128)S(1)}, u32[]{:S(2)}, u32[]{:S(2)}) collective-permute-start(f32[32,2048]{1,0:T(8,128)S(1)} %get-tuple-element.96), channel_id=1, source_target_pairs={{0,8},{1,9},{2,10},{3,11},{4,12},{5,13},{6,14},{7,15},{8,0},{9,1},... | collective-permute-start | bytes 786440 | tf_op jit(solution)/shard_map/ppermute | solution.py:394
  51.4 3.2 %collective-permute-start.14 = (f32[32,2048]{1,0:T(8,128)S(1)}, f32[32,2048]{1,0:T(8,128)S(1)}, u32[]{:S(2)}, u32[]{:S(2)}) collective-permute-start(f32[32,2048]{1,0:T(8,128)S(1)} %get-tuple-element.99), channel_id=1, source_target_pairs={{0,8},{1,9},{2,10},{3,11},{4,12},{5,13},{6,14},{7,15},{8,0},{9,1},... | collective-permute-start | bytes 786440 | tf_op jit(solution)/shard_map/ppermute | solution.py:394
  57.1 3.2 %collective-permute-start.23 = (f32[32,2048]{1,0:T(8,128)S(1)}, f32[32,2048]{1,0:T(8,128)S(1)}, u32[]{:S(2)}, u32[]{:S(2)}) collective-permute-start(f32[32,2048]{1,0:T(8,128)S(1)} %get-tuple-element.108), channel_id=1, source_target_pairs={{0,8},{1,9},{2,10},{3,11},{4,12},{5,13},{6,14},{7,15},{8,0},{9,1},... | collective-permute-start | bytes 786440 | tf_op jit(solution)/shard_map/ppermute | solution.py:394
  62.7 3.2 %collective-permute-start.24 = (f32[32,2048]{1,0:T(8,128)S(1)}, f32[32,2048]{1,0:T(8,128)S(1)}, u32[]{:S(2)}, u32[]{:S(2)}) collective-permute-start(f32[32,2048]{1,0:T(8,128)S(1)} %get-tuple-element.109), channel_id=1, source_target_pairs={{0,8},{1,9},{2,10},{3,11},{4,12},{5,13},{6,14},{7,15},{8,0},{9,1},... | collective-permute-start | bytes 786440 | tf_op jit(solution)/shard_map/ppermute | solution.py:394
  68.4 5.2 %collective-permute-start.26 = (f32[32,2048]{1,0:T(8,128)S(1)}, f32[32,2048]{1,0:T(8,128)S(1)}, u32[]{:S(2)}, u32[]{:S(2)}) collective-permute-start(f32[32,2048]{1,0:T(8,128)S(1)} %get-tuple-element.111), channel_id=1, source_target_pairs={{0,8},{1,9},{2,10},{3,11},{4,12},{5,13},{6,14},{7,15},{8,0},{9,1},... | collective-permute-start | bytes 786440 | tf_op jit(solution)/shard_map/ppermute | solution.py:394
  74.3 2.8 %collective-permute-start.28 = (f32[32,2048]{1,0:T(8,128)S(1)}, f32[32,2048]{1,0:T(8,128)S(1)}, u32[]{:S(2)}, u32[]{:S(2)}) collective-permute-start(f32[32,2048]{1,0:T(8,128)S(1)} %get-tuple-element.114), channel_id=1, source_target_pairs={{0,8},{1,9},{2,10},{3,11},{4,12},{5,13},{6,14},{7,15},{8,0},{9,1},... | collective-permute-start | bytes 786440 | tf_op jit(solution)/shard_map/ppermute | solution.py:394
  77.6 2.3 %collective-permute-done.26.refs_10_ = f32[32,2048]{1,0:T(8,128)S(1)} collective-permute-done((f32[32,2048]{1,0:T(8,128)S(1)}, f32[32,2048]{1,0:T(8,128)S(1)}, u32[]{:S(2)}, u32[]{:S(2)}) %collective-permute-start.26) | collective-permute-done | bytes 262176 | tf_op jit(solution)/shard_map/ppermute | solution.py:394
  79.9 1.9 %collective-permute-start.17 = (f32[16,4096]{1,0:T(8,128)}, f32[16,4096]{1,0:T(8,128)S(1)}, u32[]{:S(2)}, u32[]{:S(2)}) collective-permute-start(f32[16,4096]{1,0:T(8,128)} %get-tuple-element.102), channel_id=1, source_target_pairs={{0,2},{1,3},{2,0},{3,1},{4,6},{5,7},{6,4},{7,5},{8,10},{9,11},{10,... | collective-permute-start | bytes 786440 | tf_op jit(solution)/shard_map/ppermute | solution.py:369
  81.8 2.3 %collective-permute-done.28.refs_11_ = f32[32,2048]{1,0:T(8,128)S(1)} collective-permute-done((f32[32,2048]{1,0:T(8,128)S(1)}, f32[32,2048]{1,0:T(8,128)S(1)}, u32[]{:S(2)}, u32[]{:S(2)}) %collective-permute-start.28) | collective-permute-done | bytes 262176 | tf_op jit(solution)/shard_map/ppermute | solution.py:394
  84.1 5.2 %assemble.1 = (bf16[192,4096]{1,0:T(8,128)(2,1)S(1)}, bf16[192,4096]{1,0:T(8,128)(2,1)S(1)}, f32[32,512]{1,0:T(8,128)S(1)}) custom-call(s32[2]{0:T(128)S(1)} %copy-done.7, s32[6]{0:T(128)S(1)} %copy-done.9, s32[6]{0:T(128)S(1)} %copy-done.10, f32[4,32,4096]{2,1,0:T(8,128)} %stack_ref.25, f32[32,2048]{1,0:T(8,128)S(1)} %collective-permute-done.refs_0_, ...), custom_call_target="tpu_custom_call" | custom-call | flops 1811939328 | bytes 6291456 | tf_op jit(solution)/shard_map/assemble/pallas_call | solution.py:191
  90.6 6.8 %inner_products.3 = (f32[96,384]{1,0:T(8,128)S(1)}, f32[96,384]{1,0:T(8,128)S(1)}) custom-call(s32[2]{0:T(128)S(1)} %copy-done.7, f32[8,48,4096]{2,1,0:T(8,128)} %all-to-all-done.refs_0_.refs_1_, bf16[192,4096]{1,0:T(8,128)(2,1)S(1)} %get-tuple-element.116.refs_8_.refs_5_.refs_1_, bf16[192,4096]{1,0:T(8,128)(2,1)} %copy-done.2), custom_call_target="tpu_custom_call" | custom-call | flops 1811939328 | bytes 6291456 | tf_op jit(solution)/shard_map/inner_products/pallas_call | solution.py:289
  97.5 1.8 %collective-permute-start.18 = (f32[16,4096]{1,0:T(8,128)S(1)}, f32[16,4096]{1,0:T(8,128)S(1)}, u32[]{:S(2)}, u32[]{:S(2)}) collective-permute-start(f32[16,4096]{1,0:T(8,128)S(1)} %copy-done.16), channel_id=1, source_target_pairs={{0,3},{1,2},{2,1},{3,0},{4,7},{5,6},{6,5},{7,4},{8,11},{9,10},{10,... | collective-permute-start | bytes 786440 | tf_op jit(solution)/shard_map/ppermute | solution.py:369
  103.7 2.2 %collective-permute-done.18.refs_3_.refs_7_ = f32[16,4096]{1,0:T(8,128)S(1)} collective-permute-done((f32[16,4096]{1,0:T(8,128)S(1)}, f32[16,4096]{1,0:T(8,128)S(1)}, u32[]{:S(2)}, u32[]{:S(2)}) %collective-permute-start.18) | collective-permute-done | bytes 262176 | tf_op jit(solution)/shard_map/ppermute | solution.py:369
  105.9 2.3 %collective-permute-start.42 = (f32[96,384]{1,0:T(8,128)S(1)}, f32[96,384]{1,0:T(8,128)S(1)}, u32[]{:S(2)}, u32[]{:S(2)}) collective-permute-start(f32[96,384]{1,0:T(8,128)S(1)} %add.20), channel_id=1, source_target_pairs={{0,6},{1,7},{2,4},{3,5},{4,2},{5,3},{6,0},{7,1},{8,14},{9,15},{10,... | collective-permute-start | bytes 442376 | tf_op jit(solution)/shard_map/ppermute | solution.py:369
  108.2 14.6 %collective-permute-done.19.refs_4_.refs_8_ = f32[16,4096]{1,0:T(8,128)S(1)} collective-permute-done((f32[16,4096]{1,0:T(8,128)S(1)}, f32[16,4096]{1,0:T(8,128)S(1)}, u32[]{:S(2)}, u32[]{:S(2)}) %collective-permute-start.19) | collective-permute-done | bytes 262176 | tf_op jit(solution)/shard_map/ppermute | solution.py:369
  124.3 3.1 %collective-permute-done.20.refs_5_.refs_9_ = f32[16,4096]{1,0:T(8,128)S(1)} collective-permute-done((f32[16,4096]{1,0:T(8,128)S(1)}, f32[16,4096]{1,0:T(8,128)S(1)}, u32[]{:S(2)}, u32[]{:S(2)}) %collective-permute-start.20) | collective-permute-done | bytes 262176 | tf_op jit(solution)/shard_map/ppermute | solution.py:369
  129.1 3.3 %inner_products.2 = f32[64,384]{1,0:T(8,128)S(1)} custom-call(s32[2]{0:T(128)S(1)} %copy-done.7, f32[16,4096]{1,0:T(8,128)S(1)} %copy-done.4, f32[16,4096]{1,0:T(8,128)S(1)} %collective-permute-done.16.refs_1_.refs_5_, f32[16,4096]{1,0:T(8,128)S(1)} %collective-permute-done.17.refs_2_.refs_6_, f32[16,4096]{1,0:T(8,128)S(1)} %collective-permute-done.18.refs_3_.refs_7_, ...), custom_call_target="tpu_custom_call" | custom-call | flops 603979776 | bytes 2097152 | tf_op jit(solution)/shard_map/inner_products/pallas_call | solution.py:289
  132.6 2.6 %collective-permute-start.38 = (f32[32,512]{1,0:T(8,128)S(1)}, f32[32,512]{1,0:T(8,128)S(1)}, u32[]{:S(2)}, u32[]{:S(2)}) collective-permute-start(f32[32,512]{1,0:T(8,128)S(1)} %add.19.refs_0_), channel_id=1, source_target_pairs={{0,6},{1,7},{2,4},{3,5},{4,2},{5,3},{6,0},{7,1},{8,14},{9,15},{10,... | collective-permute-start | bytes 196616 | tf_op jit(solution)/shard_map/ppermute | solution.py:369
  136.3 2.6 %collective-permute-start.34 = (f32[64,384]{1,0:T(8,128)S(1)}, f32[64,384]{1,0:T(8,128)S(1)}, u32[]{:S(2)}, u32[]{:S(2)}) collective-permute-start(f32[64,384]{1,0:T(8,128)S(1)} %add.18.refs_0_), channel_id=1, source_target_pairs={{0,6},{1,7},{2,4},{3,5},{4,2},{5,3},{6,0},{7,1},{8,14},{9,15},{10,... | collective-permute-start | bytes 294920 | tf_op jit(solution)/shard_map/ppermute | solution.py:369
  139.7 1.8 %collective-permute-start.32 = (f32[64,384]{1,0:T(8,128)S(1)}, f32[64,384]{1,0:T(8,128)S(1)}, u32[]{:S(2)}, u32[]{:S(2)}) collective-permute-start(f32[64,384]{1,0:T(8,128)S(1)} %add.18.refs_0_), channel_id=1, source_target_pairs={{0,2},{1,3},{2,0},{3,1},{4,6},{5,7},{6,4},{7,5},{8,10},{9,11},{10,... | collective-permute-start | bytes 294920 | tf_op jit(solution)/shard_map/ppermute | solution.py:369
  141.6 6.5 %merge.1 = (bf16[192,4096]{1,0:T(8,128)(2,1)S(1)}, bf16[192,4096]{1,0:T(8,128)(2,1)}) custom-call(f32[32,512]{1,0:T(8,128)S(1)} %add.19.refs_0_, f32[32,512]{1,0:T(8,128)S(1)} %collective-permute-done.36.refs_1_, f32[32,512]{1,0:T(8,128)S(1)} %collective-permute-done.37.refs_2_, f32[32,512]{1,0:T(8,128)S(1)} %collective-permute-done.38.refs_3_, ...), custom_call_target="tpu_custom_call" | custom-call | flops 905969664 | bytes 6291456 | tf_op jit(solution)/shard_map/merge/pallas_call | solution.py:225
  148.1 8.7 %update.2.refs_14_ = f32[8,64,4096]{2,1,0:T(8,128)} custom-call(s32[2]{0:T(128)S(1)} %copy-done.7, f32[96,384]{1,0:T(8,128)S(1)} %add_add_fusion.refs_0_, f32[8,48,4096]{2,1,0:T(8,128)} %all-to-all-done.refs_0_.refs_1_, bf16[192,4096]{1,0:T(8,128)(2,1)S(1)} %get-tuple-element.119.refs_2_.refs_12_, bf16[192,4096]{1,0:T(8,128)(2,1)} %get-tuple-element.120.refs_3_.refs_13_, ...), custom_call_target="tpu_custom_call" | custom-call | flops 1811939328 | bytes 12582912 | tf_op jit(solution)/shard_map/update/pallas_call | solution.py:353
  156.8 4.6 %update.3 = f32[8,64,4096]{2,1,0:T(8,128)} custom-call(s32[2]{0:T(128)S(1)} %copy-done.7, f32[64,384]{1,0:T(8,128)S(1)} %add.18.refs_0_, f32[64,384]{1,0:T(8,128)S(1)} %collective-permute-done.32.refs_1_, f32[64,384]{1,0:T(8,128)S(1)} %collective-permute-done.33.refs_2_, ...), custom_call_target="tpu_custom_call", output_to_operand_aliasing={{}: (15, {})} | custom-call | flops 603979776 | bytes 4194304 | tf_op jit(solution)/shard_map/update/pallas_call | solution.py:353
  (117 shorter events, 34.6 us)
Async XLA Ops:
  6.8 83.8 %all-to-all-start = ((f32[8,48,4096]{2,1,0:T(8,128)}), f32[8,48,4096]{2,1,0:T(8,128)}, u32[]{:S(2)}, u32[]{:S(2)}) async-start(f32[8,48,4096]{2,1,0:T(8,128)} %pack.2), calls=%async_computation | async-start | bytes 12582912 | tf_op jit(solution)/shard_map/all_to_all | solution.py:400
  12.8 9.9 %collective-permute-start = (f32[32,2048]{1,0:T(8,128)S(1)}, f32[32,2048]{1,0:T(8,128)S(1)}, u32[]{:S(2)}, u32[]{:S(2)}) collective-permute-start(f32[32,2048]{1,0:T(8,128)S(1)} %get-tuple-element.78), channel_id=1, source_target_pairs={{0,8},{1,9},{2,10},{3,11},{4,12},{5,13},{6,14},{7,15},{8,0},{9,1},... | collective-permute-start | bytes 786440 | tf_op jit(solution)/shard_map/ppermute | solution.py:394
  16.2 12.0 %collective-permute-start.2 = (f32[32,2048]{1,0:T(8,128)S(1)}, f32[32,2048]{1,0:T(8,128)S(1)}, u32[]{:S(2)}, u32[]{:S(2)}) collective-permute-start(f32[32,2048]{1,0:T(8,128)S(1)} %get-tuple-element.81), channel_id=1, source_target_pairs={{0,8},{1,9},{2,10},{3,11},{4,12},{5,13},{6,14},{7,15},{8,0},{9,1},... | collective-permute-start | bytes 786440 | tf_op jit(solution)/shard_map/ppermute | solution.py:394
  19.4 8.9 %collective-permute-start.3 = (f32[32,2048]{1,0:T(8,128)S(1)}, f32[32,2048]{1,0:T(8,128)S(1)}, u32[]{:S(2)}, u32[]{:S(2)}) collective-permute-start(f32[32,2048]{1,0:T(8,128)S(1)} %get-tuple-element.70), channel_id=1, source_target_pairs={{0,1},{1,0},{2,3},{3,2},{4,5},{5,4},{6,7},{7,6},{8,16},{9,17},{10,... | collective-permute-start | bytes 786440 | tf_op jit(solution)/shard_map/ppermute | solution.py:394
  23.3 10.6 %collective-permute-start.4 = (f32[32,2048]{1,0:T(8,128)S(1)}, f32[32,2048]{1,0:T(8,128)S(1)}, u32[]{:S(2)}, u32[]{:S(2)}) collective-permute-start(f32[32,2048]{1,0:T(8,128)S(1)} %get-tuple-element.84), channel_id=1, source_target_pairs={{0,8},{1,9},{2,10},{3,11},{4,12},{5,13},{6,14},{7,15},{8,0},{9,1},... | collective-permute-start | bytes 786440 | tf_op jit(solution)/shard_map/ppermute | solution.py:394
  26.5 7.4 %collective-permute-start.5 = (f32[32,2048]{1,0:T(8,128)S(1)}, f32[32,2048]{1,0:T(8,128)S(1)}, u32[]{:S(2)}, u32[]{:S(2)}) collective-permute-start(f32[32,2048]{1,0:T(8,128)S(1)} %get-tuple-element.79), channel_id=1, source_target_pairs={{0,1},{1,0},{2,3},{3,2},{4,5},{5,4},{6,7},{7,6},{8,16},{9,17},{10,... | collective-permute-start | bytes 786440 | tf_op jit(solution)/shard_map/ppermute | solution.py:394
  29.0 10.6 %collective-permute-start.6 = (f32[32,2048]{1,0:T(8,128)S(1)}, f32[32,2048]{1,0:T(8,128)S(1)}, u32[]{:S(2)}, u32[]{:S(2)}) collective-permute-start(f32[32,2048]{1,0:T(8,128)S(1)} %get-tuple-element.87), channel_id=1, source_target_pairs={{0,8},{1,9},{2,10},{3,11},{4,12},{5,13},{6,14},{7,15},{8,0},{9,1},... | collective-permute-start | bytes 786440 | tf_op jit(solution)/shard_map/ppermute | solution.py:394
  32.1 7.4 %collective-permute-start.7 = (f32[32,2048]{1,0:T(8,128)S(1)}, f32[32,2048]{1,0:T(8,128)S(1)}, u32[]{:S(2)}, u32[]{:S(2)}) collective-permute-start(f32[32,2048]{1,0:T(8,128)S(1)} %get-tuple-element.82), channel_id=1, source_target_pairs={{0,1},{1,0},{2,3},{3,2},{4,5},{5,4},{6,7},{7,6},{8,16},{9,17},{10,... | collective-permute-start | bytes 786440 | tf_op jit(solution)/shard_map/ppermute | solution.py:394
  34.6 10.6 %collective-permute-start.8 = (f32[32,2048]{1,0:T(8,128)S(1)}, f32[32,2048]{1,0:T(8,128)S(1)}, u32[]{:S(2)}, u32[]{:S(2)}) collective-permute-start(f32[32,2048]{1,0:T(8,128)S(1)} %get-tuple-element.90), channel_id=1, source_target_pairs={{0,8},{1,9},{2,10},{3,11},{4,12},{5,13},{6,14},{7,15},{8,0},{9,1},... | collective-permute-start | bytes 786440 | tf_op jit(solution)/shard_map/ppermute | solution.py:394
  40.2 10.6 %collective-permute-start.10 = (f32[32,2048]{1,0:T(8,128)S(1)}, f32[32,2048]{1,0:T(8,128)S(1)}, u32[]{:S(2)}, u32[]{:S(2)}) collective-permute-start(f32[32,2048]{1,0:T(8,128)S(1)} %get-tuple-element.93), channel_id=1, source_target_pairs={{0,8},{1,9},{2,10},{3,11},{4,12},{5,13},{6,14},{7,15},{8,0},{9,1},... | collective-permute-start | bytes 786440 | tf_op jit(solution)/shard_map/ppermute | solution.py:394
  45.8 10.5 %collective-permute-start.12 = (f32[32,2048]{1,0:T(8,128)S(1)}, f32[32,2048]{1,0:T(8,128)S(1)}, u32[]{:S(2)}, u32[]{:S(2)}) collective-permute-start(f32[32,2048]{1,0:T(8,128)S(1)} %get-tuple-element.96), channel_id=1, source_target_pairs={{0,8},{1,9},{2,10},{3,11},{4,12},{5,13},{6,14},{7,15},{8,0},{9,1},... | collective-permute-start | bytes 786440 | tf_op jit(solution)/shard_map/ppermute | solution.py:394
  51.4 10.5 %collective-permute-start.14 = (f32[32,2048]{1,0:T(8,128)S(1)}, f32[32,2048]{1,0:T(8,128)S(1)}, u32[]{:S(2)}, u32[]{:S(2)}) collective-permute-start(f32[32,2048]{1,0:T(8,128)S(1)} %get-tuple-element.99), channel_id=1, source_target_pairs={{0,8},{1,9},{2,10},{3,11},{4,12},{5,13},{6,14},{7,15},{8,0},{9,1},... | collective-permute-start | bytes 786440 | tf_op jit(solution)/shard_map/ppermute | solution.py:394
  57.1 10.5 %collective-permute-start.23 = (f32[32,2048]{1,0:T(8,128)S(1)}, f32[32,2048]{1,0:T(8,128)S(1)}, u32[]{:S(2)}, u32[]{:S(2)}) collective-permute-start(f32[32,2048]{1,0:T(8,128)S(1)} %get-tuple-element.108), channel_id=1, source_target_pairs={{0,8},{1,9},{2,10},{3,11},{4,12},{5,13},{6,14},{7,15},{8,0},{9,1},... | collective-permute-start | bytes 786440 | tf_op jit(solution)/shard_map/ppermute | solution.py:394
  62.7 10.9 %collective-permute-start.24 = (f32[32,2048]{1,0:T(8,128)S(1)}, f32[32,2048]{1,0:T(8,128)S(1)}, u32[]{:S(2)}, u32[]{:S(2)}) collective-permute-start(f32[32,2048]{1,0:T(8,128)S(1)} %get-tuple-element.109), channel_id=1, source_target_pairs={{0,8},{1,9},{2,10},{3,11},{4,12},{5,13},{6,14},{7,15},{8,0},{9,1},... | collective-permute-start | bytes 786440 | tf_op jit(solution)/shard_map/ppermute | solution.py:394
  65.9 7.7 %collective-permute-start.27 = (f32[32,2048]{1,0:T(8,128)S(1)}, f32[32,2048]{1,0:T(8,128)S(1)}, u32[]{:S(2)}, u32[]{:S(2)}) collective-permute-start(f32[32,2048]{1,0:T(8,128)S(1)} %get-tuple-element.100), channel_id=1, source_target_pairs={{0,1},{1,0},{2,3},{3,2},{4,5},{5,4},{6,7},{7,6},{8,16},{9,17},{10,... | collective-permute-start | bytes 786440 | tf_op jit(solution)/shard_map/ppermute | solution.py:394
  68.3 13.5 %collective-permute-start.29 = (f32[32,2048]{1,0:T(8,128)S(1)}, f32[32,2048]{1,0:T(8,128)S(1)}, u32[]{:S(2)}, u32[]{:S(2)}) collective-permute-start(f32[32,2048]{1,0:T(8,128)S(1)} %get-tuple-element.112), channel_id=1, source_target_pairs={{0,1},{1,0},{2,3},{3,2},{4,5},{5,4},{6,7},{7,6},{8,16},{9,17},{10,... | collective-permute-start | bytes 786440 | tf_op jit(solution)/shard_map/ppermute | solution.py:394
  68.4 11.5 %collective-permute-start.26 = (f32[32,2048]{1,0:T(8,128)S(1)}, f32[32,2048]{1,0:T(8,128)S(1)}, u32[]{:S(2)}, u32[]{:S(2)}) collective-permute-start(f32[32,2048]{1,0:T(8,128)S(1)} %get-tuple-element.111), channel_id=1, source_target_pairs={{0,8},{1,9},{2,10},{3,11},{4,12},{5,13},{6,14},{7,15},{8,0},{9,1},... | collective-permute-start | bytes 786440 | tf_op jit(solution)/shard_map/ppermute | solution.py:394
  74.3 9.9 %collective-permute-start.28 = (f32[32,2048]{1,0:T(8,128)S(1)}, f32[32,2048]{1,0:T(8,128)S(1)}, u32[]{:S(2)}, u32[]{:S(2)}) collective-permute-start(f32[32,2048]{1,0:T(8,128)S(1)} %get-tuple-element.114), channel_id=1, source_target_pairs={{0,8},{1,9},{2,10},{3,11},{4,12},{5,13},{6,14},{7,15},{8,0},{9,1},... | collective-permute-start | bytes 786440 | tf_op jit(solution)/shard_map/ppermute | solution.py:394
  77.1 23.7 %collective-permute-start.16 = (f32[16,4096]{1,0:T(8,128)}, f32[16,4096]{1,0:T(8,128)S(1)}, u32[]{:S(2)}, u32[]{:S(2)}) collective-permute-start(f32[16,4096]{1,0:T(8,128)} %get-tuple-element.101), channel_id=1, source_target_pairs={{0,1},{1,0},{2,3},{3,2},{4,5},{5,4},{6,7},{7,6},{8,9},{9,8},{10,11... | collective-permute-start | bytes 786440 | tf_op jit(solution)/shard_map/ppermute | solution.py:369
  79.9 20.9 %collective-permute-start.17 = (f32[16,4096]{1,0:T(8,128)}, f32[16,4096]{1,0:T(8,128)S(1)}, u32[]{:S(2)}, u32[]{:S(2)}) collective-permute-start(f32[16,4096]{1,0:T(8,128)} %get-tuple-element.102), channel_id=1, source_target_pairs={{0,2},{1,3},{2,0},{3,1},{4,6},{5,7},{6,4},{7,5},{8,10},{9,11},{10,... | collective-permute-start | bytes 786440 | tf_op jit(solution)/shard_map/ppermute | solution.py:369
  97.5 8.4 %collective-permute-start.18 = (f32[16,4096]{1,0:T(8,128)S(1)}, f32[16,4096]{1,0:T(8,128)S(1)}, u32[]{:S(2)}, u32[]{:S(2)}) collective-permute-start(f32[16,4096]{1,0:T(8,128)S(1)} %copy-done.16), channel_id=1, source_target_pairs={{0,3},{1,2},{2,1},{3,0},{4,7},{5,6},{6,5},{7,4},{8,11},{9,10},{10,... | collective-permute-start | bytes 786440 | tf_op jit(solution)/shard_map/ppermute | solution.py:369
  99.3 23.6 %collective-permute-start.19 = (f32[16,4096]{1,0:T(8,128)S(1)}, f32[16,4096]{1,0:T(8,128)S(1)}, u32[]{:S(2)}, u32[]{:S(2)}) collective-permute-start(f32[16,4096]{1,0:T(8,128)S(1)} %copy-done.15), channel_id=1, source_target_pairs={{0,4},{1,5},{2,6},{3,7},{4,0},{5,1},{6,2},{7,3},{8,12},{9,13},{10,... | collective-permute-start | bytes 786440 | tf_op jit(solution)/shard_map/ppermute | solution.py:369
  100.8 26.7 %collective-permute-start.20 = (f32[16,4096]{1,0:T(8,128)S(1)}, f32[16,4096]{1,0:T(8,128)S(1)}, u32[]{:S(2)}, u32[]{:S(2)}) collective-permute-start(f32[16,4096]{1,0:T(8,128)S(1)} %copy-done.14), channel_id=1, source_target_pairs={{0,5},{1,4},{2,7},{3,6},{4,1},{5,0},{6,3},{7,2},{8,13},{9,12},{10,... | collective-permute-start | bytes 786440 | tf_op jit(solution)/shard_map/ppermute | solution.py:369
  100.8 27.2 %collective-permute-start.21 = (f32[16,4096]{1,0:T(8,128)S(1)}, f32[16,4096]{1,0:T(8,128)S(1)}, u32[]{:S(2)}, u32[]{:S(2)}) collective-permute-start(f32[16,4096]{1,0:T(8,128)S(1)} %copy-done.13), channel_id=1, source_target_pairs={{0,6},{1,7},{2,4},{3,5},{4,2},{5,3},{6,0},{7,1},{8,14},{9,15},{10,... | collective-permute-start | bytes 786440 | tf_op jit(solution)/shard_map/ppermute | solution.py:369
  102.2 26.2 %collective-permute-start.22 = (f32[16,4096]{1,0:T(8,128)S(1)}, f32[16,4096]{1,0:T(8,128)S(1)}, u32[]{:S(2)}, u32[]{:S(2)}) collective-permute-start(f32[16,4096]{1,0:T(8,128)S(1)} %copy-done.12), channel_id=1, source_target_pairs={{0,7},{1,6},{2,5},{3,4},{4,3},{5,2},{6,1},{7,0},{8,15},{9,14},{10,... | collective-permute-start | bytes 786440 | tf_op jit(solution)/shard_map/ppermute | solution.py:369
  105.9 29.3 %collective-permute-start.42 = (f32[96,384]{1,0:T(8,128)S(1)}, f32[96,384]{1,0:T(8,128)S(1)}, u32[]{:S(2)}, u32[]{:S(2)}) collective-permute-start(f32[96,384]{1,0:T(8,128)S(1)} %add.20), channel_id=1, source_target_pairs={{0,6},{1,7},{2,4},{3,5},{4,2},{5,3},{6,0},{7,1},{8,14},{9,15},{10,... | collective-permute-start | bytes 442376 | tf_op jit(solution)/shard_map/ppermute | solution.py:369
  122.8 12.9 %collective-permute-start.41 = (f32[96,384]{1,0:T(8,128)S(1)}, f32[96,384]{1,0:T(8,128)S(1)}, u32[]{:S(2)}, u32[]{:S(2)}) collective-permute-start(f32[96,384]{1,0:T(8,128)S(1)} %add.20), channel_id=1, source_target_pairs={{0,4},{1,5},{2,6},{3,7},{4,0},{5,1},{6,2},{7,3},{8,12},{9,13},{10,... | collective-permute-start | bytes 442376 | tf_op jit(solution)/shard_map/ppermute | solution.py:369
  127.5 8.7 %collective-permute-start.40 = (f32[96,384]{1,0:T(8,128)S(1)}, f32[96,384]{1,0:T(8,128)S(1)}, u32[]{:S(2)}, u32[]{:S(2)}) collective-permute-start(f32[96,384]{1,0:T(8,128)S(1)} %add.20), channel_id=1, source_target_pairs={{0,2},{1,3},{2,0},{3,1},{4,6},{5,7},{6,4},{7,5},{8,10},{9,11},{10,... | collective-permute-start | bytes 442376 | tf_op jit(solution)/shard_map/ppermute | solution.py:369
  136.2 11.8 %collective-permute-start.43 = (f32[96,384]{1,0:T(8,128)S(1)}, f32[96,384]{1,0:T(8,128)S(1)}, u32[]{:S(2)}, u32[]{:S(2)}) collective-permute-start(f32[96,384]{1,0:T(8,128)S(1)} %add_add_fusion.refs_0_), channel_id=1, source_target_pairs={{0,1},{1,0},{2,3},{3,2},{4,5},{5,4},{6,7},{7,6},{8,9},{9,8},{10,11... | collective-permute-start | bytes 442376 | tf_op jit(solution)/shard_map/ppermute | solution.py:369
  136.3 20.5 %collective-permute-start.34 = (f32[64,384]{1,0:T(8,128)S(1)}, f32[64,384]{1,0:T(8,128)S(1)}, u32[]{:S(2)}, u32[]{:S(2)}) collective-permute-start(f32[64,384]{1,0:T(8,128)S(1)} %add.18.refs_0_), channel_id=1, source_target_pairs={{0,6},{1,7},{2,4},{3,5},{4,2},{5,3},{6,0},{7,1},{8,14},{9,15},{10,... | collective-permute-start | bytes 294920 | tf_op jit(solution)/shard_map/ppermute | solution.py:369
  138.9 17.9 %collective-permute-start.33 = (f32[64,384]{1,0:T(8,128)S(1)}, f32[64,384]{1,0:T(8,128)S(1)}, u32[]{:S(2)}, u32[]{:S(2)}) collective-permute-start(f32[64,384]{1,0:T(8,128)S(1)} %add.18.refs_0_), channel_id=1, source_target_pairs={{0,4},{1,5},{2,6},{3,7},{4,0},{5,1},{6,2},{7,3},{8,12},{9,13},{10,... | collective-permute-start | bytes 294920 | tf_op jit(solution)/shard_map/ppermute | solution.py:369
  139.7 17.1 %collective-permute-start.32 = (f32[64,384]{1,0:T(8,128)S(1)}, f32[64,384]{1,0:T(8,128)S(1)}, u32[]{:S(2)}, u32[]{:S(2)}) collective-permute-start(f32[64,384]{1,0:T(8,128)S(1)} %add.18.refs_0_), channel_id=1, source_target_pairs={{0,2},{1,3},{2,0},{3,1},{4,6},{5,7},{6,4},{7,5},{8,10},{9,11},{10,... | collective-permute-start | bytes 294920 | tf_op jit(solution)/shard_map/ppermute | solution.py:369
  (30 other events, 345.9 us)
where the time goes:
time: 162 us; the launch traced here: 161 us
  starting transfers between devices  67.1 us (41%)
  Pallas kernels  52.5 us (32%)
  waiting for transfers between devices  38.9 us (24%)
  local copies, waits for them, and re-layouts  1.95 us (1%)
    ppermute x24, starting transfers between devices, exchange(): return lax.ppermute(array, ('row', 'wide'), pairs)  39.4 us
    ppermute x20, starting transfers between devices, swap(): return lax.ppermute(array, 'wide', [(i, i ^ k) for i in range(size)])  22.4 us
    ppermute x20, waiting for transfers between devices, swap(): return lax.ppermute(array, 'wide', [(i, i ^ k) for i in range(size)])  20 us
    ppermute x24, waiting for transfers between devices, exchange(): return lax.ppermute(array, ('row', 'wide'), pairs)  18.9 us
    pallas_call x2, Pallas kernels, update(): pl.pallas_call(kernel, out_shape=jax.ShapeDtypeStruct((lead, total, ncols...  13.4 us
    pallas_call x2, Pallas kernels, inner_products(): pl.pallas_call(kernel, out_shape=[jax.ShapeDtypeStruct((half // 2, 2 * he...  10.1 us
    pallas_call x2, Pallas kernels, pack(): pl.pallas_call(kernel, out_shape=[jax.ShapeDtypeStruct(shape, jnp.float32...  9.26 us
    pallas_call x12, Pallas kernels, feed(): pl.pallas_call(kernel, out_shape=[jax.ShapeDtypeStruct((width, cols), jnp...  8.07 us
  transfers between devices with their start and end apart: 45, of which 14 were waited for; matrix products, arithmetic and copies ran while one was open for 0% of the time, Pallas kernels for 26%

commit v1 on v0

--- a/solution.py
+++ b/solution.py
@@ -12,7 +12,6 @@
 VMEM_LIMIT = 52 * 1024 * 1024
 LARGE_LIMIT = 58 * 1024 * 1024
 TAIL = 16
-TAIL_TURN = (4, 1)
 SPLITS = 2
 
 
@@ -234,8 +233,8 @@
     )(*cross, factors, *vecs)
 
 
-def column_block(rows, ncols):
-    return 1024 if rows > 128 and ncols % 1024 == 0 else ncols
+def column_block(rows, ncols, cols):
+    return cols if rows > 128 and ncols % cols == 0 else ncols
 
 
 def fold(w):
@@ -254,7 +253,7 @@
     lead = len(pieces) if apart else x.shape[0]
     rows, ncols = pieces[0].shape[-2:]
     height = vecs[0].shape[0]
-    cols = column_block(lead * rows, ncols)
+    cols = column_block(lead * rows, ncols, 1024)
     blocks = ncols // cols
     parts = 2 if split else 1
     half = lead * rows // parts
@@ -306,7 +305,7 @@
     rows, ncols = pieces[0].shape[-2:]
     n_sums = len(sums)
     height = changes[0].shape[0]
-    cols = column_block(lead * rows, ncols)
+    cols = column_block(lead * rows, ncols, 512)
     blocks = ncols // cols
     half = lead * rows // 2
 
@@ -395,29 +394,28 @@
 
     tail = TAIL if rows % 8 == 0 and rows > TAIL else 0
     bulk = rows - tail
-    if tail:
-        piece, = pack(here, eigvec_t, 0, bulk, n_wide, False)
-        early = lax.all_to_all(piece, "wide", split_axis=0, concat_axis=0, tiled=True)
-        pieces = pack(here, after(eigvec_t, piece), bulk, tail, n_wide, True)
-    else:
-        piece = here
+    if not tail:
         early = lax.all_to_all(eigvec_t, "wide", split_axis=1, concat_axis=0, tiled=True)[None]
-        pieces = []
-
-    tokens = [piece]
+
+    tokens = []
     for turn in range(turns):
         for part in range(SPLITS):
             evens, odds = streams[part]
             to_even, to_odd = feed(after(here, *tokens), block_place, householder, evens, odds, n_row, part, cols)
             tokens = [to_odd]
             streams[part] = (evens + [exchange(to_even, 0)], odds + [exchange(to_odd, 1)])
-            if (turn, part) == (0, 1):
-                tokens += pieces
-            if (turn, part) == TAIL_TURN and tail:
-                late = [pieces[0]] + [swap(after(pieces[k], to_odd), k, n_wide) for k in range(1, n_wide)]
+            if (turn, part) == (0, 0) and tail:
+                piece, = pack(here, after(eigvec_t, to_odd), 0, bulk, n_wide, False)
+                early = lax.all_to_all(piece, "wide", split_axis=0, concat_axis=0, tiled=True)
+                tokens = [piece]
+            if (turn, part) == (1, 0) and tail:
+                piece, = pack(here, after(eigvec_t, to_odd), bulk, tail, n_wide, False)
+                tokens = [piece]
     evens = list(zip(*[stream[0] for stream in streams]))
     odds = list(zip(*[stream[1] for stream in streams]))
     high, low, gram = assemble(here, block_place, offsets, householder, evens, odds, n_row)
+    if tail:
+        late = lax.all_to_all(after(piece, gram), "wide", split_axis=0, concat_axis=0, tiled=True)
     cross = spread(gram + swap(gram, 1, n_wide), n_wide)
     changes = merge(cross, wy_factor, (high, low))
 

time: 162 us -> 158 us (0.975)
  starting transfers between devices: 67.1 us -> 59.2 us
  waiting for transfers between devices: 38.9 us -> 41.7 us
    ppermute x20 -> x13, starting transfers between devices: 22.4 us -> 12.1 us  [swap(): return lax.ppermute(array, 'wide', [(i, i ^ k) for i in range(size)])]
    all_to_all x0 -> x1, starting transfers between devices: none -> 4.53 us  [body(): lax.all_to_all(after(piece, gram), 'wide', split_axis=0, concat_axis=0, t...]
    ppermute x24, waiting for transfers between devices: 18.9 us -> 23.4 us  [exchange(): return lax.ppermute(array, ('row', 'wide'), pairs)]
    ppermute x24, starting transfers between devices: 39.4 us -> 37.2 us  [exchange(): return lax.ppermute(array, ('row', 'wide'), pairs)]
    ppermute x20 -> x13, waiting for transfers between devices: 20 us -> 18.4 us  [swap(): return lax.ppermute(array, 'wide', [(i, i ^ k) for i in range(size)])]
    unnamed x34 -> x22, local copies, waits for them, and re-layouts: 1.95 us -> 3.47 us
  transfers between devices with their start and end apart: 45 -> 39, of which waited for: 14 -> 15; matrix products, arithmetic and copies ran while one was open for 0% -> 0% of each run, Pallas kernels for 26% -> 26%
where the time goes in v1:
time: 158 us; the launch traced here: 157 us
  starting transfers between devices  59.2 us (37%)
  Pallas kernels  52.5 us (33%)
  waiting for transfers between devices  41.7 us (26%)
  local copies, waits for them, and re-layouts  3.47 us (2%)
    ppermute x24, starting transfers between devices, exchange(): return lax.ppermute(array, ('row', 'wide'), pairs)  37.2 us
    ppermute x24, waiting for transfers between devices, exchange(): return lax.ppermute(array, ('row', 'wide'), pairs)  23.4 us
    ppermute x13, waiting for transfers between devices, swap(): return lax.ppermute(array, 'wide', [(i, i ^ k) for i in range(size)])  18.4 us
    pallas_call x2, Pallas kernels, update(): pl.pallas_call(kernel, out_shape=jax.ShapeDtypeStruct((lead, total, ncols...  14 us
    ppermute x13, starting transfers between devices, swap(): return lax.ppermute(array, 'wide', [(i, i ^ k) for i in range(size)])  12.1 us
    pallas_call x2, Pallas kernels, inner_products(): pl.pallas_call(kernel, out_shape=[jax.ShapeDtypeStruct((half // 2, 2 * he...  9.41 us
    pallas_call x2, Pallas kernels, pack(): pl.pallas_call(kernel, out_shape=[jax.ShapeDtypeStruct(shape, jnp.float32...  9.25 us
    pallas_call x12, Pallas kernels, feed(): pl.pallas_call(kernel, out_shape=[jax.ShapeDtypeStruct((width, cols), jnp...  8.07 us
  transfers between devices with their start and end apart: 39, of which 15 were waited for; matrix products, arithmetic and copies ran while one was open for 0% of the time, Pallas kernels for 26%

profile of v1, /device:TPU:0, one launch (start us, length us, event | category | flops | bytes accessed | tf_op | source)
XLA Modules:
  0.0 157.4 jit_solution(15713510766218996723)
XLA Ops:
  3.0 6.2 %pack.2 = f32[8,48,4096]{2,1,0:T(8,128)} custom-call(s32[2]{0:T(128)} %copy-done.4, f32[64,32768]{1,0:T(8,128)} %x_ref.1), custom_call_target="tpu_custom_call" | custom-call | bytes 12582912 | tf_op jit(solution)/shard_map/pack/pallas_call | solution.py:76
  9.2 5.3 %all-to-all-start.1 = ((f32[8,48,4096]{2,1,0:T(8,128)}), f32[8,48,4096]{2,1,0:T(8,128)}, u32[]{:S(2)}, u32[]{:S(2)}) async-start(f32[8,48,4096]{2,1,0:T(8,128)} %pack.2), calls=%async_computation.1 | async-start | bytes 12582912 | tf_op jit(solution)/shard_map/all_to_all | solution.py:409
  14.5 2.7 %collective-permute-start = (f32[32,2048]{1,0:T(8,128)S(1)}, f32[32,2048]{1,0:T(8,128)S(1)}, u32[]{:S(2)}, u32[]{:S(2)}) collective-permute-start(f32[32,2048]{1,0:T(8,128)S(1)} %get-tuple-element.55), channel_id=1, source_target_pairs={{0,8},{1,9},{2,10},{3,11},{4,12},{5,13},{6,14},{7,15},{8,0},{9,1},... | collective-permute-start | bytes 786440 | tf_op jit(solution)/shard_map/ppermute | solution.py:393
  17.9 3.2 %collective-permute-start.2 = (f32[32,2048]{1,0:T(8,128)S(1)}, f32[32,2048]{1,0:T(8,128)S(1)}, u32[]{:S(2)}, u32[]{:S(2)}) collective-permute-start(f32[32,2048]{1,0:T(8,128)S(1)} %get-tuple-element.58), channel_id=1, source_target_pairs={{0,8},{1,9},{2,10},{3,11},{4,12},{5,13},{6,14},{7,15},{8,0},{9,1},... | collective-permute-start | bytes 786440 | tf_op jit(solution)/shard_map/ppermute | solution.py:393
  21.1 3.2 %collective-permute-done.refs_0_ = f32[32,2048]{1,0:T(8,128)S(1)} collective-permute-done((f32[32,2048]{1,0:T(8,128)S(1)}, f32[32,2048]{1,0:T(8,128)S(1)}, u32[]{:S(2)}, u32[]{:S(2)}) %collective-permute-start) | collective-permute-done | bytes 262176 | tf_op jit(solution)/shard_map/ppermute | solution.py:393
  25.0 5.2 %collective-permute-start.3 = (f32[32,2048]{1,0:T(8,128)S(1)}, f32[32,2048]{1,0:T(8,128)S(1)}, u32[]{:S(2)}, u32[]{:S(2)}) collective-permute-start(f32[32,2048]{1,0:T(8,128)S(1)} %get-tuple-element.59), channel_id=1, source_target_pairs={{0,8},{1,9},{2,10},{3,11},{4,12},{5,13},{6,14},{7,15},{8,0},{9,1},... | collective-permute-start | bytes 786440 | tf_op jit(solution)/shard_map/ppermute | solution.py:393
  30.3 3.1 %pack.3 = f32[8,16,4096]{2,1,0:T(8,128)} custom-call(s32[2]{0:T(128)} %copy-done.4, f32[64,32768]{1,0:T(8,128)} %x_ref.1), custom_call_target="tpu_custom_call" | custom-call | bytes 4194304 | tf_op jit(solution)/shard_map/pack/pallas_call | solution.py:76
  36.7 2.8 %collective-permute-start.7 = (f32[32,2048]{1,0:T(8,128)S(1)}, f32[32,2048]{1,0:T(8,128)S(1)}, u32[]{:S(2)}, u32[]{:S(2)}) collective-permute-start(f32[32,2048]{1,0:T(8,128)S(1)} %get-tuple-element.64), channel_id=1, source_target_pairs={{0,8},{1,9},{2,10},{3,11},{4,12},{5,13},{6,14},{7,15},{8,0},{9,1},... | collective-permute-start | bytes 786440 | tf_op jit(solution)/shard_map/ppermute | solution.py:393
  39.5 3.0 %collective-permute-done.5.refs_1_.refs_3_ = f32[32,2048]{1,0:T(8,128)S(1)} collective-permute-done((f32[32,2048]{1,0:T(8,128)S(1)}, f32[32,2048]{1,0:T(8,128)S(1)}, u32[]{:S(2)}, u32[]{:S(2)}) %collective-permute-start.5) | collective-permute-done | bytes 262176 | tf_op jit(solution)/shard_map/ppermute | solution.py:393
  43.1 3.0 %collective-permute-start.9 = (f32[32,2048]{1,0:T(8,128)S(1)}, f32[32,2048]{1,0:T(8,128)S(1)}, u32[]{:S(2)}, u32[]{:S(2)}) collective-permute-start(f32[32,2048]{1,0:T(8,128)S(1)} %get-tuple-element.67), channel_id=1, source_target_pairs={{0,8},{1,9},{2,10},{3,11},{4,12},{5,13},{6,14},{7,15},{8,0},{9,1},... | collective-permute-start | bytes 786440 | tf_op jit(solution)/shard_map/ppermute | solution.py:393
  46.1 1.9 %collective-permute-done.7.refs_2_.refs_4_ = f32[32,2048]{1,0:T(8,128)S(1)} collective-permute-done((f32[32,2048]{1,0:T(8,128)S(1)}, f32[32,2048]{1,0:T(8,128)S(1)}, u32[]{:S(2)}, u32[]{:S(2)}) %collective-permute-start.7) | collective-permute-done | bytes 262176 | tf_op jit(solution)/shard_map/ppermute | solution.py:393
  48.7 3.0 %collective-permute-start.11 = (f32[32,2048]{1,0:T(8,128)S(1)}, f32[32,2048]{1,0:T(8,128)S(1)}, u32[]{:S(2)}, u32[]{:S(2)}) collective-permute-start(f32[32,2048]{1,0:T(8,128)S(1)} %get-tuple-element.70), channel_id=1, source_target_pairs={{0,8},{1,9},{2,10},{3,11},{4,12},{5,13},{6,14},{7,15},{8,0},{9,1},... | collective-permute-start | bytes 786440 | tf_op jit(solution)/shard_map/ppermute | solution.py:393
  51.8 1.9 %collective-permute-done.9.refs_2_.refs_5_ = f32[32,2048]{1,0:T(8,128)S(1)} collective-permute-done((f32[32,2048]{1,0:T(8,128)S(1)}, f32[32,2048]{1,0:T(8,128)S(1)}, u32[]{:S(2)}, u32[]{:S(2)}) %collective-permute-start.9) | collective-permute-done | bytes 262176 | tf_op jit(solution)/shard_map/ppermute | solution.py:393
  54.3 3.0 %collective-permute-start.13 = (f32[32,2048]{1,0:T(8,128)S(1)}, f32[32,2048]{1,0:T(8,128)S(1)}, u32[]{:S(2)}, u32[]{:S(2)}) collective-permute-start(f32[32,2048]{1,0:T(8,128)S(1)} %get-tuple-element.73), channel_id=1, source_target_pairs={{0,8},{1,9},{2,10},{3,11},{4,12},{5,13},{6,14},{7,15},{8,0},{9,1},... | collective-permute-start | bytes 786440 | tf_op jit(solution)/shard_map/ppermute | solution.py:393
  57.4 1.9 %collective-permute-done.11.refs_3_.refs_6_ = f32[32,2048]{1,0:T(8,128)S(1)} collective-permute-done((f32[32,2048]{1,0:T(8,128)S(1)}, f32[32,2048]{1,0:T(8,128)S(1)}, u32[]{:S(2)}, u32[]{:S(2)}) %collective-permute-start.11) | collective-permute-done | bytes 262176 | tf_op jit(solution)/shard_map/ppermute | solution.py:393
  60.0 3.0 %collective-permute-start.15 = (f32[32,2048]{1,0:T(8,128)S(1)}, f32[32,2048]{1,0:T(8,128)S(1)}, u32[]{:S(2)}, u32[]{:S(2)}) collective-permute-start(f32[32,2048]{1,0:T(8,128)S(1)} %get-tuple-element.76), channel_id=1, source_target_pairs={{0,8},{1,9},{2,10},{3,11},{4,12},{5,13},{6,14},{7,15},{8,0},{9,1},... | collective-permute-start | bytes 786440 | tf_op jit(solution)/shard_map/ppermute | solution.py:393
  65.6 3.0 %collective-permute-start.17 = (f32[32,2048]{1,0:T(8,128)S(1)}, f32[32,2048]{1,0:T(8,128)S(1)}, u32[]{:S(2)}, u32[]{:S(2)}) collective-permute-start(f32[32,2048]{1,0:T(8,128)S(1)} %get-tuple-element.79), channel_id=1, source_target_pairs={{0,8},{1,9},{2,10},{3,11},{4,12},{5,13},{6,14},{7,15},{8,0},{9,1},... | collective-permute-start | bytes 786440 | tf_op jit(solution)/shard_map/ppermute | solution.py:393
  68.6 1.9 %collective-permute-done.15.refs_4_.refs_8_ = f32[32,2048]{1,0:T(8,128)S(1)} collective-permute-done((f32[32,2048]{1,0:T(8,128)S(1)}, f32[32,2048]{1,0:T(8,128)S(1)}, u32[]{:S(2)}, u32[]{:S(2)}) %collective-permute-start.15) | collective-permute-done | bytes 262176 | tf_op jit(solution)/shard_map/ppermute | solution.py:393
  71.3 3.9 %collective-permute-start.19 = (f32[32,2048]{1,0:T(8,128)S(1)}, f32[32,2048]{1,0:T(8,128)S(1)}, u32[]{:S(2)}, u32[]{:S(2)}) collective-permute-start(f32[32,2048]{1,0:T(8,128)S(1)} %get-tuple-element.82), channel_id=1, source_target_pairs={{0,8},{1,9},{2,10},{3,11},{4,12},{5,13},{6,14},{7,15},{8,0},{9,1},... | collective-permute-start | bytes 786440 | tf_op jit(solution)/shard_map/ppermute | solution.py:393
  76.0 3.9 %collective-permute-start.21 = (f32[32,2048]{1,0:T(8,128)S(1)}, f32[32,2048]{1,0:T(8,128)S(1)}, u32[]{:S(2)}, u32[]{:S(2)}) collective-permute-start(f32[32,2048]{1,0:T(8,128)S(1)} %get-tuple-element.85), channel_id=1, source_target_pairs={{0,8},{1,9},{2,10},{3,11},{4,12},{5,13},{6,14},{7,15},{8,0},{9,1},... | collective-permute-start | bytes 786440 | tf_op jit(solution)/shard_map/ppermute | solution.py:393
  79.9 2.6 %collective-permute-done.19.refs_10_ = f32[32,2048]{1,0:T(8,128)S(1)} collective-permute-done((f32[32,2048]{1,0:T(8,128)S(1)}, f32[32,2048]{1,0:T(8,128)S(1)}, u32[]{:S(2)}, u32[]{:S(2)}) %collective-permute-start.19) | collective-permute-done | bytes 262176 | tf_op jit(solution)/shard_map/ppermute | solution.py:393
  82.5 3.3 %collective-permute-done.21.refs_11_ = f32[32,2048]{1,0:T(8,128)S(1)} collective-permute-done((f32[32,2048]{1,0:T(8,128)S(1)}, f32[32,2048]{1,0:T(8,128)S(1)}, u32[]{:S(2)}, u32[]{:S(2)}) %collective-permute-start.21) | collective-permute-done | bytes 262176 | tf_op jit(solution)/shard_map/ppermute | solution.py:393
  85.8 5.2 %assemble.1 = (bf16[192,4096]{1,0:T(8,128)(2,1)S(1)}, bf16[192,4096]{1,0:T(8,128)(2,1)S(1)}, f32[32,512]{1,0:T(8,128)S(1)}) custom-call(s32[2]{0:T(128)S(1)} %copy-done.6, s32[6]{0:T(128)S(1)} %copy-done.9, s32[6]{0:T(128)S(1)} %copy-done.10, f32[4,32,4096]{2,1,0:T(8,128)} %stack_ref.25, f32[32,2048]{1,0:T(8,128)S(1)} %collective-permute-done.refs_0_, ...), custom_call_target="tpu_custom_call" | custom-call | flops 1811939328 | bytes 6291456 | tf_op jit(solution)/shard_map/assemble/pallas_call | solution.py:190
  92.2 4.5 %all-to-all-start = ((f32[8,16,4096]{2,1,0:T(8,128)}), f32[8,16,4096]{2,1,0:T(8,128)}, u32[]{:S(2)}, u32[]{:S(2)}) async-start(f32[8,16,4096]{2,1,0:T(8,128)} %pack.3), calls=%async_computation | async-start | bytes 4194304 | tf_op jit(solution)/shard_map/all_to_all | solution.py:418
  96.7 6.1 %inner_products.3 = (f32[96,384]{1,0:T(8,128)S(1)}, f32[96,384]{1,0:T(8,128)S(1)}) custom-call(s32[2]{0:T(128)S(1)} %copy-done.6, f32[8,48,4096]{2,1,0:T(8,128)} %all-to-all-done.1.refs_0_.refs_1_, bf16[192,4096]{1,0:T(8,128)(2,1)S(1)} %get-tuple-element.89.refs_1_.refs_5_, bf16[192,4096]{1,0:T(8,128)(2,1)} %copy-done.3), custom_call_target="tpu_custom_call" | custom-call | flops 1811939328 | bytes 6291456 | tf_op jit(solution)/shard_map/inner_products/pallas_call | solution.py:288
  104.3 2.9 %collective-permute-start.35 = (f32[96,384]{1,0:T(8,128)S(1)}, f32[96,384]{1,0:T(8,128)S(1)}, u32[]{:S(2)}, u32[]{:S(2)}) collective-permute-start(f32[96,384]{1,0:T(8,128)S(1)} %add.20), channel_id=1, source_target_pairs={{0,6},{1,7},{2,4},{3,5},{4,2},{5,3},{6,0},{7,1},{8,14},{9,15},{10,... | collective-permute-start | bytes 442376 | tf_op jit(solution)/shard_map/ppermute | solution.py:368
  109.1 2.9 %collective-permute-start.31 = (f32[32,512]{1,0:T(8,128)S(1)}, f32[32,512]{1,0:T(8,128)S(1)}, u32[]{:S(2)}, u32[]{:S(2)}) collective-permute-start(f32[32,512]{1,0:T(8,128)S(1)} %add.19.refs_0_), channel_id=1, source_target_pairs={{0,6},{1,7},{2,4},{3,5},{4,2},{5,3},{6,0},{7,1},{8,14},{9,15},{10,... | collective-permute-start | bytes 196616 | tf_op jit(solution)/shard_map/ppermute | solution.py:368
  112.5 14.4 %collective-permute-done.35 = f32[96,384]{1,0:T(8,128)S(1)} collective-permute-done((f32[96,384]{1,0:T(8,128)S(1)}, f32[96,384]{1,0:T(8,128)S(1)}, u32[]{:S(2)}, u32[]{:S(2)}) %collective-permute-start.35) | collective-permute-done | bytes 147488 | tf_op jit(solution)/shard_map/ppermute | solution.py:368
  129.3 3.3 %inner_products.2 = f32[64,384]{1,0:T(8,128)S(1)} custom-call(s32[2]{0:T(128)S(1)} %copy-done.6, f32[8,16,4096]{2,1,0:T(8,128)} %all-to-all-done.refs_0_.refs_4_, bf16[192,4096]{1,0:T(8,128)(2,1)S(1)} %get-tuple-element.89.refs_1_.refs_5_, bf16[192,4096]{1,0:T(8,128)(2,1)} %copy-done.3), custom_call_target="tpu_custom_call" | custom-call | flops 603979776 | bytes 2097152 | tf_op jit(solution)/shard_map/inner_products/pallas_call | solution.py:288
  133.2 6.5 %merge.1 = (bf16[192,4096]{1,0:T(8,128)(2,1)S(1)}, bf16[192,4096]{1,0:T(8,128)(2,1)}) custom-call(f32[32,512]{1,0:T(8,128)S(1)} %add.19.refs_0_, f32[32,512]{1,0:T(8,128)S(1)} %collective-permute-done.29.refs_1_, f32[32,512]{1,0:T(8,128)S(1)} %collective-permute-done.30.refs_2_, f32[32,512]{1,0:T(8,128)S(1)} %collective-permute-done.31.refs_3_, ...), custom_call_target="tpu_custom_call" | custom-call | flops 905969664 | bytes 6291456 | tf_op jit(solution)/shard_map/merge/pallas_call | solution.py:224
  143.3 9.6 %update.2.refs_7_ = f32[8,64,4096]{2,1,0:T(8,128)} custom-call(s32[2]{0:T(128)S(1)} %copy-done.6, f32[96,384]{1,0:T(8,128)S(1)} %add_add_fusion.refs_0_, f32[8,48,4096]{2,1,0:T(8,128)} %all-to-all-done.1.refs_0_.refs_1_, bf16[192,4096]{1,0:T(8,128)(2,1)S(1)} %get-tuple-element.91.refs_2_.refs_5_, bf16[192,4096]{1,0:T(8,128)(2,1)} %get-tuple-element.92.refs_3_.refs_6_, ...), custom_call_target="tpu_custom_call" | custom-call | flops 1811939328 | bytes 12582912 | tf_op jit(solution)/shard_map/update/pallas_call | solution.py:352
  153.0 4.4 %update.3 = f32[8,64,4096]{2,1,0:T(8,128)} custom-call(s32[2]{0:T(128)S(1)} %copy-done.6, f32[64,384]{1,0:T(8,128)S(1)} %add.18.refs_0_, f32[64,384]{1,0:T(8,128)S(1)} %collective-permute-done.25.refs_1_, f32[64,384]{1,0:T(8,128)S(1)} %collective-permute-done.26.refs_2_, ...), custom_call_target="tpu_custom_call", output_to_operand_aliasing={{}: (8, {})} | custom-call | flops 603979776 | bytes 4194304 | tf_op jit(solution)/shard_map/update/pallas_call | solution.py:352
  (93 shorter events, 26.1 us)
Async XLA Ops:
  9.2 83.0 %all-to-all-start.1 = ((f32[8,48,4096]{2,1,0:T(8,128)}), f32[8,48,4096]{2,1,0:T(8,128)}, u32[]{:S(2)}, u32[]{:S(2)}) async-start(f32[8,48,4096]{2,1,0:T(8,128)} %pack.2), calls=%async_computation.1 | async-start | bytes 12582912 | tf_op jit(solution)/shard_map/all_to_all | solution.py:409
  14.5 9.8 %collective-permute-start = (f32[32,2048]{1,0:T(8,128)S(1)}, f32[32,2048]{1,0:T(8,128)S(1)}, u32[]{:S(2)}, u32[]{:S(2)}) collective-permute-start(f32[32,2048]{1,0:T(8,128)S(1)} %get-tuple-element.55), channel_id=1, source_target_pairs={{0,8},{1,9},{2,10},{3,11},{4,12},{5,13},{6,14},{7,15},{8,0},{9,1},... | collective-permute-start | bytes 786440 | tf_op jit(solution)/shard_map/ppermute | solution.py:393
  17.9 15.4 %collective-permute-start.2 = (f32[32,2048]{1,0:T(8,128)S(1)}, f32[32,2048]{1,0:T(8,128)S(1)}, u32[]{:S(2)}, u32[]{:S(2)}) collective-permute-start(f32[32,2048]{1,0:T(8,128)S(1)} %get-tuple-element.58), channel_id=1, source_target_pairs={{0,8},{1,9},{2,10},{3,11},{4,12},{5,13},{6,14},{7,15},{8,0},{9,1},... | collective-permute-start | bytes 786440 | tf_op jit(solution)/shard_map/ppermute | solution.py:393
  21.1 12.3 %collective-permute-start.4 = (f32[32,2048]{1,0:T(8,128)S(1)}, f32[32,2048]{1,0:T(8,128)S(1)}, u32[]{:S(2)}, u32[]{:S(2)}) collective-permute-start(f32[32,2048]{1,0:T(8,128)S(1)} %get-tuple-element.53), channel_id=1, source_target_pairs={{0,1},{1,0},{2,3},{3,2},{4,5},{5,4},{6,7},{7,6},{8,16},{9,17},{10,... | collective-permute-start | bytes 786440 | tf_op jit(solution)/shard_map/ppermute | solution.py:393
  25.0 11.0 %collective-permute-start.6 = (f32[32,2048]{1,0:T(8,128)S(1)}, f32[32,2048]{1,0:T(8,128)S(1)}, u32[]{:S(2)}, u32[]{:S(2)}) collective-permute-start(f32[32,2048]{1,0:T(8,128)S(1)} %get-tuple-element.56), channel_id=1, source_target_pairs={{0,1},{1,0},{2,3},{3,2},{4,5},{5,4},{6,7},{7,6},{8,16},{9,17},{10,... | collective-permute-start | bytes 786440 | tf_op jit(solution)/shard_map/ppermute | solution.py:393
  25.0 10.9 %collective-permute-start.3 = (f32[32,2048]{1,0:T(8,128)S(1)}, f32[32,2048]{1,0:T(8,128)S(1)}, u32[]{:S(2)}, u32[]{:S(2)}) collective-permute-start(f32[32,2048]{1,0:T(8,128)S(1)} %get-tuple-element.59), channel_id=1, source_target_pairs={{0,8},{1,9},{2,10},{3,11},{4,12},{5,13},{6,14},{7,15},{8,0},{9,1},... | collective-permute-start | bytes 786440 | tf_op jit(solution)/shard_map/ppermute | solution.py:393
  34.1 8.4 %collective-permute-start.5 = (f32[32,2048]{1,0:T(8,128)S(1)}, f32[32,2048]{1,0:T(8,128)S(1)}, u32[]{:S(2)}, u32[]{:S(2)}) collective-permute-start(f32[32,2048]{1,0:T(8,128)S(1)} %get-tuple-element.61), channel_id=1, source_target_pairs={{0,8},{1,9},{2,10},{3,11},{4,12},{5,13},{6,14},{7,15},{8,0},{9,1},... | collective-permute-start | bytes 786440 | tf_op jit(solution)/shard_map/ppermute | solution.py:393
  34.2 8.2 %collective-permute-start.8 = (f32[32,2048]{1,0:T(8,128)S(1)}, f32[32,2048]{1,0:T(8,128)S(1)}, u32[]{:S(2)}, u32[]{:S(2)}) collective-permute-start(f32[32,2048]{1,0:T(8,128)S(1)} %get-tuple-element.62), channel_id=1, source_target_pairs={{0,1},{1,0},{2,3},{3,2},{4,5},{5,4},{6,7},{7,6},{8,16},{9,17},{10,... | collective-permute-start | bytes 786440 | tf_op jit(solution)/shard_map/ppermute | solution.py:393
  36.7 11.4 %collective-permute-start.7 = (f32[32,2048]{1,0:T(8,128)S(1)}, f32[32,2048]{1,0:T(8,128)S(1)}, u32[]{:S(2)}, u32[]{:S(2)}) collective-permute-start(f32[32,2048]{1,0:T(8,128)S(1)} %get-tuple-element.64), channel_id=1, source_target_pairs={{0,8},{1,9},{2,10},{3,11},{4,12},{5,13},{6,14},{7,15},{8,0},{9,1},... | collective-permute-start | bytes 786440 | tf_op jit(solution)/shard_map/ppermute | solution.py:393
  39.4 8.6 %collective-permute-start.10 = (f32[32,2048]{1,0:T(8,128)S(1)}, f32[32,2048]{1,0:T(8,128)S(1)}, u32[]{:S(2)}, u32[]{:S(2)}) collective-permute-start(f32[32,2048]{1,0:T(8,128)S(1)} %get-tuple-element.65), channel_id=1, source_target_pairs={{0,1},{1,0},{2,3},{3,2},{4,5},{5,4},{6,7},{7,6},{8,16},{9,17},{10,... | collective-permute-start | bytes 786440 | tf_op jit(solution)/shard_map/ppermute | solution.py:393
  43.1 10.6 %collective-permute-start.9 = (f32[32,2048]{1,0:T(8,128)S(1)}, f32[32,2048]{1,0:T(8,128)S(1)}, u32[]{:S(2)}, u32[]{:S(2)}) collective-permute-start(f32[32,2048]{1,0:T(8,128)S(1)} %get-tuple-element.67), channel_id=1, source_target_pairs={{0,8},{1,9},{2,10},{3,11},{4,12},{5,13},{6,14},{7,15},{8,0},{9,1},... | collective-permute-start | bytes 786440 | tf_op jit(solution)/shard_map/ppermute | solution.py:393
  46.1 7.5 %collective-permute-start.12 = (f32[32,2048]{1,0:T(8,128)S(1)}, f32[32,2048]{1,0:T(8,128)S(1)}, u32[]{:S(2)}, u32[]{:S(2)}) collective-permute-start(f32[32,2048]{1,0:T(8,128)S(1)} %get-tuple-element.68), channel_id=1, source_target_pairs={{0,1},{1,0},{2,3},{3,2},{4,5},{5,4},{6,7},{7,6},{8,16},{9,17},{10,... | collective-permute-start | bytes 786440 | tf_op jit(solution)/shard_map/ppermute | solution.py:393
  48.7 10.5 %collective-permute-start.11 = (f32[32,2048]{1,0:T(8,128)S(1)}, f32[32,2048]{1,0:T(8,128)S(1)}, u32[]{:S(2)}, u32[]{:S(2)}) collective-permute-start(f32[32,2048]{1,0:T(8,128)S(1)} %get-tuple-element.70), channel_id=1, source_target_pairs={{0,8},{1,9},{2,10},{3,11},{4,12},{5,13},{6,14},{7,15},{8,0},{9,1},... | collective-permute-start | bytes 786440 | tf_op jit(solution)/shard_map/ppermute | solution.py:393
  51.8 7.5 %collective-permute-start.14 = (f32[32,2048]{1,0:T(8,128)S(1)}, f32[32,2048]{1,0:T(8,128)S(1)}, u32[]{:S(2)}, u32[]{:S(2)}) collective-permute-start(f32[32,2048]{1,0:T(8,128)S(1)} %get-tuple-element.71), channel_id=1, source_target_pairs={{0,1},{1,0},{2,3},{3,2},{4,5},{5,4},{6,7},{7,6},{8,16},{9,17},{10,... | collective-permute-start | bytes 786440 | tf_op jit(solution)/shard_map/ppermute | solution.py:393
  54.3 10.5 %collective-permute-start.13 = (f32[32,2048]{1,0:T(8,128)S(1)}, f32[32,2048]{1,0:T(8,128)S(1)}, u32[]{:S(2)}, u32[]{:S(2)}) collective-permute-start(f32[32,2048]{1,0:T(8,128)S(1)} %get-tuple-element.73), channel_id=1, source_target_pairs={{0,8},{1,9},{2,10},{3,11},{4,12},{5,13},{6,14},{7,15},{8,0},{9,1},... | collective-permute-start | bytes 786440 | tf_op jit(solution)/shard_map/ppermute | solution.py:393
  57.4 7.5 %collective-permute-start.16 = (f32[32,2048]{1,0:T(8,128)S(1)}, f32[32,2048]{1,0:T(8,128)S(1)}, u32[]{:S(2)}, u32[]{:S(2)}) collective-permute-start(f32[32,2048]{1,0:T(8,128)S(1)} %get-tuple-element.74), channel_id=1, source_target_pairs={{0,1},{1,0},{2,3},{3,2},{4,5},{5,4},{6,7},{7,6},{8,16},{9,17},{10,... | collective-permute-start | bytes 786440 | tf_op jit(solution)/shard_map/ppermute | solution.py:393
  60.0 10.5 %collective-permute-start.15 = (f32[32,2048]{1,0:T(8,128)S(1)}, f32[32,2048]{1,0:T(8,128)S(1)}, u32[]{:S(2)}, u32[]{:S(2)}) collective-permute-start(f32[32,2048]{1,0:T(8,128)S(1)} %get-tuple-element.76), channel_id=1, source_target_pairs={{0,8},{1,9},{2,10},{3,11},{4,12},{5,13},{6,14},{7,15},{8,0},{9,1},... | collective-permute-start | bytes 786440 | tf_op jit(solution)/shard_map/ppermute | solution.py:393
  63.0 7.5 %collective-permute-start.18 = (f32[32,2048]{1,0:T(8,128)S(1)}, f32[32,2048]{1,0:T(8,128)S(1)}, u32[]{:S(2)}, u32[]{:S(2)}) collective-permute-start(f32[32,2048]{1,0:T(8,128)S(1)} %get-tuple-element.77), channel_id=1, source_target_pairs={{0,1},{1,0},{2,3},{3,2},{4,5},{5,4},{6,7},{7,6},{8,16},{9,17},{10,... | collective-permute-start | bytes 786440 | tf_op jit(solution)/shard_map/ppermute | solution.py:393
  65.6 9.7 %collective-permute-start.17 = (f32[32,2048]{1,0:T(8,128)S(1)}, f32[32,2048]{1,0:T(8,128)S(1)}, u32[]{:S(2)}, u32[]{:S(2)}) collective-permute-start(f32[32,2048]{1,0:T(8,128)S(1)} %get-tuple-element.79), channel_id=1, source_target_pairs={{0,8},{1,9},{2,10},{3,11},{4,12},{5,13},{6,14},{7,15},{8,0},{9,1},... | collective-permute-start | bytes 786440 | tf_op jit(solution)/shard_map/ppermute | solution.py:393
  71.2 11.3 %collective-permute-start.22 = (f32[32,2048]{1,0:T(8,128)S(1)}, f32[32,2048]{1,0:T(8,128)S(1)}, u32[]{:S(2)}, u32[]{:S(2)}) collective-permute-start(f32[32,2048]{1,0:T(8,128)S(1)} %get-tuple-element.83), channel_id=1, source_target_pairs={{0,1},{1,0},{2,3},{3,2},{4,5},{5,4},{6,7},{7,6},{8,16},{9,17},{10,... | collective-permute-start | bytes 786440 | tf_op jit(solution)/shard_map/ppermute | solution.py:393
  71.3 11.2 %collective-permute-start.19 = (f32[32,2048]{1,0:T(8,128)S(1)}, f32[32,2048]{1,0:T(8,128)S(1)}, u32[]{:S(2)}, u32[]{:S(2)}) collective-permute-start(f32[32,2048]{1,0:T(8,128)S(1)} %get-tuple-element.82), channel_id=1, source_target_pairs={{0,8},{1,9},{2,10},{3,11},{4,12},{5,13},{6,14},{7,15},{8,0},{9,1},... | collective-permute-start | bytes 786440 | tf_op jit(solution)/shard_map/ppermute | solution.py:393
  76.0 9.8 %collective-permute-start.21 = (f32[32,2048]{1,0:T(8,128)S(1)}, f32[32,2048]{1,0:T(8,128)S(1)}, u32[]{:S(2)}, u32[]{:S(2)}) collective-permute-start(f32[32,2048]{1,0:T(8,128)S(1)} %get-tuple-element.85), channel_id=1, source_target_pairs={{0,8},{1,9},{2,10},{3,11},{4,12},{5,13},{6,14},{7,15},{8,0},{9,1},... | collective-permute-start | bytes 786440 | tf_op jit(solution)/shard_map/ppermute | solution.py:393
  92.2 37.1 %all-to-all-start = ((f32[8,16,4096]{2,1,0:T(8,128)}), f32[8,16,4096]{2,1,0:T(8,128)}, u32[]{:S(2)}, u32[]{:S(2)}) async-start(f32[8,16,4096]{2,1,0:T(8,128)} %pack.3), calls=%async_computation | async-start | bytes 4194304 | tf_op jit(solution)/shard_map/all_to_all | solution.py:418
  104.3 22.7 %collective-permute-start.35 = (f32[96,384]{1,0:T(8,128)S(1)}, f32[96,384]{1,0:T(8,128)S(1)}, u32[]{:S(2)}, u32[]{:S(2)}) collective-permute-start(f32[96,384]{1,0:T(8,128)S(1)} %add.20), channel_id=1, source_target_pairs={{0,6},{1,7},{2,4},{3,5},{4,2},{5,3},{6,0},{7,1},{8,14},{9,15},{10,... | collective-permute-start | bytes 442376 | tf_op jit(solution)/shard_map/ppermute | solution.py:368
  107.2 21.9 %collective-permute-start.34 = (f32[96,384]{1,0:T(8,128)S(1)}, f32[96,384]{1,0:T(8,128)S(1)}, u32[]{:S(2)}, u32[]{:S(2)}) collective-permute-start(f32[96,384]{1,0:T(8,128)S(1)} %add.20), channel_id=1, source_target_pairs={{0,4},{1,5},{2,6},{3,7},{4,0},{5,1},{6,2},{7,3},{8,12},{9,13},{10,... | collective-permute-start | bytes 442376 | tf_op jit(solution)/shard_map/ppermute | solution.py:368
  107.7 21.5 %collective-permute-start.33 = (f32[96,384]{1,0:T(8,128)S(1)}, f32[96,384]{1,0:T(8,128)S(1)}, u32[]{:S(2)}, u32[]{:S(2)}) collective-permute-start(f32[96,384]{1,0:T(8,128)S(1)} %add.20), channel_id=1, source_target_pairs={{0,2},{1,3},{2,0},{3,1},{4,6},{5,7},{6,4},{7,5},{8,10},{9,11},{10,... | collective-permute-start | bytes 442376 | tf_op jit(solution)/shard_map/ppermute | solution.py:368
  109.1 24.1 %collective-permute-start.31 = (f32[32,512]{1,0:T(8,128)S(1)}, f32[32,512]{1,0:T(8,128)S(1)}, u32[]{:S(2)}, u32[]{:S(2)}) collective-permute-start(f32[32,512]{1,0:T(8,128)S(1)} %add.19.refs_0_), channel_id=1, source_target_pairs={{0,6},{1,7},{2,4},{3,5},{4,2},{5,3},{6,0},{7,1},{8,14},{9,15},{10,... | collective-permute-start | bytes 196616 | tf_op jit(solution)/shard_map/ppermute | solution.py:368
  112.0 21.2 %collective-permute-start.30 = (f32[32,512]{1,0:T(8,128)S(1)}, f32[32,512]{1,0:T(8,128)S(1)}, u32[]{:S(2)}, u32[]{:S(2)}) collective-permute-start(f32[32,512]{1,0:T(8,128)S(1)} %add.19.refs_0_), channel_id=1, source_target_pairs={{0,4},{1,5},{2,6},{3,7},{4,0},{5,1},{6,2},{7,3},{8,12},{9,13},{10,... | collective-permute-start | bytes 196616 | tf_op jit(solution)/shard_map/ppermute | solution.py:368
  129.2 14.1 %collective-permute-start.36 = (f32[96,384]{1,0:T(8,128)S(1)}, f32[96,384]{1,0:T(8,128)S(1)}, u32[]{:S(2)}, u32[]{:S(2)}) collective-permute-start(f32[96,384]{1,0:T(8,128)S(1)} %add_add_fusion.refs_0_), channel_id=1, source_target_pairs={{0,1},{1,0},{2,3},{3,2},{4,5},{5,4},{6,7},{7,6},{8,9},{9,8},{10,11... | collective-permute-start | bytes 442376 | tf_op jit(solution)/shard_map/ppermute | solution.py:368
  139.8 13.2 %collective-permute-start.27 = (f32[64,384]{1,0:T(8,128)S(1)}, f32[64,384]{1,0:T(8,128)S(1)}, u32[]{:S(2)}, u32[]{:S(2)}) collective-permute-start(f32[64,384]{1,0:T(8,128)S(1)} %add.18.refs_0_), channel_id=1, source_target_pairs={{0,6},{1,7},{2,4},{3,5},{4,2},{5,3},{6,0},{7,1},{8,14},{9,15},{10,... | collective-permute-start | bytes 294920 | tf_op jit(solution)/shard_map/ppermute | solution.py:368
  141.3 11.6 %collective-permute-start.26 = (f32[64,384]{1,0:T(8,128)S(1)}, f32[64,384]{1,0:T(8,128)S(1)}, u32[]{:S(2)}, u32[]{:S(2)}) collective-permute-start(f32[64,384]{1,0:T(8,128)S(1)} %add.18.refs_0_), channel_id=1, source_target_pairs={{0,4},{1,5},{2,6},{3,7},{4,0},{5,1},{6,2},{7,3},{8,12},{9,13},{10,... | collective-permute-start | bytes 294920 | tf_op jit(solution)/shard_map/ppermute | solution.py:368
  142.6 10.3 %collective-permute-start.25 = (f32[64,384]{1,0:T(8,128)S(1)}, f32[64,384]{1,0:T(8,128)S(1)}, u32[]{:S(2)}, u32[]{:S(2)}) collective-permute-start(f32[64,384]{1,0:T(8,128)S(1)} %add.18.refs_0_), channel_id=1, source_target_pairs={{0,2},{1,3},{2,0},{3,1},{4,6},{5,7},{6,4},{7,5},{8,10},{9,11},{10,... | collective-permute-start | bytes 294920 | tf_op jit(solution)/shard_map/ppermute | solution.py:368
  (18 other events, 127.9 us)

commit v2 on v1

--- a/solution.py
+++ b/solution.py
@@ -9,9 +9,9 @@
 
 HIGHEST = lax.Precision.HIGHEST
 SMALL_LIMIT = 44 * 1024 * 1024
-VMEM_LIMIT = 52 * 1024 * 1024
+VMEM_LIMIT = 40 * 1024 * 1024
 LARGE_LIMIT = 58 * 1024 * 1024
-TAIL = 16
+COLUMNS = 512
 SPLITS = 2
 
 
@@ -39,9 +39,8 @@
     return lax.optimization_barrier((x, *tokens))[0]
 
 
-def params(dims=0, limit=VMEM_LIMIT):
-    semantics = ("arbitrary",) * dims if dims else None
-    return pltpu.CompilerParams(dimension_semantics=semantics, vmem_limit_bytes=limit)
+def params(limit=VMEM_LIMIT):
+    return pltpu.CompilerParams(vmem_limit_bytes=limit)
 
 
 def cost(flops, nbytes):
@@ -53,17 +52,19 @@
 VMEM = pl.BlockSpec(memory_space=pltpu.VMEM)
 
 
-def pack(here, x, first, rows, n_wide, apart):
-    ncols = x.shape[1] // n_wide
-
-    def kernel(here_ref, x_ref, *refs):
-        outs, (held, in_sems, out_sems) = refs[:-3], refs[-3:]
-        into, out_of = [], []
-        for k in range(n_wide):
-            start = pl.multiple_of((here_ref[1] ^ k) * ncols, ncols) if apart else k * ncols
-            source = x_ref.at[pl.ds(first, rows), pl.ds(start, ncols)]
-            into.append(pltpu.make_async_copy(source, held.at[k], in_sems.at[k]))
-            out_of.append(pltpu.make_async_copy(held.at[k], outs[k] if apart else outs[0].at[k], out_sems.at[k]))
+def in_hbm(x):
+    return pltpu.with_memory_space_constraint(x, pltpu.HBM)
+
+
+def pack(x, n_wide):
+    rows, order = x.shape
+    ncols = order // n_wide
+
+    def kernel(x_ref, out_ref, held, in_sems, out_sems):
+        into = [
+            pltpu.make_async_copy(x_ref.at[:, pl.ds(k * ncols, ncols)], held.at[k], in_sems.at[k]) for k in range(n_wide)
+        ]
+        out_of = [pltpu.make_async_copy(held.at[k], out_ref.at[k], out_sems.at[k]) for k in range(n_wide)]
         for copy in into:
             copy.start()
         for k in range(n_wide):
@@ -72,21 +73,20 @@
         for copy in out_of:
             copy.wait()
 
-    shapes = [(rows, ncols)] * n_wide if apart else [(n_wide, rows, ncols)]
-    return pl.pallas_call(
-        kernel,
-        out_shape=[jax.ShapeDtypeStruct(shape, jnp.float32) for shape in shapes],
-        in_specs=[SMEM, ANY],
-        out_specs=[ANY] * len(shapes),
+    return pl.pallas_call(
+        kernel,
+        out_shape=jax.ShapeDtypeStruct((n_wide, rows, ncols), jnp.float32),
+        in_specs=[ANY],
+        out_specs=ANY,
         scratch_shapes=[
             pltpu.VMEM((n_wide, rows, ncols), jnp.float32),
             pltpu.SemaphoreType.DMA((n_wide,)),
             pltpu.SemaphoreType.DMA((n_wide,)),
         ],
         compiler_params=params(limit=LARGE_LIMIT),
-        cost_estimate=cost(0, 8 * rows * x.shape[1]),
+        cost_estimate=cost(0, 8 * rows * order),
         name="pack",
-    )(here, x)
+    )(in_hbm(x))
 
 
 def plan(place_ref, slots, n_rows):
@@ -233,10 +233,6 @@
     )(*cross, factors, *vecs)
 
 
-def column_block(rows, ncols, cols):
-    return cols if rows > 128 and ncols % cols == 0 else ncols
-
-
 def fold(w):
     half = w.shape[0] // 2
     return jnp.concatenate([w[:half], w[half:]], axis=1)
@@ -247,121 +243,78 @@
     return jnp.concatenate([w[:, :height], w[:, height:]], axis=0)
 
 
-def inner_products(here, x, vecs, split):
-    apart = isinstance(x, list)
-    pieces = x if apart else [x]
-    lead = len(pieces) if apart else x.shape[0]
-    rows, ncols = pieces[0].shape[-2:]
+def column_blocks(ncols):
+    cols = COLUMNS if ncols % COLUMNS == 0 else ncols
+    return [pl.ds(start, cols) for start in range(0, ncols, cols)]
+
+
+def inner_products(here, x, vecs):
+    lead, rows, ncols = x.shape
     height = vecs[0].shape[0]
-    cols = column_block(lead * rows, ncols, 1024)
-    blocks = ncols // cols
-    parts = 2 if split else 1
-    half = lead * rows // parts
-
-    def kernel(here_ref, *refs):
-        x_refs, (high_ref, low_ref), outs, total = refs[:len(pieces)], refs[len(pieces):len(pieces) + 2], refs[-1 - parts:-1], refs[-1]
-        block = pl.program_id(0)
-        here_cols = pl.ds(pl.multiple_of(block * cols, cols), cols) if blocks > 1 else slice(None)
-        values = jnp.concatenate([ref[...] for ref in x_refs], axis=0).reshape(lead * rows, cols)
-        part = dot3(halves(values), (high_ref[:, here_cols], low_ref[:, here_cols]), ((1,), (1,)))
-
-        @pl.when(block == 0)
-        def _():
-            total[...] = part
-
-        @pl.when(block > 0)
-        def _():
-            total[...] += part
-
-        @pl.when(block == blocks - 1)
-        def _():
-            if apart:
-                value = total[...]
-                for k in range(lead):
-                    total[pl.ds(pl.multiple_of((here_ref[1] ^ k) * rows, 8), rows), :] = value[k * rows:(k + 1) * rows]
-            core = lax.rem(here_ref[1], 2)
-            for i, out in enumerate(outs):
-                start = pl.multiple_of((core ^ i) * half, 8) if split else 0
-                out[...] = fold(total[pl.ds(start, half), :])
-
-    block_shape, index = ((rows, cols), lambda c: (0, c)) if apart else ((lead, rows, cols), lambda c: (0, 0, c))
-    return pl.pallas_call(
-        kernel,
-        out_shape=[jax.ShapeDtypeStruct((half // 2, 2 * height), jnp.float32)] * parts,
-        grid=(blocks,),
-        in_specs=[SMEM] + [pl.BlockSpec(block_shape, index)] * len(pieces) + [VMEM, VMEM],
-        out_specs=[pl.BlockSpec((half // 2, 2 * height), lambda c: (0, 0))] * parts,
-        scratch_shapes=[pltpu.VMEM((lead * rows, height), jnp.float32)],
-        compiler_params=params(1),
+    half = lead * rows // 2
+    blocks = column_blocks(ncols)
+
+    def kernel(here_ref, x_ref, high_ref, low_ref, mine_ref, theirs_ref, held, total, sems):
+        copies = [pltpu.make_async_copy(x_ref.at[:, :, at], held.at[:, :, at], sems.at[i]) for i, at in enumerate(blocks)]
+        for copy in copies:
+            copy.start()
+        for i, at in enumerate(blocks):
+            copies[i].wait()
+            block = held[:, :, at].reshape(lead * rows, at.size)
+            part = dot3(halves(block), (high_ref[:, at], low_ref[:, at]), ((1,), (1,)))
+            total[...] = part if i == 0 else total[...] + part
+        core = lax.rem(here_ref[1], 2)
+        mine_ref[...] = fold(total[pl.ds(pl.multiple_of(core * half, 8), half), :])
+        theirs_ref[...] = fold(total[pl.ds(pl.multiple_of((1 - core) * half, 8), half), :])
+
+    return pl.pallas_call(
+        kernel,
+        out_shape=[jax.ShapeDtypeStruct((half // 2, 2 * height), jnp.float32)] * 2 + [pltpu.VMEM(x.shape, jnp.float32)],
+        in_specs=[SMEM, ANY, VMEM, VMEM],
+        out_specs=[VMEM] * 3,
+        scratch_shapes=[pltpu.VMEM((lead * rows, height), jnp.float32), pltpu.SemaphoreType.DMA((len(blocks),))],
+        compiler_params=params(),
         cost_estimate=cost(6 * lead * rows * ncols * height, 4 * lead * rows * ncols),
         name="inner_products",
-    )(here, *pieces, *vecs)
-
-
-def update(here, x, sums, other, changes, out, first, total):
-    apart = isinstance(x, list)
-    pieces = x if apart else [x]
-    lead = len(pieces) if apart else x.shape[0]
-    rows, ncols = pieces[0].shape[-2:]
-    n_sums = len(sums)
+    )(here, in_hbm(x), *vecs)
+
+
+def update(here, x, mine, theirs, changes):
+    lead, rows, ncols = x.shape
     height = changes[0].shape[0]
-    cols = column_block(lead * rows, ncols, 512)
-    blocks = ncols // cols
     half = lead * rows // 2
-
-    def kernel(here_ref, *refs):
-        sum_refs, x_refs = refs[:n_sums], refs[n_sums:n_sums + len(pieces)]
-        high_ref, low_ref, *more = refs[n_sums + len(pieces):-4]
-        out_ref, w_ref, w_high, w_low = refs[-4:]
-        block = pl.program_id(0)
-
-        @pl.when(block == 0)
-        def _():
-            w = unfold(sum([ref[...] for ref in sum_refs[1:]], sum_refs[0][...]))
-            if other is not None:
-                core = lax.rem(here_ref[1], 2)
-                w_ref[pl.ds(pl.multiple_of(core * half, 8), half), :] = w
-                w_ref[pl.ds(pl.multiple_of((1 - core) * half, 8), half), :] = unfold(more[0][...])
-                w = w_ref[...]
-            if apart:
-                w_ref[...] = w
-                w = jnp.concatenate(
-                    [w_ref[pl.ds(pl.multiple_of((here_ref[1] ^ k) * rows, 8), rows), :] for k in range(lead)], axis=0
-                )
-            w_high[...], w_low[...] = halves(w)
-
-        here_cols = pl.ds(pl.multiple_of(block * cols, cols), cols) if blocks > 1 else slice(None)
-        change = dot3((w_high[...], w_low[...]), (high_ref[:, here_cols], low_ref[:, here_cols]), ((1,), (0,)))
-        if apart:
-            for k in range(lead):
-                out_ref[pl.ds(here_ref[1] ^ k, 1)] = (x_refs[k][...] - change[k * rows:(k + 1) * rows])[None]
-        else:
-            out_ref[...] = (x_refs[0][...].reshape(lead * rows, cols) - change).reshape(lead, rows, cols)
-
-    block_shape, index = ((rows, cols), lambda c: (0, c)) if apart else ((lead, rows, cols), lambda c: (0, 0, c))
-    operands = [here] + list(sums) + pieces + list(changes)
-    in_specs = [SMEM] + [VMEM] * n_sums + [pl.BlockSpec(block_shape, index)] * len(pieces) + [VMEM, VMEM]
-    if other is not None:
-        operands.append(other)
-        in_specs.append(VMEM)
-    aliases = {}
-    if out is not None:
-        aliases = {len(operands): 0}
-        operands.append(out)
-        in_specs.append(ANY)
-    return pl.pallas_call(
-        kernel,
-        out_shape=jax.ShapeDtypeStruct((lead, total, ncols), jnp.float32),
-        grid=(blocks,),
-        in_specs=in_specs,
-        out_specs=pl.BlockSpec((pl.Element(lead), pl.Element(rows), pl.Element(cols)), lambda c: (0, first, c * cols)),
-        scratch_shapes=[pltpu.VMEM((lead * rows, height), jnp.float32)]
-        + [pltpu.VMEM((lead * rows, height), jnp.bfloat16)] * 2,
-        input_output_aliases=aliases,
-        compiler_params=params(1),
+    blocks = column_blocks(ncols)
+    depth = min(2, len(blocks))
+
+    def kernel(here_ref, mine_ref, theirs_ref, x_ref, high_ref, low_ref, out_ref, w_ref, held, sems):
+        core = lax.rem(here_ref[1], 2)
+        w_ref[pl.ds(pl.multiple_of(core * half, 8), half), :] = unfold(mine_ref[...])
+        w_ref[pl.ds(pl.multiple_of((1 - core) * half, 8), half), :] = unfold(theirs_ref[...])
+        w = halves(w_ref[...])
+        copies = [pltpu.make_async_copy(held.at[i % depth], out_ref.at[:, :, at], sems.at[i]) for i, at in enumerate(blocks)]
+        for i, at in enumerate(blocks):
+            change = dot3(w, (high_ref[:, at], low_ref[:, at]), ((1,), (0,)))
+            if i >= depth:
+                copies[i - depth].wait()
+            held[i % depth] = x_ref[:, :, at] - change.reshape(lead, rows, at.size)
+            copies[i].start()
+        for copy in copies[-depth:]:
+            copy.wait()
+
+    return pl.pallas_call(
+        kernel,
+        out_shape=jax.ShapeDtypeStruct(x.shape, jnp.float32),
+        in_specs=[SMEM] + [VMEM] * 5,
+        out_specs=ANY,
+        scratch_shapes=[
+            pltpu.VMEM((lead * rows, height), jnp.float32),
+            pltpu.VMEM((depth, lead, rows, blocks[0].size), jnp.float32),
+            pltpu.SemaphoreType.DMA((len(blocks),)),
+        ],
+        compiler_params=params(),
         cost_estimate=cost(6 * lead * rows * ncols * height, 8 * lead * rows * ncols),
         name="update",
-    )(*operands)
+    )(here, mine, theirs, x, *changes)
 
 
 def swap(array, k, size):
@@ -392,41 +345,29 @@
                 pairs.append((z * n_wide + w, target))
         return lax.ppermute(array, ("row", "wide"), pairs)
 
-    tail = TAIL if rows % 8 == 0 and rows > TAIL else 0
-    bulk = rows - tail
-    if not tail:
-        early = lax.all_to_all(eigvec_t, "wide", split_axis=1, concat_axis=0, tiled=True)[None]
-
-    tokens = []
+    whole = rows % 8 == 0
+    if whole:
+        piece = pack(eigvec_t, n_wide)
+        x = lax.all_to_all(piece, "wide", split_axis=0, concat_axis=0, tiled=True)
+        tokens = [piece]
+    else:
+        x = lax.all_to_all(eigvec_t, "wide", split_axis=1, concat_axis=0, tiled=True)[None]
+        tokens = []
     for turn in range(turns):
         for part in range(SPLITS):
             evens, odds = streams[part]
             to_even, to_odd = feed(after(here, *tokens), block_place, householder, evens, odds, n_row, part, cols)
             tokens = [to_odd]
             streams[part] = (evens + [exchange(to_even, 0)], odds + [exchange(to_odd, 1)])
-            if (turn, part) == (0, 0) and tail:
-                piece, = pack(here, after(eigvec_t, to_odd), 0, bulk, n_wide, False)
-                early = lax.all_to_all(piece, "wide", split_axis=0, concat_axis=0, tiled=True)
-                tokens = [piece]
-            if (turn, part) == (1, 0) and tail:
-                piece, = pack(here, after(eigvec_t, to_odd), bulk, tail, n_wide, False)
-                tokens = [piece]
     evens = list(zip(*[stream[0] for stream in streams]))
     odds = list(zip(*[stream[1] for stream in streams]))
     high, low, gram = assemble(here, block_place, offsets, householder, evens, odds, n_row)
-    if tail:
-        late = lax.all_to_all(after(piece, gram), "wide", split_axis=0, concat_axis=0, tiled=True)
     cross = spread(gram + swap(gram, 1, n_wide), n_wide)
     changes = merge(cross, wy_factor, (high, low))
 
-    mine, theirs = inner_products(here, early, (high, low), True)
+    mine, theirs, x = inner_products(here, x, (high, low))
     mine = functools.reduce(jnp.add, spread(mine + swap(theirs, 1, n_wide), n_wide))
-    total = rows if tail else rows * n_wide
-    out = update(here, early, [mine], swap(mine, 1, n_wide), changes, None, 0, total)
-    if tail:
-        part, = inner_products(here, late, (high, low), False)
-        out = update(here, late, spread(part + swap(part, 1, n_wide), n_wide), None, changes, out, bulk, total)
-    return out.reshape(n_wide * rows, ncols)
+    return update(here, x, mine, swap(mine, 1, n_wide), changes).reshape(n_wide * rows, ncols)
 
 
 def solution(mesh):

time: 158 us -> 147 us (0.930)
  waiting for transfers between devices: 41.7 us -> 54.2 us
  Pallas kernels: 52.5 us -> 40.4 us
  starting transfers between devices: 59.2 us -> 52.1 us
  local copies, waits for them, and re-layouts: 3.47 us -> 0.02 us
    all_to_all x2 -> x1, waiting for transfers between devices: 0.01 us -> 17 us  [body(): x = lax.all_to_all(piece, 'wide', split_axis=0, concat_axis=0, tiled=True)]
    pallas_call x4 -> x2, Pallas kernels: 23.3 us -> 13.7 us  [the longest x1 7.28 us: update(): pl.pallas_call(kernel, out_shape=jax.ShapeDtypeStruct(x.shape, jnp.float3...]
    ppermute x13 -> x9, waiting for transfers between devices: 18.4 us -> 12.8 us  [swap(): return lax.ppermute(array, 'wide', [(i, i ^ k) for i in range(size)])]
    ppermute x13 -> x9, starting transfers between devices: 12.1 us -> 7.25 us  [swap(): return lax.ppermute(array, 'wide', [(i, i ^ k) for i in range(size)])]
    all_to_all x2 -> x1, starting transfers between devices: 9.84 us -> 5.31 us  [body(): x = lax.all_to_all(piece, 'wide', split_axis=0, concat_axis=0, tiled=True)]
    unnamed x22 -> x8, local copies, waits for them, and re-layouts: 3.47 us -> 0.02 us
    pallas_call x1, Pallas kernels: 6.51 us -> 3.46 us  [merge(): pl.pallas_call(kernel, out_shape=[jax.ShapeDtypeStruct((height, ncols), j...]
    ppermute x24, starting transfers between devices: 37.2 us -> 39.6 us  [exchange(): return lax.ppermute(array, ('row', 'wide'), pairs)]
  transfers between devices with their start and end apart: 39 -> 34, of which waited for: 15 -> 18; matrix products, arithmetic and copies ran while one was open for 0% -> 0% of each run, Pallas kernels for 26% -> 11%
where the time goes in v2:
time: 147 us
  waiting for transfers between devices  54.2 us (37%)
  starting transfers between devices  52.1 us (35%)
  Pallas kernels  40.4 us (27%)
    ppermute x24, starting transfers between devices, exchange(): return lax.ppermute(array, ('row', 'wide'), pairs)  39.6 us
    ppermute x24, waiting for transfers between devices, exchange(): return lax.ppermute(array, ('row', 'wide'), pairs)  24.4 us
    all_to_all x1, waiting for transfers between devices, body(): x = lax.all_to_all(piece, 'wide', split_axis=0, concat_axis=0, tiled=True)  17 us
    ppermute x9, waiting for transfers between devices, swap(): return lax.ppermute(array, 'wide', [(i, i ^ k) for i in range(size)])  12.8 us
    pallas_call x1, Pallas kernels, inner_products(): pl.pallas_call(kernel, out_shape=[jax.ShapeDtypeStruct((half // 2, 2 * he...  9.88 us
    pallas_call x12, Pallas kernels, feed(): pl.pallas_call(kernel, out_shape=[jax.ShapeDtypeStruct((width, cols), jnp...  8.07 us
    pallas_call x1, Pallas kernels, update(): pl.pallas_call(kernel, out_shape=jax.ShapeDtypeStruct(x.shape, jnp.float3...  7.28 us
    ppermute x9, starting transfers between devices, swap(): return lax.ppermute(array, 'wide', [(i, i ^ k) for i in range(size)])  7.25 us
  transfers between devices with their start and end apart: 34, of which 18 were waited for; matrix products, arithmetic and copies ran while one was open for 0% of the time, Pallas kernels for 11%

profile of v2, /device:TPU:0, one launch (start us, length us, event | category | flops | bytes accessed | tf_op | source)
XLA Modules:
  0.0 147.3 jit_solution(887586155190046837)
XLA Ops:
  0.0 6.4 %pack.1 = f32[8,64,4096]{2,1,0:T(8,128)} custom-call(f32[64,32768]{1,0:T(8,128)} %x_ref.1), custom_call_target="tpu_custom_call" | custom-call | bytes 16777216 | tf_op jit(solution)/shard_map/pack/pallas_call | solution.py:76
  6.5 5.3 %all-to-all-start = ((f32[8,64,4096]{2,1,0:T(8,128)}), f32[8,64,4096]{2,1,0:T(8,128)}, u32[]{:S(2)}, u32[]{:S(2)}) async-start(f32[8,64,4096]{2,1,0:T(8,128)} %pack.1), calls=%async_computation | async-start | bytes 16777216 | tf_op jit(solution)/shard_map/all_to_all | solution.py:351
  12.5 2.9 %collective-permute-start = (f32[32,2048]{1,0:T(8,128)S(1)}, f32[32,2048]{1,0:T(8,128)S(1)}, u32[]{:S(2)}, u32[]{:S(2)}) collective-permute-start(f32[32,2048]{1,0:T(8,128)S(1)} %get-tuple-element.50), channel_id=1, source_target_pairs={{0,8},{1,9},{2,10},{3,11},{4,12},{5,13},{6,14},{7,15},{8,0},{9,1},... | collective-permute-start | bytes 786440 | tf_op jit(solution)/shard_map/ppermute | solution.py:346
  16.1 3.1 %collective-permute-start.1 = (f32[32,2048]{1,0:T(8,128)S(1)}, f32[32,2048]{1,0:T(8,128)S(1)}, u32[]{:S(2)}, u32[]{:S(2)}) collective-permute-start(f32[32,2048]{1,0:T(8,128)S(1)} %get-tuple-element.53), channel_id=1, source_target_pairs={{0,8},{1,9},{2,10},{3,11},{4,12},{5,13},{6,14},{7,15},{8,0},{9,1},... | collective-permute-start | bytes 786440 | tf_op jit(solution)/shard_map/ppermute | solution.py:346
  19.3 3.3 %collective-permute-done.refs_0_ = f32[32,2048]{1,0:T(8,128)S(1)} collective-permute-done((f32[32,2048]{1,0:T(8,128)S(1)}, f32[32,2048]{1,0:T(8,128)S(1)}, u32[]{:S(2)}, u32[]{:S(2)}) %collective-permute-start) | collective-permute-done | bytes 262176 | tf_op jit(solution)/shard_map/ppermute | solution.py:346
  23.2 3.2 %collective-permute-start.3 = (f32[32,2048]{1,0:T(8,128)S(1)}, f32[32,2048]{1,0:T(8,128)S(1)}, u32[]{:S(2)}, u32[]{:S(2)}) collective-permute-start(f32[32,2048]{1,0:T(8,128)S(1)} %get-tuple-element.56), channel_id=1, source_target_pairs={{0,8},{1,9},{2,10},{3,11},{4,12},{5,13},{6,14},{7,15},{8,0},{9,1},... | collective-permute-start | bytes 786440 | tf_op jit(solution)/shard_map/ppermute | solution.py:346
  26.4 1.8 %collective-permute-done.1.refs_0_.refs_1_ = f32[32,2048]{1,0:T(8,128)S(1)} collective-permute-done((f32[32,2048]{1,0:T(8,128)S(1)}, f32[32,2048]{1,0:T(8,128)S(1)}, u32[]{:S(2)}, u32[]{:S(2)}) %collective-permute-start.1) | collective-permute-done | bytes 262176 | tf_op jit(solution)/shard_map/ppermute | solution.py:346
  28.9 3.2 %collective-permute-start.5 = (f32[32,2048]{1,0:T(8,128)S(1)}, f32[32,2048]{1,0:T(8,128)S(1)}, u32[]{:S(2)}, u32[]{:S(2)}) collective-permute-start(f32[32,2048]{1,0:T(8,128)S(1)} %get-tuple-element.59), channel_id=1, source_target_pairs={{0,8},{1,9},{2,10},{3,11},{4,12},{5,13},{6,14},{7,15},{8,0},{9,1},... | collective-permute-start | bytes 786440 | tf_op jit(solution)/shard_map/ppermute | solution.py:346
  32.0 1.8 %collective-permute-done.3.refs_1_.refs_2_ = f32[32,2048]{1,0:T(8,128)S(1)} collective-permute-done((f32[32,2048]{1,0:T(8,128)S(1)}, f32[32,2048]{1,0:T(8,128)S(1)}, u32[]{:S(2)}, u32[]{:S(2)}) %collective-permute-start.3) | collective-permute-done | bytes 262176 | tf_op jit(solution)/shard_map/ppermute | solution.py:346
  34.5 3.2 %collective-permute-start.7 = (f32[32,2048]{1,0:T(8,128)S(1)}, f32[32,2048]{1,0:T(8,128)S(1)}, u32[]{:S(2)}, u32[]{:S(2)}) collective-permute-start(f32[32,2048]{1,0:T(8,128)S(1)} %get-tuple-element.62), channel_id=1, source_target_pairs={{0,8},{1,9},{2,10},{3,11},{4,12},{5,13},{6,14},{7,15},{8,0},{9,1},... | collective-permute-start | bytes 786440 | tf_op jit(solution)/shard_map/ppermute | solution.py:346
  37.6 1.8 %collective-permute-done.5.refs_1_.refs_3_ = f32[32,2048]{1,0:T(8,128)S(1)} collective-permute-done((f32[32,2048]{1,0:T(8,128)S(1)}, f32[32,2048]{1,0:T(8,128)S(1)}, u32[]{:S(2)}, u32[]{:S(2)}) %collective-permute-start.5) | collective-permute-done | bytes 262176 | tf_op jit(solution)/shard_map/ppermute | solution.py:346
  40.1 3.2 %collective-permute-start.9 = (f32[32,2048]{1,0:T(8,128)S(1)}, f32[32,2048]{1,0:T(8,128)S(1)}, u32[]{:S(2)}, u32[]{:S(2)}) collective-permute-start(f32[32,2048]{1,0:T(8,128)S(1)} %get-tuple-element.65), channel_id=1, source_target_pairs={{0,8},{1,9},{2,10},{3,11},{4,12},{5,13},{6,14},{7,15},{8,0},{9,1},... | collective-permute-start | bytes 786440 | tf_op jit(solution)/shard_map/ppermute | solution.py:346
  43.3 1.8 %collective-permute-done.7.refs_2_.refs_4_ = f32[32,2048]{1,0:T(8,128)S(1)} collective-permute-done((f32[32,2048]{1,0:T(8,128)S(1)}, f32[32,2048]{1,0:T(8,128)S(1)}, u32[]{:S(2)}, u32[]{:S(2)}) %collective-permute-start.7) | collective-permute-done | bytes 262176 | tf_op jit(solution)/shard_map/ppermute | solution.py:346
  45.7 3.2 %collective-permute-start.11 = (f32[32,2048]{1,0:T(8,128)S(1)}, f32[32,2048]{1,0:T(8,128)S(1)}, u32[]{:S(2)}, u32[]{:S(2)}) collective-permute-start(f32[32,2048]{1,0:T(8,128)S(1)} %get-tuple-element.68), channel_id=1, source_target_pairs={{0,8},{1,9},{2,10},{3,11},{4,12},{5,13},{6,14},{7,15},{8,0},{9,1},... | collective-permute-start | bytes 786440 | tf_op jit(solution)/shard_map/ppermute | solution.py:346
  48.9 1.8 %collective-permute-done.9.refs_2_.refs_5_ = f32[32,2048]{1,0:T(8,128)S(1)} collective-permute-done((f32[32,2048]{1,0:T(8,128)S(1)}, f32[32,2048]{1,0:T(8,128)S(1)}, u32[]{:S(2)}, u32[]{:S(2)}) %collective-permute-start.9) | collective-permute-done | bytes 262176 | tf_op jit(solution)/shard_map/ppermute | solution.py:346
  51.3 3.2 %collective-permute-start.13 = (f32[32,2048]{1,0:T(8,128)S(1)}, f32[32,2048]{1,0:T(8,128)S(1)}, u32[]{:S(2)}, u32[]{:S(2)}) collective-permute-start(f32[32,2048]{1,0:T(8,128)S(1)} %get-tuple-element.71), channel_id=1, source_target_pairs={{0,8},{1,9},{2,10},{3,11},{4,12},{5,13},{6,14},{7,15},{8,0},{9,1},... | collective-permute-start | bytes 786440 | tf_op jit(solution)/shard_map/ppermute | solution.py:346
  54.5 1.8 %collective-permute-done.11.refs_3_.refs_6_ = f32[32,2048]{1,0:T(8,128)S(1)} collective-permute-done((f32[32,2048]{1,0:T(8,128)S(1)}, f32[32,2048]{1,0:T(8,128)S(1)}, u32[]{:S(2)}, u32[]{:S(2)}) %collective-permute-start.11) | collective-permute-done | bytes 262176 | tf_op jit(solution)/shard_map/ppermute | solution.py:346
  57.0 3.2 %collective-permute-start.15 = (f32[32,2048]{1,0:T(8,128)S(1)}, f32[32,2048]{1,0:T(8,128)S(1)}, u32[]{:S(2)}, u32[]{:S(2)}) collective-permute-start(f32[32,2048]{1,0:T(8,128)S(1)} %get-tuple-element.74), channel_id=1, source_target_pairs={{0,8},{1,9},{2,10},{3,11},{4,12},{5,13},{6,14},{7,15},{8,0},{9,1},... | collective-permute-start | bytes 786440 | tf_op jit(solution)/shard_map/ppermute | solution.py:346
  60.1 1.7 %collective-permute-done.13.refs_3_.refs_7_ = f32[32,2048]{1,0:T(8,128)S(1)} collective-permute-done((f32[32,2048]{1,0:T(8,128)S(1)}, f32[32,2048]{1,0:T(8,128)S(1)}, u32[]{:S(2)}, u32[]{:S(2)}) %collective-permute-start.13) | collective-permute-done | bytes 262176 | tf_op jit(solution)/shard_map/ppermute | solution.py:346
  62.6 3.2 %collective-permute-start.17 = (f32[32,2048]{1,0:T(8,128)S(1)}, f32[32,2048]{1,0:T(8,128)S(1)}, u32[]{:S(2)}, u32[]{:S(2)}) collective-permute-start(f32[32,2048]{1,0:T(8,128)S(1)} %get-tuple-element.77), channel_id=1, source_target_pairs={{0,8},{1,9},{2,10},{3,11},{4,12},{5,13},{6,14},{7,15},{8,0},{9,1},... | collective-permute-start | bytes 786440 | tf_op jit(solution)/shard_map/ppermute | solution.py:346
  65.8 1.7 %collective-permute-done.15.refs_4_.refs_8_ = f32[32,2048]{1,0:T(8,128)S(1)} collective-permute-done((f32[32,2048]{1,0:T(8,128)S(1)}, f32[32,2048]{1,0:T(8,128)S(1)}, u32[]{:S(2)}, u32[]{:S(2)}) %collective-permute-start.15) | collective-permute-done | bytes 262176 | tf_op jit(solution)/shard_map/ppermute | solution.py:346
  68.3 5.1 %collective-permute-start.19 = (f32[32,2048]{1,0:T(8,128)S(1)}, f32[32,2048]{1,0:T(8,128)S(1)}, u32[]{:S(2)}, u32[]{:S(2)}) collective-permute-start(f32[32,2048]{1,0:T(8,128)S(1)} %get-tuple-element.80), channel_id=1, source_target_pairs={{0,8},{1,9},{2,10},{3,11},{4,12},{5,13},{6,14},{7,15},{8,0},{9,1},... | collective-permute-start | bytes 786440 | tf_op jit(solution)/shard_map/ppermute | solution.py:346
  74.2 2.8 %collective-permute-start.21 = (f32[32,2048]{1,0:T(8,128)S(1)}, f32[32,2048]{1,0:T(8,128)S(1)}, u32[]{:S(2)}, u32[]{:S(2)}) collective-permute-start(f32[32,2048]{1,0:T(8,128)S(1)} %get-tuple-element.83), channel_id=1, source_target_pairs={{0,8},{1,9},{2,10},{3,11},{4,12},{5,13},{6,14},{7,15},{8,0},{9,1},... | collective-permute-start | bytes 786440 | tf_op jit(solution)/shard_map/ppermute | solution.py:346
  77.0 2.8 %collective-permute-done.19.refs_10_ = f32[32,2048]{1,0:T(8,128)S(1)} collective-permute-done((f32[32,2048]{1,0:T(8,128)S(1)}, f32[32,2048]{1,0:T(8,128)S(1)}, u32[]{:S(2)}, u32[]{:S(2)}) %collective-permute-start.19) | collective-permute-done | bytes 262176 | tf_op jit(solution)/shard_map/ppermute | solution.py:346
  79.8 4.2 %collective-permute-done.21.refs_11_ = f32[32,2048]{1,0:T(8,128)S(1)} collective-permute-done((f32[32,2048]{1,0:T(8,128)S(1)}, f32[32,2048]{1,0:T(8,128)S(1)}, u32[]{:S(2)}, u32[]{:S(2)}) %collective-permute-start.21) | collective-permute-done | bytes 262176 | tf_op jit(solution)/shard_map/ppermute | solution.py:346
  84.0 5.3 %assemble.1 = (bf16[192,4096]{1,0:T(8,128)(2,1)S(1)}, bf16[192,4096]{1,0:T(8,128)(2,1)S(1)}, f32[32,512]{1,0:T(8,128)S(1)}) custom-call(s32[2]{0:T(128)S(1)} %pad_add_fusion.here_ref, s32[6]{0:T(128)S(1)} %copy-done.2, s32[6]{0:T(128)S(1)} %copy-done.3, f32[4,32,4096]{2,1,0:T(8,128)} %stack_ref.25, f32[32,2048]{1,0:T(8,128)S(1)} %collective-permute-done.refs_0_, ...), custom_call_target="tpu_custom_call" | custom-call | flops 1811939328 | bytes 6291456 | tf_op jit(solution)/shard_map/assemble/pallas_call | solution.py:190
  89.4 17.0 %all-to-all-done.x_ref = f32[8,64,4096]{2,1,0:T(8,128)} async-done(((f32[8,64,4096]{2,1,0:T(8,128)}), f32[8,64,4096]{2,1,0:T(8,128)}, u32[]{:S(2)}, u32[]{:S(2)}) %all-to-all-start) | async-done | bytes 8388640 | tf_op jit(solution)/shard_map/all_to_all | solution.py:351
  106.3 9.9 %inner_products.1 = (f32[128,384]{1,0:T(8,128)S(1)}, f32[128,384]{1,0:T(8,128)S(1)}, f32[8,64,4096]{2,1,0:T(8,128)S(1)}) custom-call(s32[2]{0:T(128)S(1)} %pad_add_fusion.here_ref, f32[8,64,4096]{2,1,0:T(8,128)} %all-to-all-done.x_ref, bf16[192,4096]{1,0:T(8,128)(2,1)S(1)} %get-tuple-element.85.high_ref.refs_5_, ...), custom_call_target="tpu_custom_call" | custom-call | flops 2415919104 | bytes 8388608 | tf_op jit(solution)/shard_map/inner_products/pallas_call | solution.py:270
  121.3 5.2 %collective-permute-done.27 = f32[128,384]{1,0:T(8,128)S(1)} collective-permute-done((f32[128,384]{1,0:T(8,128)S(1)}, f32[128,384]{1,0:T(8,128)S(1)}, u32[]{:S(2)}, u32[]{:S(2)}) %collective-permute-start.27) | collective-permute-done | bytes 196640 | tf_op jit(solution)/shard_map/ppermute | solution.py:321
  126.5 2.7 %collective-permute-done.26 = f32[128,384]{1,0:T(8,128)S(1)} collective-permute-done((f32[128,384]{1,0:T(8,128)S(1)}, f32[128,384]{1,0:T(8,128)S(1)}, u32[]{:S(2)}, u32[]{:S(2)}) %collective-permute-start.26) | collective-permute-done | bytes 196640 | tf_op jit(solution)/shard_map/ppermute | solution.py:321
  136.3 3.5 %merge.1 = (bf16[192,4096]{1,0:T(8,128)(2,1)S(1)}, bf16[192,4096]{1,0:T(8,128)(2,1)S(1)}) custom-call(f32[32,512]{1,0:T(8,128)S(1)} %add.19.refs_0_, f32[32,512]{1,0:T(8,128)S(1)} %collective-permute-done.30.refs_1_, f32[32,512]{1,0:T(8,128)S(1)} %collective-permute-done.31.refs_2_, f32[32,512]{1,0:T(8,128)S(1)} %collective-permute-done.32.refs_3_, ...), custom_call_target="tpu_custom_call" | custom-call | flops 905969664 | bytes 6291456 | tf_op jit(solution)/shard_map/merge/pallas_call | solution.py:224
  139.8 7.3 %update.1 = f32[8,64,4096]{2,1,0:T(8,128)} custom-call(s32[2]{0:T(128)S(1)} %pad_add_fusion.here_ref, f32[128,384]{1,0:T(8,128)S(1)} %add_add_fusion.mine_ref, f32[128,384]{1,0:T(8,128)S(1)} %collective-permute-done.28.theirs_ref, f32[8,64,4096]{2,1,0:T(8,128)S(1)} %get-tuple-element.89.x_ref, bf16[192,4096]{1,0:T(8,128)(2,1)S(1)} %get-tuple-element.91.high_ref, ...), custom_call_target="tpu_custom_call" | custom-call | flops 2415919104 | bytes 16777216 | tf_op jit(solution)/shard_map/update/pallas_call | solution.py:304
  (65 shorter events, 20.6 us)
Async XLA Ops:
  6.5 99.9 %all-to-all-start = ((f32[8,64,4096]{2,1,0:T(8,128)}), f32[8,64,4096]{2,1,0:T(8,128)}, u32[]{:S(2)}, u32[]{:S(2)}) async-start(f32[8,64,4096]{2,1,0:T(8,128)} %pack.1), calls=%async_computation | async-start | bytes 16777216 | tf_op jit(solution)/shard_map/all_to_all | solution.py:351
  12.5 10.1 %collective-permute-start = (f32[32,2048]{1,0:T(8,128)S(1)}, f32[32,2048]{1,0:T(8,128)S(1)}, u32[]{:S(2)}, u32[]{:S(2)}) collective-permute-start(f32[32,2048]{1,0:T(8,128)S(1)} %get-tuple-element.50), channel_id=1, source_target_pairs={{0,8},{1,9},{2,10},{3,11},{4,12},{5,13},{6,14},{7,15},{8,0},{9,1},... | collective-permute-start | bytes 786440 | tf_op jit(solution)/shard_map/ppermute | solution.py:346
  15.4 7.1 %collective-permute-start.2 = (f32[32,2048]{1,0:T(8,128)S(1)}, f32[32,2048]{1,0:T(8,128)S(1)}, u32[]{:S(2)}, u32[]{:S(2)}) collective-permute-start(f32[32,2048]{1,0:T(8,128)S(1)} %get-tuple-element.51), channel_id=1, source_target_pairs={{0,1},{1,0},{2,3},{3,2},{4,5},{5,4},{6,7},{7,6},{8,16},{9,17},{10,... | collective-permute-start | bytes 786440 | tf_op jit(solution)/shard_map/ppermute | solution.py:346
  16.1 12.0 %collective-permute-start.1 = (f32[32,2048]{1,0:T(8,128)S(1)}, f32[32,2048]{1,0:T(8,128)S(1)}, u32[]{:S(2)}, u32[]{:S(2)}) collective-permute-start(f32[32,2048]{1,0:T(8,128)S(1)} %get-tuple-element.53), channel_id=1, source_target_pairs={{0,8},{1,9},{2,10},{3,11},{4,12},{5,13},{6,14},{7,15},{8,0},{9,1},... | collective-permute-start | bytes 786440 | tf_op jit(solution)/shard_map/ppermute | solution.py:346
  19.3 8.9 %collective-permute-start.4 = (f32[32,2048]{1,0:T(8,128)S(1)}, f32[32,2048]{1,0:T(8,128)S(1)}, u32[]{:S(2)}, u32[]{:S(2)}) collective-permute-start(f32[32,2048]{1,0:T(8,128)S(1)} %get-tuple-element.54), channel_id=1, source_target_pairs={{0,1},{1,0},{2,3},{3,2},{4,5},{5,4},{6,7},{7,6},{8,16},{9,17},{10,... | collective-permute-start | bytes 786440 | tf_op jit(solution)/shard_map/ppermute | solution.py:346
  23.2 10.6 %collective-permute-start.3 = (f32[32,2048]{1,0:T(8,128)S(1)}, f32[32,2048]{1,0:T(8,128)S(1)}, u32[]{:S(2)}, u32[]{:S(2)}) collective-permute-start(f32[32,2048]{1,0:T(8,128)S(1)} %get-tuple-element.56), channel_id=1, source_target_pairs={{0,8},{1,9},{2,10},{3,11},{4,12},{5,13},{6,14},{7,15},{8,0},{9,1},... | collective-permute-start | bytes 786440 | tf_op jit(solution)/shard_map/ppermute | solution.py:346
  26.4 7.4 %collective-permute-start.6 = (f32[32,2048]{1,0:T(8,128)S(1)}, f32[32,2048]{1,0:T(8,128)S(1)}, u32[]{:S(2)}, u32[]{:S(2)}) collective-permute-start(f32[32,2048]{1,0:T(8,128)S(1)} %get-tuple-element.57), channel_id=1, source_target_pairs={{0,1},{1,0},{2,3},{3,2},{4,5},{5,4},{6,7},{7,6},{8,16},{9,17},{10,... | collective-permute-start | bytes 786440 | tf_op jit(solution)/shard_map/ppermute | solution.py:346
  28.9 10.6 %collective-permute-start.5 = (f32[32,2048]{1,0:T(8,128)S(1)}, f32[32,2048]{1,0:T(8,128)S(1)}, u32[]{:S(2)}, u32[]{:S(2)}) collective-permute-start(f32[32,2048]{1,0:T(8,128)S(1)} %get-tuple-element.59), channel_id=1, source_target_pairs={{0,8},{1,9},{2,10},{3,11},{4,12},{5,13},{6,14},{7,15},{8,0},{9,1},... | collective-permute-start | bytes 786440 | tf_op jit(solution)/shard_map/ppermute | solution.py:346
  32.0 7.4 %collective-permute-start.8 = (f32[32,2048]{1,0:T(8,128)S(1)}, f32[32,2048]{1,0:T(8,128)S(1)}, u32[]{:S(2)}, u32[]{:S(2)}) collective-permute-start(f32[32,2048]{1,0:T(8,128)S(1)} %get-tuple-element.60), channel_id=1, source_target_pairs={{0,1},{1,0},{2,3},{3,2},{4,5},{5,4},{6,7},{7,6},{8,16},{9,17},{10,... | collective-permute-start | bytes 786440 | tf_op jit(solution)/shard_map/ppermute | solution.py:346
  34.5 10.6 %collective-permute-start.7 = (f32[32,2048]{1,0:T(8,128)S(1)}, f32[32,2048]{1,0:T(8,128)S(1)}, u32[]{:S(2)}, u32[]{:S(2)}) collective-permute-start(f32[32,2048]{1,0:T(8,128)S(1)} %get-tuple-element.62), channel_id=1, source_target_pairs={{0,8},{1,9},{2,10},{3,11},{4,12},{5,13},{6,14},{7,15},{8,0},{9,1},... | collective-permute-start | bytes 786440 | tf_op jit(solution)/shard_map/ppermute | solution.py:346
  37.6 7.4 %collective-permute-start.10 = (f32[32,2048]{1,0:T(8,128)S(1)}, f32[32,2048]{1,0:T(8,128)S(1)}, u32[]{:S(2)}, u32[]{:S(2)}) collective-permute-start(f32[32,2048]{1,0:T(8,128)S(1)} %get-tuple-element.63), channel_id=1, source_target_pairs={{0,1},{1,0},{2,3},{3,2},{4,5},{5,4},{6,7},{7,6},{8,16},{9,17},{10,... | collective-permute-start | bytes 786440 | tf_op jit(solution)/shard_map/ppermute | solution.py:346
  40.1 10.6 %collective-permute-start.9 = (f32[32,2048]{1,0:T(8,128)S(1)}, f32[32,2048]{1,0:T(8,128)S(1)}, u32[]{:S(2)}, u32[]{:S(2)}) collective-permute-start(f32[32,2048]{1,0:T(8,128)S(1)} %get-tuple-element.65), channel_id=1, source_target_pairs={{0,8},{1,9},{2,10},{3,11},{4,12},{5,13},{6,14},{7,15},{8,0},{9,1},... | collective-permute-start | bytes 786440 | tf_op jit(solution)/shard_map/ppermute | solution.py:346
  43.3 7.4 %collective-permute-start.12 = (f32[32,2048]{1,0:T(8,128)S(1)}, f32[32,2048]{1,0:T(8,128)S(1)}, u32[]{:S(2)}, u32[]{:S(2)}) collective-permute-start(f32[32,2048]{1,0:T(8,128)S(1)} %get-tuple-element.66), channel_id=1, source_target_pairs={{0,1},{1,0},{2,3},{3,2},{4,5},{5,4},{6,7},{7,6},{8,16},{9,17},{10,... | collective-permute-start | bytes 786440 | tf_op jit(solution)/shard_map/ppermute | solution.py:346
  45.7 10.5 %collective-permute-start.11 = (f32[32,2048]{1,0:T(8,128)S(1)}, f32[32,2048]{1,0:T(8,128)S(1)}, u32[]{:S(2)}, u32[]{:S(2)}) collective-permute-start(f32[32,2048]{1,0:T(8,128)S(1)} %get-tuple-element.68), channel_id=1, source_target_pairs={{0,8},{1,9},{2,10},{3,11},{4,12},{5,13},{6,14},{7,15},{8,0},{9,1},... | collective-permute-start | bytes 786440 | tf_op jit(solution)/shard_map/ppermute | solution.py:346
  48.9 7.4 %collective-permute-start.14 = (f32[32,2048]{1,0:T(8,128)S(1)}, f32[32,2048]{1,0:T(8,128)S(1)}, u32[]{:S(2)}, u32[]{:S(2)}) collective-permute-start(f32[32,2048]{1,0:T(8,128)S(1)} %get-tuple-element.69), channel_id=1, source_target_pairs={{0,1},{1,0},{2,3},{3,2},{4,5},{5,4},{6,7},{7,6},{8,16},{9,17},{10,... | collective-permute-start | bytes 786440 | tf_op jit(solution)/shard_map/ppermute | solution.py:346
  51.3 10.5 %collective-permute-start.13 = (f32[32,2048]{1,0:T(8,128)S(1)}, f32[32,2048]{1,0:T(8,128)S(1)}, u32[]{:S(2)}, u32[]{:S(2)}) collective-permute-start(f32[32,2048]{1,0:T(8,128)S(1)} %get-tuple-element.71), channel_id=1, source_target_pairs={{0,8},{1,9},{2,10},{3,11},{4,12},{5,13},{6,14},{7,15},{8,0},{9,1},... | collective-permute-start | bytes 786440 | tf_op jit(solution)/shard_map/ppermute | solution.py:346
  54.5 7.4 %collective-permute-start.16 = (f32[32,2048]{1,0:T(8,128)S(1)}, f32[32,2048]{1,0:T(8,128)S(1)}, u32[]{:S(2)}, u32[]{:S(2)}) collective-permute-start(f32[32,2048]{1,0:T(8,128)S(1)} %get-tuple-element.72), channel_id=1, source_target_pairs={{0,1},{1,0},{2,3},{3,2},{4,5},{5,4},{6,7},{7,6},{8,16},{9,17},{10,... | collective-permute-start | bytes 786440 | tf_op jit(solution)/shard_map/ppermute | solution.py:346
  57.0 10.5 %collective-permute-start.15 = (f32[32,2048]{1,0:T(8,128)S(1)}, f32[32,2048]{1,0:T(8,128)S(1)}, u32[]{:S(2)}, u32[]{:S(2)}) collective-permute-start(f32[32,2048]{1,0:T(8,128)S(1)} %get-tuple-element.74), channel_id=1, source_target_pairs={{0,8},{1,9},{2,10},{3,11},{4,12},{5,13},{6,14},{7,15},{8,0},{9,1},... | collective-permute-start | bytes 786440 | tf_op jit(solution)/shard_map/ppermute | solution.py:346
  60.1 7.4 %collective-permute-start.18 = (f32[32,2048]{1,0:T(8,128)S(1)}, f32[32,2048]{1,0:T(8,128)S(1)}, u32[]{:S(2)}, u32[]{:S(2)}) collective-permute-start(f32[32,2048]{1,0:T(8,128)S(1)} %get-tuple-element.75), channel_id=1, source_target_pairs={{0,1},{1,0},{2,3},{3,2},{4,5},{5,4},{6,7},{7,6},{8,16},{9,17},{10,... | collective-permute-start | bytes 786440 | tf_op jit(solution)/shard_map/ppermute | solution.py:346
  62.6 10.9 %collective-permute-start.17 = (f32[32,2048]{1,0:T(8,128)S(1)}, f32[32,2048]{1,0:T(8,128)S(1)}, u32[]{:S(2)}, u32[]{:S(2)}) collective-permute-start(f32[32,2048]{1,0:T(8,128)S(1)} %get-tuple-element.77), channel_id=1, source_target_pairs={{0,8},{1,9},{2,10},{3,11},{4,12},{5,13},{6,14},{7,15},{8,0},{9,1},... | collective-permute-start | bytes 786440 | tf_op jit(solution)/shard_map/ppermute | solution.py:346
  65.7 7.7 %collective-permute-start.20 = (f32[32,2048]{1,0:T(8,128)S(1)}, f32[32,2048]{1,0:T(8,128)S(1)}, u32[]{:S(2)}, u32[]{:S(2)}) collective-permute-start(f32[32,2048]{1,0:T(8,128)S(1)} %get-tuple-element.78), channel_id=1, source_target_pairs={{0,1},{1,0},{2,3},{3,2},{4,5},{5,4},{6,7},{7,6},{8,16},{9,17},{10,... | collective-permute-start | bytes 786440 | tf_op jit(solution)/shard_map/ppermute | solution.py:346
  68.2 15.8 %collective-permute-start.22 = (f32[32,2048]{1,0:T(8,128)S(1)}, f32[32,2048]{1,0:T(8,128)S(1)}, u32[]{:S(2)}, u32[]{:S(2)}) collective-permute-start(f32[32,2048]{1,0:T(8,128)S(1)} %get-tuple-element.81), channel_id=1, source_target_pairs={{0,1},{1,0},{2,3},{3,2},{4,5},{5,4},{6,7},{7,6},{8,16},{9,17},{10,... | collective-permute-start | bytes 786440 | tf_op jit(solution)/shard_map/ppermute | solution.py:346
  68.3 11.5 %collective-permute-start.19 = (f32[32,2048]{1,0:T(8,128)S(1)}, f32[32,2048]{1,0:T(8,128)S(1)}, u32[]{:S(2)}, u32[]{:S(2)}) collective-permute-start(f32[32,2048]{1,0:T(8,128)S(1)} %get-tuple-element.80), channel_id=1, source_target_pairs={{0,8},{1,9},{2,10},{3,11},{4,12},{5,13},{6,14},{7,15},{8,0},{9,1},... | collective-permute-start | bytes 786440 | tf_op jit(solution)/shard_map/ppermute | solution.py:346
  74.2 9.9 %collective-permute-start.21 = (f32[32,2048]{1,0:T(8,128)S(1)}, f32[32,2048]{1,0:T(8,128)S(1)}, u32[]{:S(2)}, u32[]{:S(2)}) collective-permute-start(f32[32,2048]{1,0:T(8,128)S(1)} %get-tuple-element.83), channel_id=1, source_target_pairs={{0,8},{1,9},{2,10},{3,11},{4,12},{5,13},{6,14},{7,15},{8,0},{9,1},... | collective-permute-start | bytes 786440 | tf_op jit(solution)/shard_map/ppermute | solution.py:346
  77.0 7.0 %collective-permute-start.23 = (f32[32,2048]{1,0:T(8,128)S(1)}, f32[32,2048]{1,0:T(8,128)S(1)}, u32[]{:S(2)}, u32[]{:S(2)}) collective-permute-start(f32[32,2048]{1,0:T(8,128)S(1)} %get-tuple-element.84), channel_id=1, source_target_pairs={{0,1},{1,0},{2,3},{3,2},{4,5},{5,4},{6,7},{7,6},{8,16},{9,17},{10,... | collective-permute-start | bytes 786440 | tf_op jit(solution)/shard_map/ppermute | solution.py:346
  117.7 8.8 %collective-permute-start.27 = (f32[128,384]{1,0:T(8,128)S(1)}, f32[128,384]{1,0:T(8,128)S(1)}, u32[]{:S(2)}, u32[]{:S(2)}) collective-permute-start(f32[128,384]{1,0:T(8,128)S(1)} %add.15), channel_id=1, source_target_pairs={{0,6},{1,7},{2,4},{3,5},{4,2},{5,3},{6,0},{7,1},{8,14},{9,15},{10,... | collective-permute-start | bytes 589832 | tf_op jit(solution)/shard_map/ppermute | solution.py:321
  118.3 10.9 %collective-permute-start.26 = (f32[128,384]{1,0:T(8,128)S(1)}, f32[128,384]{1,0:T(8,128)S(1)}, u32[]{:S(2)}, u32[]{:S(2)}) collective-permute-start(f32[128,384]{1,0:T(8,128)S(1)} %add.15), channel_id=1, source_target_pairs={{0,4},{1,5},{2,6},{3,7},{4,0},{5,1},{6,2},{7,3},{8,12},{9,13},{10,... | collective-permute-start | bytes 589832 | tf_op jit(solution)/shard_map/ppermute | solution.py:321
  119.7 9.5 %collective-permute-start.25 = (f32[128,384]{1,0:T(8,128)S(1)}, f32[128,384]{1,0:T(8,128)S(1)}, u32[]{:S(2)}, u32[]{:S(2)}) collective-permute-start(f32[128,384]{1,0:T(8,128)S(1)} %add.15), channel_id=1, source_target_pairs={{0,2},{1,3},{2,0},{3,1},{4,6},{5,7},{6,4},{7,5},{8,10},{9,11},{10,... | collective-permute-start | bytes 589832 | tf_op jit(solution)/shard_map/ppermute | solution.py:321
  121.3 8.0 %collective-permute-start.29 = (f32[32,512]{1,0:T(8,128)S(1)}, f32[32,512]{1,0:T(8,128)S(1)}, u32[]{:S(2)}, u32[]{:S(2)}) collective-permute-start(f32[32,512]{1,0:T(8,128)S(1)} %get-tuple-element.90), channel_id=1, source_target_pairs={{0,1},{1,0},{2,3},{3,2},{4,5},{5,4},{6,7},{7,6},{8,9},{9,8},{10,11... | collective-permute-start | bytes 196616 | tf_op jit(solution)/shard_map/ppermute | solution.py:321
  129.3 10.6 %collective-permute-start.28 = (f32[128,384]{1,0:T(8,128)S(1)}, f32[128,384]{1,0:T(8,128)S(1)}, u32[]{:S(2)}, u32[]{:S(2)}) collective-permute-start(f32[128,384]{1,0:T(8,128)S(1)} %add_add_fusion.mine_ref), channel_id=1, source_target_pairs={{0,1},{1,0},{2,3},{3,2},{4,5},{5,4},{6,7},{7,6},{8,9},{9,8},{10,11... | collective-permute-start | bytes 589832 | tf_op jit(solution)/shard_map/ppermute | solution.py:321
  130.5 5.0 %collective-permute-start.31 = (f32[32,512]{1,0:T(8,128)S(1)}, f32[32,512]{1,0:T(8,128)S(1)}, u32[]{:S(2)}, u32[]{:S(2)}) collective-permute-start(f32[32,512]{1,0:T(8,128)S(1)} %add.19.refs_0_), channel_id=1, source_target_pairs={{0,4},{1,5},{2,6},{3,7},{4,0},{5,1},{6,2},{7,3},{8,12},{9,13},{10,... | collective-permute-start | bytes 196616 | tf_op jit(solution)/shard_map/ppermute | solution.py:321
  131.2 5.2 %collective-permute-start.32 = (f32[32,512]{1,0:T(8,128)S(1)}, f32[32,512]{1,0:T(8,128)S(1)}, u32[]{:S(2)}, u32[]{:S(2)}) collective-permute-start(f32[32,512]{1,0:T(8,128)S(1)} %add.19.refs_0_), channel_id=1, source_target_pairs={{0,6},{1,7},{2,4},{3,5},{4,2},{5,3},{6,0},{7,1},{8,14},{9,15},{10,... | collective-permute-start | bytes 196616 | tf_op jit(solution)/shard_map/ppermute | solution.py:321
  (6 other events, 93.4 us)

commit v3 on v2

--- a/solution.py
+++ b/solution.py
@@ -59,17 +59,22 @@
 def pack(x, n_wide):
     rows, order = x.shape
     ncols = order // n_wide
+    step = 16 if rows % 16 == 0 else rows
+    n_copies = n_wide * rows // step
 
     def kernel(x_ref, out_ref, held, in_sems, out_sems):
-        into = [
-            pltpu.make_async_copy(x_ref.at[:, pl.ds(k * ncols, ncols)], held.at[k], in_sems.at[k]) for k in range(n_wide)
-        ]
-        out_of = [pltpu.make_async_copy(held.at[k], out_ref.at[k], out_sems.at[k]) for k in range(n_wide)]
+        into, out_of = [], []
+        for first in range(0, rows, step):
+            for k in range(n_wide):
+                i, at = len(into), pl.ds(first, step)
+                source = x_ref.at[at, pl.ds(k * ncols, ncols)]
+                into.append(pltpu.make_async_copy(source, held.at[k, at], in_sems.at[i]))
+                out_of.append(pltpu.make_async_copy(held.at[k, at], out_ref.at[k, at], out_sems.at[i]))
         for copy in into:
             copy.start()
-        for k in range(n_wide):
-            into[k].wait()
-            out_of[k].start()
+        for came, goes in zip(into, out_of):
+            came.wait()
+            goes.start()
         for copy in out_of:
             copy.wait()
 
@@ -80,8 +85,8 @@
         out_specs=ANY,
         scratch_shapes=[
             pltpu.VMEM((n_wide, rows, ncols), jnp.float32),
-            pltpu.SemaphoreType.DMA((n_wide,)),
-            pltpu.SemaphoreType.DMA((n_wide,)),
+            pltpu.SemaphoreType.DMA((n_copies,)),
+            pltpu.SemaphoreType.DMA((n_copies,)),
         ],
         compiler_params=params(limit=LARGE_LIMIT),
         cost_estimate=cost(0, 8 * rows * order),
@@ -147,7 +152,7 @@
     cols = ncols // splits
 
     def kernel(here_ref, place_ref, offset_ref, stack_ref, *refs):
-        arrived, (high_ref, low_ref, gram_ref, held, sems) = refs[:-5], refs[-5:]
+        arrived, (high_ref, low_ref, high_t_ref, low_t_ref, gram_ref, held, sems) = refs[:-7], refs[-7:]
         even, odd = arrived[:turns * splits], arrived[turns * splits:]
         roots, slot, ranks, counts = plan(place_ref, slots, n_rows)
         me = here_ref[0]
@@ -180,6 +185,8 @@
             high, low = halves(masked)
             high_ref[rows, :] = high
             low_ref[rows, :] = low
+        for at in column_blocks(ncols):
+            high_t_ref[at, :], low_t_ref[at, :] = halves(held[:, at].T)
         gram = dot_t(held[...], held[...])
         gram_ref[...] = jnp.zeros_like(gram_ref)
         first = 0
@@ -192,10 +199,12 @@
         out_shape=[
             jax.ShapeDtypeStruct((height, ncols), jnp.bfloat16),
             jax.ShapeDtypeStruct((height, ncols), jnp.bfloat16),
+            jax.ShapeDtypeStruct((ncols, height), jnp.bfloat16),
+            jax.ShapeDtypeStruct((ncols, height), jnp.bfloat16),
             jax.ShapeDtypeStruct((width, packed_width(steps, width)), jnp.float32),
         ],
         in_specs=[SMEM, SMEM, SMEM, ANY] + [ANY] * (2 * turns * splits),
-        out_specs=[VMEM] * 3,
+        out_specs=[VMEM] * 5,
         scratch_shapes=[pltpu.VMEM((height, ncols), jnp.float32), pltpu.SemaphoreType.DMA((steps,))],
         compiler_params=params(limit=SMALL_LIMIT),
         cost_estimate=cost(12 * height * height * ncols, 8 * height * ncols),
@@ -208,7 +217,7 @@
     height, ncols = vecs[0].shape
 
     def kernel(*refs):
-        cross_refs, (factor_ref, v_high, v_low, p_high, p_low, total, m_ref) = refs[:-7], refs[-7:]
+        cross_refs, (factor_ref, v_high, v_low, p_ref, total, m_ref) = refs[:-6], refs[-6:]
         total[...] = sum([ref[...] for ref in cross_refs[1:]], cross_refs[0][...])
         first = 0
         for k in range(steps):
@@ -219,12 +228,14 @@
                 first += k * width
             m_ref[k * width:(k + 1) * width, :] = dot(factor_ref[k], rest)
         product = dot3(halves(m_ref[...].T), (v_high[...], v_low[...]), ((1,), (0,)))
-        p_high[...], p_low[...] = halves(product)
-
-    return pl.pallas_call(
-        kernel,
-        out_shape=[jax.ShapeDtypeStruct((height, ncols), jnp.bfloat16)] * 2,
-        out_specs=[VMEM] * 2,
+        high, low = halves(product)
+        for i, half in enumerate((high, high, low)):
+            p_ref[i * height:(i + 1) * height, :] = half
+
+    return pl.pallas_call(
+        kernel,
+        out_shape=jax.ShapeDtypeStruct((3 * height, ncols), jnp.bfloat16),
+        out_specs=VMEM,
         in_specs=[VMEM] * (len(cross) + 3),
         scratch_shapes=[pltpu.VMEM(cross[0].shape, jnp.float32), pltpu.VMEM((height, height), jnp.float32)],
         compiler_params=params(),
@@ -248,21 +259,21 @@
     return [pl.ds(start, cols) for start in range(0, ncols, cols)]
 
 
-def inner_products(here, x, vecs):
+def inner_products(here, x, vecs_t):
     lead, rows, ncols = x.shape
-    height = vecs[0].shape[0]
+    height = vecs_t[0].shape[1]
     half = lead * rows // 2
-    blocks = column_blocks(ncols)
+    cuts = [0, lead // 4, lead] if lead % 4 == 0 else [0, lead]
 
     def kernel(here_ref, x_ref, high_ref, low_ref, mine_ref, theirs_ref, held, total, sems):
-        copies = [pltpu.make_async_copy(x_ref.at[:, :, at], held.at[:, :, at], sems.at[i]) for i, at in enumerate(blocks)]
+        copies = [pltpu.make_async_copy(x_ref.at[i], held.at[i], sems.at[i]) for i in range(lead)]
         for copy in copies:
             copy.start()
-        for i, at in enumerate(blocks):
-            copies[i].wait()
-            block = held[:, :, at].reshape(lead * rows, at.size)
-            part = dot3(halves(block), (high_ref[:, at], low_ref[:, at]), ((1,), (1,)))
-            total[...] = part if i == 0 else total[...] + part
+        for start, end in zip(cuts[:-1], cuts[1:]):
+            for copy in copies[start:end]:
+                copy.wait()
+            block = held[start:end].reshape((end - start) * rows, ncols)
+            total[start * rows:end * rows, :] = dot3(halves(block), (high_ref[...], low_ref[...]), ((1,), (0,)))
         core = lax.rem(here_ref[1], 2)
         mine_ref[...] = fold(total[pl.ds(pl.multiple_of(core * half, 8), half), :])
         theirs_ref[...] = fold(total[pl.ds(pl.multiple_of((1 - core) * half, 8), half), :])
@@ -272,28 +283,29 @@
         out_shape=[jax.ShapeDtypeStruct((half // 2, 2 * height), jnp.float32)] * 2 + [pltpu.VMEM(x.shape, jnp.float32)],
         in_specs=[SMEM, ANY, VMEM, VMEM],
         out_specs=[VMEM] * 3,
-        scratch_shapes=[pltpu.VMEM((lead * rows, height), jnp.float32), pltpu.SemaphoreType.DMA((len(blocks),))],
+        scratch_shapes=[pltpu.VMEM((lead * rows, height), jnp.float32), pltpu.SemaphoreType.DMA((lead,))],
         compiler_params=params(),
         cost_estimate=cost(6 * lead * rows * ncols * height, 4 * lead * rows * ncols),
         name="inner_products",
-    )(here, in_hbm(x), *vecs)
+    )(here, in_hbm(x), *vecs_t)
 
 
 def update(here, x, mine, theirs, changes):
     lead, rows, ncols = x.shape
-    height = changes[0].shape[0]
+    height = changes.shape[0] // 3
     half = lead * rows // 2
     blocks = column_blocks(ncols)
     depth = min(2, len(blocks))
 
-    def kernel(here_ref, mine_ref, theirs_ref, x_ref, high_ref, low_ref, out_ref, w_ref, held, sems):
+    def kernel(here_ref, mine_ref, theirs_ref, x_ref, p_ref, out_ref, w_ref, held, sems):
         core = lax.rem(here_ref[1], 2)
         w_ref[pl.ds(pl.multiple_of(core * half, 8), half), :] = unfold(mine_ref[...])
         w_ref[pl.ds(pl.multiple_of((1 - core) * half, 8), half), :] = unfold(theirs_ref[...])
-        w = halves(w_ref[...])
+        high, low = halves(w_ref[...])
+        w = jnp.concatenate([high, low, high], axis=1)
         copies = [pltpu.make_async_copy(held.at[i % depth], out_ref.at[:, :, at], sems.at[i]) for i, at in enumerate(blocks)]
         for i, at in enumerate(blocks):
-            change = dot3(w, (high_ref[:, at], low_ref[:, at]), ((1,), (0,)))
+            change = lax.dot_general(w, p_ref[:, at], (((1,), (0,)), ((), ())), preferred_element_type=jnp.float32)
             if i >= depth:
                 copies[i - depth].wait()
             held[i % depth] = x_ref[:, :, at] - change.reshape(lead, rows, at.size)
@@ -304,7 +316,7 @@
     return pl.pallas_call(
         kernel,
         out_shape=jax.ShapeDtypeStruct(x.shape, jnp.float32),
-        in_specs=[SMEM] + [VMEM] * 5,
+        in_specs=[SMEM] + [VMEM] * 4,
         out_specs=ANY,
         scratch_shapes=[
             pltpu.VMEM((lead * rows, height), jnp.float32),
@@ -314,7 +326,7 @@
         compiler_params=params(),
         cost_estimate=cost(6 * lead * rows * ncols * height, 8 * lead * rows * ncols),
         name="update",
-    )(here, mine, theirs, x, *changes)
+    )(here, mine, theirs, x, changes)
 
 
 def swap(array, k, size):
@@ -361,11 +373,11 @@
             streams[part] = (evens + [exchange(to_even, 0)], odds + [exchange(to_odd, 1)])
     evens = list(zip(*[stream[0] for stream in streams]))
     odds = list(zip(*[stream[1] for stream in streams]))
-    high, low, gram = assemble(here, block_place, offsets, householder, evens, odds, n_row)
+    high, low, high_t, low_t, gram = assemble(here, block_place, offsets, householder, evens, odds, n_row)
     cross = spread(gram + swap(gram, 1, n_wide), n_wide)
     changes = merge(cross, wy_factor, (high, low))
 
-    mine, theirs, x = inner_products(here, x, (high, low))
+    mine, theirs, x = inner_products(after(here, *cross), x, (high_t, low_t))
     mine = functools.reduce(jnp.add, spread(mine + swap(theirs, 1, n_wide), n_wide))
     return update(here, x, mine, swap(mine, 1, n_wide), changes).reshape(n_wide * rows, ncols)
 

time: 147 us -> 146 us (level)
  waiting for transfers between devices: 54.2 us -> 46.4 us
  local copies, waits for them, and re-layouts: 0.02 us -> 5.71 us
    all_to_all x1, waiting for transfers between devices: 17 us -> 0.01 us  [body(): x = lax.all_to_all(piece, 'wide', split_axis=0, concat_axis=0, tiled=True)]
    ppermute x9, waiting for transfers between devices: 12.8 us -> 22 us  [swap(): return lax.ppermute(array, 'wide', [(i, i ^ k) for i in range(size)])]
    unnamed x8 -> x28, local copies, waits for them, and re-layouts: 0.02 us -> 5.71 us
    pallas_call x1, Pallas kernels: 9.88 us -> 7.64 us  [inner_products(): pl.pallas_call(kernel, out_shape=[jax.ShapeDtypeStruct((half // 2, 2 * he...]
    pallas_call x1, Pallas kernels: 5.29 us -> 7.26 us  [assemble(): pl.pallas_call(kernel, out_shape=[jax.ShapeDtypeStruct((height, ncols), j...]
  transfers between devices with their start and end apart: 34 -> 34, of which waited for: 18 -> 16; matrix products, arithmetic and copies ran while one was open for 0% -> 0% of each run, Pallas kernels for 11% -> 13%
where the time goes in v3:
time: 146 us
  starting transfers between devices  52.3 us (36%)
  waiting for transfers between devices  46.4 us (32%)
  Pallas kernels  40.9 us (28%)
  local copies, waits for them, and re-layouts  5.71 us (4%)
    ppermute x24, starting transfers between devices, exchange(): return lax.ppermute(array, ('row', 'wide'), pairs)  39.6 us
    ppermute x24, waiting for transfers between devices, exchange(): return lax.ppermute(array, ('row', 'wide'), pairs)  24.4 us
    ppermute x9, waiting for transfers between devices, swap(): return lax.ppermute(array, 'wide', [(i, i ^ k) for i in range(size)])  22 us
    pallas_call x12, Pallas kernels, feed(): pl.pallas_call(kernel, out_shape=[jax.ShapeDtypeStruct((width, cols), jnp...  8.06 us
    pallas_call x1, Pallas kernels, inner_products(): pl.pallas_call(kernel, out_shape=[jax.ShapeDtypeStruct((half // 2, 2 * he...  7.64 us
    pallas_call x1, Pallas kernels, update(): pl.pallas_call(kernel, out_shape=jax.ShapeDtypeStruct(x.shape, jnp.float3...  7.41 us
    ppermute x9, starting transfers between devices, swap(): return lax.ppermute(array, 'wide', [(i, i ^ k) for i in range(size)])  7.33 us
    pallas_call x1, Pallas kernels, assemble(): pl.pallas_call(kernel, out_shape=[jax.ShapeDtypeStruct((height, ncols), j...  7.26 us
  transfers between devices with their start and end apart: 34, of which 16 were waited for; matrix products, arithmetic and copies ran while one was open for 0% of the time, Pallas kernels for 13%

profile of v3, /device:TPU:0, one launch (start us, length us, event | category | flops | bytes accessed | tf_op | source)
XLA Modules:
  0.0 145.8 jit_solution(16208185941670161666)
XLA Ops:
  0.0 7.0 %pack.1 = f32[8,64,4096]{2,1,0:T(8,128)} custom-call(f32[64,32768]{1,0:T(8,128)} %x_ref.1), custom_call_target="tpu_custom_call" | custom-call | bytes 16777216 | tf_op jit(solution)/shard_map/pack/pallas_call | solution.py:81
  7.0 5.3 %all-to-all-start = ((f32[8,64,4096]{2,1,0:T(8,128)}), f32[8,64,4096]{2,1,0:T(8,128)}, u32[]{:S(2)}, u32[]{:S(2)}) async-start(f32[8,64,4096]{2,1,0:T(8,128)} %pack.1), calls=%async_computation | async-start | bytes 16777216 | tf_op jit(solution)/shard_map/all_to_all | solution.py:363
  13.1 3.0 %collective-permute-start = (f32[32,2048]{1,0:T(8,128)S(1)}, f32[32,2048]{1,0:T(8,128)S(1)}, u32[]{:S(2)}, u32[]{:S(2)}) collective-permute-start(f32[32,2048]{1,0:T(8,128)S(1)} %get-tuple-element.51), channel_id=1, source_target_pairs={{0,8},{1,9},{2,10},{3,11},{4,12},{5,13},{6,14},{7,15},{8,0},{9,1},... | collective-permute-start | bytes 786440 | tf_op jit(solution)/shard_map/ppermute | solution.py:358
  16.8 3.1 %collective-permute-start.1 = (f32[32,2048]{1,0:T(8,128)S(1)}, f32[32,2048]{1,0:T(8,128)S(1)}, u32[]{:S(2)}, u32[]{:S(2)}) collective-permute-start(f32[32,2048]{1,0:T(8,128)S(1)} %get-tuple-element.54), channel_id=1, source_target_pairs={{0,8},{1,9},{2,10},{3,11},{4,12},{5,13},{6,14},{7,15},{8,0},{9,1},... | collective-permute-start | bytes 786440 | tf_op jit(solution)/shard_map/ppermute | solution.py:358
  19.9 3.3 %collective-permute-done.refs_0_ = f32[32,2048]{1,0:T(8,128)S(1)} collective-permute-done((f32[32,2048]{1,0:T(8,128)S(1)}, f32[32,2048]{1,0:T(8,128)S(1)}, u32[]{:S(2)}, u32[]{:S(2)}) %collective-permute-start) | collective-permute-done | bytes 262176 | tf_op jit(solution)/shard_map/ppermute | solution.py:358
  23.9 3.2 %collective-permute-start.3 = (f32[32,2048]{1,0:T(8,128)S(1)}, f32[32,2048]{1,0:T(8,128)S(1)}, u32[]{:S(2)}, u32[]{:S(2)}) collective-permute-start(f32[32,2048]{1,0:T(8,128)S(1)} %get-tuple-element.57), channel_id=1, source_target_pairs={{0,8},{1,9},{2,10},{3,11},{4,12},{5,13},{6,14},{7,15},{8,0},{9,1},... | collective-permute-start | bytes 786440 | tf_op jit(solution)/shard_map/ppermute | solution.py:358
  27.0 1.8 %collective-permute-done.1.refs_0_.refs_1_ = f32[32,2048]{1,0:T(8,128)S(1)} collective-permute-done((f32[32,2048]{1,0:T(8,128)S(1)}, f32[32,2048]{1,0:T(8,128)S(1)}, u32[]{:S(2)}, u32[]{:S(2)}) %collective-permute-start.1) | collective-permute-done | bytes 262176 | tf_op jit(solution)/shard_map/ppermute | solution.py:358
  29.5 3.2 %collective-permute-start.5 = (f32[32,2048]{1,0:T(8,128)S(1)}, f32[32,2048]{1,0:T(8,128)S(1)}, u32[]{:S(2)}, u32[]{:S(2)}) collective-permute-start(f32[32,2048]{1,0:T(8,128)S(1)} %get-tuple-element.60), channel_id=1, source_target_pairs={{0,8},{1,9},{2,10},{3,11},{4,12},{5,13},{6,14},{7,15},{8,0},{9,1},... | collective-permute-start | bytes 786440 | tf_op jit(solution)/shard_map/ppermute | solution.py:358
  32.7 1.8 %collective-permute-done.3.refs_1_.refs_2_ = f32[32,2048]{1,0:T(8,128)S(1)} collective-permute-done((f32[32,2048]{1,0:T(8,128)S(1)}, f32[32,2048]{1,0:T(8,128)S(1)}, u32[]{:S(2)}, u32[]{:S(2)}) %collective-permute-start.3) | collective-permute-done | bytes 262176 | tf_op jit(solution)/shard_map/ppermute | solution.py:358
  35.1 3.2 %collective-permute-start.7 = (f32[32,2048]{1,0:T(8,128)S(1)}, f32[32,2048]{1,0:T(8,128)S(1)}, u32[]{:S(2)}, u32[]{:S(2)}) collective-permute-start(f32[32,2048]{1,0:T(8,128)S(1)} %get-tuple-element.63), channel_id=1, source_target_pairs={{0,8},{1,9},{2,10},{3,11},{4,12},{5,13},{6,14},{7,15},{8,0},{9,1},... | collective-permute-start | bytes 786440 | tf_op jit(solution)/shard_map/ppermute | solution.py:358
  38.3 1.8 %collective-permute-done.5.refs_1_.refs_3_ = f32[32,2048]{1,0:T(8,128)S(1)} collective-permute-done((f32[32,2048]{1,0:T(8,128)S(1)}, f32[32,2048]{1,0:T(8,128)S(1)}, u32[]{:S(2)}, u32[]{:S(2)}) %collective-permute-start.5) | collective-permute-done | bytes 262176 | tf_op jit(solution)/shard_map/ppermute | solution.py:358
  40.7 3.2 %collective-permute-start.9 = (f32[32,2048]{1,0:T(8,128)S(1)}, f32[32,2048]{1,0:T(8,128)S(1)}, u32[]{:S(2)}, u32[]{:S(2)}) collective-permute-start(f32[32,2048]{1,0:T(8,128)S(1)} %get-tuple-element.66), channel_id=1, source_target_pairs={{0,8},{1,9},{2,10},{3,11},{4,12},{5,13},{6,14},{7,15},{8,0},{9,1},... | collective-permute-start | bytes 786440 | tf_op jit(solution)/shard_map/ppermute | solution.py:358
  43.9 1.8 %collective-permute-done.7.refs_2_.refs_4_ = f32[32,2048]{1,0:T(8,128)S(1)} collective-permute-done((f32[32,2048]{1,0:T(8,128)S(1)}, f32[32,2048]{1,0:T(8,128)S(1)}, u32[]{:S(2)}, u32[]{:S(2)}) %collective-permute-start.7) | collective-permute-done | bytes 262176 | tf_op jit(solution)/shard_map/ppermute | solution.py:358
  46.4 3.2 %collective-permute-start.11 = (f32[32,2048]{1,0:T(8,128)S(1)}, f32[32,2048]{1,0:T(8,128)S(1)}, u32[]{:S(2)}, u32[]{:S(2)}) collective-permute-start(f32[32,2048]{1,0:T(8,128)S(1)} %get-tuple-element.69), channel_id=1, source_target_pairs={{0,8},{1,9},{2,10},{3,11},{4,12},{5,13},{6,14},{7,15},{8,0},{9,1},... | collective-permute-start | bytes 786440 | tf_op jit(solution)/shard_map/ppermute | solution.py:358
  49.5 1.8 %collective-permute-done.9.refs_2_.refs_5_ = f32[32,2048]{1,0:T(8,128)S(1)} collective-permute-done((f32[32,2048]{1,0:T(8,128)S(1)}, f32[32,2048]{1,0:T(8,128)S(1)}, u32[]{:S(2)}, u32[]{:S(2)}) %collective-permute-start.9) | collective-permute-done | bytes 262176 | tf_op jit(solution)/shard_map/ppermute | solution.py:358
  52.0 3.2 %collective-permute-start.13 = (f32[32,2048]{1,0:T(8,128)S(1)}, f32[32,2048]{1,0:T(8,128)S(1)}, u32[]{:S(2)}, u32[]{:S(2)}) collective-permute-start(f32[32,2048]{1,0:T(8,128)S(1)} %get-tuple-element.72), channel_id=1, source_target_pairs={{0,8},{1,9},{2,10},{3,11},{4,12},{5,13},{6,14},{7,15},{8,0},{9,1},... | collective-permute-start | bytes 786440 | tf_op jit(solution)/shard_map/ppermute | solution.py:358
  55.1 1.8 %collective-permute-done.11.refs_3_.refs_6_ = f32[32,2048]{1,0:T(8,128)S(1)} collective-permute-done((f32[32,2048]{1,0:T(8,128)S(1)}, f32[32,2048]{1,0:T(8,128)S(1)}, u32[]{:S(2)}, u32[]{:S(2)}) %collective-permute-start.11) | collective-permute-done | bytes 262176 | tf_op jit(solution)/shard_map/ppermute | solution.py:358
  57.6 3.2 %collective-permute-start.15 = (f32[32,2048]{1,0:T(8,128)S(1)}, f32[32,2048]{1,0:T(8,128)S(1)}, u32[]{:S(2)}, u32[]{:S(2)}) collective-permute-start(f32[32,2048]{1,0:T(8,128)S(1)} %get-tuple-element.75), channel_id=1, source_target_pairs={{0,8},{1,9},{2,10},{3,11},{4,12},{5,13},{6,14},{7,15},{8,0},{9,1},... | collective-permute-start | bytes 786440 | tf_op jit(solution)/shard_map/ppermute | solution.py:358
  63.2 3.2 %collective-permute-start.17 = (f32[32,2048]{1,0:T(8,128)S(1)}, f32[32,2048]{1,0:T(8,128)S(1)}, u32[]{:S(2)}, u32[]{:S(2)}) collective-permute-start(f32[32,2048]{1,0:T(8,128)S(1)} %get-tuple-element.78), channel_id=1, source_target_pairs={{0,8},{1,9},{2,10},{3,11},{4,12},{5,13},{6,14},{7,15},{8,0},{9,1},... | collective-permute-start | bytes 786440 | tf_op jit(solution)/shard_map/ppermute | solution.py:358
  68.9 5.1 %collective-permute-start.19 = (f32[32,2048]{1,0:T(8,128)S(1)}, f32[32,2048]{1,0:T(8,128)S(1)}, u32[]{:S(2)}, u32[]{:S(2)}) collective-permute-start(f32[32,2048]{1,0:T(8,128)S(1)} %get-tuple-element.81), channel_id=1, source_target_pairs={{0,8},{1,9},{2,10},{3,11},{4,12},{5,13},{6,14},{7,15},{8,0},{9,1},... | collective-permute-start | bytes 786440 | tf_op jit(solution)/shard_map/ppermute | solution.py:358
  74.8 2.8 %collective-permute-start.21 = (f32[32,2048]{1,0:T(8,128)S(1)}, f32[32,2048]{1,0:T(8,128)S(1)}, u32[]{:S(2)}, u32[]{:S(2)}) collective-permute-start(f32[32,2048]{1,0:T(8,128)S(1)} %get-tuple-element.84), channel_id=1, source_target_pairs={{0,8},{1,9},{2,10},{3,11},{4,12},{5,13},{6,14},{7,15},{8,0},{9,1},... | collective-permute-start | bytes 786440 | tf_op jit(solution)/shard_map/ppermute | solution.py:358
  77.6 2.8 %collective-permute-done.19.refs_10_ = f32[32,2048]{1,0:T(8,128)S(1)} collective-permute-done((f32[32,2048]{1,0:T(8,128)S(1)}, f32[32,2048]{1,0:T(8,128)S(1)}, u32[]{:S(2)}, u32[]{:S(2)}) %collective-permute-start.19) | collective-permute-done | bytes 262176 | tf_op jit(solution)/shard_map/ppermute | solution.py:358
  80.4 4.2 %collective-permute-done.21.refs_11_ = f32[32,2048]{1,0:T(8,128)S(1)} collective-permute-done((f32[32,2048]{1,0:T(8,128)S(1)}, f32[32,2048]{1,0:T(8,128)S(1)}, u32[]{:S(2)}, u32[]{:S(2)}) %collective-permute-start.21) | collective-permute-done | bytes 262176 | tf_op jit(solution)/shard_map/ppermute | solution.py:358
  84.7 7.3 %assemble.1 = (bf16[192,4096]{1,0:T(8,128)(2,1)S(1)}, bf16[192,4096]{1,0:T(8,128)(2,1)S(1)}, bf16[4096,192]{1,0:T(8,128)(2,1)}, bf16[4096,192]{1,0:T(8,128)(2,1)}, f32[32,512]{1,0:T(8,128)S(1)}) custom-call(s32[2]{0:T(128)S(1)} %pad_add_fusion.here_ref, s32[6]{0:T(128)S(1)} %copy-done.6, s32[6]{0:T(128)S(1)} %copy-done.13, f32[4,32,4096]{2,1,0:T(8,128)} %stack_ref.25, ...), custom_call_target="tpu_custom_call" | custom-call | flops 1811939328 | bytes 6291456 | tf_op jit(solution)/shard_map/assemble/pallas_call | solution.py:197
  93.3 2.7 %collective-permute-start.27 = (f32[32,512]{1,0:T(8,128)S(1)}, f32[32,512]{1,0:T(8,128)S(1)}, u32[]{:S(2)}, u32[]{:S(2)}) collective-permute-start(f32[32,512]{1,0:T(8,128)S(1)} %add.15.refs_0_), channel_id=1, source_target_pairs={{0,6},{1,7},{2,4},{3,5},{4,2},{5,3},{6,0},{7,1},{8,14},{9,15},{10,... | collective-permute-start | bytes 196616 | tf_op jit(solution)/shard_map/ppermute | solution.py:333
  97.5 11.5 %collective-permute-done.27.refs_3_ = f32[32,512]{1,0:T(8,128)S(1)} collective-permute-done((f32[32,512]{1,0:T(8,128)S(1)}, f32[32,512]{1,0:T(8,128)S(1)}, u32[]{:S(2)}, u32[]{:S(2)}) %collective-permute-start.27) | collective-permute-done | bytes 65568 | tf_op jit(solution)/shard_map/ppermute | solution.py:333
  114.1 7.6 %inner_products.1 = (f32[128,384]{1,0:T(8,128)S(1)}, f32[128,384]{1,0:T(8,128)S(1)}, f32[8,64,4096]{2,1,0:T(8,128)S(1)}) custom-call(s32[2]{0:T(128)S(1)} %pad_add_fusion.here_ref, f32[8,64,4096]{2,1,0:T(8,128)} %all-to-all-done.x_ref, bf16[4096,192]{1,0:T(8,128)(2,1)S(1)} %copy-done.1, bf16[4096,192]{1,0:T(8,128)(2,1)S(1)} %copy-done.2), custom_call_target="tpu_custom_call" | custom-call | flops 2415919104 | bytes 8388608 | tf_op jit(solution)/shard_map/inner_products/pallas_call | solution.py:281
  123.4 2.0 %collective-permute-start.30 = (f32[128,384]{1,0:T(8,128)S(1)}, f32[128,384]{1,0:T(8,128)S(1)}, u32[]{:S(2)}, u32[]{:S(2)}) collective-permute-start(f32[128,384]{1,0:T(8,128)S(1)} %add.16), channel_id=1, source_target_pairs={{0,4},{1,5},{2,6},{3,7},{4,0},{5,1},{6,2},{7,3},{8,12},{9,13},{10,... | collective-permute-start | bytes 589832 | tf_op jit(solution)/shard_map/ppermute | solution.py:333
  126.9 5.2 %collective-permute-done.31 = f32[128,384]{1,0:T(8,128)S(1)} collective-permute-done((f32[128,384]{1,0:T(8,128)S(1)}, f32[128,384]{1,0:T(8,128)S(1)}, u32[]{:S(2)}, u32[]{:S(2)}) %collective-permute-start.31) | collective-permute-done | bytes 196640 | tf_op jit(solution)/shard_map/ppermute | solution.py:333
  132.1 2.5 %collective-permute-done.30 = f32[128,384]{1,0:T(8,128)S(1)} collective-permute-done((f32[128,384]{1,0:T(8,128)S(1)}, f32[128,384]{1,0:T(8,128)S(1)}, u32[]{:S(2)}, u32[]{:S(2)}) %collective-permute-start.30) | collective-permute-done | bytes 196640 | tf_op jit(solution)/shard_map/ppermute | solution.py:333
  134.8 3.5 %merge.1.p_ref = bf16[576,4096]{1,0:T(8,128)(2,1)S(1)} custom-call(f32[32,512]{1,0:T(8,128)S(1)} %copy-done.4, f32[32,512]{1,0:T(8,128)S(1)} %copy-done.12, f32[32,512]{1,0:T(8,128)S(1)} %copy-done.10, f32[32,512]{1,0:T(8,128)S(1)} %copy-done.8, f32[6,32,32]{2,1,0:T(8,128)S(1)} %copy-done.5, bf16[192,4096]{1,0:T(8,128)(2,1)S(1)} %get-tuple-element.93.refs_5_, ...), custom_call_target="tpu_custom_call" | custom-call | flops 905969664 | bytes 6291456 | tf_op jit(solution)/shard_map/merge/pallas_call | solution.py:235
  138.3 7.4 %update.1 = f32[8,64,4096]{2,1,0:T(8,128)} custom-call(s32[2]{0:T(128)S(1)} %pad_add_fusion.here_ref, f32[128,384]{1,0:T(8,128)S(1)} %add_add_fusion.mine_ref, f32[128,384]{1,0:T(8,128)S(1)} %collective-permute-done.32.theirs_ref, f32[8,64,4096]{2,1,0:T(8,128)S(1)} %get-tuple-element.92.x_ref, bf16[576,4096]{1,0:T(8,128)(2,1)S(1)} %merge.1.p_ref), custom_call_target="tpu_custom_call" | custom-call | flops 2415919104 | bytes 16777216 | tf_op jit(solution)/shard_map/update/pallas_call | solution.py:316
  (85 shorter events, 23.0 us)
Async XLA Ops:
  7.0 103.9 %all-to-all-start = ((f32[8,64,4096]{2,1,0:T(8,128)}), f32[8,64,4096]{2,1,0:T(8,128)}, u32[]{:S(2)}, u32[]{:S(2)}) async-start(f32[8,64,4096]{2,1,0:T(8,128)} %pack.1), calls=%async_computation | async-start | bytes 16777216 | tf_op jit(solution)/shard_map/all_to_all | solution.py:363
  13.1 10.1 %collective-permute-start = (f32[32,2048]{1,0:T(8,128)S(1)}, f32[32,2048]{1,0:T(8,128)S(1)}, u32[]{:S(2)}, u32[]{:S(2)}) collective-permute-start(f32[32,2048]{1,0:T(8,128)S(1)} %get-tuple-element.51), channel_id=1, source_target_pairs={{0,8},{1,9},{2,10},{3,11},{4,12},{5,13},{6,14},{7,15},{8,0},{9,1},... | collective-permute-start | bytes 786440 | tf_op jit(solution)/shard_map/ppermute | solution.py:358
  16.0 7.1 %collective-permute-start.2 = (f32[32,2048]{1,0:T(8,128)S(1)}, f32[32,2048]{1,0:T(8,128)S(1)}, u32[]{:S(2)}, u32[]{:S(2)}) collective-permute-start(f32[32,2048]{1,0:T(8,128)S(1)} %get-tuple-element.52), channel_id=1, source_target_pairs={{0,1},{1,0},{2,3},{3,2},{4,5},{5,4},{6,7},{7,6},{8,16},{9,17},{10,... | collective-permute-start | bytes 786440 | tf_op jit(solution)/shard_map/ppermute | solution.py:358
  16.8 12.0 %collective-permute-start.1 = (f32[32,2048]{1,0:T(8,128)S(1)}, f32[32,2048]{1,0:T(8,128)S(1)}, u32[]{:S(2)}, u32[]{:S(2)}) collective-permute-start(f32[32,2048]{1,0:T(8,128)S(1)} %get-tuple-element.54), channel_id=1, source_target_pairs={{0,8},{1,9},{2,10},{3,11},{4,12},{5,13},{6,14},{7,15},{8,0},{9,1},... | collective-permute-start | bytes 786440 | tf_op jit(solution)/shard_map/ppermute | solution.py:358
  19.9 8.9 %collective-permute-start.4 = (f32[32,2048]{1,0:T(8,128)S(1)}, f32[32,2048]{1,0:T(8,128)S(1)}, u32[]{:S(2)}, u32[]{:S(2)}) collective-permute-start(f32[32,2048]{1,0:T(8,128)S(1)} %get-tuple-element.55), channel_id=1, source_target_pairs={{0,1},{1,0},{2,3},{3,2},{4,5},{5,4},{6,7},{7,6},{8,16},{9,17},{10,... | collective-permute-start | bytes 786440 | tf_op jit(solution)/shard_map/ppermute | solution.py:358
  23.9 10.6 %collective-permute-start.3 = (f32[32,2048]{1,0:T(8,128)S(1)}, f32[32,2048]{1,0:T(8,128)S(1)}, u32[]{:S(2)}, u32[]{:S(2)}) collective-permute-start(f32[32,2048]{1,0:T(8,128)S(1)} %get-tuple-element.57), channel_id=1, source_target_pairs={{0,8},{1,9},{2,10},{3,11},{4,12},{5,13},{6,14},{7,15},{8,0},{9,1},... | collective-permute-start | bytes 786440 | tf_op jit(solution)/shard_map/ppermute | solution.py:358
  27.0 7.4 %collective-permute-start.6 = (f32[32,2048]{1,0:T(8,128)S(1)}, f32[32,2048]{1,0:T(8,128)S(1)}, u32[]{:S(2)}, u32[]{:S(2)}) collective-permute-start(f32[32,2048]{1,0:T(8,128)S(1)} %get-tuple-element.58), channel_id=1, source_target_pairs={{0,1},{1,0},{2,3},{3,2},{4,5},{5,4},{6,7},{7,6},{8,16},{9,17},{10,... | collective-permute-start | bytes 786440 | tf_op jit(solution)/shard_map/ppermute | solution.py:358
  29.5 10.6 %collective-permute-start.5 = (f32[32,2048]{1,0:T(8,128)S(1)}, f32[32,2048]{1,0:T(8,128)S(1)}, u32[]{:S(2)}, u32[]{:S(2)}) collective-permute-start(f32[32,2048]{1,0:T(8,128)S(1)} %get-tuple-element.60), channel_id=1, source_target_pairs={{0,8},{1,9},{2,10},{3,11},{4,12},{5,13},{6,14},{7,15},{8,0},{9,1},... | collective-permute-start | bytes 786440 | tf_op jit(solution)/shard_map/ppermute | solution.py:358
  32.7 7.4 %collective-permute-start.8 = (f32[32,2048]{1,0:T(8,128)S(1)}, f32[32,2048]{1,0:T(8,128)S(1)}, u32[]{:S(2)}, u32[]{:S(2)}) collective-permute-start(f32[32,2048]{1,0:T(8,128)S(1)} %get-tuple-element.61), channel_id=1, source_target_pairs={{0,1},{1,0},{2,3},{3,2},{4,5},{5,4},{6,7},{7,6},{8,16},{9,17},{10,... | collective-permute-start | bytes 786440 | tf_op jit(solution)/shard_map/ppermute | solution.py:358
  35.1 10.6 %collective-permute-start.7 = (f32[32,2048]{1,0:T(8,128)S(1)}, f32[32,2048]{1,0:T(8,128)S(1)}, u32[]{:S(2)}, u32[]{:S(2)}) collective-permute-start(f32[32,2048]{1,0:T(8,128)S(1)} %get-tuple-element.63), channel_id=1, source_target_pairs={{0,8},{1,9},{2,10},{3,11},{4,12},{5,13},{6,14},{7,15},{8,0},{9,1},... | collective-permute-start | bytes 786440 | tf_op jit(solution)/shard_map/ppermute | solution.py:358
  38.3 7.4 %collective-permute-start.10 = (f32[32,2048]{1,0:T(8,128)S(1)}, f32[32,2048]{1,0:T(8,128)S(1)}, u32[]{:S(2)}, u32[]{:S(2)}) collective-permute-start(f32[32,2048]{1,0:T(8,128)S(1)} %get-tuple-element.64), channel_id=1, source_target_pairs={{0,1},{1,0},{2,3},{3,2},{4,5},{5,4},{6,7},{7,6},{8,16},{9,17},{10,... | collective-permute-start | bytes 786440 | tf_op jit(solution)/shard_map/ppermute | solution.py:358
  40.7 10.6 %collective-permute-start.9 = (f32[32,2048]{1,0:T(8,128)S(1)}, f32[32,2048]{1,0:T(8,128)S(1)}, u32[]{:S(2)}, u32[]{:S(2)}) collective-permute-start(f32[32,2048]{1,0:T(8,128)S(1)} %get-tuple-element.66), channel_id=1, source_target_pairs={{0,8},{1,9},{2,10},{3,11},{4,12},{5,13},{6,14},{7,15},{8,0},{9,1},... | collective-permute-start | bytes 786440 | tf_op jit(solution)/shard_map/ppermute | solution.py:358
  43.9 7.4 %collective-permute-start.12 = (f32[32,2048]{1,0:T(8,128)S(1)}, f32[32,2048]{1,0:T(8,128)S(1)}, u32[]{:S(2)}, u32[]{:S(2)}) collective-permute-start(f32[32,2048]{1,0:T(8,128)S(1)} %get-tuple-element.67), channel_id=1, source_target_pairs={{0,1},{1,0},{2,3},{3,2},{4,5},{5,4},{6,7},{7,6},{8,16},{9,17},{10,... | collective-permute-start | bytes 786440 | tf_op jit(solution)/shard_map/ppermute | solution.py:358
  46.4 10.5 %collective-permute-start.11 = (f32[32,2048]{1,0:T(8,128)S(1)}, f32[32,2048]{1,0:T(8,128)S(1)}, u32[]{:S(2)}, u32[]{:S(2)}) collective-permute-start(f32[32,2048]{1,0:T(8,128)S(1)} %get-tuple-element.69), channel_id=1, source_target_pairs={{0,8},{1,9},{2,10},{3,11},{4,12},{5,13},{6,14},{7,15},{8,0},{9,1},... | collective-permute-start | bytes 786440 | tf_op jit(solution)/shard_map/ppermute | solution.py:358
  49.5 7.4 %collective-permute-start.14 = (f32[32,2048]{1,0:T(8,128)S(1)}, f32[32,2048]{1,0:T(8,128)S(1)}, u32[]{:S(2)}, u32[]{:S(2)}) collective-permute-start(f32[32,2048]{1,0:T(8,128)S(1)} %get-tuple-element.70), channel_id=1, source_target_pairs={{0,1},{1,0},{2,3},{3,2},{4,5},{5,4},{6,7},{7,6},{8,16},{9,17},{10,... | collective-permute-start | bytes 786440 | tf_op jit(solution)/shard_map/ppermute | solution.py:358
  52.0 10.5 %collective-permute-start.13 = (f32[32,2048]{1,0:T(8,128)S(1)}, f32[32,2048]{1,0:T(8,128)S(1)}, u32[]{:S(2)}, u32[]{:S(2)}) collective-permute-start(f32[32,2048]{1,0:T(8,128)S(1)} %get-tuple-element.72), channel_id=1, source_target_pairs={{0,8},{1,9},{2,10},{3,11},{4,12},{5,13},{6,14},{7,15},{8,0},{9,1},... | collective-permute-start | bytes 786440 | tf_op jit(solution)/shard_map/ppermute | solution.py:358
  55.1 7.4 %collective-permute-start.16 = (f32[32,2048]{1,0:T(8,128)S(1)}, f32[32,2048]{1,0:T(8,128)S(1)}, u32[]{:S(2)}, u32[]{:S(2)}) collective-permute-start(f32[32,2048]{1,0:T(8,128)S(1)} %get-tuple-element.73), channel_id=1, source_target_pairs={{0,1},{1,0},{2,3},{3,2},{4,5},{5,4},{6,7},{7,6},{8,16},{9,17},{10,... | collective-permute-start | bytes 786440 | tf_op jit(solution)/shard_map/ppermute | solution.py:358
  57.6 10.5 %collective-permute-start.15 = (f32[32,2048]{1,0:T(8,128)S(1)}, f32[32,2048]{1,0:T(8,128)S(1)}, u32[]{:S(2)}, u32[]{:S(2)}) collective-permute-start(f32[32,2048]{1,0:T(8,128)S(1)} %get-tuple-element.75), channel_id=1, source_target_pairs={{0,8},{1,9},{2,10},{3,11},{4,12},{5,13},{6,14},{7,15},{8,0},{9,1},... | collective-permute-start | bytes 786440 | tf_op jit(solution)/shard_map/ppermute | solution.py:358
  60.8 7.4 %collective-permute-start.18 = (f32[32,2048]{1,0:T(8,128)S(1)}, f32[32,2048]{1,0:T(8,128)S(1)}, u32[]{:S(2)}, u32[]{:S(2)}) collective-permute-start(f32[32,2048]{1,0:T(8,128)S(1)} %get-tuple-element.76), channel_id=1, source_target_pairs={{0,1},{1,0},{2,3},{3,2},{4,5},{5,4},{6,7},{7,6},{8,16},{9,17},{10,... | collective-permute-start | bytes 786440 | tf_op jit(solution)/shard_map/ppermute | solution.py:358
  63.2 10.9 %collective-permute-start.17 = (f32[32,2048]{1,0:T(8,128)S(1)}, f32[32,2048]{1,0:T(8,128)S(1)}, u32[]{:S(2)}, u32[]{:S(2)}) collective-permute-start(f32[32,2048]{1,0:T(8,128)S(1)} %get-tuple-element.78), channel_id=1, source_target_pairs={{0,8},{1,9},{2,10},{3,11},{4,12},{5,13},{6,14},{7,15},{8,0},{9,1},... | collective-permute-start | bytes 786440 | tf_op jit(solution)/shard_map/ppermute | solution.py:358
  66.4 7.7 %collective-permute-start.20 = (f32[32,2048]{1,0:T(8,128)S(1)}, f32[32,2048]{1,0:T(8,128)S(1)}, u32[]{:S(2)}, u32[]{:S(2)}) collective-permute-start(f32[32,2048]{1,0:T(8,128)S(1)} %get-tuple-element.79), channel_id=1, source_target_pairs={{0,1},{1,0},{2,3},{3,2},{4,5},{5,4},{6,7},{7,6},{8,16},{9,17},{10,... | collective-permute-start | bytes 786440 | tf_op jit(solution)/shard_map/ppermute | solution.py:358
  68.8 11.6 %collective-permute-start.22 = (f32[32,2048]{1,0:T(8,128)S(1)}, f32[32,2048]{1,0:T(8,128)S(1)}, u32[]{:S(2)}, u32[]{:S(2)}) collective-permute-start(f32[32,2048]{1,0:T(8,128)S(1)} %get-tuple-element.82), channel_id=1, source_target_pairs={{0,1},{1,0},{2,3},{3,2},{4,5},{5,4},{6,7},{7,6},{8,16},{9,17},{10,... | collective-permute-start | bytes 786440 | tf_op jit(solution)/shard_map/ppermute | solution.py:358
  68.9 11.5 %collective-permute-start.19 = (f32[32,2048]{1,0:T(8,128)S(1)}, f32[32,2048]{1,0:T(8,128)S(1)}, u32[]{:S(2)}, u32[]{:S(2)}) collective-permute-start(f32[32,2048]{1,0:T(8,128)S(1)} %get-tuple-element.81), channel_id=1, source_target_pairs={{0,8},{1,9},{2,10},{3,11},{4,12},{5,13},{6,14},{7,15},{8,0},{9,1},... | collective-permute-start | bytes 786440 | tf_op jit(solution)/shard_map/ppermute | solution.py:358
  74.8 9.9 %collective-permute-start.21 = (f32[32,2048]{1,0:T(8,128)S(1)}, f32[32,2048]{1,0:T(8,128)S(1)}, u32[]{:S(2)}, u32[]{:S(2)}) collective-permute-start(f32[32,2048]{1,0:T(8,128)S(1)} %get-tuple-element.84), channel_id=1, source_target_pairs={{0,8},{1,9},{2,10},{3,11},{4,12},{5,13},{6,14},{7,15},{8,0},{9,1},... | collective-permute-start | bytes 786440 | tf_op jit(solution)/shard_map/ppermute | solution.py:358
  77.6 7.0 %collective-permute-start.23 = (f32[32,2048]{1,0:T(8,128)S(1)}, f32[32,2048]{1,0:T(8,128)S(1)}, u32[]{:S(2)}, u32[]{:S(2)}) collective-permute-start(f32[32,2048]{1,0:T(8,128)S(1)} %get-tuple-element.85), channel_id=1, source_target_pairs={{0,1},{1,0},{2,3},{3,2},{4,5},{5,4},{6,7},{7,6},{8,16},{9,17},{10,... | collective-permute-start | bytes 786440 | tf_op jit(solution)/shard_map/ppermute | solution.py:358
  93.3 15.7 %collective-permute-start.27 = (f32[32,512]{1,0:T(8,128)S(1)}, f32[32,512]{1,0:T(8,128)S(1)}, u32[]{:S(2)}, u32[]{:S(2)}) collective-permute-start(f32[32,512]{1,0:T(8,128)S(1)} %add.15.refs_0_), channel_id=1, source_target_pairs={{0,6},{1,7},{2,4},{3,5},{4,2},{5,3},{6,0},{7,1},{8,14},{9,15},{10,... | collective-permute-start | bytes 196616 | tf_op jit(solution)/shard_map/ppermute | solution.py:333
  95.9 13.7 %collective-permute-start.26 = (f32[32,512]{1,0:T(8,128)S(1)}, f32[32,512]{1,0:T(8,128)S(1)}, u32[]{:S(2)}, u32[]{:S(2)}) collective-permute-start(f32[32,512]{1,0:T(8,128)S(1)} %add.15.refs_0_), channel_id=1, source_target_pairs={{0,4},{1,5},{2,6},{3,7},{4,0},{5,1},{6,2},{7,3},{8,12},{9,13},{10,... | collective-permute-start | bytes 196616 | tf_op jit(solution)/shard_map/ppermute | solution.py:333
  96.5 13.8 %collective-permute-start.25 = (f32[32,512]{1,0:T(8,128)S(1)}, f32[32,512]{1,0:T(8,128)S(1)}, u32[]{:S(2)}, u32[]{:S(2)}) collective-permute-start(f32[32,512]{1,0:T(8,128)S(1)} %add.15.refs_0_), channel_id=1, source_target_pairs={{0,2},{1,3},{2,0},{3,1},{4,6},{5,7},{6,4},{7,5},{8,10},{9,11},{10,... | collective-permute-start | bytes 196616 | tf_op jit(solution)/shard_map/ppermute | solution.py:333
  123.3 8.8 %collective-permute-start.31 = (f32[128,384]{1,0:T(8,128)S(1)}, f32[128,384]{1,0:T(8,128)S(1)}, u32[]{:S(2)}, u32[]{:S(2)}) collective-permute-start(f32[128,384]{1,0:T(8,128)S(1)} %add.16), channel_id=1, source_target_pairs={{0,6},{1,7},{2,4},{3,5},{4,2},{5,3},{6,0},{7,1},{8,14},{9,15},{10,... | collective-permute-start | bytes 589832 | tf_op jit(solution)/shard_map/ppermute | solution.py:333
  123.4 11.2 %collective-permute-start.30 = (f32[128,384]{1,0:T(8,128)S(1)}, f32[128,384]{1,0:T(8,128)S(1)}, u32[]{:S(2)}, u32[]{:S(2)}) collective-permute-start(f32[128,384]{1,0:T(8,128)S(1)} %add.16), channel_id=1, source_target_pairs={{0,4},{1,5},{2,6},{3,7},{4,0},{5,1},{6,2},{7,3},{8,12},{9,13},{10,... | collective-permute-start | bytes 589832 | tf_op jit(solution)/shard_map/ppermute | solution.py:333
  125.4 9.2 %collective-permute-start.29 = (f32[128,384]{1,0:T(8,128)S(1)}, f32[128,384]{1,0:T(8,128)S(1)}, u32[]{:S(2)}, u32[]{:S(2)}) collective-permute-start(f32[128,384]{1,0:T(8,128)S(1)} %add.16), channel_id=1, source_target_pairs={{0,2},{1,3},{2,0},{3,1},{4,6},{5,7},{6,4},{7,5},{8,10},{9,11},{10,... | collective-permute-start | bytes 589832 | tf_op jit(solution)/shard_map/ppermute | solution.py:333
  134.6 3.6 %collective-permute-start.32 = (f32[128,384]{1,0:T(8,128)S(1)}, f32[128,384]{1,0:T(8,128)S(1)}, u32[]{:S(2)}, u32[]{:S(2)}) collective-permute-start(f32[128,384]{1,0:T(8,128)S(1)} %add_add_fusion.mine_ref), channel_id=1, source_target_pairs={{0,1},{1,0},{2,3},{3,2},{4,5},{5,4},{6,7},{7,6},{8,9},{9,8},{10,11... | collective-permute-start | bytes 589832 | tf_op jit(solution)/shard_map/ppermute | solution.py:333
  (16 other events, 140.9 us)

commit v4 on v3

--- a/solution.py
+++ b/solution.py
@@ -197,10 +197,10 @@
     return pl.pallas_call(
         kernel,
         out_shape=[
-            jax.ShapeDtypeStruct((height, ncols), jnp.bfloat16),
-            jax.ShapeDtypeStruct((height, ncols), jnp.bfloat16),
-            jax.ShapeDtypeStruct((ncols, height), jnp.bfloat16),
-            jax.ShapeDtypeStruct((ncols, height), jnp.bfloat16),
+            pltpu.HBM((height, ncols), jnp.bfloat16),
+            pltpu.HBM((height, ncols), jnp.bfloat16),
+            pltpu.HBM((ncols, height), jnp.bfloat16),
+            pltpu.HBM((ncols, height), jnp.bfloat16),
             jax.ShapeDtypeStruct((width, packed_width(steps, width)), jnp.float32),
         ],
         in_specs=[SMEM, SMEM, SMEM, ANY] + [ANY] * (2 * turns * splits),
@@ -265,13 +265,21 @@
     half = lead * rows // 2
     cuts = [0, lead // 4, lead] if lead % 4 == 0 else [0, lead]
 
-    def kernel(here_ref, x_ref, high_ref, low_ref, mine_ref, theirs_ref, held, total, sems):
+    def kernel(here_ref, x_ref, high_hbm, low_hbm, mine_ref, theirs_ref, held, high_ref, low_ref, total, sems):
+        vecs = [pltpu.make_async_copy(high_hbm, high_ref, sems.at[lead]), pltpu.make_async_copy(low_hbm, low_ref, sems.at[lead + 1])]
         copies = [pltpu.make_async_copy(x_ref.at[i], held.at[i], sems.at[i]) for i in range(lead)]
-        for copy in copies:
+        vecs[0].start()
+        for copy in copies[:cuts[1]]:
+            copy.start()
+        vecs[1].start()
+        for copy in copies[cuts[1]:]:
             copy.start()
         for start, end in zip(cuts[:-1], cuts[1:]):
             for copy in copies[start:end]:
                 copy.wait()
+            if start == 0:
+                for copy in vecs:
+                    copy.wait()
             block = held[start:end].reshape((end - start) * rows, ncols)
             total[start * rows:end * rows, :] = dot3(halves(block), (high_ref[...], low_ref[...]), ((1,), (0,)))
         core = lax.rem(here_ref[1], 2)
@@ -281,13 +289,18 @@
     return pl.pallas_call(
         kernel,
         out_shape=[jax.ShapeDtypeStruct((half // 2, 2 * height), jnp.float32)] * 2 + [pltpu.VMEM(x.shape, jnp.float32)],
-        in_specs=[SMEM, ANY, VMEM, VMEM],
+        in_specs=[SMEM, ANY, ANY, ANY],
         out_specs=[VMEM] * 3,
-        scratch_shapes=[pltpu.VMEM((lead * rows, height), jnp.float32), pltpu.SemaphoreType.DMA((lead,))],
+        scratch_shapes=[
+            pltpu.VMEM((ncols, height), jnp.bfloat16),
+            pltpu.VMEM((ncols, height), jnp.bfloat16),
+            pltpu.VMEM((lead * rows, height), jnp.float32),
+            pltpu.SemaphoreType.DMA((lead + 2,)),
+        ],
         compiler_params=params(),
         cost_estimate=cost(6 * lead * rows * ncols * height, 4 * lead * rows * ncols),
         name="inner_products",
-    )(here, in_hbm(x), *vecs_t)
+    )(here, in_hbm(x), *[in_hbm(v) for v in vecs_t])
 
 
 def update(here, x, mine, theirs, changes):
@@ -377,8 +390,10 @@
     cross = spread(gram + swap(gram, 1, n_wide), n_wide)
     changes = merge(cross, wy_factor, (high, low))
 
-    mine, theirs, x = inner_products(after(here, *cross), x, (high_t, low_t))
-    mine = functools.reduce(jnp.add, spread(mine + swap(theirs, 1, n_wide), n_wide))
+    mine, theirs, x = inner_products(after(here, cross[0]), x, (high_t, low_t))
+    sums = spread(mine + swap(theirs, 1, n_wide), n_wide)
+    sums[0] = after(sums[0], changes)
+    mine = functools.reduce(jnp.add, sums)
     return update(here, x, mine, swap(mine, 1, n_wide), changes).reshape(n_wide * rows, ncols)
 
 

time: 146 us -> 144 us (0.986)
  local copies, waits for them, and re-layouts: 5.71 us -> 0.03 us
  waiting for transfers between devices: 46.4 us -> 49.5 us
  Pallas kernels: 40.9 us -> 42.9 us
    all_to_all x1, waiting for transfers between devices: 0.01 us -> 13.3 us  [body(): x = lax.all_to_all(piece, 'wide', split_axis=0, concat_axis=0, tiled=True)]
    ppermute x9, waiting for transfers between devices: 22 us -> 11.8 us  [swap(): return lax.ppermute(array, 'wide', [(i, i ^ k) for i in range(size)])]
    unnamed x28 -> x12, local copies, waits for them, and re-layouts: 5.71 us -> 0.03 us
    pallas_call x1, Pallas kernels: 7.64 us -> 9.24 us  [inner_products(): pl.pallas_call(kernel, out_shape=[jax.ShapeDtypeStruct((half // 2, 2 * he...]
  transfers between devices with their start and end apart: 34 -> 34, of which waited for: 16 -> 17; matrix products, arithmetic and copies ran while one was open for 0% -> 0% of each run, Pallas kernels for 13% -> 13%
where the time goes in v4:
time: 144 us
  starting transfers between devices  51.2 us (36%)
  waiting for transfers between devices  49.5 us (34%)
  Pallas kernels  42.9 us (30%)
    ppermute x24, starting transfers between devices, exchange(): return lax.ppermute(array, ('row', 'wide'), pairs)  39.6 us
    ppermute x24, waiting for transfers between devices, exchange(): return lax.ppermute(array, ('row', 'wide'), pairs)  24.4 us
    all_to_all x1, waiting for transfers between devices, body(): x = lax.all_to_all(piece, 'wide', split_axis=0, concat_axis=0, tiled=True)  13.3 us
    ppermute x9, waiting for transfers between devices, swap(): return lax.ppermute(array, 'wide', [(i, i ^ k) for i in range(size)])  11.8 us
    pallas_call x1, Pallas kernels, inner_products(): pl.pallas_call(kernel, out_shape=[jax.ShapeDtypeStruct((half // 2, 2 * he...  9.24 us
    pallas_call x12, Pallas kernels, feed(): pl.pallas_call(kernel, out_shape=[jax.ShapeDtypeStruct((width, cols), jnp...  8.06 us
    pallas_call x1, Pallas kernels, assemble(): pl.pallas_call(kernel, out_shape=[pltpu.HBM((height, ncols), jnp.bfloat16...  7.64 us
    pallas_call x1, Pallas kernels, update(): pl.pallas_call(kernel, out_shape=jax.ShapeDtypeStruct(x.shape, jnp.float3...  7.43 us
  transfers between devices with their start and end apart: 34, of which 17 were waited for; matrix products, arithmetic and copies ran while one was open for 0% of the time, Pallas kernels for 13%

profile of v4, /device:TPU:0, one launch (start us, length us, event | category | flops | bytes accessed | tf_op | source)
XLA Modules:
  0.0 144.2 jit_solution(6730570525571507724)
XLA Ops:
  0.0 7.0 %pack.1 = f32[8,64,4096]{2,1,0:T(8,128)} custom-call(f32[64,32768]{1,0:T(8,128)} %x_ref.1), custom_call_target="tpu_custom_call" | custom-call | bytes 16777216 | tf_op jit(solution)/shard_map/pack/pallas_call | solution.py:81
  7.0 5.3 %all-to-all-start = ((f32[8,64,4096]{2,1,0:T(8,128)}), f32[8,64,4096]{2,1,0:T(8,128)}, u32[]{:S(2)}, u32[]{:S(2)}) async-start(f32[8,64,4096]{2,1,0:T(8,128)} %pack.1), calls=%async_computation | async-start | bytes 16777216 | tf_op jit(solution)/shard_map/all_to_all | solution.py:376
  13.1 2.9 %collective-permute-start = (f32[32,2048]{1,0:T(8,128)S(1)}, f32[32,2048]{1,0:T(8,128)S(1)}, u32[]{:S(2)}, u32[]{:S(2)}) collective-permute-start(f32[32,2048]{1,0:T(8,128)S(1)} %get-tuple-element.52), channel_id=1, source_target_pairs={{0,8},{1,9},{2,10},{3,11},{4,12},{5,13},{6,14},{7,15},{8,0},{9,1},... | collective-permute-start | bytes 786440 | tf_op jit(solution)/shard_map/ppermute | solution.py:371
  16.7 3.1 %collective-permute-start.1 = (f32[32,2048]{1,0:T(8,128)S(1)}, f32[32,2048]{1,0:T(8,128)S(1)}, u32[]{:S(2)}, u32[]{:S(2)}) collective-permute-start(f32[32,2048]{1,0:T(8,128)S(1)} %get-tuple-element.55), channel_id=1, source_target_pairs={{0,8},{1,9},{2,10},{3,11},{4,12},{5,13},{6,14},{7,15},{8,0},{9,1},... | collective-permute-start | bytes 786440 | tf_op jit(solution)/shard_map/ppermute | solution.py:371
  19.9 3.3 %collective-permute-done.refs_0_ = f32[32,2048]{1,0:T(8,128)S(1)} collective-permute-done((f32[32,2048]{1,0:T(8,128)S(1)}, f32[32,2048]{1,0:T(8,128)S(1)}, u32[]{:S(2)}, u32[]{:S(2)}) %collective-permute-start) | collective-permute-done | bytes 262176 | tf_op jit(solution)/shard_map/ppermute | solution.py:371
  23.8 3.2 %collective-permute-start.3 = (f32[32,2048]{1,0:T(8,128)S(1)}, f32[32,2048]{1,0:T(8,128)S(1)}, u32[]{:S(2)}, u32[]{:S(2)}) collective-permute-start(f32[32,2048]{1,0:T(8,128)S(1)} %get-tuple-element.58), channel_id=1, source_target_pairs={{0,8},{1,9},{2,10},{3,11},{4,12},{5,13},{6,14},{7,15},{8,0},{9,1},... | collective-permute-start | bytes 786440 | tf_op jit(solution)/shard_map/ppermute | solution.py:371
  27.0 1.8 %collective-permute-done.1.refs_0_.refs_1_ = f32[32,2048]{1,0:T(8,128)S(1)} collective-permute-done((f32[32,2048]{1,0:T(8,128)S(1)}, f32[32,2048]{1,0:T(8,128)S(1)}, u32[]{:S(2)}, u32[]{:S(2)}) %collective-permute-start.1) | collective-permute-done | bytes 262176 | tf_op jit(solution)/shard_map/ppermute | solution.py:371
  29.4 3.2 %collective-permute-start.5 = (f32[32,2048]{1,0:T(8,128)S(1)}, f32[32,2048]{1,0:T(8,128)S(1)}, u32[]{:S(2)}, u32[]{:S(2)}) collective-permute-start(f32[32,2048]{1,0:T(8,128)S(1)} %get-tuple-element.61), channel_id=1, source_target_pairs={{0,8},{1,9},{2,10},{3,11},{4,12},{5,13},{6,14},{7,15},{8,0},{9,1},... | collective-permute-start | bytes 786440 | tf_op jit(solution)/shard_map/ppermute | solution.py:371
  32.6 1.8 %collective-permute-done.3.refs_1_.refs_2_ = f32[32,2048]{1,0:T(8,128)S(1)} collective-permute-done((f32[32,2048]{1,0:T(8,128)S(1)}, f32[32,2048]{1,0:T(8,128)S(1)}, u32[]{:S(2)}, u32[]{:S(2)}) %collective-permute-start.3) | collective-permute-done | bytes 262176 | tf_op jit(solution)/shard_map/ppermute | solution.py:371
  35.1 3.2 %collective-permute-start.7 = (f32[32,2048]{1,0:T(8,128)S(1)}, f32[32,2048]{1,0:T(8,128)S(1)}, u32[]{:S(2)}, u32[]{:S(2)}) collective-permute-start(f32[32,2048]{1,0:T(8,128)S(1)} %get-tuple-element.64), channel_id=1, source_target_pairs={{0,8},{1,9},{2,10},{3,11},{4,12},{5,13},{6,14},{7,15},{8,0},{9,1},... | collective-permute-start | bytes 786440 | tf_op jit(solution)/shard_map/ppermute | solution.py:371
  38.2 1.8 %collective-permute-done.5.refs_1_.refs_3_ = f32[32,2048]{1,0:T(8,128)S(1)} collective-permute-done((f32[32,2048]{1,0:T(8,128)S(1)}, f32[32,2048]{1,0:T(8,128)S(1)}, u32[]{:S(2)}, u32[]{:S(2)}) %collective-permute-start.5) | collective-permute-done | bytes 262176 | tf_op jit(solution)/shard_map/ppermute | solution.py:371
  40.7 3.2 %collective-permute-start.9 = (f32[32,2048]{1,0:T(8,128)S(1)}, f32[32,2048]{1,0:T(8,128)S(1)}, u32[]{:S(2)}, u32[]{:S(2)}) collective-permute-start(f32[32,2048]{1,0:T(8,128)S(1)} %get-tuple-element.67), channel_id=1, source_target_pairs={{0,8},{1,9},{2,10},{3,11},{4,12},{5,13},{6,14},{7,15},{8,0},{9,1},... | collective-permute-start | bytes 786440 | tf_op jit(solution)/shard_map/ppermute | solution.py:371
  43.8 1.8 %collective-permute-done.7.refs_2_.refs_4_ = f32[32,2048]{1,0:T(8,128)S(1)} collective-permute-done((f32[32,2048]{1,0:T(8,128)S(1)}, f32[32,2048]{1,0:T(8,128)S(1)}, u32[]{:S(2)}, u32[]{:S(2)}) %collective-permute-start.7) | collective-permute-done | bytes 262176 | tf_op jit(solution)/shard_map/ppermute | solution.py:371
  46.3 3.2 %collective-permute-start.11 = (f32[32,2048]{1,0:T(8,128)S(1)}, f32[32,2048]{1,0:T(8,128)S(1)}, u32[]{:S(2)}, u32[]{:S(2)}) collective-permute-start(f32[32,2048]{1,0:T(8,128)S(1)} %get-tuple-element.70), channel_id=1, source_target_pairs={{0,8},{1,9},{2,10},{3,11},{4,12},{5,13},{6,14},{7,15},{8,0},{9,1},... | collective-permute-start | bytes 786440 | tf_op jit(solution)/shard_map/ppermute | solution.py:371
  49.5 1.8 %collective-permute-done.9.refs_2_.refs_5_ = f32[32,2048]{1,0:T(8,128)S(1)} collective-permute-done((f32[32,2048]{1,0:T(8,128)S(1)}, f32[32,2048]{1,0:T(8,128)S(1)}, u32[]{:S(2)}, u32[]{:S(2)}) %collective-permute-start.9) | collective-permute-done | bytes 262176 | tf_op jit(solution)/shard_map/ppermute | solution.py:371
  51.9 3.2 %collective-permute-start.13 = (f32[32,2048]{1,0:T(8,128)S(1)}, f32[32,2048]{1,0:T(8,128)S(1)}, u32[]{:S(2)}, u32[]{:S(2)}) collective-permute-start(f32[32,2048]{1,0:T(8,128)S(1)} %get-tuple-element.73), channel_id=1, source_target_pairs={{0,8},{1,9},{2,10},{3,11},{4,12},{5,13},{6,14},{7,15},{8,0},{9,1},... | collective-permute-start | bytes 786440 | tf_op jit(solution)/shard_map/ppermute | solution.py:371
  55.1 1.8 %collective-permute-done.11.refs_3_.refs_6_ = f32[32,2048]{1,0:T(8,128)S(1)} collective-permute-done((f32[32,2048]{1,0:T(8,128)S(1)}, f32[32,2048]{1,0:T(8,128)S(1)}, u32[]{:S(2)}, u32[]{:S(2)}) %collective-permute-start.11) | collective-permute-done | bytes 262176 | tf_op jit(solution)/shard_map/ppermute | solution.py:371
  57.5 3.2 %collective-permute-start.15 = (f32[32,2048]{1,0:T(8,128)S(1)}, f32[32,2048]{1,0:T(8,128)S(1)}, u32[]{:S(2)}, u32[]{:S(2)}) collective-permute-start(f32[32,2048]{1,0:T(8,128)S(1)} %get-tuple-element.76), channel_id=1, source_target_pairs={{0,8},{1,9},{2,10},{3,11},{4,12},{5,13},{6,14},{7,15},{8,0},{9,1},... | collective-permute-start | bytes 786440 | tf_op jit(solution)/shard_map/ppermute | solution.py:371
  60.7 1.7 %collective-permute-done.13.refs_3_.refs_7_ = f32[32,2048]{1,0:T(8,128)S(1)} collective-permute-done((f32[32,2048]{1,0:T(8,128)S(1)}, f32[32,2048]{1,0:T(8,128)S(1)}, u32[]{:S(2)}, u32[]{:S(2)}) %collective-permute-start.13) | collective-permute-done | bytes 262176 | tf_op jit(solution)/shard_map/ppermute | solution.py:371
  63.2 3.2 %collective-permute-start.17 = (f32[32,2048]{1,0:T(8,128)S(1)}, f32[32,2048]{1,0:T(8,128)S(1)}, u32[]{:S(2)}, u32[]{:S(2)}) collective-permute-start(f32[32,2048]{1,0:T(8,128)S(1)} %get-tuple-element.79), channel_id=1, source_target_pairs={{0,8},{1,9},{2,10},{3,11},{4,12},{5,13},{6,14},{7,15},{8,0},{9,1},... | collective-permute-start | bytes 786440 | tf_op jit(solution)/shard_map/ppermute | solution.py:371
  66.3 1.7 %collective-permute-done.15.refs_4_.refs_8_ = f32[32,2048]{1,0:T(8,128)S(1)} collective-permute-done((f32[32,2048]{1,0:T(8,128)S(1)}, f32[32,2048]{1,0:T(8,128)S(1)}, u32[]{:S(2)}, u32[]{:S(2)}) %collective-permute-start.15) | collective-permute-done | bytes 262176 | tf_op jit(solution)/shard_map/ppermute | solution.py:371
  68.9 5.1 %collective-permute-start.19 = (f32[32,2048]{1,0:T(8,128)S(1)}, f32[32,2048]{1,0:T(8,128)S(1)}, u32[]{:S(2)}, u32[]{:S(2)}) collective-permute-start(f32[32,2048]{1,0:T(8,128)S(1)} %get-tuple-element.82), channel_id=1, source_target_pairs={{0,8},{1,9},{2,10},{3,11},{4,12},{5,13},{6,14},{7,15},{8,0},{9,1},... | collective-permute-start | bytes 786440 | tf_op jit(solution)/shard_map/ppermute | solution.py:371
  74.7 2.8 %collective-permute-start.21 = (f32[32,2048]{1,0:T(8,128)S(1)}, f32[32,2048]{1,0:T(8,128)S(1)}, u32[]{:S(2)}, u32[]{:S(2)}) collective-permute-start(f32[32,2048]{1,0:T(8,128)S(1)} %get-tuple-element.85), channel_id=1, source_target_pairs={{0,8},{1,9},{2,10},{3,11},{4,12},{5,13},{6,14},{7,15},{8,0},{9,1},... | collective-permute-start | bytes 786440 | tf_op jit(solution)/shard_map/ppermute | solution.py:371
  77.6 2.8 %collective-permute-done.19.refs_10_ = f32[32,2048]{1,0:T(8,128)S(1)} collective-permute-done((f32[32,2048]{1,0:T(8,128)S(1)}, f32[32,2048]{1,0:T(8,128)S(1)}, u32[]{:S(2)}, u32[]{:S(2)}) %collective-permute-start.19) | collective-permute-done | bytes 262176 | tf_op jit(solution)/shard_map/ppermute | solution.py:371
  80.4 4.2 %collective-permute-done.21.refs_11_ = f32[32,2048]{1,0:T(8,128)S(1)} collective-permute-done((f32[32,2048]{1,0:T(8,128)S(1)}, f32[32,2048]{1,0:T(8,128)S(1)}, u32[]{:S(2)}, u32[]{:S(2)}) %collective-permute-start.21) | collective-permute-done | bytes 262176 | tf_op jit(solution)/shard_map/ppermute | solution.py:371
  84.6 7.6 %assemble.1 = (bf16[192,4096]{1,0:T(8,128)(2,1)}, bf16[192,4096]{1,0:T(8,128)(2,1)}, bf16[4096,192]{1,0:T(8,128)(2,1)}, bf16[4096,192]{1,0:T(8,128)(2,1)}, f32[32,512]{1,0:T(8,128)S(1)}) custom-call(s32[2]{0:T(128)S(1)} %pad_add_fusion.here_ref, s32[6]{0:T(128)S(1)} %copy-done.4, s32[6]{0:T(128)S(1)} %copy-done.5, f32[4,32,4096]{2,1,0:T(8,128)S(1)} %copy-done, ...), custom_call_target="tpu_custom_call" | custom-call | flops 1811939328 | bytes 6291456 | tf_op jit(solution)/shard_map/assemble/pallas_call | solution.py:197
  93.6 13.3 %all-to-all-done.x_ref = f32[8,64,4096]{2,1,0:T(8,128)} async-done(((f32[8,64,4096]{2,1,0:T(8,128)}), f32[8,64,4096]{2,1,0:T(8,128)}, u32[]{:S(2)}, u32[]{:S(2)}) %all-to-all-start) | async-done | bytes 8388640 | tf_op jit(solution)/shard_map/all_to_all | solution.py:376
  106.9 9.2 %inner_products.1 = (f32[128,384]{1,0:T(8,128)S(1)}, f32[128,384]{1,0:T(8,128)S(1)}, f32[8,64,4096]{2,1,0:T(8,128)S(1)}) custom-call(s32[2]{0:T(128)S(1)} %pad_add_fusion.here_ref, f32[8,64,4096]{2,1,0:T(8,128)} %all-to-all-done.x_ref, bf16[4096,192]{1,0:T(8,128)(2,1)} %get-tuple-element.89.high_hbm, bf16[4096,192]{1,0:T(8,128)(2,1)} %get-tuple-element.90.low_hbm), custom_call_target="tpu_custom_call" | custom-call | flops 2415919104 | bytes 8388608 | tf_op jit(solution)/shard_map/inner_products/pallas_call | solution.py:289
  117.7 1.6 %collective-permute-start.31 = (f32[128,384]{1,0:T(8,128)S(1)}, f32[128,384]{1,0:T(8,128)S(1)}, u32[]{:S(2)}, u32[]{:S(2)}) collective-permute-start(f32[128,384]{1,0:T(8,128)S(1)} %add.16), channel_id=1, source_target_pairs={{0,6},{1,7},{2,4},{3,5},{4,2},{5,3},{6,0},{7,1},{8,14},{9,15},{10,... | collective-permute-start | bytes 589832 | tf_op jit(solution)/shard_map/ppermute | solution.py:346
  123.4 8.1 %collective-permute-done.27.refs_2_ = f32[32,512]{1,0:T(8,128)S(1)} collective-permute-done((f32[32,512]{1,0:T(8,128)S(1)}, f32[32,512]{1,0:T(8,128)S(1)}, u32[]{:S(2)}, u32[]{:S(2)}) %collective-permute-start.27) | collective-permute-done | bytes 65568 | tf_op jit(solution)/shard_map/ppermute | solution.py:346
  131.5 3.5 %merge.1.p_ref = bf16[576,4096]{1,0:T(8,128)(2,1)S(1)} custom-call(f32[32,512]{1,0:T(8,128)S(1)} %add.15.refs_0_, f32[32,512]{1,0:T(8,128)S(1)} %collective-permute-done.26.refs_1_, f32[32,512]{1,0:T(8,128)S(1)} %collective-permute-done.27.refs_2_, f32[32,512]{1,0:T(8,128)S(1)} %collective-permute-done.28.refs_3_, f32[6,32,32]{2,1,0:T(8,128)S(1)} %copy-done.3, ...), custom_call_target="tpu_custom_call" | custom-call | flops 905969664 | bytes 6291456 | tf_op jit(solution)/shard_map/merge/pallas_call | solution.py:235
  136.6 7.4 %update.1 = f32[8,64,4096]{2,1,0:T(8,128)} custom-call(s32[2]{0:T(128)S(1)} %pad_add_fusion.here_ref, f32[128,384]{1,0:T(8,128)S(1)} %add_add_fusion.mine_ref, f32[128,384]{1,0:T(8,128)S(1)} %collective-permute-done.32.theirs_ref, f32[8,64,4096]{2,1,0:T(8,128)S(1)} %get-tuple-element.96.x_ref, bf16[576,4096]{1,0:T(8,128)(2,1)S(1)} %merge.1.p_ref), custom_call_target="tpu_custom_call" | custom-call | flops 2415919104 | bytes 16777216 | tf_op jit(solution)/shard_map/update/pallas_call | solution.py:329
  (69 shorter events, 16.8 us)
Async XLA Ops:
  7.0 99.9 %all-to-all-start = ((f32[8,64,4096]{2,1,0:T(8,128)}), f32[8,64,4096]{2,1,0:T(8,128)}, u32[]{:S(2)}, u32[]{:S(2)}) async-start(f32[8,64,4096]{2,1,0:T(8,128)} %pack.1), calls=%async_computation | async-start | bytes 16777216 | tf_op jit(solution)/shard_map/all_to_all | solution.py:376
  13.1 10.1 %collective-permute-start = (f32[32,2048]{1,0:T(8,128)S(1)}, f32[32,2048]{1,0:T(8,128)S(1)}, u32[]{:S(2)}, u32[]{:S(2)}) collective-permute-start(f32[32,2048]{1,0:T(8,128)S(1)} %get-tuple-element.52), channel_id=1, source_target_pairs={{0,8},{1,9},{2,10},{3,11},{4,12},{5,13},{6,14},{7,15},{8,0},{9,1},... | collective-permute-start | bytes 786440 | tf_op jit(solution)/shard_map/ppermute | solution.py:371
  16.0 7.1 %collective-permute-start.2 = (f32[32,2048]{1,0:T(8,128)S(1)}, f32[32,2048]{1,0:T(8,128)S(1)}, u32[]{:S(2)}, u32[]{:S(2)}) collective-permute-start(f32[32,2048]{1,0:T(8,128)S(1)} %get-tuple-element.53), channel_id=1, source_target_pairs={{0,1},{1,0},{2,3},{3,2},{4,5},{5,4},{6,7},{7,6},{8,16},{9,17},{10,... | collective-permute-start | bytes 786440 | tf_op jit(solution)/shard_map/ppermute | solution.py:371
  16.7 12.0 %collective-permute-start.1 = (f32[32,2048]{1,0:T(8,128)S(1)}, f32[32,2048]{1,0:T(8,128)S(1)}, u32[]{:S(2)}, u32[]{:S(2)}) collective-permute-start(f32[32,2048]{1,0:T(8,128)S(1)} %get-tuple-element.55), channel_id=1, source_target_pairs={{0,8},{1,9},{2,10},{3,11},{4,12},{5,13},{6,14},{7,15},{8,0},{9,1},... | collective-permute-start | bytes 786440 | tf_op jit(solution)/shard_map/ppermute | solution.py:371
  19.9 8.9 %collective-permute-start.4 = (f32[32,2048]{1,0:T(8,128)S(1)}, f32[32,2048]{1,0:T(8,128)S(1)}, u32[]{:S(2)}, u32[]{:S(2)}) collective-permute-start(f32[32,2048]{1,0:T(8,128)S(1)} %get-tuple-element.56), channel_id=1, source_target_pairs={{0,1},{1,0},{2,3},{3,2},{4,5},{5,4},{6,7},{7,6},{8,16},{9,17},{10,... | collective-permute-start | bytes 786440 | tf_op jit(solution)/shard_map/ppermute | solution.py:371
  23.8 10.6 %collective-permute-start.3 = (f32[32,2048]{1,0:T(8,128)S(1)}, f32[32,2048]{1,0:T(8,128)S(1)}, u32[]{:S(2)}, u32[]{:S(2)}) collective-permute-start(f32[32,2048]{1,0:T(8,128)S(1)} %get-tuple-element.58), channel_id=1, source_target_pairs={{0,8},{1,9},{2,10},{3,11},{4,12},{5,13},{6,14},{7,15},{8,0},{9,1},... | collective-permute-start | bytes 786440 | tf_op jit(solution)/shard_map/ppermute | solution.py:371
  27.0 7.4 %collective-permute-start.6 = (f32[32,2048]{1,0:T(8,128)S(1)}, f32[32,2048]{1,0:T(8,128)S(1)}, u32[]{:S(2)}, u32[]{:S(2)}) collective-permute-start(f32[32,2048]{1,0:T(8,128)S(1)} %get-tuple-element.59), channel_id=1, source_target_pairs={{0,1},{1,0},{2,3},{3,2},{4,5},{5,4},{6,7},{7,6},{8,16},{9,17},{10,... | collective-permute-start | bytes 786440 | tf_op jit(solution)/shard_map/ppermute | solution.py:371
  29.4 10.6 %collective-permute-start.5 = (f32[32,2048]{1,0:T(8,128)S(1)}, f32[32,2048]{1,0:T(8,128)S(1)}, u32[]{:S(2)}, u32[]{:S(2)}) collective-permute-start(f32[32,2048]{1,0:T(8,128)S(1)} %get-tuple-element.61), channel_id=1, source_target_pairs={{0,8},{1,9},{2,10},{3,11},{4,12},{5,13},{6,14},{7,15},{8,0},{9,1},... | collective-permute-start | bytes 786440 | tf_op jit(solution)/shard_map/ppermute | solution.py:371
  32.6 7.4 %collective-permute-start.8 = (f32[32,2048]{1,0:T(8,128)S(1)}, f32[32,2048]{1,0:T(8,128)S(1)}, u32[]{:S(2)}, u32[]{:S(2)}) collective-permute-start(f32[32,2048]{1,0:T(8,128)S(1)} %get-tuple-element.62), channel_id=1, source_target_pairs={{0,1},{1,0},{2,3},{3,2},{4,5},{5,4},{6,7},{7,6},{8,16},{9,17},{10,... | collective-permute-start | bytes 786440 | tf_op jit(solution)/shard_map/ppermute | solution.py:371
  35.1 10.6 %collective-permute-start.7 = (f32[32,2048]{1,0:T(8,128)S(1)}, f32[32,2048]{1,0:T(8,128)S(1)}, u32[]{:S(2)}, u32[]{:S(2)}) collective-permute-start(f32[32,2048]{1,0:T(8,128)S(1)} %get-tuple-element.64), channel_id=1, source_target_pairs={{0,8},{1,9},{2,10},{3,11},{4,12},{5,13},{6,14},{7,15},{8,0},{9,1},... | collective-permute-start | bytes 786440 | tf_op jit(solution)/shard_map/ppermute | solution.py:371
  38.2 7.4 %collective-permute-start.10 = (f32[32,2048]{1,0:T(8,128)S(1)}, f32[32,2048]{1,0:T(8,128)S(1)}, u32[]{:S(2)}, u32[]{:S(2)}) collective-permute-start(f32[32,2048]{1,0:T(8,128)S(1)} %get-tuple-element.65), channel_id=1, source_target_pairs={{0,1},{1,0},{2,3},{3,2},{4,5},{5,4},{6,7},{7,6},{8,16},{9,17},{10,... | collective-permute-start | bytes 786440 | tf_op jit(solution)/shard_map/ppermute | solution.py:371
  40.7 10.6 %collective-permute-start.9 = (f32[32,2048]{1,0:T(8,128)S(1)}, f32[32,2048]{1,0:T(8,128)S(1)}, u32[]{:S(2)}, u32[]{:S(2)}) collective-permute-start(f32[32,2048]{1,0:T(8,128)S(1)} %get-tuple-element.67), channel_id=1, source_target_pairs={{0,8},{1,9},{2,10},{3,11},{4,12},{5,13},{6,14},{7,15},{8,0},{9,1},... | collective-permute-start | bytes 786440 | tf_op jit(solution)/shard_map/ppermute | solution.py:371
  43.8 7.4 %collective-permute-start.12 = (f32[32,2048]{1,0:T(8,128)S(1)}, f32[32,2048]{1,0:T(8,128)S(1)}, u32[]{:S(2)}, u32[]{:S(2)}) collective-permute-start(f32[32,2048]{1,0:T(8,128)S(1)} %get-tuple-element.68), channel_id=1, source_target_pairs={{0,1},{1,0},{2,3},{3,2},{4,5},{5,4},{6,7},{7,6},{8,16},{9,17},{10,... | collective-permute-start | bytes 786440 | tf_op jit(solution)/shard_map/ppermute | solution.py:371
  46.3 10.5 %collective-permute-start.11 = (f32[32,2048]{1,0:T(8,128)S(1)}, f32[32,2048]{1,0:T(8,128)S(1)}, u32[]{:S(2)}, u32[]{:S(2)}) collective-permute-start(f32[32,2048]{1,0:T(8,128)S(1)} %get-tuple-element.70), channel_id=1, source_target_pairs={{0,8},{1,9},{2,10},{3,11},{4,12},{5,13},{6,14},{7,15},{8,0},{9,1},... | collective-permute-start | bytes 786440 | tf_op jit(solution)/shard_map/ppermute | solution.py:371
  49.5 7.4 %collective-permute-start.14 = (f32[32,2048]{1,0:T(8,128)S(1)}, f32[32,2048]{1,0:T(8,128)S(1)}, u32[]{:S(2)}, u32[]{:S(2)}) collective-permute-start(f32[32,2048]{1,0:T(8,128)S(1)} %get-tuple-element.71), channel_id=1, source_target_pairs={{0,1},{1,0},{2,3},{3,2},{4,5},{5,4},{6,7},{7,6},{8,16},{9,17},{10,... | collective-permute-start | bytes 786440 | tf_op jit(solution)/shard_map/ppermute | solution.py:371
  51.9 10.5 %collective-permute-start.13 = (f32[32,2048]{1,0:T(8,128)S(1)}, f32[32,2048]{1,0:T(8,128)S(1)}, u32[]{:S(2)}, u32[]{:S(2)}) collective-permute-start(f32[32,2048]{1,0:T(8,128)S(1)} %get-tuple-element.73), channel_id=1, source_target_pairs={{0,8},{1,9},{2,10},{3,11},{4,12},{5,13},{6,14},{7,15},{8,0},{9,1},... | collective-permute-start | bytes 786440 | tf_op jit(solution)/shard_map/ppermute | solution.py:371
  55.1 7.4 %collective-permute-start.16 = (f32[32,2048]{1,0:T(8,128)S(1)}, f32[32,2048]{1,0:T(8,128)S(1)}, u32[]{:S(2)}, u32[]{:S(2)}) collective-permute-start(f32[32,2048]{1,0:T(8,128)S(1)} %get-tuple-element.74), channel_id=1, source_target_pairs={{0,1},{1,0},{2,3},{3,2},{4,5},{5,4},{6,7},{7,6},{8,16},{9,17},{10,... | collective-permute-start | bytes 786440 | tf_op jit(solution)/shard_map/ppermute | solution.py:371
  57.5 10.5 %collective-permute-start.15 = (f32[32,2048]{1,0:T(8,128)S(1)}, f32[32,2048]{1,0:T(8,128)S(1)}, u32[]{:S(2)}, u32[]{:S(2)}) collective-permute-start(f32[32,2048]{1,0:T(8,128)S(1)} %get-tuple-element.76), channel_id=1, source_target_pairs={{0,8},{1,9},{2,10},{3,11},{4,12},{5,13},{6,14},{7,15},{8,0},{9,1},... | collective-permute-start | bytes 786440 | tf_op jit(solution)/shard_map/ppermute | solution.py:371
  60.7 7.4 %collective-permute-start.18 = (f32[32,2048]{1,0:T(8,128)S(1)}, f32[32,2048]{1,0:T(8,128)S(1)}, u32[]{:S(2)}, u32[]{:S(2)}) collective-permute-start(f32[32,2048]{1,0:T(8,128)S(1)} %get-tuple-element.77), channel_id=1, source_target_pairs={{0,1},{1,0},{2,3},{3,2},{4,5},{5,4},{6,7},{7,6},{8,16},{9,17},{10,... | collective-permute-start | bytes 786440 | tf_op jit(solution)/shard_map/ppermute | solution.py:371
  63.2 10.9 %collective-permute-start.17 = (f32[32,2048]{1,0:T(8,128)S(1)}, f32[32,2048]{1,0:T(8,128)S(1)}, u32[]{:S(2)}, u32[]{:S(2)}) collective-permute-start(f32[32,2048]{1,0:T(8,128)S(1)} %get-tuple-element.79), channel_id=1, source_target_pairs={{0,8},{1,9},{2,10},{3,11},{4,12},{5,13},{6,14},{7,15},{8,0},{9,1},... | collective-permute-start | bytes 786440 | tf_op jit(solution)/shard_map/ppermute | solution.py:371
  66.3 7.7 %collective-permute-start.20 = (f32[32,2048]{1,0:T(8,128)S(1)}, f32[32,2048]{1,0:T(8,128)S(1)}, u32[]{:S(2)}, u32[]{:S(2)}) collective-permute-start(f32[32,2048]{1,0:T(8,128)S(1)} %get-tuple-element.80), channel_id=1, source_target_pairs={{0,1},{1,0},{2,3},{3,2},{4,5},{5,4},{6,7},{7,6},{8,16},{9,17},{10,... | collective-permute-start | bytes 786440 | tf_op jit(solution)/shard_map/ppermute | solution.py:371
  68.8 11.6 %collective-permute-start.22 = (f32[32,2048]{1,0:T(8,128)S(1)}, f32[32,2048]{1,0:T(8,128)S(1)}, u32[]{:S(2)}, u32[]{:S(2)}) collective-permute-start(f32[32,2048]{1,0:T(8,128)S(1)} %get-tuple-element.83), channel_id=1, source_target_pairs={{0,1},{1,0},{2,3},{3,2},{4,5},{5,4},{6,7},{7,6},{8,16},{9,17},{10,... | collective-permute-start | bytes 786440 | tf_op jit(solution)/shard_map/ppermute | solution.py:371
  68.9 11.5 %collective-permute-start.19 = (f32[32,2048]{1,0:T(8,128)S(1)}, f32[32,2048]{1,0:T(8,128)S(1)}, u32[]{:S(2)}, u32[]{:S(2)}) collective-permute-start(f32[32,2048]{1,0:T(8,128)S(1)} %get-tuple-element.82), channel_id=1, source_target_pairs={{0,8},{1,9},{2,10},{3,11},{4,12},{5,13},{6,14},{7,15},{8,0},{9,1},... | collective-permute-start | bytes 786440 | tf_op jit(solution)/shard_map/ppermute | solution.py:371
  74.7 9.9 %collective-permute-start.21 = (f32[32,2048]{1,0:T(8,128)S(1)}, f32[32,2048]{1,0:T(8,128)S(1)}, u32[]{:S(2)}, u32[]{:S(2)}) collective-permute-start(f32[32,2048]{1,0:T(8,128)S(1)} %get-tuple-element.85), channel_id=1, source_target_pairs={{0,8},{1,9},{2,10},{3,11},{4,12},{5,13},{6,14},{7,15},{8,0},{9,1},... | collective-permute-start | bytes 786440 | tf_op jit(solution)/shard_map/ppermute | solution.py:371
  77.6 7.0 %collective-permute-start.23 = (f32[32,2048]{1,0:T(8,128)S(1)}, f32[32,2048]{1,0:T(8,128)S(1)}, u32[]{:S(2)}, u32[]{:S(2)}) collective-permute-start(f32[32,2048]{1,0:T(8,128)S(1)} %get-tuple-element.86), channel_id=1, source_target_pairs={{0,1},{1,0},{2,3},{3,2},{4,5},{5,4},{6,7},{7,6},{8,16},{9,17},{10,... | collective-permute-start | bytes 786440 | tf_op jit(solution)/shard_map/ppermute | solution.py:371
  116.2 1.5 %collective-permute-start.25 = (f32[128,384]{1,0:T(8,128)S(1)}, f32[128,384]{1,0:T(8,128)S(1)}, u32[]{:S(2)}, u32[]{:S(2)}) collective-permute-start(f32[128,384]{1,0:T(8,128)S(1)} %get-tuple-element.92), channel_id=1, source_target_pairs={{0,1},{1,0},{2,3},{3,2},{4,5},{5,4},{6,7},{7,6},{8,9},{9,8},{10,11... | collective-permute-start | bytes 589832 | tf_op jit(solution)/shard_map/ppermute | solution.py:346
  116.3 5.7 %collective-permute-start.28 = (f32[32,512]{1,0:T(8,128)S(1)}, f32[32,512]{1,0:T(8,128)S(1)}, u32[]{:S(2)}, u32[]{:S(2)}) collective-permute-start(f32[32,512]{1,0:T(8,128)S(1)} %add.15.refs_0_), channel_id=1, source_target_pairs={{0,6},{1,7},{2,4},{3,5},{4,2},{5,3},{6,0},{7,1},{8,14},{9,15},{10,... | collective-permute-start | bytes 196616 | tf_op jit(solution)/shard_map/ppermute | solution.py:346
  117.7 17.3 %collective-permute-start.31 = (f32[128,384]{1,0:T(8,128)S(1)}, f32[128,384]{1,0:T(8,128)S(1)}, u32[]{:S(2)}, u32[]{:S(2)}) collective-permute-start(f32[128,384]{1,0:T(8,128)S(1)} %add.16), channel_id=1, source_target_pairs={{0,6},{1,7},{2,4},{3,5},{4,2},{5,3},{6,0},{7,1},{8,14},{9,15},{10,... | collective-permute-start | bytes 589832 | tf_op jit(solution)/shard_map/ppermute | solution.py:346
  119.3 15.7 %collective-permute-start.30 = (f32[128,384]{1,0:T(8,128)S(1)}, f32[128,384]{1,0:T(8,128)S(1)}, u32[]{:S(2)}, u32[]{:S(2)}) collective-permute-start(f32[128,384]{1,0:T(8,128)S(1)} %add.16), channel_id=1, source_target_pairs={{0,4},{1,5},{2,6},{3,7},{4,0},{5,1},{6,2},{7,3},{8,12},{9,13},{10,... | collective-permute-start | bytes 589832 | tf_op jit(solution)/shard_map/ppermute | solution.py:346
  119.8 15.3 %collective-permute-start.29 = (f32[128,384]{1,0:T(8,128)S(1)}, f32[128,384]{1,0:T(8,128)S(1)}, u32[]{:S(2)}, u32[]{:S(2)}) collective-permute-start(f32[128,384]{1,0:T(8,128)S(1)} %add.16), channel_id=1, source_target_pairs={{0,2},{1,3},{2,0},{3,1},{4,6},{5,7},{6,4},{7,5},{8,10},{9,11},{10,... | collective-permute-start | bytes 589832 | tf_op jit(solution)/shard_map/ppermute | solution.py:346
  121.3 10.2 %collective-permute-start.27 = (f32[32,512]{1,0:T(8,128)S(1)}, f32[32,512]{1,0:T(8,128)S(1)}, u32[]{:S(2)}, u32[]{:S(2)}) collective-permute-start(f32[32,512]{1,0:T(8,128)S(1)} %add.15.refs_0_), channel_id=1, source_target_pairs={{0,4},{1,5},{2,6},{3,7},{4,0},{5,1},{6,2},{7,3},{8,12},{9,13},{10,... | collective-permute-start | bytes 196616 | tf_op jit(solution)/shard_map/ppermute | solution.py:346
  122.0 9.5 %collective-permute-start.26 = (f32[32,512]{1,0:T(8,128)S(1)}, f32[32,512]{1,0:T(8,128)S(1)}, u32[]{:S(2)}, u32[]{:S(2)}) collective-permute-start(f32[32,512]{1,0:T(8,128)S(1)} %add.15.refs_0_), channel_id=1, source_target_pairs={{0,2},{1,3},{2,0},{3,1},{4,6},{5,7},{6,4},{7,5},{8,10},{9,11},{10,... | collective-permute-start | bytes 196616 | tf_op jit(solution)/shard_map/ppermute | solution.py:346
  (8 other events, 105.7 us)

commit v5 on v4

--- a/solution.py
+++ b/solution.py
@@ -263,25 +263,25 @@
     lead, rows, ncols = x.shape
     height = vecs_t[0].shape[1]
     half = lead * rows // 2
-    cuts = [0, lead // 4, lead] if lead % 4 == 0 else [0, lead]
+    blocks = column_blocks(ncols)
 
     def kernel(here_ref, x_ref, high_hbm, low_hbm, mine_ref, theirs_ref, held, high_ref, low_ref, total, sems):
-        vecs = [pltpu.make_async_copy(high_hbm, high_ref, sems.at[lead]), pltpu.make_async_copy(low_hbm, low_ref, sems.at[lead + 1])]
-        copies = [pltpu.make_async_copy(x_ref.at[i], held.at[i], sems.at[i]) for i in range(lead)]
-        vecs[0].start()
-        for copy in copies[:cuts[1]]:
-            copy.start()
-        vecs[1].start()
-        for copy in copies[cuts[1]:]:
-            copy.start()
-        for start, end in zip(cuts[:-1], cuts[1:]):
-            for copy in copies[start:end]:
+        copies = []
+        for i, at in enumerate(blocks):
+            copies.append([
+                pltpu.make_async_copy(high_hbm.at[at], high_ref.at[at], sems.at[i, 0]),
+                pltpu.make_async_copy(low_hbm.at[at], low_ref.at[at], sems.at[i, 1]),
+                pltpu.make_async_copy(x_ref.at[:, :, at], held.at[:, :, at], sems.at[i, 2]),
+            ])
+        for block in copies:
+            for copy in block:
+                copy.start()
+        for i, at in enumerate(blocks):
+            for copy in copies[i]:
                 copy.wait()
-            if start == 0:
-                for copy in vecs:
-                    copy.wait()
-            block = held[start:end].reshape((end - start) * rows, ncols)
-            total[start * rows:end * rows, :] = dot3(halves(block), (high_ref[...], low_ref[...]), ((1,), (0,)))
+            block = held[:, :, at].reshape(lead * rows, at.size)
+            part = dot3(halves(block), (high_ref[at, :], low_ref[at, :]), ((1,), (0,)))
+            total[...] = part if i == 0 else total[...] + part
         core = lax.rem(here_ref[1], 2)
         mine_ref[...] = fold(total[pl.ds(pl.multiple_of(core * half, 8), half), :])
         theirs_ref[...] = fold(total[pl.ds(pl.multiple_of((1 - core) * half, 8), half), :])
@@ -295,7 +295,7 @@
             pltpu.VMEM((ncols, height), jnp.bfloat16),
             pltpu.VMEM((ncols, height), jnp.bfloat16),
             pltpu.VMEM((lead * rows, height), jnp.float32),
-            pltpu.SemaphoreType.DMA((lead + 2,)),
+            pltpu.SemaphoreType.DMA((len(blocks), 3)),
         ],
         compiler_params=params(),
         cost_estimate=cost(6 * lead * rows * ncols * height, 4 * lead * rows * ncols),
@@ -348,6 +348,18 @@
 
 def spread(pair, size):
     return [pair] + [swap(pair, k, size) for k in range(2, size, 2)]
+
+
+def chips_sum(pair, size, token):
+    shifts = [k for k in (1 << i for i in range(1, size.bit_length())) if k < size]
+    half = pair.shape[0] // 2
+    upper, lower = pair[:half], pair[half:]
+    for i, (first, second) in enumerate(zip(shifts, reversed(shifts))):
+        come_upper, come_lower = swap(upper, first, size), swap(lower, second, size)
+        if i == len(shifts) - 1:
+            upper = after(upper, token)
+        upper, lower = upper + come_upper, lower + come_lower
+    return jnp.concatenate([upper, lower], axis=0)
 
 
 def body(n_row, n_wide, eigvec_t, householder, wy_factor, block_place, offsets):
@@ -387,13 +399,11 @@
     evens = list(zip(*[stream[0] for stream in streams]))
     odds = list(zip(*[stream[1] for stream in streams]))
     high, low, high_t, low_t, gram = assemble(here, block_place, offsets, householder, evens, odds, n_row)
-    cross = spread(gram + swap(gram, 1, n_wide), n_wide)
-    changes = merge(cross, wy_factor, (high, low))
-
-    mine, theirs, x = inner_products(after(here, cross[0]), x, (high_t, low_t))
-    sums = spread(mine + swap(theirs, 1, n_wide), n_wide)
-    sums[0] = after(sums[0], changes)
-    mine = functools.reduce(jnp.add, sums)
+    cross = functools.reduce(jnp.add, spread(gram + swap(gram, 1, n_wide), n_wide))
+    changes = merge([cross], wy_factor, (high, low))
+
+    mine, theirs, x = inner_products(after(here, cross), x, (high_t, low_t))
+    mine = chips_sum(mine + swap(theirs, 1, n_wide), n_wide, changes)
     return update(here, x, mine, swap(mine, 1, n_wide), changes).reshape(n_wide * rows, ncols)
 
 

time: 144 us -> 143 us (level)
  waiting for transfers between devices: 49.5 us -> 45.4 us
    all_to_all x1, waiting for transfers between devices: 13.3 us -> 0.01 us  [body(): x = lax.all_to_all(piece, 'wide', split_axis=0, concat_axis=0, tiled=True)]
    ppermute x9 -> x10, waiting for transfers between devices: 11.8 us -> 21 us  [swap(): return lax.ppermute(array, 'wide', [(i, i ^ k) for i in range(size)])]
    ppermute x9 -> x10, starting transfers between devices: 6.33 us -> 7.18 us  [swap(): return lax.ppermute(array, 'wide', [(i, i ^ k) for i in range(size)])]
  transfers between devices with their start and end apart: 34 -> 35, of which waited for: 17 -> 19; matrix products, arithmetic and copies ran while one was open for 0% -> 0% of each run, Pallas kernels for 13% -> 13%
where the time goes in v5:
time: 143 us; the launch traced here: 142 us
  starting transfers between devices  52.1 us (36%)
  waiting for transfers between devices  45.4 us (32%)
  Pallas kernels  44.2 us (31%)
    ppermute x24, starting transfers between devices, exchange(): return lax.ppermute(array, ('row', 'wide'), pairs)  39.6 us
    ppermute x24, waiting for transfers between devices, exchange(): return lax.ppermute(array, ('row', 'wide'), pairs)  24.4 us
    ppermute x10, waiting for transfers between devices, swap(): return lax.ppermute(array, 'wide', [(i, i ^ k) for i in range(size)])  21 us
    pallas_call x1, Pallas kernels, inner_products(): pl.pallas_call(kernel, out_shape=[jax.ShapeDtypeStruct((half // 2, 2 * he...  10.3 us
    pallas_call x12, Pallas kernels, feed(): pl.pallas_call(kernel, out_shape=[jax.ShapeDtypeStruct((width, cols), jnp...  8.06 us
    pallas_call x1, Pallas kernels, update(): pl.pallas_call(kernel, out_shape=jax.ShapeDtypeStruct(x.shape, jnp.float3...  7.66 us
    pallas_call x1, Pallas kernels, assemble(): pl.pallas_call(kernel, out_shape=[pltpu.HBM((height, ncols), jnp.bfloat16...  7.65 us
    ppermute x10, starting transfers between devices, swap(): return lax.ppermute(array, 'wide', [(i, i ^ k) for i in range(size)])  7.18 us
  transfers between devices with their start and end apart: 35, of which 19 were waited for; matrix products, arithmetic and copies ran while one was open for 0% of the time, Pallas kernels for 13%

profile of v5, /device:TPU:0, one launch (start us, length us, event | category | flops | bytes accessed | tf_op | source)
XLA Modules:
  0.0 142.4 jit_solution(17770891326140192078)
XLA Ops:
  0.0 7.0 %pack.1 = f32[8,64,4096]{2,1,0:T(8,128)} custom-call(f32[64,32768]{1,0:T(8,128)} %x_ref.1), custom_call_target="tpu_custom_call" | custom-call | bytes 16777216 | tf_op jit(solution)/shard_map/pack/pallas_call | solution.py:81
  7.0 5.3 %all-to-all-start = ((f32[8,64,4096]{2,1,0:T(8,128)}), f32[8,64,4096]{2,1,0:T(8,128)}, u32[]{:S(2)}, u32[]{:S(2)}) async-start(f32[8,64,4096]{2,1,0:T(8,128)} %pack.1), calls=%async_computation | async-start | bytes 16777216 | tf_op jit(solution)/shard_map/all_to_all | solution.py:388
  13.1 2.9 %collective-permute-start = (f32[32,2048]{1,0:T(8,128)S(1)}, f32[32,2048]{1,0:T(8,128)S(1)}, u32[]{:S(2)}, u32[]{:S(2)}) collective-permute-start(f32[32,2048]{1,0:T(8,128)S(1)} %get-tuple-element.52), channel_id=1, source_target_pairs={{0,8},{1,9},{2,10},{3,11},{4,12},{5,13},{6,14},{7,15},{8,0},{9,1},... | collective-permute-start | bytes 786440 | tf_op jit(solution)/shard_map/ppermute | solution.py:383
  16.7 3.1 %collective-permute-start.1 = (f32[32,2048]{1,0:T(8,128)S(1)}, f32[32,2048]{1,0:T(8,128)S(1)}, u32[]{:S(2)}, u32[]{:S(2)}) collective-permute-start(f32[32,2048]{1,0:T(8,128)S(1)} %get-tuple-element.55), channel_id=1, source_target_pairs={{0,8},{1,9},{2,10},{3,11},{4,12},{5,13},{6,14},{7,15},{8,0},{9,1},... | collective-permute-start | bytes 786440 | tf_op jit(solution)/shard_map/ppermute | solution.py:383
  19.9 3.3 %collective-permute-done.refs_0_ = f32[32,2048]{1,0:T(8,128)S(1)} collective-permute-done((f32[32,2048]{1,0:T(8,128)S(1)}, f32[32,2048]{1,0:T(8,128)S(1)}, u32[]{:S(2)}, u32[]{:S(2)}) %collective-permute-start) | collective-permute-done | bytes 262176 | tf_op jit(solution)/shard_map/ppermute | solution.py:383
  23.8 3.2 %collective-permute-start.3 = (f32[32,2048]{1,0:T(8,128)S(1)}, f32[32,2048]{1,0:T(8,128)S(1)}, u32[]{:S(2)}, u32[]{:S(2)}) collective-permute-start(f32[32,2048]{1,0:T(8,128)S(1)} %get-tuple-element.58), channel_id=1, source_target_pairs={{0,8},{1,9},{2,10},{3,11},{4,12},{5,13},{6,14},{7,15},{8,0},{9,1},... | collective-permute-start | bytes 786440 | tf_op jit(solution)/shard_map/ppermute | solution.py:383
  27.0 1.8 %collective-permute-done.1.refs_0_.refs_1_ = f32[32,2048]{1,0:T(8,128)S(1)} collective-permute-done((f32[32,2048]{1,0:T(8,128)S(1)}, f32[32,2048]{1,0:T(8,128)S(1)}, u32[]{:S(2)}, u32[]{:S(2)}) %collective-permute-start.1) | collective-permute-done | bytes 262176 | tf_op jit(solution)/shard_map/ppermute | solution.py:383
  29.5 3.2 %collective-permute-start.5 = (f32[32,2048]{1,0:T(8,128)S(1)}, f32[32,2048]{1,0:T(8,128)S(1)}, u32[]{:S(2)}, u32[]{:S(2)}) collective-permute-start(f32[32,2048]{1,0:T(8,128)S(1)} %get-tuple-element.61), channel_id=1, source_target_pairs={{0,8},{1,9},{2,10},{3,11},{4,12},{5,13},{6,14},{7,15},{8,0},{9,1},... | collective-permute-start | bytes 786440 | tf_op jit(solution)/shard_map/ppermute | solution.py:383
  32.6 1.8 %collective-permute-done.3.refs_1_.refs_2_ = f32[32,2048]{1,0:T(8,128)S(1)} collective-permute-done((f32[32,2048]{1,0:T(8,128)S(1)}, f32[32,2048]{1,0:T(8,128)S(1)}, u32[]{:S(2)}, u32[]{:S(2)}) %collective-permute-start.3) | collective-permute-done | bytes 262176 | tf_op jit(solution)/shard_map/ppermute | solution.py:383
  35.1 3.2 %collective-permute-start.7 = (f32[32,2048]{1,0:T(8,128)S(1)}, f32[32,2048]{1,0:T(8,128)S(1)}, u32[]{:S(2)}, u32[]{:S(2)}) collective-permute-start(f32[32,2048]{1,0:T(8,128)S(1)} %get-tuple-element.64), channel_id=1, source_target_pairs={{0,8},{1,9},{2,10},{3,11},{4,12},{5,13},{6,14},{7,15},{8,0},{9,1},... | collective-permute-start | bytes 786440 | tf_op jit(solution)/shard_map/ppermute | solution.py:383
  38.3 1.8 %collective-permute-done.5.refs_1_.refs_3_ = f32[32,2048]{1,0:T(8,128)S(1)} collective-permute-done((f32[32,2048]{1,0:T(8,128)S(1)}, f32[32,2048]{1,0:T(8,128)S(1)}, u32[]{:S(2)}, u32[]{:S(2)}) %collective-permute-start.5) | collective-permute-done | bytes 262176 | tf_op jit(solution)/shard_map/ppermute | solution.py:383
  40.7 3.2 %collective-permute-start.9 = (f32[32,2048]{1,0:T(8,128)S(1)}, f32[32,2048]{1,0:T(8,128)S(1)}, u32[]{:S(2)}, u32[]{:S(2)}) collective-permute-start(f32[32,2048]{1,0:T(8,128)S(1)} %get-tuple-element.67), channel_id=1, source_target_pairs={{0,8},{1,9},{2,10},{3,11},{4,12},{5,13},{6,14},{7,15},{8,0},{9,1},... | collective-permute-start | bytes 786440 | tf_op jit(solution)/shard_map/ppermute | solution.py:383
  43.9 1.8 %collective-permute-done.7.refs_2_.refs_4_ = f32[32,2048]{1,0:T(8,128)S(1)} collective-permute-done((f32[32,2048]{1,0:T(8,128)S(1)}, f32[32,2048]{1,0:T(8,128)S(1)}, u32[]{:S(2)}, u32[]{:S(2)}) %collective-permute-start.7) | collective-permute-done | bytes 262176 | tf_op jit(solution)/shard_map/ppermute | solution.py:383
  46.3 3.2 %collective-permute-start.11 = (f32[32,2048]{1,0:T(8,128)S(1)}, f32[32,2048]{1,0:T(8,128)S(1)}, u32[]{:S(2)}, u32[]{:S(2)}) collective-permute-start(f32[32,2048]{1,0:T(8,128)S(1)} %get-tuple-element.70), channel_id=1, source_target_pairs={{0,8},{1,9},{2,10},{3,11},{4,12},{5,13},{6,14},{7,15},{8,0},{9,1},... | collective-permute-start | bytes 786440 | tf_op jit(solution)/shard_map/ppermute | solution.py:383
  49.5 1.8 %collective-permute-done.9.refs_2_.refs_5_ = f32[32,2048]{1,0:T(8,128)S(1)} collective-permute-done((f32[32,2048]{1,0:T(8,128)S(1)}, f32[32,2048]{1,0:T(8,128)S(1)}, u32[]{:S(2)}, u32[]{:S(2)}) %collective-permute-start.9) | collective-permute-done | bytes 262176 | tf_op jit(solution)/shard_map/ppermute | solution.py:383
  51.9 3.2 %collective-permute-start.13 = (f32[32,2048]{1,0:T(8,128)S(1)}, f32[32,2048]{1,0:T(8,128)S(1)}, u32[]{:S(2)}, u32[]{:S(2)}) collective-permute-start(f32[32,2048]{1,0:T(8,128)S(1)} %get-tuple-element.73), channel_id=1, source_target_pairs={{0,8},{1,9},{2,10},{3,11},{4,12},{5,13},{6,14},{7,15},{8,0},{9,1},... | collective-permute-start | bytes 786440 | tf_op jit(solution)/shard_map/ppermute | solution.py:383
  55.1 1.8 %collective-permute-done.11.refs_3_.refs_6_ = f32[32,2048]{1,0:T(8,128)S(1)} collective-permute-done((f32[32,2048]{1,0:T(8,128)S(1)}, f32[32,2048]{1,0:T(8,128)S(1)}, u32[]{:S(2)}, u32[]{:S(2)}) %collective-permute-start.11) | collective-permute-done | bytes 262176 | tf_op jit(solution)/shard_map/ppermute | solution.py:383
  57.6 3.2 %collective-permute-start.15 = (f32[32,2048]{1,0:T(8,128)S(1)}, f32[32,2048]{1,0:T(8,128)S(1)}, u32[]{:S(2)}, u32[]{:S(2)}) collective-permute-start(f32[32,2048]{1,0:T(8,128)S(1)} %get-tuple-element.76), channel_id=1, source_target_pairs={{0,8},{1,9},{2,10},{3,11},{4,12},{5,13},{6,14},{7,15},{8,0},{9,1},... | collective-permute-start | bytes 786440 | tf_op jit(solution)/shard_map/ppermute | solution.py:383
  60.7 1.7 %collective-permute-done.13.refs_3_.refs_7_ = f32[32,2048]{1,0:T(8,128)S(1)} collective-permute-done((f32[32,2048]{1,0:T(8,128)S(1)}, f32[32,2048]{1,0:T(8,128)S(1)}, u32[]{:S(2)}, u32[]{:S(2)}) %collective-permute-start.13) | collective-permute-done | bytes 262176 | tf_op jit(solution)/shard_map/ppermute | solution.py:383
  63.2 3.2 %collective-permute-start.17 = (f32[32,2048]{1,0:T(8,128)S(1)}, f32[32,2048]{1,0:T(8,128)S(1)}, u32[]{:S(2)}, u32[]{:S(2)}) collective-permute-start(f32[32,2048]{1,0:T(8,128)S(1)} %get-tuple-element.79), channel_id=1, source_target_pairs={{0,8},{1,9},{2,10},{3,11},{4,12},{5,13},{6,14},{7,15},{8,0},{9,1},... | collective-permute-start | bytes 786440 | tf_op jit(solution)/shard_map/ppermute | solution.py:383
  66.4 1.7 %collective-permute-done.15.refs_4_.refs_8_ = f32[32,2048]{1,0:T(8,128)S(1)} collective-permute-done((f32[32,2048]{1,0:T(8,128)S(1)}, f32[32,2048]{1,0:T(8,128)S(1)}, u32[]{:S(2)}, u32[]{:S(2)}) %collective-permute-start.15) | collective-permute-done | bytes 262176 | tf_op jit(solution)/shard_map/ppermute | solution.py:383
  68.9 5.1 %collective-permute-start.19 = (f32[32,2048]{1,0:T(8,128)S(1)}, f32[32,2048]{1,0:T(8,128)S(1)}, u32[]{:S(2)}, u32[]{:S(2)}) collective-permute-start(f32[32,2048]{1,0:T(8,128)S(1)} %get-tuple-element.82), channel_id=1, source_target_pairs={{0,8},{1,9},{2,10},{3,11},{4,12},{5,13},{6,14},{7,15},{8,0},{9,1},... | collective-permute-start | bytes 786440 | tf_op jit(solution)/shard_map/ppermute | solution.py:383
  74.8 2.8 %collective-permute-start.21 = (f32[32,2048]{1,0:T(8,128)S(1)}, f32[32,2048]{1,0:T(8,128)S(1)}, u32[]{:S(2)}, u32[]{:S(2)}) collective-permute-start(f32[32,2048]{1,0:T(8,128)S(1)} %get-tuple-element.85), channel_id=1, source_target_pairs={{0,8},{1,9},{2,10},{3,11},{4,12},{5,13},{6,14},{7,15},{8,0},{9,1},... | collective-permute-start | bytes 786440 | tf_op jit(solution)/shard_map/ppermute | solution.py:383
  77.6 2.8 %collective-permute-done.19.refs_10_ = f32[32,2048]{1,0:T(8,128)S(1)} collective-permute-done((f32[32,2048]{1,0:T(8,128)S(1)}, f32[32,2048]{1,0:T(8,128)S(1)}, u32[]{:S(2)}, u32[]{:S(2)}) %collective-permute-start.19) | collective-permute-done | bytes 262176 | tf_op jit(solution)/shard_map/ppermute | solution.py:383
  80.4 4.2 %collective-permute-done.21.refs_11_ = f32[32,2048]{1,0:T(8,128)S(1)} collective-permute-done((f32[32,2048]{1,0:T(8,128)S(1)}, f32[32,2048]{1,0:T(8,128)S(1)}, u32[]{:S(2)}, u32[]{:S(2)}) %collective-permute-start.21) | collective-permute-done | bytes 262176 | tf_op jit(solution)/shard_map/ppermute | solution.py:383
  84.6 7.6 %assemble.1 = (bf16[192,4096]{1,0:T(8,128)(2,1)}, bf16[192,4096]{1,0:T(8,128)(2,1)}, bf16[4096,192]{1,0:T(8,128)(2,1)}, bf16[4096,192]{1,0:T(8,128)(2,1)}, f32[32,512]{1,0:T(8,128)S(1)}) custom-call(s32[2]{0:T(128)S(1)} %pad_add_fusion.here_ref, s32[6]{0:T(128)S(1)} %copy-done.4, s32[6]{0:T(128)S(1)} %copy-done.5, f32[4,32,4096]{2,1,0:T(8,128)S(1)} %copy-done, ...), custom_call_target="tpu_custom_call" | custom-call | flops 1811939328 | bytes 6291456 | tf_op jit(solution)/shard_map/assemble/pallas_call | solution.py:197
  93.6 2.7 %collective-permute-start.27 = (f32[32,512]{1,0:T(8,128)S(1)}, f32[32,512]{1,0:T(8,128)S(1)}, u32[]{:S(2)}, u32[]{:S(2)}) collective-permute-start(f32[32,512]{1,0:T(8,128)S(1)} %add.27), channel_id=1, source_target_pairs={{0,6},{1,7},{2,4},{3,5},{4,2},{5,3},{6,0},{7,1},{8,14},{9,15},{10,... | collective-permute-start | bytes 196616 | tf_op jit(solution)/shard_map/ppermute | solution.py:346
  97.2 11.8 %collective-permute-done.27 = f32[32,512]{1,0:T(8,128)S(1)} collective-permute-done((f32[32,512]{1,0:T(8,128)S(1)}, f32[32,512]{1,0:T(8,128)S(1)}, u32[]{:S(2)}, u32[]{:S(2)}) %collective-permute-start.27) | collective-permute-done | bytes 65568 | tf_op jit(solution)/shard_map/ppermute | solution.py:346
  109.7 10.3 %inner_products.1 = (f32[128,384]{1,0:T(8,128)S(1)}, f32[128,384]{1,0:T(8,128)S(1)}, f32[8,64,4096]{2,1,0:T(8,128)S(1)}) custom-call(s32[2]{0:T(128)S(1)} %pad_add_fusion.here_ref, f32[8,64,4096]{2,1,0:T(8,128)} %all-to-all-done.x_ref, bf16[4096,192]{1,0:T(8,128)(2,1)} %get-tuple-element.89.high_hbm, bf16[4096,192]{1,0:T(8,128)(2,1)} %get-tuple-element.90.low_hbm), custom_call_target="tpu_custom_call" | custom-call | flops 2415919104 | bytes 8388608 | tf_op jit(solution)/shard_map/inner_products/pallas_call | solution.py:289
  122.7 3.8 %collective-permute-done.29 = f32[64,384]{1,0:T(8,128)S(1)} collective-permute-done((f32[64,384]{1,0:T(8,128)S(1)}, f32[64,384]{1,0:T(8,128)S(1)}, u32[]{:S(2)}, u32[]{:S(2)}) %collective-permute-start.29) | collective-permute-done | bytes 98336 | tf_op jit(solution)/shard_map/ppermute | solution.py:346
  129.0 3.5 %merge.1.p_ref = bf16[576,4096]{1,0:T(8,128)(2,1)S(1)} custom-call(f32[32,512]{1,0:T(8,128)S(1)} %add_add_fusion.refs_0_, f32[6,32,32]{2,1,0:T(8,128)S(1)} %copy-done.3, bf16[192,4096]{1,0:T(8,128)(2,1)S(1)} %copy-done.1, bf16[192,4096]{1,0:T(8,128)(2,1)S(1)} %copy-done.2), custom_call_target="tpu_custom_call" | custom-call | flops 905969664 | bytes 6291456 | tf_op jit(solution)/shard_map/merge/pallas_call | solution.py:235
  134.5 7.7 %update.1 = f32[8,64,4096]{2,1,0:T(8,128)} custom-call(s32[2]{0:T(128)S(1)} %pad_add_fusion.here_ref, f32[128,384]{1,0:T(8,128)S(1)} %pad_maximum_fusion.mine_ref, f32[128,384]{1,0:T(8,128)S(1)} %collective-permute-done.33.theirs_ref, f32[8,64,4096]{2,1,0:T(8,128)S(1)} %get-tuple-element.96.x_ref, bf16[576,4096]{1,0:T(8,128)(2,1)S(1)} %merge.1.p_ref), custom_call_target="tpu_custom_call" | custom-call | flops 2415919104 | bytes 16777216 | tf_op jit(solution)/shard_map/update/pallas_call | solution.py:329
  (76 shorter events, 18.5 us)
Async XLA Ops:
  7.0 102.6 %all-to-all-start = ((f32[8,64,4096]{2,1,0:T(8,128)}), f32[8,64,4096]{2,1,0:T(8,128)}, u32[]{:S(2)}, u32[]{:S(2)}) async-start(f32[8,64,4096]{2,1,0:T(8,128)} %pack.1), calls=%async_computation | async-start | bytes 16777216 | tf_op jit(solution)/shard_map/all_to_all | solution.py:388
  13.1 10.1 %collective-permute-start = (f32[32,2048]{1,0:T(8,128)S(1)}, f32[32,2048]{1,0:T(8,128)S(1)}, u32[]{:S(2)}, u32[]{:S(2)}) collective-permute-start(f32[32,2048]{1,0:T(8,128)S(1)} %get-tuple-element.52), channel_id=1, source_target_pairs={{0,8},{1,9},{2,10},{3,11},{4,12},{5,13},{6,14},{7,15},{8,0},{9,1},... | collective-permute-start | bytes 786440 | tf_op jit(solution)/shard_map/ppermute | solution.py:383
  16.0 7.1 %collective-permute-start.2 = (f32[32,2048]{1,0:T(8,128)S(1)}, f32[32,2048]{1,0:T(8,128)S(1)}, u32[]{:S(2)}, u32[]{:S(2)}) collective-permute-start(f32[32,2048]{1,0:T(8,128)S(1)} %get-tuple-element.53), channel_id=1, source_target_pairs={{0,1},{1,0},{2,3},{3,2},{4,5},{5,4},{6,7},{7,6},{8,16},{9,17},{10,... | collective-permute-start | bytes 786440 | tf_op jit(solution)/shard_map/ppermute | solution.py:383
  16.7 12.0 %collective-permute-start.1 = (f32[32,2048]{1,0:T(8,128)S(1)}, f32[32,2048]{1,0:T(8,128)S(1)}, u32[]{:S(2)}, u32[]{:S(2)}) collective-permute-start(f32[32,2048]{1,0:T(8,128)S(1)} %get-tuple-element.55), channel_id=1, source_target_pairs={{0,8},{1,9},{2,10},{3,11},{4,12},{5,13},{6,14},{7,15},{8,0},{9,1},... | collective-permute-start | bytes 786440 | tf_op jit(solution)/shard_map/ppermute | solution.py:383
  19.9 8.9 %collective-permute-start.4 = (f32[32,2048]{1,0:T(8,128)S(1)}, f32[32,2048]{1,0:T(8,128)S(1)}, u32[]{:S(2)}, u32[]{:S(2)}) collective-permute-start(f32[32,2048]{1,0:T(8,128)S(1)} %get-tuple-element.56), channel_id=1, source_target_pairs={{0,1},{1,0},{2,3},{3,2},{4,5},{5,4},{6,7},{7,6},{8,16},{9,17},{10,... | collective-permute-start | bytes 786440 | tf_op jit(solution)/shard_map/ppermute | solution.py:383
  23.8 10.6 %collective-permute-start.3 = (f32[32,2048]{1,0:T(8,128)S(1)}, f32[32,2048]{1,0:T(8,128)S(1)}, u32[]{:S(2)}, u32[]{:S(2)}) collective-permute-start(f32[32,2048]{1,0:T(8,128)S(1)} %get-tuple-element.58), channel_id=1, source_target_pairs={{0,8},{1,9},{2,10},{3,11},{4,12},{5,13},{6,14},{7,15},{8,0},{9,1},... | collective-permute-start | bytes 786440 | tf_op jit(solution)/shard_map/ppermute | solution.py:383
  27.0 7.4 %collective-permute-start.6 = (f32[32,2048]{1,0:T(8,128)S(1)}, f32[32,2048]{1,0:T(8,128)S(1)}, u32[]{:S(2)}, u32[]{:S(2)}) collective-permute-start(f32[32,2048]{1,0:T(8,128)S(1)} %get-tuple-element.59), channel_id=1, source_target_pairs={{0,1},{1,0},{2,3},{3,2},{4,5},{5,4},{6,7},{7,6},{8,16},{9,17},{10,... | collective-permute-start | bytes 786440 | tf_op jit(solution)/shard_map/ppermute | solution.py:383
  29.5 10.6 %collective-permute-start.5 = (f32[32,2048]{1,0:T(8,128)S(1)}, f32[32,2048]{1,0:T(8,128)S(1)}, u32[]{:S(2)}, u32[]{:S(2)}) collective-permute-start(f32[32,2048]{1,0:T(8,128)S(1)} %get-tuple-element.61), channel_id=1, source_target_pairs={{0,8},{1,9},{2,10},{3,11},{4,12},{5,13},{6,14},{7,15},{8,0},{9,1},... | collective-permute-start | bytes 786440 | tf_op jit(solution)/shard_map/ppermute | solution.py:383
  32.6 7.4 %collective-permute-start.8 = (f32[32,2048]{1,0:T(8,128)S(1)}, f32[32,2048]{1,0:T(8,128)S(1)}, u32[]{:S(2)}, u32[]{:S(2)}) collective-permute-start(f32[32,2048]{1,0:T(8,128)S(1)} %get-tuple-element.62), channel_id=1, source_target_pairs={{0,1},{1,0},{2,3},{3,2},{4,5},{5,4},{6,7},{7,6},{8,16},{9,17},{10,... | collective-permute-start | bytes 786440 | tf_op jit(solution)/shard_map/ppermute | solution.py:383
  35.1 10.6 %collective-permute-start.7 = (f32[32,2048]{1,0:T(8,128)S(1)}, f32[32,2048]{1,0:T(8,128)S(1)}, u32[]{:S(2)}, u32[]{:S(2)}) collective-permute-start(f32[32,2048]{1,0:T(8,128)S(1)} %get-tuple-element.64), channel_id=1, source_target_pairs={{0,8},{1,9},{2,10},{3,11},{4,12},{5,13},{6,14},{7,15},{8,0},{9,1},... | collective-permute-start | bytes 786440 | tf_op jit(solution)/shard_map/ppermute | solution.py:383
  38.2 7.4 %collective-permute-start.10 = (f32[32,2048]{1,0:T(8,128)S(1)}, f32[32,2048]{1,0:T(8,128)S(1)}, u32[]{:S(2)}, u32[]{:S(2)}) collective-permute-start(f32[32,2048]{1,0:T(8,128)S(1)} %get-tuple-element.65), channel_id=1, source_target_pairs={{0,1},{1,0},{2,3},{3,2},{4,5},{5,4},{6,7},{7,6},{8,16},{9,17},{10,... | collective-permute-start | bytes 786440 | tf_op jit(solution)/shard_map/ppermute | solution.py:383
  40.7 10.6 %collective-permute-start.9 = (f32[32,2048]{1,0:T(8,128)S(1)}, f32[32,2048]{1,0:T(8,128)S(1)}, u32[]{:S(2)}, u32[]{:S(2)}) collective-permute-start(f32[32,2048]{1,0:T(8,128)S(1)} %get-tuple-element.67), channel_id=1, source_target_pairs={{0,8},{1,9},{2,10},{3,11},{4,12},{5,13},{6,14},{7,15},{8,0},{9,1},... | collective-permute-start | bytes 786440 | tf_op jit(solution)/shard_map/ppermute | solution.py:383
  43.9 7.4 %collective-permute-start.12 = (f32[32,2048]{1,0:T(8,128)S(1)}, f32[32,2048]{1,0:T(8,128)S(1)}, u32[]{:S(2)}, u32[]{:S(2)}) collective-permute-start(f32[32,2048]{1,0:T(8,128)S(1)} %get-tuple-element.68), channel_id=1, source_target_pairs={{0,1},{1,0},{2,3},{3,2},{4,5},{5,4},{6,7},{7,6},{8,16},{9,17},{10,... | collective-permute-start | bytes 786440 | tf_op jit(solution)/shard_map/ppermute | solution.py:383
  46.3 10.5 %collective-permute-start.11 = (f32[32,2048]{1,0:T(8,128)S(1)}, f32[32,2048]{1,0:T(8,128)S(1)}, u32[]{:S(2)}, u32[]{:S(2)}) collective-permute-start(f32[32,2048]{1,0:T(8,128)S(1)} %get-tuple-element.70), channel_id=1, source_target_pairs={{0,8},{1,9},{2,10},{3,11},{4,12},{5,13},{6,14},{7,15},{8,0},{9,1},... | collective-permute-start | bytes 786440 | tf_op jit(solution)/shard_map/ppermute | solution.py:383
  49.5 7.4 %collective-permute-start.14 = (f32[32,2048]{1,0:T(8,128)S(1)}, f32[32,2048]{1,0:T(8,128)S(1)}, u32[]{:S(2)}, u32[]{:S(2)}) collective-permute-start(f32[32,2048]{1,0:T(8,128)S(1)} %get-tuple-element.71), channel_id=1, source_target_pairs={{0,1},{1,0},{2,3},{3,2},{4,5},{5,4},{6,7},{7,6},{8,16},{9,17},{10,... | collective-permute-start | bytes 786440 | tf_op jit(solution)/shard_map/ppermute | solution.py:383
  51.9 10.5 %collective-permute-start.13 = (f32[32,2048]{1,0:T(8,128)S(1)}, f32[32,2048]{1,0:T(8,128)S(1)}, u32[]{:S(2)}, u32[]{:S(2)}) collective-permute-start(f32[32,2048]{1,0:T(8,128)S(1)} %get-tuple-element.73), channel_id=1, source_target_pairs={{0,8},{1,9},{2,10},{3,11},{4,12},{5,13},{6,14},{7,15},{8,0},{9,1},... | collective-permute-start | bytes 786440 | tf_op jit(solution)/shard_map/ppermute | solution.py:383
  55.1 7.4 %collective-permute-start.16 = (f32[32,2048]{1,0:T(8,128)S(1)}, f32[32,2048]{1,0:T(8,128)S(1)}, u32[]{:S(2)}, u32[]{:S(2)}) collective-permute-start(f32[32,2048]{1,0:T(8,128)S(1)} %get-tuple-element.74), channel_id=1, source_target_pairs={{0,1},{1,0},{2,3},{3,2},{4,5},{5,4},{6,7},{7,6},{8,16},{9,17},{10,... | collective-permute-start | bytes 786440 | tf_op jit(solution)/shard_map/ppermute | solution.py:383
  57.6 10.5 %collective-permute-start.15 = (f32[32,2048]{1,0:T(8,128)S(1)}, f32[32,2048]{1,0:T(8,128)S(1)}, u32[]{:S(2)}, u32[]{:S(2)}) collective-permute-start(f32[32,2048]{1,0:T(8,128)S(1)} %get-tuple-element.76), channel_id=1, source_target_pairs={{0,8},{1,9},{2,10},{3,11},{4,12},{5,13},{6,14},{7,15},{8,0},{9,1},... | collective-permute-start | bytes 786440 | tf_op jit(solution)/shard_map/ppermute | solution.py:383
  60.7 7.4 %collective-permute-start.18 = (f32[32,2048]{1,0:T(8,128)S(1)}, f32[32,2048]{1,0:T(8,128)S(1)}, u32[]{:S(2)}, u32[]{:S(2)}) collective-permute-start(f32[32,2048]{1,0:T(8,128)S(1)} %get-tuple-element.77), channel_id=1, source_target_pairs={{0,1},{1,0},{2,3},{3,2},{4,5},{5,4},{6,7},{7,6},{8,16},{9,17},{10,... | collective-permute-start | bytes 786440 | tf_op jit(solution)/shard_map/ppermute | solution.py:383
  63.2 10.9 %collective-permute-start.17 = (f32[32,2048]{1,0:T(8,128)S(1)}, f32[32,2048]{1,0:T(8,128)S(1)}, u32[]{:S(2)}, u32[]{:S(2)}) collective-permute-start(f32[32,2048]{1,0:T(8,128)S(1)} %get-tuple-element.79), channel_id=1, source_target_pairs={{0,8},{1,9},{2,10},{3,11},{4,12},{5,13},{6,14},{7,15},{8,0},{9,1},... | collective-permute-start | bytes 786440 | tf_op jit(solution)/shard_map/ppermute | solution.py:383
  66.4 7.7 %collective-permute-start.20 = (f32[32,2048]{1,0:T(8,128)S(1)}, f32[32,2048]{1,0:T(8,128)S(1)}, u32[]{:S(2)}, u32[]{:S(2)}) collective-permute-start(f32[32,2048]{1,0:T(8,128)S(1)} %get-tuple-element.80), channel_id=1, source_target_pairs={{0,1},{1,0},{2,3},{3,2},{4,5},{5,4},{6,7},{7,6},{8,16},{9,17},{10,... | collective-permute-start | bytes 786440 | tf_op jit(solution)/shard_map/ppermute | solution.py:383
  68.8 11.6 %collective-permute-start.22 = (f32[32,2048]{1,0:T(8,128)S(1)}, f32[32,2048]{1,0:T(8,128)S(1)}, u32[]{:S(2)}, u32[]{:S(2)}) collective-permute-start(f32[32,2048]{1,0:T(8,128)S(1)} %get-tuple-element.83), channel_id=1, source_target_pairs={{0,1},{1,0},{2,3},{3,2},{4,5},{5,4},{6,7},{7,6},{8,16},{9,17},{10,... | collective-permute-start | bytes 786440 | tf_op jit(solution)/shard_map/ppermute | solution.py:383
  68.9 11.5 %collective-permute-start.19 = (f32[32,2048]{1,0:T(8,128)S(1)}, f32[32,2048]{1,0:T(8,128)S(1)}, u32[]{:S(2)}, u32[]{:S(2)}) collective-permute-start(f32[32,2048]{1,0:T(8,128)S(1)} %get-tuple-element.82), channel_id=1, source_target_pairs={{0,8},{1,9},{2,10},{3,11},{4,12},{5,13},{6,14},{7,15},{8,0},{9,1},... | collective-permute-start | bytes 786440 | tf_op jit(solution)/shard_map/ppermute | solution.py:383
  74.8 9.9 %collective-permute-start.21 = (f32[32,2048]{1,0:T(8,128)S(1)}, f32[32,2048]{1,0:T(8,128)S(1)}, u32[]{:S(2)}, u32[]{:S(2)}) collective-permute-start(f32[32,2048]{1,0:T(8,128)S(1)} %get-tuple-element.85), channel_id=1, source_target_pairs={{0,8},{1,9},{2,10},{3,11},{4,12},{5,13},{6,14},{7,15},{8,0},{9,1},... | collective-permute-start | bytes 786440 | tf_op jit(solution)/shard_map/ppermute | solution.py:383
  77.6 7.0 %collective-permute-start.23 = (f32[32,2048]{1,0:T(8,128)S(1)}, f32[32,2048]{1,0:T(8,128)S(1)}, u32[]{:S(2)}, u32[]{:S(2)}) collective-permute-start(f32[32,2048]{1,0:T(8,128)S(1)} %get-tuple-element.86), channel_id=1, source_target_pairs={{0,1},{1,0},{2,3},{3,2},{4,5},{5,4},{6,7},{7,6},{8,16},{9,17},{10,... | collective-permute-start | bytes 786440 | tf_op jit(solution)/shard_map/ppermute | solution.py:383
  93.6 15.3 %collective-permute-start.27 = (f32[32,512]{1,0:T(8,128)S(1)}, f32[32,512]{1,0:T(8,128)S(1)}, u32[]{:S(2)}, u32[]{:S(2)}) collective-permute-start(f32[32,512]{1,0:T(8,128)S(1)} %add.27), channel_id=1, source_target_pairs={{0,6},{1,7},{2,4},{3,5},{4,2},{5,3},{6,0},{7,1},{8,14},{9,15},{10,... | collective-permute-start | bytes 196616 | tf_op jit(solution)/shard_map/ppermute | solution.py:346
  96.3 13.3 %collective-permute-start.26 = (f32[32,512]{1,0:T(8,128)S(1)}, f32[32,512]{1,0:T(8,128)S(1)}, u32[]{:S(2)}, u32[]{:S(2)}) collective-permute-start(f32[32,512]{1,0:T(8,128)S(1)} %add.27), channel_id=1, source_target_pairs={{0,4},{1,5},{2,6},{3,7},{4,0},{5,1},{6,2},{7,3},{8,12},{9,13},{10,... | collective-permute-start | bytes 196616 | tf_op jit(solution)/shard_map/ppermute | solution.py:346
  96.8 12.8 %collective-permute-start.25 = (f32[32,512]{1,0:T(8,128)S(1)}, f32[32,512]{1,0:T(8,128)S(1)}, u32[]{:S(2)}, u32[]{:S(2)}) collective-permute-start(f32[32,512]{1,0:T(8,128)S(1)} %add.27), channel_id=1, source_target_pairs={{0,2},{1,3},{2,0},{3,1},{4,6},{5,7},{6,4},{7,5},{8,10},{9,11},{10,... | collective-permute-start | bytes 196616 | tf_op jit(solution)/shard_map/ppermute | solution.py:346
  121.6 4.9 %collective-permute-start.29 = (f32[64,384]{1,0:T(8,128)S(1)}, f32[64,384]{1,0:T(8,128)S(1)}, u32[]{:S(2)}, u32[]{:S(2)}) collective-permute-start(f32[64,384]{1,0:T(8,128)S(1)} %get-tuple-element.99), channel_id=1, source_target_pairs={{0,2},{1,3},{2,0},{3,1},{4,6},{5,7},{6,4},{7,5},{8,10},{9,11},{10,... | collective-permute-start | bytes 294920 | tf_op jit(solution)/shard_map/ppermute | solution.py:346
  122.1 4.6 %collective-permute-start.31 = (f32[64,384]{1,0:T(8,128)S(1)}, f32[64,384]{1,0:T(8,128)S(1)}, u32[]{:S(2)}, u32[]{:S(2)}) collective-permute-start(f32[64,384]{1,0:T(8,128)S(1)} %get-tuple-element.100), channel_id=1, source_target_pairs={{0,4},{1,5},{2,6},{3,7},{4,0},{5,1},{6,2},{7,3},{8,12},{9,13},{10,... | collective-permute-start | bytes 294920 | tf_op jit(solution)/shard_map/ppermute | solution.py:346
  126.7 5.8 %collective-permute-start.32 = (f32[64,384]{1,0:T(8,128)S(1)}, f32[64,384]{1,0:T(8,128)S(1)}, u32[]{:S(2)}, u32[]{:S(2)}) collective-permute-start(f32[64,384]{1,0:T(8,128)S(1)} %get-tuple-element.98), channel_id=1, source_target_pairs={{0,2},{1,3},{2,0},{3,1},{4,6},{5,7},{6,4},{7,5},{8,10},{9,11},{10,... | collective-permute-start | bytes 294920 | tf_op jit(solution)/shard_map/ppermute | solution.py:346
  128.4 4.6 %collective-permute-start.30 = (f32[64,384]{1,0:T(8,128)S(1)}, f32[64,384]{1,0:T(8,128)S(1)}, u32[]{:S(2)}, u32[]{:S(2)}) collective-permute-start(f32[64,384]{1,0:T(8,128)S(1)} %get-tuple-element.95), channel_id=1, source_target_pairs={{0,4},{1,5},{2,6},{3,7},{4,0},{5,1},{6,2},{7,3},{8,12},{9,13},{10,... | collective-permute-start | bytes 294920 | tf_op jit(solution)/shard_map/ppermute | solution.py:346
  (9 other events, 91.4 us)

commit v6 on v5

--- a/solution.py
+++ b/solution.py
@@ -12,6 +12,7 @@
 VMEM_LIMIT = 40 * 1024 * 1024
 LARGE_LIMIT = 58 * 1024 * 1024
 COLUMNS = 512
+QUEUES = 2
 SPLITS = 2
 
 
@@ -70,11 +71,11 @@
                 source = x_ref.at[at, pl.ds(k * ncols, ncols)]
                 into.append(pltpu.make_async_copy(source, held.at[k, at], in_sems.at[i]))
                 out_of.append(pltpu.make_async_copy(held.at[k, at], out_ref.at[k, at], out_sems.at[i]))
-        for copy in into:
-            copy.start()
-        for came, goes in zip(into, out_of):
+        for i, copy in enumerate(into):
+            copy.start(priority=i % QUEUES)
+        for i, (came, goes) in enumerate(zip(into, out_of)):
             came.wait()
-            goes.start()
+            goes.start(priority=i % QUEUES)
         for copy in out_of:
             copy.wait()
 
@@ -152,7 +153,7 @@
     cols = ncols // splits
 
     def kernel(here_ref, place_ref, offset_ref, stack_ref, *refs):
-        arrived, (high_ref, low_ref, high_t_ref, low_t_ref, gram_ref, held, sems) = refs[:-7], refs[-7:]
+        arrived, (high_ref, low_ref, both_t_ref, gram_ref, held, sems) = refs[:-6], refs[-6:]
         even, odd = arrived[:turns * splits], arrived[turns * splits:]
         roots, slot, ranks, counts = plan(place_ref, slots, n_rows)
         me = here_ref[0]
@@ -186,7 +187,8 @@
             high_ref[rows, :] = high
             low_ref[rows, :] = low
         for at in column_blocks(ncols):
-            high_t_ref[at, :], low_t_ref[at, :] = halves(held[:, at].T)
+            high, low = halves(held[:, at].T)
+            both_t_ref[at, :] = jnp.concatenate([high, low], axis=1)
         gram = dot_t(held[...], held[...])
         gram_ref[...] = jnp.zeros_like(gram_ref)
         first = 0
@@ -199,12 +201,11 @@
         out_shape=[
             pltpu.HBM((height, ncols), jnp.bfloat16),
             pltpu.HBM((height, ncols), jnp.bfloat16),
-            pltpu.HBM((ncols, height), jnp.bfloat16),
-            pltpu.HBM((ncols, height), jnp.bfloat16),
+            pltpu.HBM((ncols, 2 * height), jnp.bfloat16),
             jax.ShapeDtypeStruct((width, packed_width(steps, width)), jnp.float32),
         ],
         in_specs=[SMEM, SMEM, SMEM, ANY] + [ANY] * (2 * turns * splits),
-        out_specs=[VMEM] * 5,
+        out_specs=[VMEM] * 4,
         scratch_shapes=[pltpu.VMEM((height, ncols), jnp.float32), pltpu.SemaphoreType.DMA((steps,))],
         compiler_params=params(limit=SMALL_LIMIT),
         cost_estimate=cost(12 * height * height * ncols, 8 * height * ncols),
@@ -261,27 +262,32 @@
 
 def inner_products(here, x, vecs_t):
     lead, rows, ncols = x.shape
-    height = vecs_t[0].shape[1]
+    height = vecs_t.shape[1] // 2
     half = lead * rows // 2
     blocks = column_blocks(ncols)
-
-    def kernel(here_ref, x_ref, high_hbm, low_hbm, mine_ref, theirs_ref, held, high_ref, low_ref, total, sems):
+    lanes = min(-(-height // 128) * 128, 2 * height)
+
+    def kernel(here_ref, x_ref, vecs_hbm, mine_ref, theirs_ref, held, vecs_ref, by_high, by_low, total, sems):
         copies = []
         for i, at in enumerate(blocks):
-            copies.append([
-                pltpu.make_async_copy(high_hbm.at[at], high_ref.at[at], sems.at[i, 0]),
-                pltpu.make_async_copy(low_hbm.at[at], low_ref.at[at], sems.at[i, 1]),
-                pltpu.make_async_copy(x_ref.at[:, :, at], held.at[:, :, at], sems.at[i, 2]),
-            ])
-        for block in copies:
-            for copy in block:
-                copy.start()
+            copies.append((
+                pltpu.make_async_copy(vecs_hbm.at[at], vecs_ref.at[at], sems.at[i, 0]),
+                pltpu.make_async_copy(x_ref.at[:lead // 2, :, at], held.at[:lead // 2, :, at], sems.at[i, 1]),
+                pltpu.make_async_copy(x_ref.at[lead // 2:, :, at], held.at[lead // 2:, :, at], sems.at[i, 2]),
+            )[:3 if lead > 1 else 1])
+            if lead == 1:
+                copies[i] += (pltpu.make_async_copy(x_ref.at[:, :, at], held.at[:, :, at], sems.at[i, 1]),)
+        for i, copy in enumerate(copy for block in copies for copy in block):
+            copy.start(priority=i % QUEUES)
         for i, at in enumerate(blocks):
             for copy in copies[i]:
                 copy.wait()
-            block = held[:, :, at].reshape(lead * rows, at.size)
-            part = dot3(halves(block), (high_ref[at, :], low_ref[at, :]), ((1,), (0,)))
-            total[...] = part if i == 0 else total[...] + part
+            high, low = halves(held[:, :, at].reshape(lead * rows, at.size))
+            one = jnp.dot(high, vecs_ref[at, :], preferred_element_type=jnp.float32)
+            two = jnp.dot(low, vecs_ref[at, :lanes], preferred_element_type=jnp.float32)
+            by_high[...] = one if i == 0 else by_high[...] + one
+            by_low[...] = two if i == 0 else by_low[...] + two
+        total[...] = by_high[:, :height] + (by_high[:, height:] + by_low[:, :height])
         core = lax.rem(here_ref[1], 2)
         mine_ref[...] = fold(total[pl.ds(pl.multiple_of(core * half, 8), half), :])
         theirs_ref[...] = fold(total[pl.ds(pl.multiple_of((1 - core) * half, 8), half), :])
@@ -289,18 +295,19 @@
     return pl.pallas_call(
         kernel,
         out_shape=[jax.ShapeDtypeStruct((half // 2, 2 * height), jnp.float32)] * 2 + [pltpu.VMEM(x.shape, jnp.float32)],
-        in_specs=[SMEM, ANY, ANY, ANY],
+        in_specs=[SMEM, ANY, ANY],
         out_specs=[VMEM] * 3,
         scratch_shapes=[
-            pltpu.VMEM((ncols, height), jnp.bfloat16),
-            pltpu.VMEM((ncols, height), jnp.bfloat16),
+            pltpu.VMEM(vecs_t.shape, jnp.bfloat16),
+            pltpu.VMEM((lead * rows, 2 * height), jnp.float32),
+            pltpu.VMEM((lead * rows, lanes), jnp.float32),
             pltpu.VMEM((lead * rows, height), jnp.float32),
             pltpu.SemaphoreType.DMA((len(blocks), 3)),
         ],
         compiler_params=params(),
         cost_estimate=cost(6 * lead * rows * ncols * height, 4 * lead * rows * ncols),
         name="inner_products",
-    )(here, in_hbm(x), *[in_hbm(v) for v in vecs_t])
+    )(here, in_hbm(x), in_hbm(vecs_t))
 
 
 def update(here, x, mine, theirs, changes):
@@ -308,7 +315,7 @@
     height = changes.shape[0] // 3
     half = lead * rows // 2
     blocks = column_blocks(ncols)
-    depth = min(2, len(blocks))
+    depth = min(4, len(blocks))
 
     def kernel(here_ref, mine_ref, theirs_ref, x_ref, p_ref, out_ref, w_ref, held, sems):
         core = lax.rem(here_ref[1], 2)
@@ -322,7 +329,7 @@
             if i >= depth:
                 copies[i - depth].wait()
             held[i % depth] = x_ref[:, :, at] - change.reshape(lead, rows, at.size)
-            copies[i].start()
+            copies[i].start(priority=i % QUEUES)
         for copy in copies[-depth:]:
             copy.wait()
 
@@ -398,11 +405,11 @@
             streams[part] = (evens + [exchange(to_even, 0)], odds + [exchange(to_odd, 1)])
     evens = list(zip(*[stream[0] for stream in streams]))
     odds = list(zip(*[stream[1] for stream in streams]))
-    high, low, high_t, low_t, gram = assemble(here, block_place, offsets, householder, evens, odds, n_row)
+    high, low, both_t, gram = assemble(here, block_place, offsets, householder, evens, odds, n_row)
     cross = functools.reduce(jnp.add, spread(gram + swap(gram, 1, n_wide), n_wide))
     changes = merge([cross], wy_factor, (high, low))
 
-    mine, theirs, x = inner_products(after(here, cross), x, (high_t, low_t))
+    mine, theirs, x = inner_products(after(here, cross), x, both_t)
     mine = chips_sum(mine + swap(theirs, 1, n_wide), n_wide, changes)
     return update(here, x, mine, swap(mine, 1, n_wide), changes).reshape(n_wide * rows, ncols)
 

time: 143 us -> 140 us (0.979)
  Pallas kernels: 44.2 us -> 39.7 us
    pallas_call x1, Pallas kernels: 7.66 us -> 6.21 us  [update(): pl.pallas_call(kernel, out_shape=jax.ShapeDtypeStruct(x.shape, jnp.float3...]
  transfers between devices with their start and end apart: 35 -> 35, of which waited for: 19 -> 18; matrix products, arithmetic and copies ran while one was open for 0% -> 1% of each run, Pallas kernels for 13% -> 13%
where the time goes in v6:
time: 140 us
  starting transfers between devices  52.1 us (37%)
  waiting for transfers between devices  46.2 us (33%)
  Pallas kernels  39.7 us (28%)
    ppermute x24, starting transfers between devices, exchange(): return lax.ppermute(array, ('row', 'wide'), pairs)  39.6 us
    ppermute x24, waiting for transfers between devices, exchange(): return lax.ppermute(array, ('row', 'wide'), pairs)  24.4 us
    ppermute x10, waiting for transfers between devices, swap(): return lax.ppermute(array, 'wide', [(i, i ^ k) for i in range(size)])  21.8 us
    pallas_call x1, Pallas kernels, inner_products(): pl.pallas_call(kernel, out_shape=[jax.ShapeDtypeStruct((half // 2, 2 * he...  9.61 us
    pallas_call x12, Pallas kernels, feed(): pl.pallas_call(kernel, out_shape=[jax.ShapeDtypeStruct((width, cols), jnp...  8.06 us
    ppermute x10, starting transfers between devices, swap(): return lax.ppermute(array, 'wide', [(i, i ^ k) for i in range(size)])  7.18 us
    pallas_call x1, Pallas kernels, assemble(): pl.pallas_call(kernel, out_shape=[pltpu.HBM((height, ncols), jnp.bfloat16...  6.34 us
    pallas_call x1, Pallas kernels, update(): pl.pallas_call(kernel, out_shape=jax.ShapeDtypeStruct(x.shape, jnp.float3...  6.21 us
  transfers between devices with their start and end apart: 35, of which 18 were waited for; matrix products, arithmetic and copies ran while one was open for 1% of the time, Pallas kernels for 13%

profile of v6, /device:TPU:0, one launch (start us, length us, event | category | flops | bytes accessed | tf_op | source)
XLA Modules:
  0.0 140.2 jit_solution(8194726999989281956)
XLA Ops:
  0.0 6.0 %pack.1 = f32[8,64,4096]{2,1,0:T(8,128)} custom-call(f32[64,32768]{1,0:T(8,128)} %x_ref.1), custom_call_target="tpu_custom_call" | custom-call | bytes 16777216 | tf_op jit(solution)/shard_map/pack/pallas_call | solution.py:82
  6.1 5.3 %all-to-all-start = ((f32[8,64,4096]{2,1,0:T(8,128)}), f32[8,64,4096]{2,1,0:T(8,128)}, u32[]{:S(2)}, u32[]{:S(2)}) async-start(f32[8,64,4096]{2,1,0:T(8,128)} %pack.1), calls=%async_computation | async-start | bytes 16777216 | tf_op jit(solution)/shard_map/all_to_all | solution.py:395
  12.1 2.9 %collective-permute-start = (f32[32,2048]{1,0:T(8,128)S(1)}, f32[32,2048]{1,0:T(8,128)S(1)}, u32[]{:S(2)}, u32[]{:S(2)}) collective-permute-start(f32[32,2048]{1,0:T(8,128)S(1)} %get-tuple-element.51), channel_id=1, source_target_pairs={{0,8},{1,9},{2,10},{3,11},{4,12},{5,13},{6,14},{7,15},{8,0},{9,1},... | collective-permute-start | bytes 786440 | tf_op jit(solution)/shard_map/ppermute | solution.py:390
  15.8 3.1 %collective-permute-start.1 = (f32[32,2048]{1,0:T(8,128)S(1)}, f32[32,2048]{1,0:T(8,128)S(1)}, u32[]{:S(2)}, u32[]{:S(2)}) collective-permute-start(f32[32,2048]{1,0:T(8,128)S(1)} %get-tuple-element.54), channel_id=1, source_target_pairs={{0,8},{1,9},{2,10},{3,11},{4,12},{5,13},{6,14},{7,15},{8,0},{9,1},... | collective-permute-start | bytes 786440 | tf_op jit(solution)/shard_map/ppermute | solution.py:390
  18.9 3.3 %collective-permute-done.refs_0_ = f32[32,2048]{1,0:T(8,128)S(1)} collective-permute-done((f32[32,2048]{1,0:T(8,128)S(1)}, f32[32,2048]{1,0:T(8,128)S(1)}, u32[]{:S(2)}, u32[]{:S(2)}) %collective-permute-start) | collective-permute-done | bytes 262176 | tf_op jit(solution)/shard_map/ppermute | solution.py:390
  22.9 3.2 %collective-permute-start.3 = (f32[32,2048]{1,0:T(8,128)S(1)}, f32[32,2048]{1,0:T(8,128)S(1)}, u32[]{:S(2)}, u32[]{:S(2)}) collective-permute-start(f32[32,2048]{1,0:T(8,128)S(1)} %get-tuple-element.57), channel_id=1, source_target_pairs={{0,8},{1,9},{2,10},{3,11},{4,12},{5,13},{6,14},{7,15},{8,0},{9,1},... | collective-permute-start | bytes 786440 | tf_op jit(solution)/shard_map/ppermute | solution.py:390
  26.1 1.8 %collective-permute-done.1.refs_0_.refs_1_ = f32[32,2048]{1,0:T(8,128)S(1)} collective-permute-done((f32[32,2048]{1,0:T(8,128)S(1)}, f32[32,2048]{1,0:T(8,128)S(1)}, u32[]{:S(2)}, u32[]{:S(2)}) %collective-permute-start.1) | collective-permute-done | bytes 262176 | tf_op jit(solution)/shard_map/ppermute | solution.py:390
  28.5 3.2 %collective-permute-start.5 = (f32[32,2048]{1,0:T(8,128)S(1)}, f32[32,2048]{1,0:T(8,128)S(1)}, u32[]{:S(2)}, u32[]{:S(2)}) collective-permute-start(f32[32,2048]{1,0:T(8,128)S(1)} %get-tuple-element.60), channel_id=1, source_target_pairs={{0,8},{1,9},{2,10},{3,11},{4,12},{5,13},{6,14},{7,15},{8,0},{9,1},... | collective-permute-start | bytes 786440 | tf_op jit(solution)/shard_map/ppermute | solution.py:390
  31.7 1.8 %collective-permute-done.3.refs_1_.refs_2_ = f32[32,2048]{1,0:T(8,128)S(1)} collective-permute-done((f32[32,2048]{1,0:T(8,128)S(1)}, f32[32,2048]{1,0:T(8,128)S(1)}, u32[]{:S(2)}, u32[]{:S(2)}) %collective-permute-start.3) | collective-permute-done | bytes 262176 | tf_op jit(solution)/shard_map/ppermute | solution.py:390
  34.1 3.2 %collective-permute-start.7 = (f32[32,2048]{1,0:T(8,128)S(1)}, f32[32,2048]{1,0:T(8,128)S(1)}, u32[]{:S(2)}, u32[]{:S(2)}) collective-permute-start(f32[32,2048]{1,0:T(8,128)S(1)} %get-tuple-element.63), channel_id=1, source_target_pairs={{0,8},{1,9},{2,10},{3,11},{4,12},{5,13},{6,14},{7,15},{8,0},{9,1},... | collective-permute-start | bytes 786440 | tf_op jit(solution)/shard_map/ppermute | solution.py:390
  37.3 1.8 %collective-permute-done.5.refs_1_.refs_3_ = f32[32,2048]{1,0:T(8,128)S(1)} collective-permute-done((f32[32,2048]{1,0:T(8,128)S(1)}, f32[32,2048]{1,0:T(8,128)S(1)}, u32[]{:S(2)}, u32[]{:S(2)}) %collective-permute-start.5) | collective-permute-done | bytes 262176 | tf_op jit(solution)/shard_map/ppermute | solution.py:390
  39.7 3.2 %collective-permute-start.9 = (f32[32,2048]{1,0:T(8,128)S(1)}, f32[32,2048]{1,0:T(8,128)S(1)}, u32[]{:S(2)}, u32[]{:S(2)}) collective-permute-start(f32[32,2048]{1,0:T(8,128)S(1)} %get-tuple-element.66), channel_id=1, source_target_pairs={{0,8},{1,9},{2,10},{3,11},{4,12},{5,13},{6,14},{7,15},{8,0},{9,1},... | collective-permute-start | bytes 786440 | tf_op jit(solution)/shard_map/ppermute | solution.py:390
  42.9 1.8 %collective-permute-done.7.refs_2_.refs_4_ = f32[32,2048]{1,0:T(8,128)S(1)} collective-permute-done((f32[32,2048]{1,0:T(8,128)S(1)}, f32[32,2048]{1,0:T(8,128)S(1)}, u32[]{:S(2)}, u32[]{:S(2)}) %collective-permute-start.7) | collective-permute-done | bytes 262176 | tf_op jit(solution)/shard_map/ppermute | solution.py:390
  45.4 3.2 %collective-permute-start.11 = (f32[32,2048]{1,0:T(8,128)S(1)}, f32[32,2048]{1,0:T(8,128)S(1)}, u32[]{:S(2)}, u32[]{:S(2)}) collective-permute-start(f32[32,2048]{1,0:T(8,128)S(1)} %get-tuple-element.69), channel_id=1, source_target_pairs={{0,8},{1,9},{2,10},{3,11},{4,12},{5,13},{6,14},{7,15},{8,0},{9,1},... | collective-permute-start | bytes 786440 | tf_op jit(solution)/shard_map/ppermute | solution.py:390
  48.5 1.8 %collective-permute-done.9.refs_2_.refs_5_ = f32[32,2048]{1,0:T(8,128)S(1)} collective-permute-done((f32[32,2048]{1,0:T(8,128)S(1)}, f32[32,2048]{1,0:T(8,128)S(1)}, u32[]{:S(2)}, u32[]{:S(2)}) %collective-permute-start.9) | collective-permute-done | bytes 262176 | tf_op jit(solution)/shard_map/ppermute | solution.py:390
  51.0 3.2 %collective-permute-start.13 = (f32[32,2048]{1,0:T(8,128)S(1)}, f32[32,2048]{1,0:T(8,128)S(1)}, u32[]{:S(2)}, u32[]{:S(2)}) collective-permute-start(f32[32,2048]{1,0:T(8,128)S(1)} %get-tuple-element.72), channel_id=1, source_target_pairs={{0,8},{1,9},{2,10},{3,11},{4,12},{5,13},{6,14},{7,15},{8,0},{9,1},... | collective-permute-start | bytes 786440 | tf_op jit(solution)/shard_map/ppermute | solution.py:390
  54.2 1.8 %collective-permute-done.11.refs_3_.refs_6_ = f32[32,2048]{1,0:T(8,128)S(1)} collective-permute-done((f32[32,2048]{1,0:T(8,128)S(1)}, f32[32,2048]{1,0:T(8,128)S(1)}, u32[]{:S(2)}, u32[]{:S(2)}) %collective-permute-start.11) | collective-permute-done | bytes 262176 | tf_op jit(solution)/shard_map/ppermute | solution.py:390
  56.6 3.2 %collective-permute-start.15 = (f32[32,2048]{1,0:T(8,128)S(1)}, f32[32,2048]{1,0:T(8,128)S(1)}, u32[]{:S(2)}, u32[]{:S(2)}) collective-permute-start(f32[32,2048]{1,0:T(8,128)S(1)} %get-tuple-element.75), channel_id=1, source_target_pairs={{0,8},{1,9},{2,10},{3,11},{4,12},{5,13},{6,14},{7,15},{8,0},{9,1},... | collective-permute-start | bytes 786440 | tf_op jit(solution)/shard_map/ppermute | solution.py:390
  59.8 1.7 %collective-permute-done.13.refs_3_.refs_7_ = f32[32,2048]{1,0:T(8,128)S(1)} collective-permute-done((f32[32,2048]{1,0:T(8,128)S(1)}, f32[32,2048]{1,0:T(8,128)S(1)}, u32[]{:S(2)}, u32[]{:S(2)}) %collective-permute-start.13) | collective-permute-done | bytes 262176 | tf_op jit(solution)/shard_map/ppermute | solution.py:390
  62.2 3.2 %collective-permute-start.17 = (f32[32,2048]{1,0:T(8,128)S(1)}, f32[32,2048]{1,0:T(8,128)S(1)}, u32[]{:S(2)}, u32[]{:S(2)}) collective-permute-start(f32[32,2048]{1,0:T(8,128)S(1)} %get-tuple-element.78), channel_id=1, source_target_pairs={{0,8},{1,9},{2,10},{3,11},{4,12},{5,13},{6,14},{7,15},{8,0},{9,1},... | collective-permute-start | bytes 786440 | tf_op jit(solution)/shard_map/ppermute | solution.py:390
  65.4 1.7 %collective-permute-done.15.refs_4_.refs_8_ = f32[32,2048]{1,0:T(8,128)S(1)} collective-permute-done((f32[32,2048]{1,0:T(8,128)S(1)}, f32[32,2048]{1,0:T(8,128)S(1)}, u32[]{:S(2)}, u32[]{:S(2)}) %collective-permute-start.15) | collective-permute-done | bytes 262176 | tf_op jit(solution)/shard_map/ppermute | solution.py:390
  67.9 5.1 %collective-permute-start.19 = (f32[32,2048]{1,0:T(8,128)S(1)}, f32[32,2048]{1,0:T(8,128)S(1)}, u32[]{:S(2)}, u32[]{:S(2)}) collective-permute-start(f32[32,2048]{1,0:T(8,128)S(1)} %get-tuple-element.81), channel_id=1, source_target_pairs={{0,8},{1,9},{2,10},{3,11},{4,12},{5,13},{6,14},{7,15},{8,0},{9,1},... | collective-permute-start | bytes 786440 | tf_op jit(solution)/shard_map/ppermute | solution.py:390
  73.8 2.8 %collective-permute-start.21 = (f32[32,2048]{1,0:T(8,128)S(1)}, f32[32,2048]{1,0:T(8,128)S(1)}, u32[]{:S(2)}, u32[]{:S(2)}) collective-permute-start(f32[32,2048]{1,0:T(8,128)S(1)} %get-tuple-element.84), channel_id=1, source_target_pairs={{0,8},{1,9},{2,10},{3,11},{4,12},{5,13},{6,14},{7,15},{8,0},{9,1},... | collective-permute-start | bytes 786440 | tf_op jit(solution)/shard_map/ppermute | solution.py:390
  76.7 2.8 %collective-permute-done.19.refs_10_ = f32[32,2048]{1,0:T(8,128)S(1)} collective-permute-done((f32[32,2048]{1,0:T(8,128)S(1)}, f32[32,2048]{1,0:T(8,128)S(1)}, u32[]{:S(2)}, u32[]{:S(2)}) %collective-permute-start.19) | collective-permute-done | bytes 262176 | tf_op jit(solution)/shard_map/ppermute | solution.py:390
  79.5 4.2 %collective-permute-done.21.refs_11_ = f32[32,2048]{1,0:T(8,128)S(1)} collective-permute-done((f32[32,2048]{1,0:T(8,128)S(1)}, f32[32,2048]{1,0:T(8,128)S(1)}, u32[]{:S(2)}, u32[]{:S(2)}) %collective-permute-start.21) | collective-permute-done | bytes 262176 | tf_op jit(solution)/shard_map/ppermute | solution.py:390
  83.7 6.3 %assemble.1 = (bf16[192,4096]{1,0:T(8,128)(2,1)}, bf16[192,4096]{1,0:T(8,128)(2,1)}, bf16[4096,384]{1,0:T(8,128)(2,1)}, f32[32,512]{1,0:T(8,128)S(1)}) custom-call(s32[2]{0:T(128)S(1)} %pad_add_fusion.here_ref, s32[6]{0:T(128)S(1)} %copy-done.5, s32[6]{0:T(128)S(1)} %copy-done.6, f32[4,32,4096]{2,1,0:T(8,128)S(1)} %copy-done, ...), custom_call_target="tpu_custom_call" | custom-call | flops 1811939328 | bytes 6291456 | tf_op jit(solution)/shard_map/assemble/pallas_call | solution.py:199
  91.4 2.7 %collective-permute-start.27 = (f32[32,512]{1,0:T(8,128)S(1)}, f32[32,512]{1,0:T(8,128)S(1)}, u32[]{:S(2)}, u32[]{:S(2)}) collective-permute-start(f32[32,512]{1,0:T(8,128)S(1)} %add.27), channel_id=1, source_target_pairs={{0,6},{1,7},{2,4},{3,5},{4,2},{5,3},{6,0},{7,1},{8,14},{9,15},{10,... | collective-permute-start | bytes 196616 | tf_op jit(solution)/shard_map/ppermute | solution.py:353
  95.0 13.1 %collective-permute-done.27 = f32[32,512]{1,0:T(8,128)S(1)} collective-permute-done((f32[32,512]{1,0:T(8,128)S(1)}, f32[32,512]{1,0:T(8,128)S(1)}, u32[]{:S(2)}, u32[]{:S(2)}) %collective-permute-start.27) | collective-permute-done | bytes 65568 | tf_op jit(solution)/shard_map/ppermute | solution.py:353
  109.3 9.6 %inner_products.1 = (f32[128,384]{1,0:T(8,128)S(1)}, f32[128,384]{1,0:T(8,128)S(1)}, f32[8,64,4096]{2,1,0:T(8,128)S(1)}) custom-call(s32[2]{0:T(128)S(1)} %pad_add_fusion.here_ref, f32[8,64,4096]{2,1,0:T(8,128)} %all-to-all-done.x_ref, bf16[4096,384]{1,0:T(8,128)(2,1)} %get-tuple-element.88.vecs_hbm), custom_call_target="tpu_custom_call" | custom-call | flops 2415919104 | bytes 8388608 | tf_op jit(solution)/shard_map/inner_products/pallas_call | solution.py:295
  121.6 3.8 %collective-permute-done.29 = f32[64,384]{1,0:T(8,128)S(1)} collective-permute-done((f32[64,384]{1,0:T(8,128)S(1)}, f32[64,384]{1,0:T(8,128)S(1)}, u32[]{:S(2)}, u32[]{:S(2)}) %collective-permute-start.29) | collective-permute-done | bytes 98336 | tf_op jit(solution)/shard_map/ppermute | solution.py:353
  128.8 3.5 %merge.1.p_ref = bf16[576,4096]{1,0:T(8,128)(2,1)S(1)} custom-call(f32[32,512]{1,0:T(8,128)S(1)} %copy-done.3, f32[6,32,32]{2,1,0:T(8,128)S(1)} %copy-done.4, bf16[192,4096]{1,0:T(8,128)(2,1)S(1)} %copy-done.1, bf16[192,4096]{1,0:T(8,128)(2,1)S(1)} %copy-done.2), custom_call_target="tpu_custom_call" | custom-call | flops 905969664 | bytes 6291456 | tf_op jit(solution)/shard_map/merge/pallas_call | solution.py:236
  133.9 6.2 %update.1 = f32[8,64,4096]{2,1,0:T(8,128)} custom-call(s32[2]{0:T(128)S(1)} %pad_add_fusion.here_ref, f32[128,384]{1,0:T(8,128)S(1)} %pad_maximum_fusion.mine_ref, f32[128,384]{1,0:T(8,128)S(1)} %collective-permute-done.33.theirs_ref, f32[8,64,4096]{2,1,0:T(8,128)S(1)} %get-tuple-element.94.x_ref, bf16[576,4096]{1,0:T(8,128)(2,1)S(1)} %merge.1.p_ref), custom_call_target="tpu_custom_call" | custom-call | flops 2415919104 | bytes 16777216 | tf_op jit(solution)/shard_map/update/pallas_call | solution.py:336
  (78 shorter events, 19.5 us)
Async XLA Ops:
  6.1 103.2 %all-to-all-start = ((f32[8,64,4096]{2,1,0:T(8,128)}), f32[8,64,4096]{2,1,0:T(8,128)}, u32[]{:S(2)}, u32[]{:S(2)}) async-start(f32[8,64,4096]{2,1,0:T(8,128)} %pack.1), calls=%async_computation | async-start | bytes 16777216 | tf_op jit(solution)/shard_map/all_to_all | solution.py:395
  12.1 10.1 %collective-permute-start = (f32[32,2048]{1,0:T(8,128)S(1)}, f32[32,2048]{1,0:T(8,128)S(1)}, u32[]{:S(2)}, u32[]{:S(2)}) collective-permute-start(f32[32,2048]{1,0:T(8,128)S(1)} %get-tuple-element.51), channel_id=1, source_target_pairs={{0,8},{1,9},{2,10},{3,11},{4,12},{5,13},{6,14},{7,15},{8,0},{9,1},... | collective-permute-start | bytes 786440 | tf_op jit(solution)/shard_map/ppermute | solution.py:390
  15.1 7.1 %collective-permute-start.2 = (f32[32,2048]{1,0:T(8,128)S(1)}, f32[32,2048]{1,0:T(8,128)S(1)}, u32[]{:S(2)}, u32[]{:S(2)}) collective-permute-start(f32[32,2048]{1,0:T(8,128)S(1)} %get-tuple-element.52), channel_id=1, source_target_pairs={{0,1},{1,0},{2,3},{3,2},{4,5},{5,4},{6,7},{7,6},{8,16},{9,17},{10,... | collective-permute-start | bytes 786440 | tf_op jit(solution)/shard_map/ppermute | solution.py:390
  15.8 12.0 %collective-permute-start.1 = (f32[32,2048]{1,0:T(8,128)S(1)}, f32[32,2048]{1,0:T(8,128)S(1)}, u32[]{:S(2)}, u32[]{:S(2)}) collective-permute-start(f32[32,2048]{1,0:T(8,128)S(1)} %get-tuple-element.54), channel_id=1, source_target_pairs={{0,8},{1,9},{2,10},{3,11},{4,12},{5,13},{6,14},{7,15},{8,0},{9,1},... | collective-permute-start | bytes 786440 | tf_op jit(solution)/shard_map/ppermute | solution.py:390
  18.9 8.9 %collective-permute-start.4 = (f32[32,2048]{1,0:T(8,128)S(1)}, f32[32,2048]{1,0:T(8,128)S(1)}, u32[]{:S(2)}, u32[]{:S(2)}) collective-permute-start(f32[32,2048]{1,0:T(8,128)S(1)} %get-tuple-element.55), channel_id=1, source_target_pairs={{0,1},{1,0},{2,3},{3,2},{4,5},{5,4},{6,7},{7,6},{8,16},{9,17},{10,... | collective-permute-start | bytes 786440 | tf_op jit(solution)/shard_map/ppermute | solution.py:390
  22.9 10.6 %collective-permute-start.3 = (f32[32,2048]{1,0:T(8,128)S(1)}, f32[32,2048]{1,0:T(8,128)S(1)}, u32[]{:S(2)}, u32[]{:S(2)}) collective-permute-start(f32[32,2048]{1,0:T(8,128)S(1)} %get-tuple-element.57), channel_id=1, source_target_pairs={{0,8},{1,9},{2,10},{3,11},{4,12},{5,13},{6,14},{7,15},{8,0},{9,1},... | collective-permute-start | bytes 786440 | tf_op jit(solution)/shard_map/ppermute | solution.py:390
  26.1 7.4 %collective-permute-start.6 = (f32[32,2048]{1,0:T(8,128)S(1)}, f32[32,2048]{1,0:T(8,128)S(1)}, u32[]{:S(2)}, u32[]{:S(2)}) collective-permute-start(f32[32,2048]{1,0:T(8,128)S(1)} %get-tuple-element.58), channel_id=1, source_target_pairs={{0,1},{1,0},{2,3},{3,2},{4,5},{5,4},{6,7},{7,6},{8,16},{9,17},{10,... | collective-permute-start | bytes 786440 | tf_op jit(solution)/shard_map/ppermute | solution.py:390
  28.5 10.6 %collective-permute-start.5 = (f32[32,2048]{1,0:T(8,128)S(1)}, f32[32,2048]{1,0:T(8,128)S(1)}, u32[]{:S(2)}, u32[]{:S(2)}) collective-permute-start(f32[32,2048]{1,0:T(8,128)S(1)} %get-tuple-element.60), channel_id=1, source_target_pairs={{0,8},{1,9},{2,10},{3,11},{4,12},{5,13},{6,14},{7,15},{8,0},{9,1},... | collective-permute-start | bytes 786440 | tf_op jit(solution)/shard_map/ppermute | solution.py:390
  31.7 7.4 %collective-permute-start.8 = (f32[32,2048]{1,0:T(8,128)S(1)}, f32[32,2048]{1,0:T(8,128)S(1)}, u32[]{:S(2)}, u32[]{:S(2)}) collective-permute-start(f32[32,2048]{1,0:T(8,128)S(1)} %get-tuple-element.61), channel_id=1, source_target_pairs={{0,1},{1,0},{2,3},{3,2},{4,5},{5,4},{6,7},{7,6},{8,16},{9,17},{10,... | collective-permute-start | bytes 786440 | tf_op jit(solution)/shard_map/ppermute | solution.py:390
  34.1 10.6 %collective-permute-start.7 = (f32[32,2048]{1,0:T(8,128)S(1)}, f32[32,2048]{1,0:T(8,128)S(1)}, u32[]{:S(2)}, u32[]{:S(2)}) collective-permute-start(f32[32,2048]{1,0:T(8,128)S(1)} %get-tuple-element.63), channel_id=1, source_target_pairs={{0,8},{1,9},{2,10},{3,11},{4,12},{5,13},{6,14},{7,15},{8,0},{9,1},... | collective-permute-start | bytes 786440 | tf_op jit(solution)/shard_map/ppermute | solution.py:390
  37.3 7.4 %collective-permute-start.10 = (f32[32,2048]{1,0:T(8,128)S(1)}, f32[32,2048]{1,0:T(8,128)S(1)}, u32[]{:S(2)}, u32[]{:S(2)}) collective-permute-start(f32[32,2048]{1,0:T(8,128)S(1)} %get-tuple-element.64), channel_id=1, source_target_pairs={{0,1},{1,0},{2,3},{3,2},{4,5},{5,4},{6,7},{7,6},{8,16},{9,17},{10,... | collective-permute-start | bytes 786440 | tf_op jit(solution)/shard_map/ppermute | solution.py:390
  39.7 10.6 %collective-permute-start.9 = (f32[32,2048]{1,0:T(8,128)S(1)}, f32[32,2048]{1,0:T(8,128)S(1)}, u32[]{:S(2)}, u32[]{:S(2)}) collective-permute-start(f32[32,2048]{1,0:T(8,128)S(1)} %get-tuple-element.66), channel_id=1, source_target_pairs={{0,8},{1,9},{2,10},{3,11},{4,12},{5,13},{6,14},{7,15},{8,0},{9,1},... | collective-permute-start | bytes 786440 | tf_op jit(solution)/shard_map/ppermute | solution.py:390
  42.9 7.4 %collective-permute-start.12 = (f32[32,2048]{1,0:T(8,128)S(1)}, f32[32,2048]{1,0:T(8,128)S(1)}, u32[]{:S(2)}, u32[]{:S(2)}) collective-permute-start(f32[32,2048]{1,0:T(8,128)S(1)} %get-tuple-element.67), channel_id=1, source_target_pairs={{0,1},{1,0},{2,3},{3,2},{4,5},{5,4},{6,7},{7,6},{8,16},{9,17},{10,... | collective-permute-start | bytes 786440 | tf_op jit(solution)/shard_map/ppermute | solution.py:390
  45.4 10.5 %collective-permute-start.11 = (f32[32,2048]{1,0:T(8,128)S(1)}, f32[32,2048]{1,0:T(8,128)S(1)}, u32[]{:S(2)}, u32[]{:S(2)}) collective-permute-start(f32[32,2048]{1,0:T(8,128)S(1)} %get-tuple-element.69), channel_id=1, source_target_pairs={{0,8},{1,9},{2,10},{3,11},{4,12},{5,13},{6,14},{7,15},{8,0},{9,1},... | collective-permute-start | bytes 786440 | tf_op jit(solution)/shard_map/ppermute | solution.py:390
  48.5 7.4 %collective-permute-start.14 = (f32[32,2048]{1,0:T(8,128)S(1)}, f32[32,2048]{1,0:T(8,128)S(1)}, u32[]{:S(2)}, u32[]{:S(2)}) collective-permute-start(f32[32,2048]{1,0:T(8,128)S(1)} %get-tuple-element.70), channel_id=1, source_target_pairs={{0,1},{1,0},{2,3},{3,2},{4,5},{5,4},{6,7},{7,6},{8,16},{9,17},{10,... | collective-permute-start | bytes 786440 | tf_op jit(solution)/shard_map/ppermute | solution.py:390
  51.0 10.5 %collective-permute-start.13 = (f32[32,2048]{1,0:T(8,128)S(1)}, f32[32,2048]{1,0:T(8,128)S(1)}, u32[]{:S(2)}, u32[]{:S(2)}) collective-permute-start(f32[32,2048]{1,0:T(8,128)S(1)} %get-tuple-element.72), channel_id=1, source_target_pairs={{0,8},{1,9},{2,10},{3,11},{4,12},{5,13},{6,14},{7,15},{8,0},{9,1},... | collective-permute-start | bytes 786440 | tf_op jit(solution)/shard_map/ppermute | solution.py:390
  54.2 7.4 %collective-permute-start.16 = (f32[32,2048]{1,0:T(8,128)S(1)}, f32[32,2048]{1,0:T(8,128)S(1)}, u32[]{:S(2)}, u32[]{:S(2)}) collective-permute-start(f32[32,2048]{1,0:T(8,128)S(1)} %get-tuple-element.73), channel_id=1, source_target_pairs={{0,1},{1,0},{2,3},{3,2},{4,5},{5,4},{6,7},{7,6},{8,16},{9,17},{10,... | collective-permute-start | bytes 786440 | tf_op jit(solution)/shard_map/ppermute | solution.py:390
  56.6 10.5 %collective-permute-start.15 = (f32[32,2048]{1,0:T(8,128)S(1)}, f32[32,2048]{1,0:T(8,128)S(1)}, u32[]{:S(2)}, u32[]{:S(2)}) collective-permute-start(f32[32,2048]{1,0:T(8,128)S(1)} %get-tuple-element.75), channel_id=1, source_target_pairs={{0,8},{1,9},{2,10},{3,11},{4,12},{5,13},{6,14},{7,15},{8,0},{9,1},... | collective-permute-start | bytes 786440 | tf_op jit(solution)/shard_map/ppermute | solution.py:390
  59.8 7.4 %collective-permute-start.18 = (f32[32,2048]{1,0:T(8,128)S(1)}, f32[32,2048]{1,0:T(8,128)S(1)}, u32[]{:S(2)}, u32[]{:S(2)}) collective-permute-start(f32[32,2048]{1,0:T(8,128)S(1)} %get-tuple-element.76), channel_id=1, source_target_pairs={{0,1},{1,0},{2,3},{3,2},{4,5},{5,4},{6,7},{7,6},{8,16},{9,17},{10,... | collective-permute-start | bytes 786440 | tf_op jit(solution)/shard_map/ppermute | solution.py:390
  62.2 10.9 %collective-permute-start.17 = (f32[32,2048]{1,0:T(8,128)S(1)}, f32[32,2048]{1,0:T(8,128)S(1)}, u32[]{:S(2)}, u32[]{:S(2)}) collective-permute-start(f32[32,2048]{1,0:T(8,128)S(1)} %get-tuple-element.78), channel_id=1, source_target_pairs={{0,8},{1,9},{2,10},{3,11},{4,12},{5,13},{6,14},{7,15},{8,0},{9,1},... | collective-permute-start | bytes 786440 | tf_op jit(solution)/shard_map/ppermute | solution.py:390
  65.4 7.7 %collective-permute-start.20 = (f32[32,2048]{1,0:T(8,128)S(1)}, f32[32,2048]{1,0:T(8,128)S(1)}, u32[]{:S(2)}, u32[]{:S(2)}) collective-permute-start(f32[32,2048]{1,0:T(8,128)S(1)} %get-tuple-element.79), channel_id=1, source_target_pairs={{0,1},{1,0},{2,3},{3,2},{4,5},{5,4},{6,7},{7,6},{8,16},{9,17},{10,... | collective-permute-start | bytes 786440 | tf_op jit(solution)/shard_map/ppermute | solution.py:390
  67.9 11.6 %collective-permute-start.22 = (f32[32,2048]{1,0:T(8,128)S(1)}, f32[32,2048]{1,0:T(8,128)S(1)}, u32[]{:S(2)}, u32[]{:S(2)}) collective-permute-start(f32[32,2048]{1,0:T(8,128)S(1)} %get-tuple-element.82), channel_id=1, source_target_pairs={{0,1},{1,0},{2,3},{3,2},{4,5},{5,4},{6,7},{7,6},{8,16},{9,17},{10,... | collective-permute-start | bytes 786440 | tf_op jit(solution)/shard_map/ppermute | solution.py:390
  67.9 11.5 %collective-permute-start.19 = (f32[32,2048]{1,0:T(8,128)S(1)}, f32[32,2048]{1,0:T(8,128)S(1)}, u32[]{:S(2)}, u32[]{:S(2)}) collective-permute-start(f32[32,2048]{1,0:T(8,128)S(1)} %get-tuple-element.81), channel_id=1, source_target_pairs={{0,8},{1,9},{2,10},{3,11},{4,12},{5,13},{6,14},{7,15},{8,0},{9,1},... | collective-permute-start | bytes 786440 | tf_op jit(solution)/shard_map/ppermute | solution.py:390
  73.8 9.9 %collective-permute-start.21 = (f32[32,2048]{1,0:T(8,128)S(1)}, f32[32,2048]{1,0:T(8,128)S(1)}, u32[]{:S(2)}, u32[]{:S(2)}) collective-permute-start(f32[32,2048]{1,0:T(8,128)S(1)} %get-tuple-element.84), channel_id=1, source_target_pairs={{0,8},{1,9},{2,10},{3,11},{4,12},{5,13},{6,14},{7,15},{8,0},{9,1},... | collective-permute-start | bytes 786440 | tf_op jit(solution)/shard_map/ppermute | solution.py:390
  76.6 7.0 %collective-permute-start.23 = (f32[32,2048]{1,0:T(8,128)S(1)}, f32[32,2048]{1,0:T(8,128)S(1)}, u32[]{:S(2)}, u32[]{:S(2)}) collective-permute-start(f32[32,2048]{1,0:T(8,128)S(1)} %get-tuple-element.85), channel_id=1, source_target_pairs={{0,1},{1,0},{2,3},{3,2},{4,5},{5,4},{6,7},{7,6},{8,16},{9,17},{10,... | collective-permute-start | bytes 786440 | tf_op jit(solution)/shard_map/ppermute | solution.py:390
  91.4 16.6 %collective-permute-start.27 = (f32[32,512]{1,0:T(8,128)S(1)}, f32[32,512]{1,0:T(8,128)S(1)}, u32[]{:S(2)}, u32[]{:S(2)}) collective-permute-start(f32[32,512]{1,0:T(8,128)S(1)} %add.27), channel_id=1, source_target_pairs={{0,6},{1,7},{2,4},{3,5},{4,2},{5,3},{6,0},{7,1},{8,14},{9,15},{10,... | collective-permute-start | bytes 196616 | tf_op jit(solution)/shard_map/ppermute | solution.py:353
  94.1 14.6 %collective-permute-start.26 = (f32[32,512]{1,0:T(8,128)S(1)}, f32[32,512]{1,0:T(8,128)S(1)}, u32[]{:S(2)}, u32[]{:S(2)}) collective-permute-start(f32[32,512]{1,0:T(8,128)S(1)} %add.27), channel_id=1, source_target_pairs={{0,4},{1,5},{2,6},{3,7},{4,0},{5,1},{6,2},{7,3},{8,12},{9,13},{10,... | collective-permute-start | bytes 196616 | tf_op jit(solution)/shard_map/ppermute | solution.py:353
  94.6 14.1 %collective-permute-start.25 = (f32[32,512]{1,0:T(8,128)S(1)}, f32[32,512]{1,0:T(8,128)S(1)}, u32[]{:S(2)}, u32[]{:S(2)}) collective-permute-start(f32[32,512]{1,0:T(8,128)S(1)} %add.27), channel_id=1, source_target_pairs={{0,2},{1,3},{2,0},{3,1},{4,6},{5,7},{6,4},{7,5},{8,10},{9,11},{10,... | collective-permute-start | bytes 196616 | tf_op jit(solution)/shard_map/ppermute | solution.py:353
  120.5 4.9 %collective-permute-start.29 = (f32[64,384]{1,0:T(8,128)S(1)}, f32[64,384]{1,0:T(8,128)S(1)}, u32[]{:S(2)}, u32[]{:S(2)}) collective-permute-start(f32[64,384]{1,0:T(8,128)S(1)} %get-tuple-element.97), channel_id=1, source_target_pairs={{0,2},{1,3},{2,0},{3,1},{4,6},{5,7},{6,4},{7,5},{8,10},{9,11},{10,... | collective-permute-start | bytes 294920 | tf_op jit(solution)/shard_map/ppermute | solution.py:353
  121.0 4.6 %collective-permute-start.31 = (f32[64,384]{1,0:T(8,128)S(1)}, f32[64,384]{1,0:T(8,128)S(1)}, u32[]{:S(2)}, u32[]{:S(2)}) collective-permute-start(f32[64,384]{1,0:T(8,128)S(1)} %get-tuple-element.98), channel_id=1, source_target_pairs={{0,4},{1,5},{2,6},{3,7},{4,0},{5,1},{6,2},{7,3},{8,12},{9,13},{10,... | collective-permute-start | bytes 294920 | tf_op jit(solution)/shard_map/ppermute | solution.py:353
  125.6 6.7 %collective-permute-start.32 = (f32[64,384]{1,0:T(8,128)S(1)}, f32[64,384]{1,0:T(8,128)S(1)}, u32[]{:S(2)}, u32[]{:S(2)}) collective-permute-start(f32[64,384]{1,0:T(8,128)S(1)} %get-tuple-element.96), channel_id=1, source_target_pairs={{0,2},{1,3},{2,0},{3,1},{4,6},{5,7},{6,4},{7,5},{8,10},{9,11},{10,... | collective-permute-start | bytes 294920 | tf_op jit(solution)/shard_map/ppermute | solution.py:353
  127.3 5.0 %collective-permute-start.30 = (f32[64,384]{1,0:T(8,128)S(1)}, f32[64,384]{1,0:T(8,128)S(1)}, u32[]{:S(2)}, u32[]{:S(2)}) collective-permute-start(f32[64,384]{1,0:T(8,128)S(1)} %get-tuple-element.93), channel_id=1, source_target_pairs={{0,4},{1,5},{2,6},{3,7},{4,0},{5,1},{6,2},{7,3},{8,12},{9,13},{10,... | collective-permute-start | bytes 294920 | tf_op jit(solution)/shard_map/ppermute | solution.py:353
  (10 other events, 139.9 us)

commit v7 on v6

--- a/solution.py
+++ b/solution.py
@@ -266,17 +266,16 @@
     half = lead * rows // 2
     blocks = column_blocks(ncols)
     lanes = min(-(-height // 128) * 128, 2 * height)
-
-    def kernel(here_ref, x_ref, vecs_hbm, mine_ref, theirs_ref, held, vecs_ref, by_high, by_low, total, sems):
-        copies = []
-        for i, at in enumerate(blocks):
-            copies.append((
-                pltpu.make_async_copy(vecs_hbm.at[at], vecs_ref.at[at], sems.at[i, 0]),
-                pltpu.make_async_copy(x_ref.at[:lead // 2, :, at], held.at[:lead // 2, :, at], sems.at[i, 1]),
-                pltpu.make_async_copy(x_ref.at[lead // 2:, :, at], held.at[lead // 2:, :, at], sems.at[i, 2]),
-            )[:3 if lead > 1 else 1])
-            if lead == 1:
-                copies[i] += (pltpu.make_async_copy(x_ref.at[:, :, at], held.at[:, :, at], sems.at[i, 1]),)
+    parts = [pl.ds(0, lead // 2), pl.ds(lead // 2, lead // 2)] if lead % 2 == 0 else [pl.ds(0, lead)]
+
+    def kernel(here_ref, x_ref, vecs_ref, mine_ref, theirs_ref, held, by_high, by_low, total, sems):
+        copies = [
+            [
+                pltpu.make_async_copy(x_ref.at[part, :, at], held.at[part, :, at], sems.at[i, j])
+                for j, part in enumerate(parts)
+            ]
+            for i, at in enumerate(blocks)
+        ]
         for i, copy in enumerate(copy for block in copies for copy in block):
             copy.start(priority=i % QUEUES)
         for i, at in enumerate(blocks):
@@ -295,19 +294,18 @@
     return pl.pallas_call(
         kernel,
         out_shape=[jax.ShapeDtypeStruct((half // 2, 2 * height), jnp.float32)] * 2 + [pltpu.VMEM(x.shape, jnp.float32)],
-        in_specs=[SMEM, ANY, ANY],
+        in_specs=[SMEM, ANY, VMEM],
         out_specs=[VMEM] * 3,
         scratch_shapes=[
-            pltpu.VMEM(vecs_t.shape, jnp.bfloat16),
             pltpu.VMEM((lead * rows, 2 * height), jnp.float32),
             pltpu.VMEM((lead * rows, lanes), jnp.float32),
             pltpu.VMEM((lead * rows, height), jnp.float32),
-            pltpu.SemaphoreType.DMA((len(blocks), 3)),
+            pltpu.SemaphoreType.DMA((len(blocks), len(parts))),
         ],
         compiler_params=params(),
         cost_estimate=cost(6 * lead * rows * ncols * height, 4 * lead * rows * ncols),
         name="inner_products",
-    )(here, in_hbm(x), in_hbm(vecs_t))
+    )(here, in_hbm(x), vecs_t)
 
 
 def update(here, x, mine, theirs, changes):
@@ -363,7 +361,7 @@
     upper, lower = pair[:half], pair[half:]
     for i, (first, second) in enumerate(zip(shifts, reversed(shifts))):
         come_upper, come_lower = swap(upper, first, size), swap(lower, second, size)
-        if i == len(shifts) - 1:
+        if i == 0:
             upper = after(upper, token)
         upper, lower = upper + come_upper, lower + come_lower
     return jnp.concatenate([upper, lower], axis=0)
@@ -406,7 +404,9 @@
     evens = list(zip(*[stream[0] for stream in streams]))
     odds = list(zip(*[stream[1] for stream in streams]))
     high, low, both_t, gram = assemble(here, block_place, offsets, householder, evens, odds, n_row)
-    cross = functools.reduce(jnp.add, spread(gram + swap(gram, 1, n_wide), n_wide))
+    cross = spread(gram + swap(gram, 1, n_wide), n_wide)
+    cross[0] = after(cross[0], x)
+    cross = functools.reduce(jnp.add, cross)
     changes = merge([cross], wy_factor, (high, low))
 
     mine, theirs, x = inner_products(after(here, cross), x, both_t)

time: 140 us -> 145 us (1.036)
  waiting for transfers between devices: 46.2 us -> 50.5 us
    all_to_all x1, waiting for transfers between devices: 0.01 us -> 11.8 us  [body(): x = lax.all_to_all(piece, 'wide', split_axis=0, concat_axis=0, tiled=True)]
    ppermute x10, waiting for transfers between devices: 21.8 us -> 14.3 us  [swap(): return lax.ppermute(array, 'wide', [(i, i ^ k) for i in range(size)])]
  transfers between devices with their start and end apart: 35 -> 35, of which waited for: 18 -> 20; matrix products, arithmetic and copies ran while one was open for 1% -> 0% of each run, Pallas kernels for 13% -> 12%
where the time goes in v7:
time: 145 us
  starting transfers between devices  52.1 us (36%)
  waiting for transfers between devices  50.5 us (35%)
  Pallas kernels  39.4 us (27%)
  local copies, waits for them, and re-layouts  1.92 us (1%)
    ppermute x24, starting transfers between devices, exchange(): return lax.ppermute(array, ('row', 'wide'), pairs)  39.6 us
    ppermute x24, waiting for transfers between devices, exchange(): return lax.ppermute(array, ('row', 'wide'), pairs)  24.4 us
    ppermute x10, waiting for transfers between devices, swap(): return lax.ppermute(array, 'wide', [(i, i ^ k) for i in range(size)])  14.3 us
    all_to_all x1, waiting for transfers between devices, body(): x = lax.all_to_all(piece, 'wide', split_axis=0, concat_axis=0, tiled=True)  11.8 us
    pallas_call x1, Pallas kernels, inner_products(): pl.pallas_call(kernel, out_shape=[jax.ShapeDtypeStruct((half // 2, 2 * he...  9.27 us
    pallas_call x12, Pallas kernels, feed(): pl.pallas_call(kernel, out_shape=[jax.ShapeDtypeStruct((width, cols), jnp...  8.07 us
    ppermute x10, starting transfers between devices, swap(): return lax.ppermute(array, 'wide', [(i, i ^ k) for i in range(size)])  7.23 us
    pallas_call x1, Pallas kernels, assemble(): pl.pallas_call(kernel, out_shape=[pltpu.HBM((height, ncols), jnp.bfloat16...  6.34 us
  transfers between devices with their start and end apart: 35, of which 20 were waited for; matrix products, arithmetic and copies ran while one was open for 0% of the time, Pallas kernels for 12%

profile of v7, /device:TPU:0, one launch (start us, length us, event | category | flops | bytes accessed | tf_op | source)
XLA Modules:
  0.0 144.6 jit_solution(4245607891984549487)
XLA Ops:
  0.0 6.0 %pack.1 = f32[8,64,4096]{2,1,0:T(8,128)} custom-call(f32[64,32768]{1,0:T(8,128)} %x_ref.1), custom_call_target="tpu_custom_call" | custom-call | bytes 16777216 | tf_op jit(solution)/shard_map/pack/pallas_call | solution.py:82
  6.1 5.3 %all-to-all-start = ((f32[8,64,4096]{2,1,0:T(8,128)}), f32[8,64,4096]{2,1,0:T(8,128)}, u32[]{:S(2)}, u32[]{:S(2)}) async-start(f32[8,64,4096]{2,1,0:T(8,128)} %pack.1), calls=%async_computation | async-start | bytes 16777216 | tf_op jit(solution)/shard_map/all_to_all | solution.py:393
  12.1 2.9 %collective-permute-start = (f32[32,2048]{1,0:T(8,128)S(1)}, f32[32,2048]{1,0:T(8,128)S(1)}, u32[]{:S(2)}, u32[]{:S(2)}) collective-permute-start(f32[32,2048]{1,0:T(8,128)S(1)} %get-tuple-element.52), channel_id=1, source_target_pairs={{0,8},{1,9},{2,10},{3,11},{4,12},{5,13},{6,14},{7,15},{8,0},{9,1},... | collective-permute-start | bytes 786440 | tf_op jit(solution)/shard_map/ppermute | solution.py:388
  15.8 3.1 %collective-permute-start.1 = (f32[32,2048]{1,0:T(8,128)S(1)}, f32[32,2048]{1,0:T(8,128)S(1)}, u32[]{:S(2)}, u32[]{:S(2)}) collective-permute-start(f32[32,2048]{1,0:T(8,128)S(1)} %get-tuple-element.55), channel_id=1, source_target_pairs={{0,8},{1,9},{2,10},{3,11},{4,12},{5,13},{6,14},{7,15},{8,0},{9,1},... | collective-permute-start | bytes 786440 | tf_op jit(solution)/shard_map/ppermute | solution.py:388
  18.9 3.3 %collective-permute-done.refs_0_ = f32[32,2048]{1,0:T(8,128)S(1)} collective-permute-done((f32[32,2048]{1,0:T(8,128)S(1)}, f32[32,2048]{1,0:T(8,128)S(1)}, u32[]{:S(2)}, u32[]{:S(2)}) %collective-permute-start) | collective-permute-done | bytes 262176 | tf_op jit(solution)/shard_map/ppermute | solution.py:388
  22.9 3.2 %collective-permute-start.3 = (f32[32,2048]{1,0:T(8,128)S(1)}, f32[32,2048]{1,0:T(8,128)S(1)}, u32[]{:S(2)}, u32[]{:S(2)}) collective-permute-start(f32[32,2048]{1,0:T(8,128)S(1)} %get-tuple-element.58), channel_id=1, source_target_pairs={{0,8},{1,9},{2,10},{3,11},{4,12},{5,13},{6,14},{7,15},{8,0},{9,1},... | collective-permute-start | bytes 786440 | tf_op jit(solution)/shard_map/ppermute | solution.py:388
  26.0 1.8 %collective-permute-done.1.refs_0_.refs_1_ = f32[32,2048]{1,0:T(8,128)S(1)} collective-permute-done((f32[32,2048]{1,0:T(8,128)S(1)}, f32[32,2048]{1,0:T(8,128)S(1)}, u32[]{:S(2)}, u32[]{:S(2)}) %collective-permute-start.1) | collective-permute-done | bytes 262176 | tf_op jit(solution)/shard_map/ppermute | solution.py:388
  28.5 3.2 %collective-permute-start.5 = (f32[32,2048]{1,0:T(8,128)S(1)}, f32[32,2048]{1,0:T(8,128)S(1)}, u32[]{:S(2)}, u32[]{:S(2)}) collective-permute-start(f32[32,2048]{1,0:T(8,128)S(1)} %get-tuple-element.61), channel_id=1, source_target_pairs={{0,8},{1,9},{2,10},{3,11},{4,12},{5,13},{6,14},{7,15},{8,0},{9,1},... | collective-permute-start | bytes 786440 | tf_op jit(solution)/shard_map/ppermute | solution.py:388
  31.7 1.8 %collective-permute-done.3.refs_1_.refs_2_ = f32[32,2048]{1,0:T(8,128)S(1)} collective-permute-done((f32[32,2048]{1,0:T(8,128)S(1)}, f32[32,2048]{1,0:T(8,128)S(1)}, u32[]{:S(2)}, u32[]{:S(2)}) %collective-permute-start.3) | collective-permute-done | bytes 262176 | tf_op jit(solution)/shard_map/ppermute | solution.py:388
  34.1 3.2 %collective-permute-start.7 = (f32[32,2048]{1,0:T(8,128)S(1)}, f32[32,2048]{1,0:T(8,128)S(1)}, u32[]{:S(2)}, u32[]{:S(2)}) collective-permute-start(f32[32,2048]{1,0:T(8,128)S(1)} %get-tuple-element.64), channel_id=1, source_target_pairs={{0,8},{1,9},{2,10},{3,11},{4,12},{5,13},{6,14},{7,15},{8,0},{9,1},... | collective-permute-start | bytes 786440 | tf_op jit(solution)/shard_map/ppermute | solution.py:388
  37.3 1.8 %collective-permute-done.5.refs_1_.refs_3_ = f32[32,2048]{1,0:T(8,128)S(1)} collective-permute-done((f32[32,2048]{1,0:T(8,128)S(1)}, f32[32,2048]{1,0:T(8,128)S(1)}, u32[]{:S(2)}, u32[]{:S(2)}) %collective-permute-start.5) | collective-permute-done | bytes 262176 | tf_op jit(solution)/shard_map/ppermute | solution.py:388
  39.7 3.2 %collective-permute-start.9 = (f32[32,2048]{1,0:T(8,128)S(1)}, f32[32,2048]{1,0:T(8,128)S(1)}, u32[]{:S(2)}, u32[]{:S(2)}) collective-permute-start(f32[32,2048]{1,0:T(8,128)S(1)} %get-tuple-element.67), channel_id=1, source_target_pairs={{0,8},{1,9},{2,10},{3,11},{4,12},{5,13},{6,14},{7,15},{8,0},{9,1},... | collective-permute-start | bytes 786440 | tf_op jit(solution)/shard_map/ppermute | solution.py:388
  42.9 1.8 %collective-permute-done.7.refs_2_.refs_4_ = f32[32,2048]{1,0:T(8,128)S(1)} collective-permute-done((f32[32,2048]{1,0:T(8,128)S(1)}, f32[32,2048]{1,0:T(8,128)S(1)}, u32[]{:S(2)}, u32[]{:S(2)}) %collective-permute-start.7) | collective-permute-done | bytes 262176 | tf_op jit(solution)/shard_map/ppermute | solution.py:388
  45.4 3.2 %collective-permute-start.11 = (f32[32,2048]{1,0:T(8,128)S(1)}, f32[32,2048]{1,0:T(8,128)S(1)}, u32[]{:S(2)}, u32[]{:S(2)}) collective-permute-start(f32[32,2048]{1,0:T(8,128)S(1)} %get-tuple-element.70), channel_id=1, source_target_pairs={{0,8},{1,9},{2,10},{3,11},{4,12},{5,13},{6,14},{7,15},{8,0},{9,1},... | collective-permute-start | bytes 786440 | tf_op jit(solution)/shard_map/ppermute | solution.py:388
  48.5 1.8 %collective-permute-done.9.refs_2_.refs_5_ = f32[32,2048]{1,0:T(8,128)S(1)} collective-permute-done((f32[32,2048]{1,0:T(8,128)S(1)}, f32[32,2048]{1,0:T(8,128)S(1)}, u32[]{:S(2)}, u32[]{:S(2)}) %collective-permute-start.9) | collective-permute-done | bytes 262176 | tf_op jit(solution)/shard_map/ppermute | solution.py:388
  51.0 3.2 %collective-permute-start.13 = (f32[32,2048]{1,0:T(8,128)S(1)}, f32[32,2048]{1,0:T(8,128)S(1)}, u32[]{:S(2)}, u32[]{:S(2)}) collective-permute-start(f32[32,2048]{1,0:T(8,128)S(1)} %get-tuple-element.73), channel_id=1, source_target_pairs={{0,8},{1,9},{2,10},{3,11},{4,12},{5,13},{6,14},{7,15},{8,0},{9,1},... | collective-permute-start | bytes 786440 | tf_op jit(solution)/shard_map/ppermute | solution.py:388
  54.1 1.8 %collective-permute-done.11.refs_3_.refs_6_ = f32[32,2048]{1,0:T(8,128)S(1)} collective-permute-done((f32[32,2048]{1,0:T(8,128)S(1)}, f32[32,2048]{1,0:T(8,128)S(1)}, u32[]{:S(2)}, u32[]{:S(2)}) %collective-permute-start.11) | collective-permute-done | bytes 262176 | tf_op jit(solution)/shard_map/ppermute | solution.py:388
  56.6 3.2 %collective-permute-start.15 = (f32[32,2048]{1,0:T(8,128)S(1)}, f32[32,2048]{1,0:T(8,128)S(1)}, u32[]{:S(2)}, u32[]{:S(2)}) collective-permute-start(f32[32,2048]{1,0:T(8,128)S(1)} %get-tuple-element.76), channel_id=1, source_target_pairs={{0,8},{1,9},{2,10},{3,11},{4,12},{5,13},{6,14},{7,15},{8,0},{9,1},... | collective-permute-start | bytes 786440 | tf_op jit(solution)/shard_map/ppermute | solution.py:388
  62.2 3.2 %collective-permute-start.17 = (f32[32,2048]{1,0:T(8,128)S(1)}, f32[32,2048]{1,0:T(8,128)S(1)}, u32[]{:S(2)}, u32[]{:S(2)}) collective-permute-start(f32[32,2048]{1,0:T(8,128)S(1)} %get-tuple-element.79), channel_id=1, source_target_pairs={{0,8},{1,9},{2,10},{3,11},{4,12},{5,13},{6,14},{7,15},{8,0},{9,1},... | collective-permute-start | bytes 786440 | tf_op jit(solution)/shard_map/ppermute | solution.py:388
  67.9 5.1 %collective-permute-start.19 = (f32[32,2048]{1,0:T(8,128)S(1)}, f32[32,2048]{1,0:T(8,128)S(1)}, u32[]{:S(2)}, u32[]{:S(2)}) collective-permute-start(f32[32,2048]{1,0:T(8,128)S(1)} %get-tuple-element.82), channel_id=1, source_target_pairs={{0,8},{1,9},{2,10},{3,11},{4,12},{5,13},{6,14},{7,15},{8,0},{9,1},... | collective-permute-start | bytes 786440 | tf_op jit(solution)/shard_map/ppermute | solution.py:388
  73.8 2.8 %collective-permute-start.21 = (f32[32,2048]{1,0:T(8,128)S(1)}, f32[32,2048]{1,0:T(8,128)S(1)}, u32[]{:S(2)}, u32[]{:S(2)}) collective-permute-start(f32[32,2048]{1,0:T(8,128)S(1)} %get-tuple-element.85), channel_id=1, source_target_pairs={{0,8},{1,9},{2,10},{3,11},{4,12},{5,13},{6,14},{7,15},{8,0},{9,1},... | collective-permute-start | bytes 786440 | tf_op jit(solution)/shard_map/ppermute | solution.py:388
  76.6 2.8 %collective-permute-done.19.refs_10_ = f32[32,2048]{1,0:T(8,128)S(1)} collective-permute-done((f32[32,2048]{1,0:T(8,128)S(1)}, f32[32,2048]{1,0:T(8,128)S(1)}, u32[]{:S(2)}, u32[]{:S(2)}) %collective-permute-start.19) | collective-permute-done | bytes 262176 | tf_op jit(solution)/shard_map/ppermute | solution.py:388
  79.5 4.2 %collective-permute-done.21.refs_11_ = f32[32,2048]{1,0:T(8,128)S(1)} collective-permute-done((f32[32,2048]{1,0:T(8,128)S(1)}, f32[32,2048]{1,0:T(8,128)S(1)}, u32[]{:S(2)}, u32[]{:S(2)}) %collective-permute-start.21) | collective-permute-done | bytes 262176 | tf_op jit(solution)/shard_map/ppermute | solution.py:388
  83.7 6.3 %assemble.1 = (bf16[192,4096]{1,0:T(8,128)(2,1)}, bf16[192,4096]{1,0:T(8,128)(2,1)}, bf16[4096,384]{1,0:T(8,128)(2,1)}, f32[32,512]{1,0:T(8,128)S(1)}) custom-call(s32[2]{0:T(128)S(1)} %pad_add_fusion.here_ref, s32[6]{0:T(128)S(1)} %copy-done.5, s32[6]{0:T(128)S(1)} %copy-done.6, f32[4,32,4096]{2,1,0:T(8,128)S(1)} %copy-done, ...), custom_call_target="tpu_custom_call" | custom-call | flops 1811939328 | bytes 6291456 | tf_op jit(solution)/shard_map/assemble/pallas_call | solution.py:199
  91.4 2.7 %collective-permute-start.27 = (f32[32,512]{1,0:T(8,128)S(1)}, f32[32,512]{1,0:T(8,128)S(1)}, u32[]{:S(2)}, u32[]{:S(2)}) collective-permute-start(f32[32,512]{1,0:T(8,128)S(1)} %add.27), channel_id=1, source_target_pairs={{0,6},{1,7},{2,4},{3,5},{4,2},{5,3},{6,0},{7,1},{8,14},{9,15},{10,... | collective-permute-start | bytes 196616 | tf_op jit(solution)/shard_map/ppermute | solution.py:351
  94.9 11.8 %all-to-all-done.x_ref = f32[8,64,4096]{2,1,0:T(8,128)} async-done(((f32[8,64,4096]{2,1,0:T(8,128)}), f32[8,64,4096]{2,1,0:T(8,128)}, u32[]{:S(2)}, u32[]{:S(2)}) %all-to-all-start) | async-done | bytes 8388640 | tf_op jit(solution)/shard_map/all_to_all | solution.py:393
  108.7 1.9 %copy-done.1 = bf16[4096,384]{1,0:T(8,128)(2,1)S(1)} copy-done((bf16[4096,384]{1,0:T(8,128)(2,1)S(1)}, bf16[4096,384]{1,0:T(8,128)(2,1)}, u32[]{:S(2)}) %copy-start.1) | copy-done | bytes 3145752
  110.6 9.3 %inner_products.1 = (f32[128,384]{1,0:T(8,128)S(1)}, f32[128,384]{1,0:T(8,128)S(1)}, f32[8,64,4096]{2,1,0:T(8,128)S(1)}) custom-call(s32[2]{0:T(128)S(1)} %pad_add_fusion.here_ref, f32[8,64,4096]{2,1,0:T(8,128)} %all-to-all-done.x_ref, bf16[4096,384]{1,0:T(8,128)(2,1)S(1)} %copy-done.1), custom_call_target="tpu_custom_call" | custom-call | flops 2415919104 | bytes 8388608 | tf_op jit(solution)/shard_map/inner_products/pallas_call | solution.py:294
  122.1 4.2 %collective-permute-done.31 = f32[64,384]{1,0:T(8,128)S(1)} collective-permute-done((f32[64,384]{1,0:T(8,128)S(1)}, f32[64,384]{1,0:T(8,128)S(1)}, u32[]{:S(2)}, u32[]{:S(2)}) %collective-permute-start.31) | collective-permute-done | bytes 98336 | tf_op jit(solution)/shard_map/ppermute | solution.py:351
  126.8 3.5 %merge.1.p_ref = bf16[576,4096]{1,0:T(8,128)(2,1)S(1)} custom-call(f32[32,512]{1,0:T(8,128)S(1)} %add_add_fusion.refs_0_, f32[6,32,32]{2,1,0:T(8,128)S(1)} %copy-done.4, bf16[192,4096]{1,0:T(8,128)(2,1)S(1)} %copy-done.2, bf16[192,4096]{1,0:T(8,128)(2,1)S(1)} %copy-done.3), custom_call_target="tpu_custom_call" | custom-call | flops 905969664 | bytes 6291456 | tf_op jit(solution)/shard_map/merge/pallas_call | solution.py:236
  132.7 2.3 %collective-permute-done.32 = f32[64,384]{1,0:T(8,128)S(1)} collective-permute-done((f32[64,384]{1,0:T(8,128)S(1)}, f32[64,384]{1,0:T(8,128)S(1)}, u32[]{:S(2)}, u32[]{:S(2)}) %collective-permute-start.32) | collective-permute-done | bytes 98336 | tf_op jit(solution)/shard_map/ppermute | solution.py:351
  138.2 6.2 %update.1 = f32[8,64,4096]{2,1,0:T(8,128)} custom-call(s32[2]{0:T(128)S(1)} %pad_add_fusion.here_ref, f32[128,384]{1,0:T(8,128)S(1)} %pad_maximum_fusion.mine_ref, f32[128,384]{1,0:T(8,128)S(1)} %collective-permute-done.33.theirs_ref, f32[8,64,4096]{2,1,0:T(8,128)S(1)} %get-tuple-element.96.x_ref, bf16[576,4096]{1,0:T(8,128)(2,1)S(1)} %merge.1.p_ref), custom_call_target="tpu_custom_call" | custom-call | flops 2415919104 | bytes 16777216 | tf_op jit(solution)/shard_map/update/pallas_call | solution.py:334
  (79 shorter events, 24.3 us)
Async XLA Ops:
  6.1 100.7 %all-to-all-start = ((f32[8,64,4096]{2,1,0:T(8,128)}), f32[8,64,4096]{2,1,0:T(8,128)}, u32[]{:S(2)}, u32[]{:S(2)}) async-start(f32[8,64,4096]{2,1,0:T(8,128)} %pack.1), calls=%async_computation | async-start | bytes 16777216 | tf_op jit(solution)/shard_map/all_to_all | solution.py:393
  12.1 10.1 %collective-permute-start = (f32[32,2048]{1,0:T(8,128)S(1)}, f32[32,2048]{1,0:T(8,128)S(1)}, u32[]{:S(2)}, u32[]{:S(2)}) collective-permute-start(f32[32,2048]{1,0:T(8,128)S(1)} %get-tuple-element.52), channel_id=1, source_target_pairs={{0,8},{1,9},{2,10},{3,11},{4,12},{5,13},{6,14},{7,15},{8,0},{9,1},... | collective-permute-start | bytes 786440 | tf_op jit(solution)/shard_map/ppermute | solution.py:388
  15.1 7.1 %collective-permute-start.2 = (f32[32,2048]{1,0:T(8,128)S(1)}, f32[32,2048]{1,0:T(8,128)S(1)}, u32[]{:S(2)}, u32[]{:S(2)}) collective-permute-start(f32[32,2048]{1,0:T(8,128)S(1)} %get-tuple-element.53), channel_id=1, source_target_pairs={{0,1},{1,0},{2,3},{3,2},{4,5},{5,4},{6,7},{7,6},{8,16},{9,17},{10,... | collective-permute-start | bytes 786440 | tf_op jit(solution)/shard_map/ppermute | solution.py:388
  15.8 12.0 %collective-permute-start.1 = (f32[32,2048]{1,0:T(8,128)S(1)}, f32[32,2048]{1,0:T(8,128)S(1)}, u32[]{:S(2)}, u32[]{:S(2)}) collective-permute-start(f32[32,2048]{1,0:T(8,128)S(1)} %get-tuple-element.55), channel_id=1, source_target_pairs={{0,8},{1,9},{2,10},{3,11},{4,12},{5,13},{6,14},{7,15},{8,0},{9,1},... | collective-permute-start | bytes 786440 | tf_op jit(solution)/shard_map/ppermute | solution.py:388
  18.9 8.9 %collective-permute-start.4 = (f32[32,2048]{1,0:T(8,128)S(1)}, f32[32,2048]{1,0:T(8,128)S(1)}, u32[]{:S(2)}, u32[]{:S(2)}) collective-permute-start(f32[32,2048]{1,0:T(8,128)S(1)} %get-tuple-element.56), channel_id=1, source_target_pairs={{0,1},{1,0},{2,3},{3,2},{4,5},{5,4},{6,7},{7,6},{8,16},{9,17},{10,... | collective-permute-start | bytes 786440 | tf_op jit(solution)/shard_map/ppermute | solution.py:388
  22.9 10.6 %collective-permute-start.3 = (f32[32,2048]{1,0:T(8,128)S(1)}, f32[32,2048]{1,0:T(8,128)S(1)}, u32[]{:S(2)}, u32[]{:S(2)}) collective-permute-start(f32[32,2048]{1,0:T(8,128)S(1)} %get-tuple-element.58), channel_id=1, source_target_pairs={{0,8},{1,9},{2,10},{3,11},{4,12},{5,13},{6,14},{7,15},{8,0},{9,1},... | collective-permute-start | bytes 786440 | tf_op jit(solution)/shard_map/ppermute | solution.py:388
  26.0 7.4 %collective-permute-start.6 = (f32[32,2048]{1,0:T(8,128)S(1)}, f32[32,2048]{1,0:T(8,128)S(1)}, u32[]{:S(2)}, u32[]{:S(2)}) collective-permute-start(f32[32,2048]{1,0:T(8,128)S(1)} %get-tuple-element.59), channel_id=1, source_target_pairs={{0,1},{1,0},{2,3},{3,2},{4,5},{5,4},{6,7},{7,6},{8,16},{9,17},{10,... | collective-permute-start | bytes 786440 | tf_op jit(solution)/shard_map/ppermute | solution.py:388
  28.5 10.6 %collective-permute-start.5 = (f32[32,2048]{1,0:T(8,128)S(1)}, f32[32,2048]{1,0:T(8,128)S(1)}, u32[]{:S(2)}, u32[]{:S(2)}) collective-permute-start(f32[32,2048]{1,0:T(8,128)S(1)} %get-tuple-element.61), channel_id=1, source_target_pairs={{0,8},{1,9},{2,10},{3,11},{4,12},{5,13},{6,14},{7,15},{8,0},{9,1},... | collective-permute-start | bytes 786440 | tf_op jit(solution)/shard_map/ppermute | solution.py:388
  31.7 7.4 %collective-permute-start.8 = (f32[32,2048]{1,0:T(8,128)S(1)}, f32[32,2048]{1,0:T(8,128)S(1)}, u32[]{:S(2)}, u32[]{:S(2)}) collective-permute-start(f32[32,2048]{1,0:T(8,128)S(1)} %get-tuple-element.62), channel_id=1, source_target_pairs={{0,1},{1,0},{2,3},{3,2},{4,5},{5,4},{6,7},{7,6},{8,16},{9,17},{10,... | collective-permute-start | bytes 786440 | tf_op jit(solution)/shard_map/ppermute | solution.py:388
  34.1 10.6 %collective-permute-start.7 = (f32[32,2048]{1,0:T(8,128)S(1)}, f32[32,2048]{1,0:T(8,128)S(1)}, u32[]{:S(2)}, u32[]{:S(2)}) collective-permute-start(f32[32,2048]{1,0:T(8,128)S(1)} %get-tuple-element.64), channel_id=1, source_target_pairs={{0,8},{1,9},{2,10},{3,11},{4,12},{5,13},{6,14},{7,15},{8,0},{9,1},... | collective-permute-start | bytes 786440 | tf_op jit(solution)/shard_map/ppermute | solution.py:388
  37.3 7.4 %collective-permute-start.10 = (f32[32,2048]{1,0:T(8,128)S(1)}, f32[32,2048]{1,0:T(8,128)S(1)}, u32[]{:S(2)}, u32[]{:S(2)}) collective-permute-start(f32[32,2048]{1,0:T(8,128)S(1)} %get-tuple-element.65), channel_id=1, source_target_pairs={{0,1},{1,0},{2,3},{3,2},{4,5},{5,4},{6,7},{7,6},{8,16},{9,17},{10,... | collective-permute-start | bytes 786440 | tf_op jit(solution)/shard_map/ppermute | solution.py:388
  39.7 10.6 %collective-permute-start.9 = (f32[32,2048]{1,0:T(8,128)S(1)}, f32[32,2048]{1,0:T(8,128)S(1)}, u32[]{:S(2)}, u32[]{:S(2)}) collective-permute-start(f32[32,2048]{1,0:T(8,128)S(1)} %get-tuple-element.67), channel_id=1, source_target_pairs={{0,8},{1,9},{2,10},{3,11},{4,12},{5,13},{6,14},{7,15},{8,0},{9,1},... | collective-permute-start | bytes 786440 | tf_op jit(solution)/shard_map/ppermute | solution.py:388
  42.9 7.4 %collective-permute-start.12 = (f32[32,2048]{1,0:T(8,128)S(1)}, f32[32,2048]{1,0:T(8,128)S(1)}, u32[]{:S(2)}, u32[]{:S(2)}) collective-permute-start(f32[32,2048]{1,0:T(8,128)S(1)} %get-tuple-element.68), channel_id=1, source_target_pairs={{0,1},{1,0},{2,3},{3,2},{4,5},{5,4},{6,7},{7,6},{8,16},{9,17},{10,... | collective-permute-start | bytes 786440 | tf_op jit(solution)/shard_map/ppermute | solution.py:388
  45.4 10.5 %collective-permute-start.11 = (f32[32,2048]{1,0:T(8,128)S(1)}, f32[32,2048]{1,0:T(8,128)S(1)}, u32[]{:S(2)}, u32[]{:S(2)}) collective-permute-start(f32[32,2048]{1,0:T(8,128)S(1)} %get-tuple-element.70), channel_id=1, source_target_pairs={{0,8},{1,9},{2,10},{3,11},{4,12},{5,13},{6,14},{7,15},{8,0},{9,1},... | collective-permute-start | bytes 786440 | tf_op jit(solution)/shard_map/ppermute | solution.py:388
  48.5 7.4 %collective-permute-start.14 = (f32[32,2048]{1,0:T(8,128)S(1)}, f32[32,2048]{1,0:T(8,128)S(1)}, u32[]{:S(2)}, u32[]{:S(2)}) collective-permute-start(f32[32,2048]{1,0:T(8,128)S(1)} %get-tuple-element.71), channel_id=1, source_target_pairs={{0,1},{1,0},{2,3},{3,2},{4,5},{5,4},{6,7},{7,6},{8,16},{9,17},{10,... | collective-permute-start | bytes 786440 | tf_op jit(solution)/shard_map/ppermute | solution.py:388
  51.0 10.5 %collective-permute-start.13 = (f32[32,2048]{1,0:T(8,128)S(1)}, f32[32,2048]{1,0:T(8,128)S(1)}, u32[]{:S(2)}, u32[]{:S(2)}) collective-permute-start(f32[32,2048]{1,0:T(8,128)S(1)} %get-tuple-element.73), channel_id=1, source_target_pairs={{0,8},{1,9},{2,10},{3,11},{4,12},{5,13},{6,14},{7,15},{8,0},{9,1},... | collective-permute-start | bytes 786440 | tf_op jit(solution)/shard_map/ppermute | solution.py:388
  54.1 7.4 %collective-permute-start.16 = (f32[32,2048]{1,0:T(8,128)S(1)}, f32[32,2048]{1,0:T(8,128)S(1)}, u32[]{:S(2)}, u32[]{:S(2)}) collective-permute-start(f32[32,2048]{1,0:T(8,128)S(1)} %get-tuple-element.74), channel_id=1, source_target_pairs={{0,1},{1,0},{2,3},{3,2},{4,5},{5,4},{6,7},{7,6},{8,16},{9,17},{10,... | collective-permute-start | bytes 786440 | tf_op jit(solution)/shard_map/ppermute | solution.py:388
  56.6 10.5 %collective-permute-start.15 = (f32[32,2048]{1,0:T(8,128)S(1)}, f32[32,2048]{1,0:T(8,128)S(1)}, u32[]{:S(2)}, u32[]{:S(2)}) collective-permute-start(f32[32,2048]{1,0:T(8,128)S(1)} %get-tuple-element.76), channel_id=1, source_target_pairs={{0,8},{1,9},{2,10},{3,11},{4,12},{5,13},{6,14},{7,15},{8,0},{9,1},... | collective-permute-start | bytes 786440 | tf_op jit(solution)/shard_map/ppermute | solution.py:388
  59.8 7.4 %collective-permute-start.18 = (f32[32,2048]{1,0:T(8,128)S(1)}, f32[32,2048]{1,0:T(8,128)S(1)}, u32[]{:S(2)}, u32[]{:S(2)}) collective-permute-start(f32[32,2048]{1,0:T(8,128)S(1)} %get-tuple-element.77), channel_id=1, source_target_pairs={{0,1},{1,0},{2,3},{3,2},{4,5},{5,4},{6,7},{7,6},{8,16},{9,17},{10,... | collective-permute-start | bytes 786440 | tf_op jit(solution)/shard_map/ppermute | solution.py:388
  62.2 10.9 %collective-permute-start.17 = (f32[32,2048]{1,0:T(8,128)S(1)}, f32[32,2048]{1,0:T(8,128)S(1)}, u32[]{:S(2)}, u32[]{:S(2)}) collective-permute-start(f32[32,2048]{1,0:T(8,128)S(1)} %get-tuple-element.79), channel_id=1, source_target_pairs={{0,8},{1,9},{2,10},{3,11},{4,12},{5,13},{6,14},{7,15},{8,0},{9,1},... | collective-permute-start | bytes 786440 | tf_op jit(solution)/shard_map/ppermute | solution.py:388
  65.4 7.7 %collective-permute-start.20 = (f32[32,2048]{1,0:T(8,128)S(1)}, f32[32,2048]{1,0:T(8,128)S(1)}, u32[]{:S(2)}, u32[]{:S(2)}) collective-permute-start(f32[32,2048]{1,0:T(8,128)S(1)} %get-tuple-element.80), channel_id=1, source_target_pairs={{0,1},{1,0},{2,3},{3,2},{4,5},{5,4},{6,7},{7,6},{8,16},{9,17},{10,... | collective-permute-start | bytes 786440 | tf_op jit(solution)/shard_map/ppermute | solution.py:388
  67.8 11.6 %collective-permute-start.22 = (f32[32,2048]{1,0:T(8,128)S(1)}, f32[32,2048]{1,0:T(8,128)S(1)}, u32[]{:S(2)}, u32[]{:S(2)}) collective-permute-start(f32[32,2048]{1,0:T(8,128)S(1)} %get-tuple-element.83), channel_id=1, source_target_pairs={{0,1},{1,0},{2,3},{3,2},{4,5},{5,4},{6,7},{7,6},{8,16},{9,17},{10,... | collective-permute-start | bytes 786440 | tf_op jit(solution)/shard_map/ppermute | solution.py:388
  67.9 11.5 %collective-permute-start.19 = (f32[32,2048]{1,0:T(8,128)S(1)}, f32[32,2048]{1,0:T(8,128)S(1)}, u32[]{:S(2)}, u32[]{:S(2)}) collective-permute-start(f32[32,2048]{1,0:T(8,128)S(1)} %get-tuple-element.82), channel_id=1, source_target_pairs={{0,8},{1,9},{2,10},{3,11},{4,12},{5,13},{6,14},{7,15},{8,0},{9,1},... | collective-permute-start | bytes 786440 | tf_op jit(solution)/shard_map/ppermute | solution.py:388
  73.8 9.9 %collective-permute-start.21 = (f32[32,2048]{1,0:T(8,128)S(1)}, f32[32,2048]{1,0:T(8,128)S(1)}, u32[]{:S(2)}, u32[]{:S(2)}) collective-permute-start(f32[32,2048]{1,0:T(8,128)S(1)} %get-tuple-element.85), channel_id=1, source_target_pairs={{0,8},{1,9},{2,10},{3,11},{4,12},{5,13},{6,14},{7,15},{8,0},{9,1},... | collective-permute-start | bytes 786440 | tf_op jit(solution)/shard_map/ppermute | solution.py:388
  76.6 7.0 %collective-permute-start.23 = (f32[32,2048]{1,0:T(8,128)S(1)}, f32[32,2048]{1,0:T(8,128)S(1)}, u32[]{:S(2)}, u32[]{:S(2)}) collective-permute-start(f32[32,2048]{1,0:T(8,128)S(1)} %get-tuple-element.86), channel_id=1, source_target_pairs={{0,1},{1,0},{2,3},{3,2},{4,5},{5,4},{6,7},{7,6},{8,16},{9,17},{10,... | collective-permute-start | bytes 786440 | tf_op jit(solution)/shard_map/ppermute | solution.py:388
  91.4 16.6 %collective-permute-start.27 = (f32[32,512]{1,0:T(8,128)S(1)}, f32[32,512]{1,0:T(8,128)S(1)}, u32[]{:S(2)}, u32[]{:S(2)}) collective-permute-start(f32[32,512]{1,0:T(8,128)S(1)} %add.27), channel_id=1, source_target_pairs={{0,6},{1,7},{2,4},{3,5},{4,2},{5,3},{6,0},{7,1},{8,14},{9,15},{10,... | collective-permute-start | bytes 196616 | tf_op jit(solution)/shard_map/ppermute | solution.py:351
  94.0 14.6 %collective-permute-start.26 = (f32[32,512]{1,0:T(8,128)S(1)}, f32[32,512]{1,0:T(8,128)S(1)}, u32[]{:S(2)}, u32[]{:S(2)}) collective-permute-start(f32[32,512]{1,0:T(8,128)S(1)} %add.27), channel_id=1, source_target_pairs={{0,4},{1,5},{2,6},{3,7},{4,0},{5,1},{6,2},{7,3},{8,12},{9,13},{10,... | collective-permute-start | bytes 196616 | tf_op jit(solution)/shard_map/ppermute | solution.py:351
  94.6 14.1 %collective-permute-start.25 = (f32[32,512]{1,0:T(8,128)S(1)}, f32[32,512]{1,0:T(8,128)S(1)}, u32[]{:S(2)}, u32[]{:S(2)}) collective-permute-start(f32[32,512]{1,0:T(8,128)S(1)} %add.27), channel_id=1, source_target_pairs={{0,2},{1,3},{2,0},{3,1},{4,6},{5,7},{6,4},{7,5},{8,10},{9,11},{10,... | collective-permute-start | bytes 196616 | tf_op jit(solution)/shard_map/ppermute | solution.py:351
  121.4 4.9 %collective-permute-start.31 = (f32[64,384]{1,0:T(8,128)S(1)}, f32[64,384]{1,0:T(8,128)S(1)}, u32[]{:S(2)}, u32[]{:S(2)}) collective-permute-start(f32[64,384]{1,0:T(8,128)S(1)} %slice.9), channel_id=1, source_target_pairs={{0,4},{1,5},{2,6},{3,7},{4,0},{5,1},{6,2},{7,3},{8,12},{9,13},{10,... | collective-permute-start | bytes 294920 | tf_op jit(solution)/shard_map/ppermute | solution.py:351
  126.3 5.7 %collective-permute-start.29 = (f32[64,384]{1,0:T(8,128)S(1)}, f32[64,384]{1,0:T(8,128)S(1)}, u32[]{:S(2)}, u32[]{:S(2)}) collective-permute-start(f32[64,384]{1,0:T(8,128)S(1)} %get-tuple-element.95), channel_id=1, source_target_pairs={{0,2},{1,3},{2,0},{3,1},{4,6},{5,7},{6,4},{7,5},{8,10},{9,11},{10,... | collective-permute-start | bytes 294920 | tf_op jit(solution)/shard_map/ppermute | solution.py:351
  130.3 4.7 %collective-permute-start.32 = (f32[64,384]{1,0:T(8,128)S(1)}, f32[64,384]{1,0:T(8,128)S(1)}, u32[]{:S(2)}, u32[]{:S(2)}) collective-permute-start(f32[64,384]{1,0:T(8,128)S(1)} %get-tuple-element.98), channel_id=1, source_target_pairs={{0,2},{1,3},{2,0},{3,1},{4,6},{5,7},{6,4},{7,5},{8,10},{9,11},{10,... | collective-permute-start | bytes 294920 | tf_op jit(solution)/shard_map/ppermute | solution.py:351
  132.0 4.7 %collective-permute-start.30 = (f32[64,384]{1,0:T(8,128)S(1)}, f32[64,384]{1,0:T(8,128)S(1)}, u32[]{:S(2)}, u32[]{:S(2)}) collective-permute-start(f32[64,384]{1,0:T(8,128)S(1)} %add.32), channel_id=1, source_target_pairs={{0,4},{1,5},{2,6},{3,7},{4,0},{5,1},{6,2},{7,3},{8,12},{9,13},{10,... | collective-permute-start | bytes 294920 | tf_op jit(solution)/shard_map/ppermute | solution.py:351
  (10 other events, 115.9 us)

commit v8 on v7

--- a/solution.py
+++ b/solution.py
@@ -264,29 +264,20 @@
     lead, rows, ncols = x.shape
     height = vecs_t.shape[1] // 2
     half = lead * rows // 2
-    blocks = column_blocks(ncols)
     lanes = min(-(-height // 128) * 128, 2 * height)
-    parts = [pl.ds(0, lead // 2), pl.ds(lead // 2, lead // 2)] if lead % 2 == 0 else [pl.ds(0, lead)]
-
-    def kernel(here_ref, x_ref, vecs_ref, mine_ref, theirs_ref, held, by_high, by_low, total, sems):
-        copies = [
-            [
-                pltpu.make_async_copy(x_ref.at[part, :, at], held.at[part, :, at], sems.at[i, j])
-                for j, part in enumerate(parts)
-            ]
-            for i, at in enumerate(blocks)
-        ]
-        for i, copy in enumerate(copy for block in copies for copy in block):
+    cuts = sorted({0, lead // 4, lead * 5 // 8, lead})
+
+    def kernel(here_ref, x_ref, vecs_ref, mine_ref, theirs_ref, held, total, sems):
+        copies = [pltpu.make_async_copy(x_ref.at[i], held.at[i], sems.at[i]) for i in range(lead)]
+        for i, copy in enumerate(copies):
             copy.start(priority=i % QUEUES)
-        for i, at in enumerate(blocks):
-            for copy in copies[i]:
+        for start, end in zip(cuts[:-1], cuts[1:]):
+            for copy in copies[start:end]:
                 copy.wait()
-            high, low = halves(held[:, :, at].reshape(lead * rows, at.size))
-            one = jnp.dot(high, vecs_ref[at, :], preferred_element_type=jnp.float32)
-            two = jnp.dot(low, vecs_ref[at, :lanes], preferred_element_type=jnp.float32)
-            by_high[...] = one if i == 0 else by_high[...] + one
-            by_low[...] = two if i == 0 else by_low[...] + two
-        total[...] = by_high[:, :height] + (by_high[:, height:] + by_low[:, :height])
+            high, low = halves(held[start:end].reshape((end - start) * rows, ncols))
+            by_high = jnp.dot(high, vecs_ref[...], preferred_element_type=jnp.float32)
+            by_low = jnp.dot(low, vecs_ref[:, :lanes], preferred_element_type=jnp.float32)
+            total[start * rows:end * rows, :] = by_high[:, :height] + (by_high[:, height:] + by_low[:, :height])
         core = lax.rem(here_ref[1], 2)
         mine_ref[...] = fold(total[pl.ds(pl.multiple_of(core * half, 8), half), :])
         theirs_ref[...] = fold(total[pl.ds(pl.multiple_of((1 - core) * half, 8), half), :])
@@ -297,10 +288,8 @@
         in_specs=[SMEM, ANY, VMEM],
         out_specs=[VMEM] * 3,
         scratch_shapes=[
-            pltpu.VMEM((lead * rows, 2 * height), jnp.float32),
-            pltpu.VMEM((lead * rows, lanes), jnp.float32),
             pltpu.VMEM((lead * rows, height), jnp.float32),
-            pltpu.SemaphoreType.DMA((len(blocks), len(parts))),
+            pltpu.SemaphoreType.DMA((lead,)),
         ],
         compiler_params=params(),
         cost_estimate=cost(6 * lead * rows * ncols * height, 4 * lead * rows * ncols),
@@ -362,7 +351,7 @@
     for i, (first, second) in enumerate(zip(shifts, reversed(shifts))):
         come_upper, come_lower = swap(upper, first, size), swap(lower, second, size)
         if i == 0:
-            upper = after(upper, token)
+            upper, lower, _ = lax.optimization_barrier((upper, lower, token))
         upper, lower = upper + come_upper, lower + come_lower
     return jnp.concatenate([upper, lower], axis=0)
 

time: 145 us -> 140 us (0.966)
  waiting for transfers between devices: 50.5 us -> 45.7 us
    ppermute x10, waiting for transfers between devices: 14.3 us -> 9.43 us  [swap(): return lax.ppermute(array, 'wide', [(i, i ^ k) for i in range(size)])]
  transfers between devices with their start and end apart: 35 -> 35, of which waited for: 20 -> 20; matrix products, arithmetic and copies ran while one was open for 0% -> 0% of each run, Pallas kernels for 12% -> 13%
where the time goes in v8:
time: 140 us
  starting transfers between devices  52.7 us (38%)
  waiting for transfers between devices  45.7 us (33%)
  Pallas kernels  38.7 us (28%)
  local copies, waits for them, and re-layouts  1.93 us (1%)
    ppermute x24, starting transfers between devices, exchange(): return lax.ppermute(array, ('row', 'wide'), pairs)  39.6 us
    ppermute x24, waiting for transfers between devices, exchange(): return lax.ppermute(array, ('row', 'wide'), pairs)  24.4 us
    all_to_all x1, waiting for transfers between devices, body(): x = lax.all_to_all(piece, 'wide', split_axis=0, concat_axis=0, tiled=True)  11.8 us
    ppermute x10, waiting for transfers between devices, swap(): return lax.ppermute(array, 'wide', [(i, i ^ k) for i in range(size)])  9.43 us
    pallas_call x1, Pallas kernels, inner_products(): pl.pallas_call(kernel, out_shape=[jax.ShapeDtypeStruct((half // 2, 2 * he...  8.54 us
    pallas_call x12, Pallas kernels, feed(): pl.pallas_call(kernel, out_shape=[jax.ShapeDtypeStruct((width, cols), jnp...  8.07 us
    ppermute x10, starting transfers between devices, swap(): return lax.ppermute(array, 'wide', [(i, i ^ k) for i in range(size)])  7.78 us
    pallas_call x1, Pallas kernels, assemble(): pl.pallas_call(kernel, out_shape=[pltpu.HBM((height, ncols), jnp.bfloat16...  6.34 us
  transfers between devices with their start and end apart: 35, of which 20 were waited for; matrix products, arithmetic and copies ran while one was open for 0% of the time, Pallas kernels for 13%

profile of v8, /device:TPU:0, one launch (start us, length us, event | category | flops | bytes accessed | tf_op | source)
XLA Modules:
  0.0 139.6 jit_solution(11316326252001266509)
XLA Ops:
  0.0 6.0 %pack.1 = f32[8,64,4096]{2,1,0:T(8,128)} custom-call(f32[64,32768]{1,0:T(8,128)} %x_ref.1), custom_call_target="tpu_custom_call" | custom-call | bytes 16777216 | tf_op jit(solution)/shard_map/pack/pallas_call | solution.py:82
  6.1 5.3 %all-to-all-start = ((f32[8,64,4096]{2,1,0:T(8,128)}), f32[8,64,4096]{2,1,0:T(8,128)}, u32[]{:S(2)}, u32[]{:S(2)}) async-start(f32[8,64,4096]{2,1,0:T(8,128)} %pack.1), calls=%async_computation | async-start | bytes 16777216 | tf_op jit(solution)/shard_map/all_to_all | solution.py:382
  12.1 2.9 %collective-permute-start = (f32[32,2048]{1,0:T(8,128)S(1)}, f32[32,2048]{1,0:T(8,128)S(1)}, u32[]{:S(2)}, u32[]{:S(2)}) collective-permute-start(f32[32,2048]{1,0:T(8,128)S(1)} %get-tuple-element.53), channel_id=1, source_target_pairs={{0,8},{1,9},{2,10},{3,11},{4,12},{5,13},{6,14},{7,15},{8,0},{9,1},... | collective-permute-start | bytes 786440 | tf_op jit(solution)/shard_map/ppermute | solution.py:377
  15.8 3.1 %collective-permute-start.1 = (f32[32,2048]{1,0:T(8,128)S(1)}, f32[32,2048]{1,0:T(8,128)S(1)}, u32[]{:S(2)}, u32[]{:S(2)}) collective-permute-start(f32[32,2048]{1,0:T(8,128)S(1)} %get-tuple-element.56), channel_id=1, source_target_pairs={{0,8},{1,9},{2,10},{3,11},{4,12},{5,13},{6,14},{7,15},{8,0},{9,1},... | collective-permute-start | bytes 786440 | tf_op jit(solution)/shard_map/ppermute | solution.py:377
  18.9 3.3 %collective-permute-done.refs_0_ = f32[32,2048]{1,0:T(8,128)S(1)} collective-permute-done((f32[32,2048]{1,0:T(8,128)S(1)}, f32[32,2048]{1,0:T(8,128)S(1)}, u32[]{:S(2)}, u32[]{:S(2)}) %collective-permute-start) | collective-permute-done | bytes 262176 | tf_op jit(solution)/shard_map/ppermute | solution.py:377
  22.9 3.2 %collective-permute-start.3 = (f32[32,2048]{1,0:T(8,128)S(1)}, f32[32,2048]{1,0:T(8,128)S(1)}, u32[]{:S(2)}, u32[]{:S(2)}) collective-permute-start(f32[32,2048]{1,0:T(8,128)S(1)} %get-tuple-element.59), channel_id=1, source_target_pairs={{0,8},{1,9},{2,10},{3,11},{4,12},{5,13},{6,14},{7,15},{8,0},{9,1},... | collective-permute-start | bytes 786440 | tf_op jit(solution)/shard_map/ppermute | solution.py:377
  26.0 1.8 %collective-permute-done.1.refs_0_.refs_1_ = f32[32,2048]{1,0:T(8,128)S(1)} collective-permute-done((f32[32,2048]{1,0:T(8,128)S(1)}, f32[32,2048]{1,0:T(8,128)S(1)}, u32[]{:S(2)}, u32[]{:S(2)}) %collective-permute-start.1) | collective-permute-done | bytes 262176 | tf_op jit(solution)/shard_map/ppermute | solution.py:377
  28.5 3.2 %collective-permute-start.5 = (f32[32,2048]{1,0:T(8,128)S(1)}, f32[32,2048]{1,0:T(8,128)S(1)}, u32[]{:S(2)}, u32[]{:S(2)}) collective-permute-start(f32[32,2048]{1,0:T(8,128)S(1)} %get-tuple-element.62), channel_id=1, source_target_pairs={{0,8},{1,9},{2,10},{3,11},{4,12},{5,13},{6,14},{7,15},{8,0},{9,1},... | collective-permute-start | bytes 786440 | tf_op jit(solution)/shard_map/ppermute | solution.py:377
  31.7 1.8 %collective-permute-done.3.refs_1_.refs_2_ = f32[32,2048]{1,0:T(8,128)S(1)} collective-permute-done((f32[32,2048]{1,0:T(8,128)S(1)}, f32[32,2048]{1,0:T(8,128)S(1)}, u32[]{:S(2)}, u32[]{:S(2)}) %collective-permute-start.3) | collective-permute-done | bytes 262176 | tf_op jit(solution)/shard_map/ppermute | solution.py:377
  34.1 3.2 %collective-permute-start.7 = (f32[32,2048]{1,0:T(8,128)S(1)}, f32[32,2048]{1,0:T(8,128)S(1)}, u32[]{:S(2)}, u32[]{:S(2)}) collective-permute-start(f32[32,2048]{1,0:T(8,128)S(1)} %get-tuple-element.65), channel_id=1, source_target_pairs={{0,8},{1,9},{2,10},{3,11},{4,12},{5,13},{6,14},{7,15},{8,0},{9,1},... | collective-permute-start | bytes 786440 | tf_op jit(solution)/shard_map/ppermute | solution.py:377
  37.3 1.8 %collective-permute-done.5.refs_1_.refs_3_ = f32[32,2048]{1,0:T(8,128)S(1)} collective-permute-done((f32[32,2048]{1,0:T(8,128)S(1)}, f32[32,2048]{1,0:T(8,128)S(1)}, u32[]{:S(2)}, u32[]{:S(2)}) %collective-permute-start.5) | collective-permute-done | bytes 262176 | tf_op jit(solution)/shard_map/ppermute | solution.py:377
  39.7 3.2 %collective-permute-start.9 = (f32[32,2048]{1,0:T(8,128)S(1)}, f32[32,2048]{1,0:T(8,128)S(1)}, u32[]{:S(2)}, u32[]{:S(2)}) collective-permute-start(f32[32,2048]{1,0:T(8,128)S(1)} %get-tuple-element.68), channel_id=1, source_target_pairs={{0,8},{1,9},{2,10},{3,11},{4,12},{5,13},{6,14},{7,15},{8,0},{9,1},... | collective-permute-start | bytes 786440 | tf_op jit(solution)/shard_map/ppermute | solution.py:377
  42.9 1.8 %collective-permute-done.7.refs_2_.refs_4_ = f32[32,2048]{1,0:T(8,128)S(1)} collective-permute-done((f32[32,2048]{1,0:T(8,128)S(1)}, f32[32,2048]{1,0:T(8,128)S(1)}, u32[]{:S(2)}, u32[]{:S(2)}) %collective-permute-start.7) | collective-permute-done | bytes 262176 | tf_op jit(solution)/shard_map/ppermute | solution.py:377
  45.4 3.2 %collective-permute-start.11 = (f32[32,2048]{1,0:T(8,128)S(1)}, f32[32,2048]{1,0:T(8,128)S(1)}, u32[]{:S(2)}, u32[]{:S(2)}) collective-permute-start(f32[32,2048]{1,0:T(8,128)S(1)} %get-tuple-element.71), channel_id=1, source_target_pairs={{0,8},{1,9},{2,10},{3,11},{4,12},{5,13},{6,14},{7,15},{8,0},{9,1},... | collective-permute-start | bytes 786440 | tf_op jit(solution)/shard_map/ppermute | solution.py:377
  48.5 1.8 %collective-permute-done.9.refs_2_.refs_5_ = f32[32,2048]{1,0:T(8,128)S(1)} collective-permute-done((f32[32,2048]{1,0:T(8,128)S(1)}, f32[32,2048]{1,0:T(8,128)S(1)}, u32[]{:S(2)}, u32[]{:S(2)}) %collective-permute-start.9) | collective-permute-done | bytes 262176 | tf_op jit(solution)/shard_map/ppermute | solution.py:377
  51.0 3.2 %collective-permute-start.13 = (f32[32,2048]{1,0:T(8,128)S(1)}, f32[32,2048]{1,0:T(8,128)S(1)}, u32[]{:S(2)}, u32[]{:S(2)}) collective-permute-start(f32[32,2048]{1,0:T(8,128)S(1)} %get-tuple-element.74), channel_id=1, source_target_pairs={{0,8},{1,9},{2,10},{3,11},{4,12},{5,13},{6,14},{7,15},{8,0},{9,1},... | collective-permute-start | bytes 786440 | tf_op jit(solution)/shard_map/ppermute | solution.py:377
  54.1 1.8 %collective-permute-done.11.refs_3_.refs_6_ = f32[32,2048]{1,0:T(8,128)S(1)} collective-permute-done((f32[32,2048]{1,0:T(8,128)S(1)}, f32[32,2048]{1,0:T(8,128)S(1)}, u32[]{:S(2)}, u32[]{:S(2)}) %collective-permute-start.11) | collective-permute-done | bytes 262176 | tf_op jit(solution)/shard_map/ppermute | solution.py:377
  56.6 3.2 %collective-permute-start.15 = (f32[32,2048]{1,0:T(8,128)S(1)}, f32[32,2048]{1,0:T(8,128)S(1)}, u32[]{:S(2)}, u32[]{:S(2)}) collective-permute-start(f32[32,2048]{1,0:T(8,128)S(1)} %get-tuple-element.77), channel_id=1, source_target_pairs={{0,8},{1,9},{2,10},{3,11},{4,12},{5,13},{6,14},{7,15},{8,0},{9,1},... | collective-permute-start | bytes 786440 | tf_op jit(solution)/shard_map/ppermute | solution.py:377
  62.2 3.2 %collective-permute-start.17 = (f32[32,2048]{1,0:T(8,128)S(1)}, f32[32,2048]{1,0:T(8,128)S(1)}, u32[]{:S(2)}, u32[]{:S(2)}) collective-permute-start(f32[32,2048]{1,0:T(8,128)S(1)} %get-tuple-element.80), channel_id=1, source_target_pairs={{0,8},{1,9},{2,10},{3,11},{4,12},{5,13},{6,14},{7,15},{8,0},{9,1},... | collective-permute-start | bytes 786440 | tf_op jit(solution)/shard_map/ppermute | solution.py:377
  65.4 1.7 %collective-permute-done.15.refs_4_.refs_8_ = f32[32,2048]{1,0:T(8,128)S(1)} collective-permute-done((f32[32,2048]{1,0:T(8,128)S(1)}, f32[32,2048]{1,0:T(8,128)S(1)}, u32[]{:S(2)}, u32[]{:S(2)}) %collective-permute-start.15) | collective-permute-done | bytes 262176 | tf_op jit(solution)/shard_map/ppermute | solution.py:377
  67.9 5.1 %collective-permute-start.19 = (f32[32,2048]{1,0:T(8,128)S(1)}, f32[32,2048]{1,0:T(8,128)S(1)}, u32[]{:S(2)}, u32[]{:S(2)}) collective-permute-start(f32[32,2048]{1,0:T(8,128)S(1)} %get-tuple-element.83), channel_id=1, source_target_pairs={{0,8},{1,9},{2,10},{3,11},{4,12},{5,13},{6,14},{7,15},{8,0},{9,1},... | collective-permute-start | bytes 786440 | tf_op jit(solution)/shard_map/ppermute | solution.py:377
  73.8 2.8 %collective-permute-start.21 = (f32[32,2048]{1,0:T(8,128)S(1)}, f32[32,2048]{1,0:T(8,128)S(1)}, u32[]{:S(2)}, u32[]{:S(2)}) collective-permute-start(f32[32,2048]{1,0:T(8,128)S(1)} %get-tuple-element.86), channel_id=1, source_target_pairs={{0,8},{1,9},{2,10},{3,11},{4,12},{5,13},{6,14},{7,15},{8,0},{9,1},... | collective-permute-start | bytes 786440 | tf_op jit(solution)/shard_map/ppermute | solution.py:377
  76.6 2.8 %collective-permute-done.19.refs_10_ = f32[32,2048]{1,0:T(8,128)S(1)} collective-permute-done((f32[32,2048]{1,0:T(8,128)S(1)}, f32[32,2048]{1,0:T(8,128)S(1)}, u32[]{:S(2)}, u32[]{:S(2)}) %collective-permute-start.19) | collective-permute-done | bytes 262176 | tf_op jit(solution)/shard_map/ppermute | solution.py:377
  79.5 4.2 %collective-permute-done.21.refs_11_ = f32[32,2048]{1,0:T(8,128)S(1)} collective-permute-done((f32[32,2048]{1,0:T(8,128)S(1)}, f32[32,2048]{1,0:T(8,128)S(1)}, u32[]{:S(2)}, u32[]{:S(2)}) %collective-permute-start.21) | collective-permute-done | bytes 262176 | tf_op jit(solution)/shard_map/ppermute | solution.py:377
  83.7 6.3 %assemble.1 = (bf16[192,4096]{1,0:T(8,128)(2,1)}, bf16[192,4096]{1,0:T(8,128)(2,1)}, bf16[4096,384]{1,0:T(8,128)(2,1)}, f32[32,512]{1,0:T(8,128)S(1)}) custom-call(s32[2]{0:T(128)S(1)} %pad_add_fusion.here_ref, s32[6]{0:T(128)S(1)} %copy-done.5, s32[6]{0:T(128)S(1)} %copy-done.6, f32[4,32,4096]{2,1,0:T(8,128)S(1)} %copy-done, ...), custom_call_target="tpu_custom_call" | custom-call | flops 1811939328 | bytes 6291456 | tf_op jit(solution)/shard_map/assemble/pallas_call | solution.py:199
  91.4 2.7 %collective-permute-start.27 = (f32[32,512]{1,0:T(8,128)S(1)}, f32[32,512]{1,0:T(8,128)S(1)}, u32[]{:S(2)}, u32[]{:S(2)}) collective-permute-start(f32[32,512]{1,0:T(8,128)S(1)} %add.27), channel_id=1, source_target_pairs={{0,6},{1,7},{2,4},{3,5},{4,2},{5,3},{6,0},{7,1},{8,14},{9,15},{10,... | collective-permute-start | bytes 196616 | tf_op jit(solution)/shard_map/ppermute | solution.py:340
  94.9 11.8 %all-to-all-done.x_ref = f32[8,64,4096]{2,1,0:T(8,128)} async-done(((f32[8,64,4096]{2,1,0:T(8,128)}), f32[8,64,4096]{2,1,0:T(8,128)}, u32[]{:S(2)}, u32[]{:S(2)}) %all-to-all-start) | async-done | bytes 8388640 | tf_op jit(solution)/shard_map/all_to_all | solution.py:382
  108.7 1.9 %copy-done.1 = bf16[4096,384]{1,0:T(8,128)(2,1)S(1)} copy-done((bf16[4096,384]{1,0:T(8,128)(2,1)S(1)}, bf16[4096,384]{1,0:T(8,128)(2,1)}, u32[]{:S(2)}) %copy-start.1) | copy-done | bytes 3145752
  110.6 8.5 %inner_products.1 = (f32[128,384]{1,0:T(8,128)S(1)}, f32[128,384]{1,0:T(8,128)S(1)}, f32[8,64,4096]{2,1,0:T(8,128)S(1)}) custom-call(s32[2]{0:T(128)S(1)} %pad_add_fusion.here_ref, f32[8,64,4096]{2,1,0:T(8,128)} %all-to-all-done.x_ref, bf16[4096,384]{1,0:T(8,128)(2,1)S(1)} %copy-done.1), custom_call_target="tpu_custom_call" | custom-call | flops 2415919104 | bytes 8388608 | tf_op jit(solution)/shard_map/inner_products/pallas_call | solution.py:285
  121.8 3.5 %merge.1.p_ref = bf16[576,4096]{1,0:T(8,128)(2,1)S(1)} custom-call(f32[32,512]{1,0:T(8,128)S(1)} %add_add_fusion.refs_0_, f32[6,32,32]{2,1,0:T(8,128)S(1)} %copy-done.4, bf16[192,4096]{1,0:T(8,128)(2,1)S(1)} %copy-done.2, bf16[192,4096]{1,0:T(8,128)(2,1)S(1)} %copy-done.3), custom_call_target="tpu_custom_call" | custom-call | flops 905969664 | bytes 6291456 | tf_op jit(solution)/shard_map/merge/pallas_call | solution.py:236
  128.5 1.8 %collective-permute-done.32 = f32[64,384]{1,0:T(8,128)S(1)} collective-permute-done((f32[64,384]{1,0:T(8,128)S(1)}, f32[64,384]{1,0:T(8,128)S(1)}, u32[]{:S(2)}, u32[]{:S(2)}) %collective-permute-start.32) | collective-permute-done | bytes 98336 | tf_op jit(solution)/shard_map/ppermute | solution.py:340
  133.2 6.2 %update.1 = f32[8,64,4096]{2,1,0:T(8,128)} custom-call(s32[2]{0:T(128)S(1)} %pad_add_fusion.here_ref, f32[128,384]{1,0:T(8,128)S(1)} %pad_maximum_fusion.mine_ref, f32[128,384]{1,0:T(8,128)S(1)} %collective-permute-done.33.theirs_ref, f32[8,64,4096]{2,1,0:T(8,128)S(1)} %get-tuple-element.98.x_ref, bf16[576,4096]{1,0:T(8,128)(2,1)S(1)} %merge.1.p_ref), custom_call_target="tpu_custom_call" | custom-call | flops 2415919104 | bytes 16777216 | tf_op jit(solution)/shard_map/update/pallas_call | solution.py:323
  (79 shorter events, 23.0 us)
Async XLA Ops:
  6.1 100.7 %all-to-all-start = ((f32[8,64,4096]{2,1,0:T(8,128)}), f32[8,64,4096]{2,1,0:T(8,128)}, u32[]{:S(2)}, u32[]{:S(2)}) async-start(f32[8,64,4096]{2,1,0:T(8,128)} %pack.1), calls=%async_computation | async-start | bytes 16777216 | tf_op jit(solution)/shard_map/all_to_all | solution.py:382
  12.1 10.1 %collective-permute-start = (f32[32,2048]{1,0:T(8,128)S(1)}, f32[32,2048]{1,0:T(8,128)S(1)}, u32[]{:S(2)}, u32[]{:S(2)}) collective-permute-start(f32[32,2048]{1,0:T(8,128)S(1)} %get-tuple-element.53), channel_id=1, source_target_pairs={{0,8},{1,9},{2,10},{3,11},{4,12},{5,13},{6,14},{7,15},{8,0},{9,1},... | collective-permute-start | bytes 786440 | tf_op jit(solution)/shard_map/ppermute | solution.py:377
  15.1 7.1 %collective-permute-start.2 = (f32[32,2048]{1,0:T(8,128)S(1)}, f32[32,2048]{1,0:T(8,128)S(1)}, u32[]{:S(2)}, u32[]{:S(2)}) collective-permute-start(f32[32,2048]{1,0:T(8,128)S(1)} %get-tuple-element.54), channel_id=1, source_target_pairs={{0,1},{1,0},{2,3},{3,2},{4,5},{5,4},{6,7},{7,6},{8,16},{9,17},{10,... | collective-permute-start | bytes 786440 | tf_op jit(solution)/shard_map/ppermute | solution.py:377
  15.8 12.0 %collective-permute-start.1 = (f32[32,2048]{1,0:T(8,128)S(1)}, f32[32,2048]{1,0:T(8,128)S(1)}, u32[]{:S(2)}, u32[]{:S(2)}) collective-permute-start(f32[32,2048]{1,0:T(8,128)S(1)} %get-tuple-element.56), channel_id=1, source_target_pairs={{0,8},{1,9},{2,10},{3,11},{4,12},{5,13},{6,14},{7,15},{8,0},{9,1},... | collective-permute-start | bytes 786440 | tf_op jit(solution)/shard_map/ppermute | solution.py:377
  18.9 8.9 %collective-permute-start.4 = (f32[32,2048]{1,0:T(8,128)S(1)}, f32[32,2048]{1,0:T(8,128)S(1)}, u32[]{:S(2)}, u32[]{:S(2)}) collective-permute-start(f32[32,2048]{1,0:T(8,128)S(1)} %get-tuple-element.57), channel_id=1, source_target_pairs={{0,1},{1,0},{2,3},{3,2},{4,5},{5,4},{6,7},{7,6},{8,16},{9,17},{10,... | collective-permute-start | bytes 786440 | tf_op jit(solution)/shard_map/ppermute | solution.py:377
  22.9 10.6 %collective-permute-start.3 = (f32[32,2048]{1,0:T(8,128)S(1)}, f32[32,2048]{1,0:T(8,128)S(1)}, u32[]{:S(2)}, u32[]{:S(2)}) collective-permute-start(f32[32,2048]{1,0:T(8,128)S(1)} %get-tuple-element.59), channel_id=1, source_target_pairs={{0,8},{1,9},{2,10},{3,11},{4,12},{5,13},{6,14},{7,15},{8,0},{9,1},... | collective-permute-start | bytes 786440 | tf_op jit(solution)/shard_map/ppermute | solution.py:377
  26.0 7.4 %collective-permute-start.6 = (f32[32,2048]{1,0:T(8,128)S(1)}, f32[32,2048]{1,0:T(8,128)S(1)}, u32[]{:S(2)}, u32[]{:S(2)}) collective-permute-start(f32[32,2048]{1,0:T(8,128)S(1)} %get-tuple-element.60), channel_id=1, source_target_pairs={{0,1},{1,0},{2,3},{3,2},{4,5},{5,4},{6,7},{7,6},{8,16},{9,17},{10,... | collective-permute-start | bytes 786440 | tf_op jit(solution)/shard_map/ppermute | solution.py:377
  28.5 10.6 %collective-permute-start.5 = (f32[32,2048]{1,0:T(8,128)S(1)}, f32[32,2048]{1,0:T(8,128)S(1)}, u32[]{:S(2)}, u32[]{:S(2)}) collective-permute-start(f32[32,2048]{1,0:T(8,128)S(1)} %get-tuple-element.62), channel_id=1, source_target_pairs={{0,8},{1,9},{2,10},{3,11},{4,12},{5,13},{6,14},{7,15},{8,0},{9,1},... | collective-permute-start | bytes 786440 | tf_op jit(solution)/shard_map/ppermute | solution.py:377
  31.7 7.4 %collective-permute-start.8 = (f32[32,2048]{1,0:T(8,128)S(1)}, f32[32,2048]{1,0:T(8,128)S(1)}, u32[]{:S(2)}, u32[]{:S(2)}) collective-permute-start(f32[32,2048]{1,0:T(8,128)S(1)} %get-tuple-element.63), channel_id=1, source_target_pairs={{0,1},{1,0},{2,3},{3,2},{4,5},{5,4},{6,7},{7,6},{8,16},{9,17},{10,... | collective-permute-start | bytes 786440 | tf_op jit(solution)/shard_map/ppermute | solution.py:377
  34.1 10.6 %collective-permute-start.7 = (f32[32,2048]{1,0:T(8,128)S(1)}, f32[32,2048]{1,0:T(8,128)S(1)}, u32[]{:S(2)}, u32[]{:S(2)}) collective-permute-start(f32[32,2048]{1,0:T(8,128)S(1)} %get-tuple-element.65), channel_id=1, source_target_pairs={{0,8},{1,9},{2,10},{3,11},{4,12},{5,13},{6,14},{7,15},{8,0},{9,1},... | collective-permute-start | bytes 786440 | tf_op jit(solution)/shard_map/ppermute | solution.py:377
  37.3 7.4 %collective-permute-start.10 = (f32[32,2048]{1,0:T(8,128)S(1)}, f32[32,2048]{1,0:T(8,128)S(1)}, u32[]{:S(2)}, u32[]{:S(2)}) collective-permute-start(f32[32,2048]{1,0:T(8,128)S(1)} %get-tuple-element.66), channel_id=1, source_target_pairs={{0,1},{1,0},{2,3},{3,2},{4,5},{5,4},{6,7},{7,6},{8,16},{9,17},{10,... | collective-permute-start | bytes 786440 | tf_op jit(solution)/shard_map/ppermute | solution.py:377
  39.7 10.6 %collective-permute-start.9 = (f32[32,2048]{1,0:T(8,128)S(1)}, f32[32,2048]{1,0:T(8,128)S(1)}, u32[]{:S(2)}, u32[]{:S(2)}) collective-permute-start(f32[32,2048]{1,0:T(8,128)S(1)} %get-tuple-element.68), channel_id=1, source_target_pairs={{0,8},{1,9},{2,10},{3,11},{4,12},{5,13},{6,14},{7,15},{8,0},{9,1},... | collective-permute-start | bytes 786440 | tf_op jit(solution)/shard_map/ppermute | solution.py:377
  42.9 7.4 %collective-permute-start.12 = (f32[32,2048]{1,0:T(8,128)S(1)}, f32[32,2048]{1,0:T(8,128)S(1)}, u32[]{:S(2)}, u32[]{:S(2)}) collective-permute-start(f32[32,2048]{1,0:T(8,128)S(1)} %get-tuple-element.69), channel_id=1, source_target_pairs={{0,1},{1,0},{2,3},{3,2},{4,5},{5,4},{6,7},{7,6},{8,16},{9,17},{10,... | collective-permute-start | bytes 786440 | tf_op jit(solution)/shard_map/ppermute | solution.py:377
  45.4 10.5 %collective-permute-start.11 = (f32[32,2048]{1,0:T(8,128)S(1)}, f32[32,2048]{1,0:T(8,128)S(1)}, u32[]{:S(2)}, u32[]{:S(2)}) collective-permute-start(f32[32,2048]{1,0:T(8,128)S(1)} %get-tuple-element.71), channel_id=1, source_target_pairs={{0,8},{1,9},{2,10},{3,11},{4,12},{5,13},{6,14},{7,15},{8,0},{9,1},... | collective-permute-start | bytes 786440 | tf_op jit(solution)/shard_map/ppermute | solution.py:377
  48.5 7.4 %collective-permute-start.14 = (f32[32,2048]{1,0:T(8,128)S(1)}, f32[32,2048]{1,0:T(8,128)S(1)}, u32[]{:S(2)}, u32[]{:S(2)}) collective-permute-start(f32[32,2048]{1,0:T(8,128)S(1)} %get-tuple-element.72), channel_id=1, source_target_pairs={{0,1},{1,0},{2,3},{3,2},{4,5},{5,4},{6,7},{7,6},{8,16},{9,17},{10,... | collective-permute-start | bytes 786440 | tf_op jit(solution)/shard_map/ppermute | solution.py:377
  51.0 10.5 %collective-permute-start.13 = (f32[32,2048]{1,0:T(8,128)S(1)}, f32[32,2048]{1,0:T(8,128)S(1)}, u32[]{:S(2)}, u32[]{:S(2)}) collective-permute-start(f32[32,2048]{1,0:T(8,128)S(1)} %get-tuple-element.74), channel_id=1, source_target_pairs={{0,8},{1,9},{2,10},{3,11},{4,12},{5,13},{6,14},{7,15},{8,0},{9,1},... | collective-permute-start | bytes 786440 | tf_op jit(solution)/shard_map/ppermute | solution.py:377
  54.1 7.4 %collective-permute-start.16 = (f32[32,2048]{1,0:T(8,128)S(1)}, f32[32,2048]{1,0:T(8,128)S(1)}, u32[]{:S(2)}, u32[]{:S(2)}) collective-permute-start(f32[32,2048]{1,0:T(8,128)S(1)} %get-tuple-element.75), channel_id=1, source_target_pairs={{0,1},{1,0},{2,3},{3,2},{4,5},{5,4},{6,7},{7,6},{8,16},{9,17},{10,... | collective-permute-start | bytes 786440 | tf_op jit(solution)/shard_map/ppermute | solution.py:377
  56.6 10.5 %collective-permute-start.15 = (f32[32,2048]{1,0:T(8,128)S(1)}, f32[32,2048]{1,0:T(8,128)S(1)}, u32[]{:S(2)}, u32[]{:S(2)}) collective-permute-start(f32[32,2048]{1,0:T(8,128)S(1)} %get-tuple-element.77), channel_id=1, source_target_pairs={{0,8},{1,9},{2,10},{3,11},{4,12},{5,13},{6,14},{7,15},{8,0},{9,1},... | collective-permute-start | bytes 786440 | tf_op jit(solution)/shard_map/ppermute | solution.py:377
  59.8 7.4 %collective-permute-start.18 = (f32[32,2048]{1,0:T(8,128)S(1)}, f32[32,2048]{1,0:T(8,128)S(1)}, u32[]{:S(2)}, u32[]{:S(2)}) collective-permute-start(f32[32,2048]{1,0:T(8,128)S(1)} %get-tuple-element.78), channel_id=1, source_target_pairs={{0,1},{1,0},{2,3},{3,2},{4,5},{5,4},{6,7},{7,6},{8,16},{9,17},{10,... | collective-permute-start | bytes 786440 | tf_op jit(solution)/shard_map/ppermute | solution.py:377
  62.2 10.9 %collective-permute-start.17 = (f32[32,2048]{1,0:T(8,128)S(1)}, f32[32,2048]{1,0:T(8,128)S(1)}, u32[]{:S(2)}, u32[]{:S(2)}) collective-permute-start(f32[32,2048]{1,0:T(8,128)S(1)} %get-tuple-element.80), channel_id=1, source_target_pairs={{0,8},{1,9},{2,10},{3,11},{4,12},{5,13},{6,14},{7,15},{8,0},{9,1},... | collective-permute-start | bytes 786440 | tf_op jit(solution)/shard_map/ppermute | solution.py:377
  65.4 7.7 %collective-permute-start.20 = (f32[32,2048]{1,0:T(8,128)S(1)}, f32[32,2048]{1,0:T(8,128)S(1)}, u32[]{:S(2)}, u32[]{:S(2)}) collective-permute-start(f32[32,2048]{1,0:T(8,128)S(1)} %get-tuple-element.81), channel_id=1, source_target_pairs={{0,1},{1,0},{2,3},{3,2},{4,5},{5,4},{6,7},{7,6},{8,16},{9,17},{10,... | collective-permute-start | bytes 786440 | tf_op jit(solution)/shard_map/ppermute | solution.py:377
  67.8 11.6 %collective-permute-start.22 = (f32[32,2048]{1,0:T(8,128)S(1)}, f32[32,2048]{1,0:T(8,128)S(1)}, u32[]{:S(2)}, u32[]{:S(2)}) collective-permute-start(f32[32,2048]{1,0:T(8,128)S(1)} %get-tuple-element.84), channel_id=1, source_target_pairs={{0,1},{1,0},{2,3},{3,2},{4,5},{5,4},{6,7},{7,6},{8,16},{9,17},{10,... | collective-permute-start | bytes 786440 | tf_op jit(solution)/shard_map/ppermute | solution.py:377
  67.9 11.5 %collective-permute-start.19 = (f32[32,2048]{1,0:T(8,128)S(1)}, f32[32,2048]{1,0:T(8,128)S(1)}, u32[]{:S(2)}, u32[]{:S(2)}) collective-permute-start(f32[32,2048]{1,0:T(8,128)S(1)} %get-tuple-element.83), channel_id=1, source_target_pairs={{0,8},{1,9},{2,10},{3,11},{4,12},{5,13},{6,14},{7,15},{8,0},{9,1},... | collective-permute-start | bytes 786440 | tf_op jit(solution)/shard_map/ppermute | solution.py:377
  73.8 9.9 %collective-permute-start.21 = (f32[32,2048]{1,0:T(8,128)S(1)}, f32[32,2048]{1,0:T(8,128)S(1)}, u32[]{:S(2)}, u32[]{:S(2)}) collective-permute-start(f32[32,2048]{1,0:T(8,128)S(1)} %get-tuple-element.86), channel_id=1, source_target_pairs={{0,8},{1,9},{2,10},{3,11},{4,12},{5,13},{6,14},{7,15},{8,0},{9,1},... | collective-permute-start | bytes 786440 | tf_op jit(solution)/shard_map/ppermute | solution.py:377
  76.6 7.0 %collective-permute-start.23 = (f32[32,2048]{1,0:T(8,128)S(1)}, f32[32,2048]{1,0:T(8,128)S(1)}, u32[]{:S(2)}, u32[]{:S(2)}) collective-permute-start(f32[32,2048]{1,0:T(8,128)S(1)} %get-tuple-element.87), channel_id=1, source_target_pairs={{0,1},{1,0},{2,3},{3,2},{4,5},{5,4},{6,7},{7,6},{8,16},{9,17},{10,... | collective-permute-start | bytes 786440 | tf_op jit(solution)/shard_map/ppermute | solution.py:377
  91.4 16.6 %collective-permute-start.27 = (f32[32,512]{1,0:T(8,128)S(1)}, f32[32,512]{1,0:T(8,128)S(1)}, u32[]{:S(2)}, u32[]{:S(2)}) collective-permute-start(f32[32,512]{1,0:T(8,128)S(1)} %add.27), channel_id=1, source_target_pairs={{0,6},{1,7},{2,4},{3,5},{4,2},{5,3},{6,0},{7,1},{8,14},{9,15},{10,... | collective-permute-start | bytes 196616 | tf_op jit(solution)/shard_map/ppermute | solution.py:340
  94.0 14.6 %collective-permute-start.26 = (f32[32,512]{1,0:T(8,128)S(1)}, f32[32,512]{1,0:T(8,128)S(1)}, u32[]{:S(2)}, u32[]{:S(2)}) collective-permute-start(f32[32,512]{1,0:T(8,128)S(1)} %add.27), channel_id=1, source_target_pairs={{0,4},{1,5},{2,6},{3,7},{4,0},{5,1},{6,2},{7,3},{8,12},{9,13},{10,... | collective-permute-start | bytes 196616 | tf_op jit(solution)/shard_map/ppermute | solution.py:340
  94.6 14.1 %collective-permute-start.25 = (f32[32,512]{1,0:T(8,128)S(1)}, f32[32,512]{1,0:T(8,128)S(1)}, u32[]{:S(2)}, u32[]{:S(2)}) collective-permute-start(f32[32,512]{1,0:T(8,128)S(1)} %add.27), channel_id=1, source_target_pairs={{0,2},{1,3},{2,0},{3,1},{4,6},{5,7},{6,4},{7,5},{8,10},{9,11},{10,... | collective-permute-start | bytes 196616 | tf_op jit(solution)/shard_map/ppermute | solution.py:340
  120.7 4.9 %collective-permute-start.31 = (f32[64,384]{1,0:T(8,128)S(1)}, f32[64,384]{1,0:T(8,128)S(1)}, u32[]{:S(2)}, u32[]{:S(2)}) collective-permute-start(f32[64,384]{1,0:T(8,128)S(1)} %get-tuple-element.97), channel_id=1, source_target_pairs={{0,4},{1,5},{2,6},{3,7},{4,0},{5,1},{6,2},{7,3},{8,12},{9,13},{10,... | collective-permute-start | bytes 294920 | tf_op jit(solution)/shard_map/ppermute | solution.py:340
  121.4 5.6 %collective-permute-start.29 = (f32[64,384]{1,0:T(8,128)S(1)}, f32[64,384]{1,0:T(8,128)S(1)}, u32[]{:S(2)}, u32[]{:S(2)}) collective-permute-start(f32[64,384]{1,0:T(8,128)S(1)} %get-tuple-element.96), channel_id=1, source_target_pairs={{0,2},{1,3},{2,0},{3,1},{4,6},{5,7},{6,4},{7,5},{8,10},{9,11},{10,... | collective-permute-start | bytes 294920 | tf_op jit(solution)/shard_map/ppermute | solution.py:340
  125.6 4.7 %collective-permute-start.32 = (f32[64,384]{1,0:T(8,128)S(1)}, f32[64,384]{1,0:T(8,128)S(1)}, u32[]{:S(2)}, u32[]{:S(2)}) collective-permute-start(f32[64,384]{1,0:T(8,128)S(1)} %add.34), channel_id=1, source_target_pairs={{0,2},{1,3},{2,0},{3,1},{4,6},{5,7},{6,4},{7,5},{8,10},{9,11},{10,... | collective-permute-start | bytes 294920 | tf_op jit(solution)/shard_map/ppermute | solution.py:340
  127.0 4.7 %collective-permute-start.30 = (f32[64,384]{1,0:T(8,128)S(1)}, f32[64,384]{1,0:T(8,128)S(1)}, u32[]{:S(2)}, u32[]{:S(2)}) collective-permute-start(f32[64,384]{1,0:T(8,128)S(1)} %add.32), channel_id=1, source_target_pairs={{0,4},{1,5},{2,6},{3,7},{4,0},{5,1},{6,2},{7,3},{8,12},{9,13},{10,... | collective-permute-start | bytes 294920 | tf_op jit(solution)/shard_map/ppermute | solution.py:340
  (10 other events, 100.9 us)

commit v9 on v8

--- a/solution.py
+++ b/solution.py
@@ -260,24 +260,56 @@
     return [pl.ds(start, cols) for start in range(0, ncols, cols)]
 
 
+def lift(x):
+    rows = x.shape[0]
+    step = rows // 4 if rows % 64 == 0 else rows
+
+    def kernel(x_ref, out_ref, sems):
+        copies = [
+            pltpu.make_async_copy(x_ref.at[pl.ds(start, step)], out_ref.at[pl.ds(start, step)], sems.at[i])
+            for i, start in enumerate(range(0, rows, step))
+        ]
+        for i, copy in enumerate(copies):
+            copy.start(priority=i % QUEUES)
+        for copy in copies:
+            copy.wait()
+
+    return pl.pallas_call(
+        kernel,
+        out_shape=pltpu.VMEM(x.shape, x.dtype),
+        in_specs=[ANY],
+        out_specs=VMEM,
+        scratch_shapes=[pltpu.SemaphoreType.DMA((rows // step,))],
+        compiler_params=params(),
+        cost_estimate=cost(0, 2 * x.size),
+        name="lift",
+    )(in_hbm(x))
+
+
 def inner_products(here, x, vecs_t):
-    lead, rows, ncols = x.shape
+    rows, ncols = x.shape
     height = vecs_t.shape[1] // 2
-    half = lead * rows // 2
+    half = rows // 2
     lanes = min(-(-height // 128) * 128, 2 * height)
-    cuts = sorted({0, lead // 4, lead * 5 // 8, lead})
+    step = rows // 8 if rows % 64 == 0 else rows
+    n_copies = rows // step
+    cuts = sorted({0, n_copies // 4, n_copies * 5 // 8, n_copies})
 
     def kernel(here_ref, x_ref, vecs_ref, mine_ref, theirs_ref, held, total, sems):
-        copies = [pltpu.make_async_copy(x_ref.at[i], held.at[i], sems.at[i]) for i in range(lead)]
+        copies = []
+        for i in range(n_copies):
+            at = pl.ds(i * step, step)
+            copies.append(pltpu.make_async_copy(x_ref.at[at], held.at[at], sems.at[i]))
         for i, copy in enumerate(copies):
             copy.start(priority=i % QUEUES)
         for start, end in zip(cuts[:-1], cuts[1:]):
             for copy in copies[start:end]:
                 copy.wait()
-            high, low = halves(held[start:end].reshape((end - start) * rows, ncols))
+            at = pl.ds(start * step, (end - start) * step)
+            high, low = halves(held[at, :])
             by_high = jnp.dot(high, vecs_ref[...], preferred_element_type=jnp.float32)
             by_low = jnp.dot(low, vecs_ref[:, :lanes], preferred_element_type=jnp.float32)
-            total[start * rows:end * rows, :] = by_high[:, :height] + (by_high[:, height:] + by_low[:, :height])
+            total[at, :] = by_high[:, :height] + (by_high[:, height:] + by_low[:, :height])
         core = lax.rem(here_ref[1], 2)
         mine_ref[...] = fold(total[pl.ds(pl.multiple_of(core * half, 8), half), :])
         theirs_ref[...] = fold(total[pl.ds(pl.multiple_of((1 - core) * half, 8), half), :])
@@ -287,53 +319,56 @@
         out_shape=[jax.ShapeDtypeStruct((half // 2, 2 * height), jnp.float32)] * 2 + [pltpu.VMEM(x.shape, jnp.float32)],
         in_specs=[SMEM, ANY, VMEM],
         out_specs=[VMEM] * 3,
-        scratch_shapes=[
-            pltpu.VMEM((lead * rows, height), jnp.float32),
-            pltpu.SemaphoreType.DMA((lead,)),
-        ],
+        scratch_shapes=[pltpu.VMEM((rows, height), jnp.float32), pltpu.SemaphoreType.DMA((n_copies,))],
         compiler_params=params(),
-        cost_estimate=cost(6 * lead * rows * ncols * height, 4 * lead * rows * ncols),
+        cost_estimate=cost(6 * rows * ncols * height, 4 * rows * ncols),
         name="inner_products",
     )(here, in_hbm(x), vecs_t)
 
 
-def update(here, x, mine, theirs, changes):
-    lead, rows, ncols = x.shape
-    height = changes.shape[0] // 3
-    half = lead * rows // 2
+def update(here, x, sums, changes, out, other):
+    rows, ncols = x.shape
+    half = rows // 2
     blocks = column_blocks(ncols)
     depth = min(4, len(blocks))
 
-    def kernel(here_ref, mine_ref, theirs_ref, x_ref, p_ref, out_ref, w_ref, held, sems):
+    def kernel(here_ref, sum_ref, x_ref, p_ref, *refs):
+        out_ref, held, sems = refs[-3:]
         core = lax.rem(here_ref[1], 2)
-        w_ref[pl.ds(pl.multiple_of(core * half, 8), half), :] = unfold(mine_ref[...])
-        w_ref[pl.ds(pl.multiple_of((1 - core) * half, 8), half), :] = unfold(theirs_ref[...])
-        high, low = halves(w_ref[...])
+        mine = pl.ds(pl.multiple_of((1 - core if other else core) * half, 8), half)
+        high, low = halves(unfold(sum_ref[...]))
         w = jnp.concatenate([high, low, high], axis=1)
-        copies = [pltpu.make_async_copy(held.at[i % depth], out_ref.at[:, :, at], sems.at[i]) for i, at in enumerate(blocks)]
+        copies = [pltpu.make_async_copy(held.at[i % depth], out_ref.at[mine, at], sems.at[i]) for i, at in enumerate(blocks)]
         for i, at in enumerate(blocks):
-            change = lax.dot_general(w, p_ref[:, at], (((1,), (0,)), ((), ())), preferred_element_type=jnp.float32)
+            change = jnp.dot(w, p_ref[:, at], preferred_element_type=jnp.float32)
             if i >= depth:
                 copies[i - depth].wait()
-            held[i % depth] = x_ref[:, :, at] - change.reshape(lead, rows, at.size)
+            held[i % depth] = x_ref[mine, at] - change
             copies[i].start(priority=i % QUEUES)
         for copy in copies[-depth:]:
             copy.wait()
 
+    operands = [here, sums, x, changes]
+    in_specs = [SMEM] + [VMEM] * 3
+    aliases = {}
+    if out is not None:
+        aliases = {len(operands): 0}
+        operands.append(out)
+        in_specs.append(ANY)
     return pl.pallas_call(
         kernel,
         out_shape=jax.ShapeDtypeStruct(x.shape, jnp.float32),
-        in_specs=[SMEM] + [VMEM] * 4,
+        in_specs=in_specs,
         out_specs=ANY,
         scratch_shapes=[
-            pltpu.VMEM((lead * rows, height), jnp.float32),
-            pltpu.VMEM((depth, lead, rows, blocks[0].size), jnp.float32),
+            pltpu.VMEM((depth, half, blocks[0].size), jnp.float32),
             pltpu.SemaphoreType.DMA((len(blocks),)),
         ],
+        input_output_aliases=aliases,
         compiler_params=params(),
-        cost_estimate=cost(6 * lead * rows * ncols * height, 8 * lead * rows * ncols),
+        cost_estimate=cost(3 * rows * ncols * changes.shape[0], 4 * rows * ncols),
         name="update",
-    )(here, mine, theirs, x, changes)
+    )(*operands)
 
 
 def swap(array, k, size):
@@ -394,13 +429,17 @@
     odds = list(zip(*[stream[1] for stream in streams]))
     high, low, both_t, gram = assemble(here, block_place, offsets, householder, evens, odds, n_row)
     cross = spread(gram + swap(gram, 1, n_wide), n_wide)
-    cross[0] = after(cross[0], x)
+    x = x.reshape(n_wide * rows, ncols)
+    both_t = lift(after(both_t, x))
+    cross[0] = after(cross[0], both_t)
     cross = functools.reduce(jnp.add, cross)
     changes = merge([cross], wy_factor, (high, low))
 
     mine, theirs, x = inner_products(after(here, cross), x, both_t)
     mine = chips_sum(mine + swap(theirs, 1, n_wide), n_wide, changes)
-    return update(here, x, mine, swap(mine, 1, n_wide), changes).reshape(n_wide * rows, ncols)
+    theirs = swap(mine, 1, n_wide)
+    out = update(here, x, mine, changes, None, False)
+    return update(here, x, theirs, changes, out, True)
 
 
 def solution(mesh):

time: 140 us -> 138 us (0.986)
  waiting for transfers between devices: 45.7 us -> 42.3 us
  Pallas kernels: 38.7 us -> 42.1 us
  local copies, waits for them, and re-layouts: 1.93 us -> 0.04 us
    ppermute x10, waiting for transfers between devices: 9.43 us -> 5.99 us  [swap(): return lax.ppermute(array, 'wide', [(i, i ^ k) for i in range(size)])]
    pallas_call x0 -> x1, Pallas kernels: none -> 2.03 us  [lift(): pl.pallas_call(kernel, out_shape=pltpu.VMEM(x.shape, x.dtype), in_specs=[...]
    unnamed x14 -> x12, local copies, waits for them, and re-layouts: 1.91 us -> 0.03 us
    pallas_call x1 -> x2, Pallas kernels: 6.21 us -> 7.8 us  [update(): pl.pallas_call(kernel, out_shape=jax.ShapeDtypeStruct(x.shape, jnp.float3...]
  transfers between devices with their start and end apart: 35 -> 35, of which waited for: 20 -> 17; matrix products, arithmetic and copies ran while one was open for 0% -> 0% of each run, Pallas kernels for 13% -> 17%
where the time goes in v9:
time: 138 us
  starting transfers between devices  52.7 us (38%)
  waiting for transfers between devices  42.3 us (31%)
  Pallas kernels  42.1 us (31%)
    ppermute x24, starting transfers between devices, exchange(): return lax.ppermute(array, ('row', 'wide'), pairs)  39.6 us
    ppermute x24, waiting for transfers between devices, exchange(): return lax.ppermute(array, ('row', 'wide'), pairs)  24.4 us
    all_to_all x1, waiting for transfers between devices, body(): x = lax.all_to_all(piece, 'wide', split_axis=0, concat_axis=0, tiled=True)  11.9 us
    pallas_call x1, Pallas kernels, inner_products(): pl.pallas_call(kernel, out_shape=[jax.ShapeDtypeStruct((half // 2, 2 * he...  8.32 us
    pallas_call x12, Pallas kernels, feed(): pl.pallas_call(kernel, out_shape=[jax.ShapeDtypeStruct((width, cols), jnp...  8.06 us
    pallas_call x2, Pallas kernels, update(): pl.pallas_call(kernel, out_shape=jax.ShapeDtypeStruct(x.shape, jnp.float3...  7.8 us
    ppermute x10, starting transfers between devices, swap(): return lax.ppermute(array, 'wide', [(i, i ^ k) for i in range(size)])  7.78 us
    pallas_call x1, Pallas kernels, assemble(): pl.pallas_call(kernel, out_shape=[pltpu.HBM((height, ncols), jnp.bfloat16...  6.34 us
  transfers between devices with their start and end apart: 35, of which 17 were waited for; matrix products, arithmetic and copies ran while one was open for 0% of the time, Pallas kernels for 17%

profile of v9, /device:TPU:0, one launch (start us, length us, event | category | flops | bytes accessed | tf_op | source)
XLA Modules:
  0.0 137.7 jit_solution(3692089235751963513)
XLA Ops:
  0.0 6.0 %pack.1 = f32[8,64,4096]{2,1,0:T(8,128)} custom-call(f32[64,32768]{1,0:T(8,128)} %x_ref.1), custom_call_target="tpu_custom_call" | custom-call | bytes 16777216 | tf_op jit(solution)/shard_map/pack/pallas_call | solution.py:82
  6.1 5.3 %all-to-all-start = ((f32[8,64,4096]{2,1,0:T(8,128)}), f32[8,64,4096]{2,1,0:T(8,128)}, u32[]{:S(2)}, u32[]{:S(2)}) async-start(f32[8,64,4096]{2,1,0:T(8,128)} %pack.1), calls=%async_computation | async-start | bytes 16777216 | tf_op jit(solution)/shard_map/all_to_all | solution.py:417
  12.1 2.9 %collective-permute-start = (f32[32,2048]{1,0:T(8,128)S(1)}, f32[32,2048]{1,0:T(8,128)S(1)}, u32[]{:S(2)}, u32[]{:S(2)}) collective-permute-start(f32[32,2048]{1,0:T(8,128)S(1)} %get-tuple-element.54), channel_id=1, source_target_pairs={{0,8},{1,9},{2,10},{3,11},{4,12},{5,13},{6,14},{7,15},{8,0},{9,1},... | collective-permute-start | bytes 786440 | tf_op jit(solution)/shard_map/ppermute | solution.py:412
  15.8 3.1 %collective-permute-start.1 = (f32[32,2048]{1,0:T(8,128)S(1)}, f32[32,2048]{1,0:T(8,128)S(1)}, u32[]{:S(2)}, u32[]{:S(2)}) collective-permute-start(f32[32,2048]{1,0:T(8,128)S(1)} %get-tuple-element.57), channel_id=1, source_target_pairs={{0,8},{1,9},{2,10},{3,11},{4,12},{5,13},{6,14},{7,15},{8,0},{9,1},... | collective-permute-start | bytes 786440 | tf_op jit(solution)/shard_map/ppermute | solution.py:412
  18.9 3.3 %collective-permute-done.refs_0_ = f32[32,2048]{1,0:T(8,128)S(1)} collective-permute-done((f32[32,2048]{1,0:T(8,128)S(1)}, f32[32,2048]{1,0:T(8,128)S(1)}, u32[]{:S(2)}, u32[]{:S(2)}) %collective-permute-start) | collective-permute-done | bytes 262176 | tf_op jit(solution)/shard_map/ppermute | solution.py:412
  22.9 3.2 %collective-permute-start.3 = (f32[32,2048]{1,0:T(8,128)S(1)}, f32[32,2048]{1,0:T(8,128)S(1)}, u32[]{:S(2)}, u32[]{:S(2)}) collective-permute-start(f32[32,2048]{1,0:T(8,128)S(1)} %get-tuple-element.60), channel_id=1, source_target_pairs={{0,8},{1,9},{2,10},{3,11},{4,12},{5,13},{6,14},{7,15},{8,0},{9,1},... | collective-permute-start | bytes 786440 | tf_op jit(solution)/shard_map/ppermute | solution.py:412
  26.0 1.8 %collective-permute-done.1.refs_0_.refs_1_ = f32[32,2048]{1,0:T(8,128)S(1)} collective-permute-done((f32[32,2048]{1,0:T(8,128)S(1)}, f32[32,2048]{1,0:T(8,128)S(1)}, u32[]{:S(2)}, u32[]{:S(2)}) %collective-permute-start.1) | collective-permute-done | bytes 262176 | tf_op jit(solution)/shard_map/ppermute | solution.py:412
  28.5 3.2 %collective-permute-start.5 = (f32[32,2048]{1,0:T(8,128)S(1)}, f32[32,2048]{1,0:T(8,128)S(1)}, u32[]{:S(2)}, u32[]{:S(2)}) collective-permute-start(f32[32,2048]{1,0:T(8,128)S(1)} %get-tuple-element.63), channel_id=1, source_target_pairs={{0,8},{1,9},{2,10},{3,11},{4,12},{5,13},{6,14},{7,15},{8,0},{9,1},... | collective-permute-start | bytes 786440 | tf_op jit(solution)/shard_map/ppermute | solution.py:412
  31.6 1.8 %collective-permute-done.3.refs_1_.refs_2_ = f32[32,2048]{1,0:T(8,128)S(1)} collective-permute-done((f32[32,2048]{1,0:T(8,128)S(1)}, f32[32,2048]{1,0:T(8,128)S(1)}, u32[]{:S(2)}, u32[]{:S(2)}) %collective-permute-start.3) | collective-permute-done | bytes 262176 | tf_op jit(solution)/shard_map/ppermute | solution.py:412
  34.1 3.2 %collective-permute-start.7 = (f32[32,2048]{1,0:T(8,128)S(1)}, f32[32,2048]{1,0:T(8,128)S(1)}, u32[]{:S(2)}, u32[]{:S(2)}) collective-permute-start(f32[32,2048]{1,0:T(8,128)S(1)} %get-tuple-element.66), channel_id=1, source_target_pairs={{0,8},{1,9},{2,10},{3,11},{4,12},{5,13},{6,14},{7,15},{8,0},{9,1},... | collective-permute-start | bytes 786440 | tf_op jit(solution)/shard_map/ppermute | solution.py:412
  37.3 1.8 %collective-permute-done.5.refs_1_.refs_3_ = f32[32,2048]{1,0:T(8,128)S(1)} collective-permute-done((f32[32,2048]{1,0:T(8,128)S(1)}, f32[32,2048]{1,0:T(8,128)S(1)}, u32[]{:S(2)}, u32[]{:S(2)}) %collective-permute-start.5) | collective-permute-done | bytes 262176 | tf_op jit(solution)/shard_map/ppermute | solution.py:412
  39.7 3.2 %collective-permute-start.9 = (f32[32,2048]{1,0:T(8,128)S(1)}, f32[32,2048]{1,0:T(8,128)S(1)}, u32[]{:S(2)}, u32[]{:S(2)}) collective-permute-start(f32[32,2048]{1,0:T(8,128)S(1)} %get-tuple-element.69), channel_id=1, source_target_pairs={{0,8},{1,9},{2,10},{3,11},{4,12},{5,13},{6,14},{7,15},{8,0},{9,1},... | collective-permute-start | bytes 786440 | tf_op jit(solution)/shard_map/ppermute | solution.py:412
  42.9 1.8 %collective-permute-done.7.refs_2_.refs_4_ = f32[32,2048]{1,0:T(8,128)S(1)} collective-permute-done((f32[32,2048]{1,0:T(8,128)S(1)}, f32[32,2048]{1,0:T(8,128)S(1)}, u32[]{:S(2)}, u32[]{:S(2)}) %collective-permute-start.7) | collective-permute-done | bytes 262176 | tf_op jit(solution)/shard_map/ppermute | solution.py:412
  45.3 3.2 %collective-permute-start.11 = (f32[32,2048]{1,0:T(8,128)S(1)}, f32[32,2048]{1,0:T(8,128)S(1)}, u32[]{:S(2)}, u32[]{:S(2)}) collective-permute-start(f32[32,2048]{1,0:T(8,128)S(1)} %get-tuple-element.72), channel_id=1, source_target_pairs={{0,8},{1,9},{2,10},{3,11},{4,12},{5,13},{6,14},{7,15},{8,0},{9,1},... | collective-permute-start | bytes 786440 | tf_op jit(solution)/shard_map/ppermute | solution.py:412
  48.5 1.8 %collective-permute-done.9.refs_2_.refs_5_ = f32[32,2048]{1,0:T(8,128)S(1)} collective-permute-done((f32[32,2048]{1,0:T(8,128)S(1)}, f32[32,2048]{1,0:T(8,128)S(1)}, u32[]{:S(2)}, u32[]{:S(2)}) %collective-permute-start.9) | collective-permute-done | bytes 262176 | tf_op jit(solution)/shard_map/ppermute | solution.py:412
  51.0 3.2 %collective-permute-start.13 = (f32[32,2048]{1,0:T(8,128)S(1)}, f32[32,2048]{1,0:T(8,128)S(1)}, u32[]{:S(2)}, u32[]{:S(2)}) collective-permute-start(f32[32,2048]{1,0:T(8,128)S(1)} %get-tuple-element.75), channel_id=1, source_target_pairs={{0,8},{1,9},{2,10},{3,11},{4,12},{5,13},{6,14},{7,15},{8,0},{9,1},... | collective-permute-start | bytes 786440 | tf_op jit(solution)/shard_map/ppermute | solution.py:412
  54.1 1.8 %collective-permute-done.11.refs_3_.refs_6_ = f32[32,2048]{1,0:T(8,128)S(1)} collective-permute-done((f32[32,2048]{1,0:T(8,128)S(1)}, f32[32,2048]{1,0:T(8,128)S(1)}, u32[]{:S(2)}, u32[]{:S(2)}) %collective-permute-start.11) | collective-permute-done | bytes 262176 | tf_op jit(solution)/shard_map/ppermute | solution.py:412
  56.6 3.2 %collective-permute-start.15 = (f32[32,2048]{1,0:T(8,128)S(1)}, f32[32,2048]{1,0:T(8,128)S(1)}, u32[]{:S(2)}, u32[]{:S(2)}) collective-permute-start(f32[32,2048]{1,0:T(8,128)S(1)} %get-tuple-element.78), channel_id=1, source_target_pairs={{0,8},{1,9},{2,10},{3,11},{4,12},{5,13},{6,14},{7,15},{8,0},{9,1},... | collective-permute-start | bytes 786440 | tf_op jit(solution)/shard_map/ppermute | solution.py:412
  62.2 3.2 %collective-permute-start.17 = (f32[32,2048]{1,0:T(8,128)S(1)}, f32[32,2048]{1,0:T(8,128)S(1)}, u32[]{:S(2)}, u32[]{:S(2)}) collective-permute-start(f32[32,2048]{1,0:T(8,128)S(1)} %get-tuple-element.81), channel_id=1, source_target_pairs={{0,8},{1,9},{2,10},{3,11},{4,12},{5,13},{6,14},{7,15},{8,0},{9,1},... | collective-permute-start | bytes 786440 | tf_op jit(solution)/shard_map/ppermute | solution.py:412
  67.9 5.1 %collective-permute-start.19 = (f32[32,2048]{1,0:T(8,128)S(1)}, f32[32,2048]{1,0:T(8,128)S(1)}, u32[]{:S(2)}, u32[]{:S(2)}) collective-permute-start(f32[32,2048]{1,0:T(8,128)S(1)} %get-tuple-element.84), channel_id=1, source_target_pairs={{0,8},{1,9},{2,10},{3,11},{4,12},{5,13},{6,14},{7,15},{8,0},{9,1},... | collective-permute-start | bytes 786440 | tf_op jit(solution)/shard_map/ppermute | solution.py:412
  73.8 2.8 %collective-permute-start.21 = (f32[32,2048]{1,0:T(8,128)S(1)}, f32[32,2048]{1,0:T(8,128)S(1)}, u32[]{:S(2)}, u32[]{:S(2)}) collective-permute-start(f32[32,2048]{1,0:T(8,128)S(1)} %get-tuple-element.87), channel_id=1, source_target_pairs={{0,8},{1,9},{2,10},{3,11},{4,12},{5,13},{6,14},{7,15},{8,0},{9,1},... | collective-permute-start | bytes 786440 | tf_op jit(solution)/shard_map/ppermute | solution.py:412
  76.6 2.8 %collective-permute-done.19.refs_10_ = f32[32,2048]{1,0:T(8,128)S(1)} collective-permute-done((f32[32,2048]{1,0:T(8,128)S(1)}, f32[32,2048]{1,0:T(8,128)S(1)}, u32[]{:S(2)}, u32[]{:S(2)}) %collective-permute-start.19) | collective-permute-done | bytes 262176 | tf_op jit(solution)/shard_map/ppermute | solution.py:412
  79.4 4.2 %collective-permute-done.21.refs_11_ = f32[32,2048]{1,0:T(8,128)S(1)} collective-permute-done((f32[32,2048]{1,0:T(8,128)S(1)}, f32[32,2048]{1,0:T(8,128)S(1)}, u32[]{:S(2)}, u32[]{:S(2)}) %collective-permute-start.21) | collective-permute-done | bytes 262176 | tf_op jit(solution)/shard_map/ppermute | solution.py:412
  83.7 6.3 %assemble.1 = (bf16[192,4096]{1,0:T(8,128)(2,1)}, bf16[192,4096]{1,0:T(8,128)(2,1)}, bf16[4096,384]{1,0:T(8,128)(2,1)}, f32[32,512]{1,0:T(8,128)S(1)}) custom-call(s32[2]{0:T(128)S(1)} %pad_add_fusion.here_ref, s32[6]{0:T(128)S(1)} %copy-done.4, s32[6]{0:T(128)S(1)} %copy-done.5, f32[4,32,4096]{2,1,0:T(8,128)S(1)} %copy-done, ...), custom_call_target="tpu_custom_call" | custom-call | flops 1811939328 | bytes 6291456 | tf_op jit(solution)/shard_map/assemble/pallas_call | solution.py:199
  91.3 2.7 %collective-permute-start.27 = (f32[32,512]{1,0:T(8,128)S(1)}, f32[32,512]{1,0:T(8,128)S(1)}, u32[]{:S(2)}, u32[]{:S(2)}) collective-permute-start(f32[32,512]{1,0:T(8,128)S(1)} %add.27), channel_id=1, source_target_pairs={{0,6},{1,7},{2,4},{3,5},{4,2},{5,3},{6,0},{7,1},{8,14},{9,15},{10,... | collective-permute-start | bytes 196616 | tf_op jit(solution)/shard_map/ppermute | solution.py:375
  94.9 11.9 %all-to-all-done = f32[8,64,4096]{2,1,0:T(8,128)} async-done(((f32[8,64,4096]{2,1,0:T(8,128)}), f32[8,64,4096]{2,1,0:T(8,128)}, u32[]{:S(2)}, u32[]{:S(2)}) %all-to-all-start) | async-done | bytes 8388640 | tf_op jit(solution)/shard_map/all_to_all | solution.py:417
  106.8 2.0 %lift.1.vecs_ref = bf16[4096,384]{1,0:T(8,128)(2,1)S(1)} custom-call(bf16[4096,384]{1,0:T(8,128)(2,1)} %get-tuple-element.91.x_ref), custom_call_target="tpu_custom_call" | custom-call | bytes 3145728 | tf_op jit(solution)/shard_map/lift/pallas_call | solution.py:277
  108.9 8.3 %inner_products.1 = (f32[128,384]{1,0:T(8,128)S(1)}, f32[128,384]{1,0:T(8,128)S(1)}, f32[512,4096]{1,0:T(8,128)S(1)}) custom-call(s32[2]{0:T(128)S(1)} %pad_add_fusion.here_ref, f32[512,4096]{1,0:T(8,128)} %bitcast.2.x_ref, bf16[4096,384]{1,0:T(8,128)(2,1)S(1)} %lift.1.vecs_ref), custom_call_target="tpu_custom_call" | custom-call | flops 2415919104 | bytes 8388608 | tf_op jit(solution)/shard_map/inner_products/pallas_call | solution.py:317
  119.9 3.5 %merge.1.p_ref = bf16[576,4096]{1,0:T(8,128)(2,1)S(1)} custom-call(f32[32,512]{1,0:T(8,128)S(1)} %add_add_fusion.refs_0_, f32[6,32,32]{2,1,0:T(8,128)S(1)} %copy-done.3, bf16[192,4096]{1,0:T(8,128)(2,1)S(1)} %copy-done.1, bf16[192,4096]{1,0:T(8,128)(2,1)S(1)} %copy-done.2), custom_call_target="tpu_custom_call" | custom-call | flops 905969664 | bytes 6291456 | tf_op jit(solution)/shard_map/merge/pallas_call | solution.py:236
  126.6 1.8 %collective-permute-done.32 = f32[64,384]{1,0:T(8,128)S(1)} collective-permute-done((f32[64,384]{1,0:T(8,128)S(1)}, f32[64,384]{1,0:T(8,128)S(1)}, u32[]{:S(2)}, u32[]{:S(2)}) %collective-permute-start.32) | collective-permute-done | bytes 98336 | tf_op jit(solution)/shard_map/ppermute | solution.py:375
  129.8 3.9 %update.2.refs_0_ = f32[512,4096]{1,0:T(8,128)} custom-call(s32[2]{0:T(128)S(1)} %pad_add_fusion.here_ref, f32[128,384]{1,0:T(8,128)S(1)} %pad_maximum_fusion.sum_ref, f32[512,4096]{1,0:T(8,128)S(1)} %get-tuple-element.100.x_ref, bf16[576,4096]{1,0:T(8,128)(2,1)S(1)} %merge.1.p_ref), custom_call_target="tpu_custom_call" | custom-call | flops 3623878656 | bytes 8388608 | tf_op jit(solution)/shard_map/update/pallas_call | solution.py:358
  133.7 3.9 %update.3 = f32[512,4096]{1,0:T(8,128)} custom-call(s32[2]{0:T(128)S(1)} %pad_add_fusion.here_ref, f32[128,384]{1,0:T(8,128)S(1)} %collective-permute-done.33.sum_ref, f32[512,4096]{1,0:T(8,128)S(1)} %get-tuple-element.100.x_ref, bf16[576,4096]{1,0:T(8,128)(2,1)S(1)} %merge.1.p_ref, f32[512,4096]{1,0:T(8,128)} %update.2.refs_0_), custom_call_target="tpu_custom_call", output_to_operand_aliasing={{}: (4, {})} | custom-call | flops 3623878656 | bytes 8388608 | tf_op jit(solution)/shard_map/update/pallas_call | solution.py:358
  (79 shorter events, 21.3 us)
Async XLA Ops:
  6.1 100.7 %all-to-all-start = ((f32[8,64,4096]{2,1,0:T(8,128)}), f32[8,64,4096]{2,1,0:T(8,128)}, u32[]{:S(2)}, u32[]{:S(2)}) async-start(f32[8,64,4096]{2,1,0:T(8,128)} %pack.1), calls=%async_computation | async-start | bytes 16777216 | tf_op jit(solution)/shard_map/all_to_all | solution.py:417
  12.1 10.1 %collective-permute-start = (f32[32,2048]{1,0:T(8,128)S(1)}, f32[32,2048]{1,0:T(8,128)S(1)}, u32[]{:S(2)}, u32[]{:S(2)}) collective-permute-start(f32[32,2048]{1,0:T(8,128)S(1)} %get-tuple-element.54), channel_id=1, source_target_pairs={{0,8},{1,9},{2,10},{3,11},{4,12},{5,13},{6,14},{7,15},{8,0},{9,1},... | collective-permute-start | bytes 786440 | tf_op jit(solution)/shard_map/ppermute | solution.py:412
  15.0 7.1 %collective-permute-start.2 = (f32[32,2048]{1,0:T(8,128)S(1)}, f32[32,2048]{1,0:T(8,128)S(1)}, u32[]{:S(2)}, u32[]{:S(2)}) collective-permute-start(f32[32,2048]{1,0:T(8,128)S(1)} %get-tuple-element.55), channel_id=1, source_target_pairs={{0,1},{1,0},{2,3},{3,2},{4,5},{5,4},{6,7},{7,6},{8,16},{9,17},{10,... | collective-permute-start | bytes 786440 | tf_op jit(solution)/shard_map/ppermute | solution.py:412
  15.8 12.0 %collective-permute-start.1 = (f32[32,2048]{1,0:T(8,128)S(1)}, f32[32,2048]{1,0:T(8,128)S(1)}, u32[]{:S(2)}, u32[]{:S(2)}) collective-permute-start(f32[32,2048]{1,0:T(8,128)S(1)} %get-tuple-element.57), channel_id=1, source_target_pairs={{0,8},{1,9},{2,10},{3,11},{4,12},{5,13},{6,14},{7,15},{8,0},{9,1},... | collective-permute-start | bytes 786440 | tf_op jit(solution)/shard_map/ppermute | solution.py:412
  18.9 8.9 %collective-permute-start.4 = (f32[32,2048]{1,0:T(8,128)S(1)}, f32[32,2048]{1,0:T(8,128)S(1)}, u32[]{:S(2)}, u32[]{:S(2)}) collective-permute-start(f32[32,2048]{1,0:T(8,128)S(1)} %get-tuple-element.58), channel_id=1, source_target_pairs={{0,1},{1,0},{2,3},{3,2},{4,5},{5,4},{6,7},{7,6},{8,16},{9,17},{10,... | collective-permute-start | bytes 786440 | tf_op jit(solution)/shard_map/ppermute | solution.py:412
  22.9 10.6 %collective-permute-start.3 = (f32[32,2048]{1,0:T(8,128)S(1)}, f32[32,2048]{1,0:T(8,128)S(1)}, u32[]{:S(2)}, u32[]{:S(2)}) collective-permute-start(f32[32,2048]{1,0:T(8,128)S(1)} %get-tuple-element.60), channel_id=1, source_target_pairs={{0,8},{1,9},{2,10},{3,11},{4,12},{5,13},{6,14},{7,15},{8,0},{9,1},... | collective-permute-start | bytes 786440 | tf_op jit(solution)/shard_map/ppermute | solution.py:412
  26.0 7.4 %collective-permute-start.6 = (f32[32,2048]{1,0:T(8,128)S(1)}, f32[32,2048]{1,0:T(8,128)S(1)}, u32[]{:S(2)}, u32[]{:S(2)}) collective-permute-start(f32[32,2048]{1,0:T(8,128)S(1)} %get-tuple-element.61), channel_id=1, source_target_pairs={{0,1},{1,0},{2,3},{3,2},{4,5},{5,4},{6,7},{7,6},{8,16},{9,17},{10,... | collective-permute-start | bytes 786440 | tf_op jit(solution)/shard_map/ppermute | solution.py:412
  28.5 10.6 %collective-permute-start.5 = (f32[32,2048]{1,0:T(8,128)S(1)}, f32[32,2048]{1,0:T(8,128)S(1)}, u32[]{:S(2)}, u32[]{:S(2)}) collective-permute-start(f32[32,2048]{1,0:T(8,128)S(1)} %get-tuple-element.63), channel_id=1, source_target_pairs={{0,8},{1,9},{2,10},{3,11},{4,12},{5,13},{6,14},{7,15},{8,0},{9,1},... | collective-permute-start | bytes 786440 | tf_op jit(solution)/shard_map/ppermute | solution.py:412
  31.6 7.4 %collective-permute-start.8 = (f32[32,2048]{1,0:T(8,128)S(1)}, f32[32,2048]{1,0:T(8,128)S(1)}, u32[]{:S(2)}, u32[]{:S(2)}) collective-permute-start(f32[32,2048]{1,0:T(8,128)S(1)} %get-tuple-element.64), channel_id=1, source_target_pairs={{0,1},{1,0},{2,3},{3,2},{4,5},{5,4},{6,7},{7,6},{8,16},{9,17},{10,... | collective-permute-start | bytes 786440 | tf_op jit(solution)/shard_map/ppermute | solution.py:412
  34.1 10.6 %collective-permute-start.7 = (f32[32,2048]{1,0:T(8,128)S(1)}, f32[32,2048]{1,0:T(8,128)S(1)}, u32[]{:S(2)}, u32[]{:S(2)}) collective-permute-start(f32[32,2048]{1,0:T(8,128)S(1)} %get-tuple-element.66), channel_id=1, source_target_pairs={{0,8},{1,9},{2,10},{3,11},{4,12},{5,13},{6,14},{7,15},{8,0},{9,1},... | collective-permute-start | bytes 786440 | tf_op jit(solution)/shard_map/ppermute | solution.py:412
  37.3 7.4 %collective-permute-start.10 = (f32[32,2048]{1,0:T(8,128)S(1)}, f32[32,2048]{1,0:T(8,128)S(1)}, u32[]{:S(2)}, u32[]{:S(2)}) collective-permute-start(f32[32,2048]{1,0:T(8,128)S(1)} %get-tuple-element.67), channel_id=1, source_target_pairs={{0,1},{1,0},{2,3},{3,2},{4,5},{5,4},{6,7},{7,6},{8,16},{9,17},{10,... | collective-permute-start | bytes 786440 | tf_op jit(solution)/shard_map/ppermute | solution.py:412
  39.7 10.6 %collective-permute-start.9 = (f32[32,2048]{1,0:T(8,128)S(1)}, f32[32,2048]{1,0:T(8,128)S(1)}, u32[]{:S(2)}, u32[]{:S(2)}) collective-permute-start(f32[32,2048]{1,0:T(8,128)S(1)} %get-tuple-element.69), channel_id=1, source_target_pairs={{0,8},{1,9},{2,10},{3,11},{4,12},{5,13},{6,14},{7,15},{8,0},{9,1},... | collective-permute-start | bytes 786440 | tf_op jit(solution)/shard_map/ppermute | solution.py:412
  42.9 7.4 %collective-permute-start.12 = (f32[32,2048]{1,0:T(8,128)S(1)}, f32[32,2048]{1,0:T(8,128)S(1)}, u32[]{:S(2)}, u32[]{:S(2)}) collective-permute-start(f32[32,2048]{1,0:T(8,128)S(1)} %get-tuple-element.70), channel_id=1, source_target_pairs={{0,1},{1,0},{2,3},{3,2},{4,5},{5,4},{6,7},{7,6},{8,16},{9,17},{10,... | collective-permute-start | bytes 786440 | tf_op jit(solution)/shard_map/ppermute | solution.py:412
  45.3 10.5 %collective-permute-start.11 = (f32[32,2048]{1,0:T(8,128)S(1)}, f32[32,2048]{1,0:T(8,128)S(1)}, u32[]{:S(2)}, u32[]{:S(2)}) collective-permute-start(f32[32,2048]{1,0:T(8,128)S(1)} %get-tuple-element.72), channel_id=1, source_target_pairs={{0,8},{1,9},{2,10},{3,11},{4,12},{5,13},{6,14},{7,15},{8,0},{9,1},... | collective-permute-start | bytes 786440 | tf_op jit(solution)/shard_map/ppermute | solution.py:412
  48.5 7.4 %collective-permute-start.14 = (f32[32,2048]{1,0:T(8,128)S(1)}, f32[32,2048]{1,0:T(8,128)S(1)}, u32[]{:S(2)}, u32[]{:S(2)}) collective-permute-start(f32[32,2048]{1,0:T(8,128)S(1)} %get-tuple-element.73), channel_id=1, source_target_pairs={{0,1},{1,0},{2,3},{3,2},{4,5},{5,4},{6,7},{7,6},{8,16},{9,17},{10,... | collective-permute-start | bytes 786440 | tf_op jit(solution)/shard_map/ppermute | solution.py:412
  51.0 10.5 %collective-permute-start.13 = (f32[32,2048]{1,0:T(8,128)S(1)}, f32[32,2048]{1,0:T(8,128)S(1)}, u32[]{:S(2)}, u32[]{:S(2)}) collective-permute-start(f32[32,2048]{1,0:T(8,128)S(1)} %get-tuple-element.75), channel_id=1, source_target_pairs={{0,8},{1,9},{2,10},{3,11},{4,12},{5,13},{6,14},{7,15},{8,0},{9,1},... | collective-permute-start | bytes 786440 | tf_op jit(solution)/shard_map/ppermute | solution.py:412
  54.1 7.4 %collective-permute-start.16 = (f32[32,2048]{1,0:T(8,128)S(1)}, f32[32,2048]{1,0:T(8,128)S(1)}, u32[]{:S(2)}, u32[]{:S(2)}) collective-permute-start(f32[32,2048]{1,0:T(8,128)S(1)} %get-tuple-element.76), channel_id=1, source_target_pairs={{0,1},{1,0},{2,3},{3,2},{4,5},{5,4},{6,7},{7,6},{8,16},{9,17},{10,... | collective-permute-start | bytes 786440 | tf_op jit(solution)/shard_map/ppermute | solution.py:412
  56.6 10.5 %collective-permute-start.15 = (f32[32,2048]{1,0:T(8,128)S(1)}, f32[32,2048]{1,0:T(8,128)S(1)}, u32[]{:S(2)}, u32[]{:S(2)}) collective-permute-start(f32[32,2048]{1,0:T(8,128)S(1)} %get-tuple-element.78), channel_id=1, source_target_pairs={{0,8},{1,9},{2,10},{3,11},{4,12},{5,13},{6,14},{7,15},{8,0},{9,1},... | collective-permute-start | bytes 786440 | tf_op jit(solution)/shard_map/ppermute | solution.py:412
  59.8 7.4 %collective-permute-start.18 = (f32[32,2048]{1,0:T(8,128)S(1)}, f32[32,2048]{1,0:T(8,128)S(1)}, u32[]{:S(2)}, u32[]{:S(2)}) collective-permute-start(f32[32,2048]{1,0:T(8,128)S(1)} %get-tuple-element.79), channel_id=1, source_target_pairs={{0,1},{1,0},{2,3},{3,2},{4,5},{5,4},{6,7},{7,6},{8,16},{9,17},{10,... | collective-permute-start | bytes 786440 | tf_op jit(solution)/shard_map/ppermute | solution.py:412
  62.2 10.9 %collective-permute-start.17 = (f32[32,2048]{1,0:T(8,128)S(1)}, f32[32,2048]{1,0:T(8,128)S(1)}, u32[]{:S(2)}, u32[]{:S(2)}) collective-permute-start(f32[32,2048]{1,0:T(8,128)S(1)} %get-tuple-element.81), channel_id=1, source_target_pairs={{0,8},{1,9},{2,10},{3,11},{4,12},{5,13},{6,14},{7,15},{8,0},{9,1},... | collective-permute-start | bytes 786440 | tf_op jit(solution)/shard_map/ppermute | solution.py:412
  65.4 7.7 %collective-permute-start.20 = (f32[32,2048]{1,0:T(8,128)S(1)}, f32[32,2048]{1,0:T(8,128)S(1)}, u32[]{:S(2)}, u32[]{:S(2)}) collective-permute-start(f32[32,2048]{1,0:T(8,128)S(1)} %get-tuple-element.82), channel_id=1, source_target_pairs={{0,1},{1,0},{2,3},{3,2},{4,5},{5,4},{6,7},{7,6},{8,16},{9,17},{10,... | collective-permute-start | bytes 786440 | tf_op jit(solution)/shard_map/ppermute | solution.py:412
  67.8 11.6 %collective-permute-start.22 = (f32[32,2048]{1,0:T(8,128)S(1)}, f32[32,2048]{1,0:T(8,128)S(1)}, u32[]{:S(2)}, u32[]{:S(2)}) collective-permute-start(f32[32,2048]{1,0:T(8,128)S(1)} %get-tuple-element.85), channel_id=1, source_target_pairs={{0,1},{1,0},{2,3},{3,2},{4,5},{5,4},{6,7},{7,6},{8,16},{9,17},{10,... | collective-permute-start | bytes 786440 | tf_op jit(solution)/shard_map/ppermute | solution.py:412
  67.9 11.5 %collective-permute-start.19 = (f32[32,2048]{1,0:T(8,128)S(1)}, f32[32,2048]{1,0:T(8,128)S(1)}, u32[]{:S(2)}, u32[]{:S(2)}) collective-permute-start(f32[32,2048]{1,0:T(8,128)S(1)} %get-tuple-element.84), channel_id=1, source_target_pairs={{0,8},{1,9},{2,10},{3,11},{4,12},{5,13},{6,14},{7,15},{8,0},{9,1},... | collective-permute-start | bytes 786440 | tf_op jit(solution)/shard_map/ppermute | solution.py:412
  73.8 9.9 %collective-permute-start.21 = (f32[32,2048]{1,0:T(8,128)S(1)}, f32[32,2048]{1,0:T(8,128)S(1)}, u32[]{:S(2)}, u32[]{:S(2)}) collective-permute-start(f32[32,2048]{1,0:T(8,128)S(1)} %get-tuple-element.87), channel_id=1, source_target_pairs={{0,8},{1,9},{2,10},{3,11},{4,12},{5,13},{6,14},{7,15},{8,0},{9,1},... | collective-permute-start | bytes 786440 | tf_op jit(solution)/shard_map/ppermute | solution.py:412
  76.6 7.0 %collective-permute-start.23 = (f32[32,2048]{1,0:T(8,128)S(1)}, f32[32,2048]{1,0:T(8,128)S(1)}, u32[]{:S(2)}, u32[]{:S(2)}) collective-permute-start(f32[32,2048]{1,0:T(8,128)S(1)} %get-tuple-element.88), channel_id=1, source_target_pairs={{0,1},{1,0},{2,3},{3,2},{4,5},{5,4},{6,7},{7,6},{8,16},{9,17},{10,... | collective-permute-start | bytes 786440 | tf_op jit(solution)/shard_map/ppermute | solution.py:412
  91.3 17.5 %collective-permute-start.27 = (f32[32,512]{1,0:T(8,128)S(1)}, f32[32,512]{1,0:T(8,128)S(1)}, u32[]{:S(2)}, u32[]{:S(2)}) collective-permute-start(f32[32,512]{1,0:T(8,128)S(1)} %add.27), channel_id=1, source_target_pairs={{0,6},{1,7},{2,4},{3,5},{4,2},{5,3},{6,0},{7,1},{8,14},{9,15},{10,... | collective-permute-start | bytes 196616 | tf_op jit(solution)/shard_map/ppermute | solution.py:375
  94.0 14.8 %collective-permute-start.26 = (f32[32,512]{1,0:T(8,128)S(1)}, f32[32,512]{1,0:T(8,128)S(1)}, u32[]{:S(2)}, u32[]{:S(2)}) collective-permute-start(f32[32,512]{1,0:T(8,128)S(1)} %add.27), channel_id=1, source_target_pairs={{0,4},{1,5},{2,6},{3,7},{4,0},{5,1},{6,2},{7,3},{8,12},{9,13},{10,... | collective-permute-start | bytes 196616 | tf_op jit(solution)/shard_map/ppermute | solution.py:375
  94.5 14.3 %collective-permute-start.25 = (f32[32,512]{1,0:T(8,128)S(1)}, f32[32,512]{1,0:T(8,128)S(1)}, u32[]{:S(2)}, u32[]{:S(2)}) collective-permute-start(f32[32,512]{1,0:T(8,128)S(1)} %add.27), channel_id=1, source_target_pairs={{0,2},{1,3},{2,0},{3,1},{4,6},{5,7},{6,4},{7,5},{8,10},{9,11},{10,... | collective-permute-start | bytes 196616 | tf_op jit(solution)/shard_map/ppermute | solution.py:375
  118.8 4.9 %collective-permute-start.31 = (f32[64,384]{1,0:T(8,128)S(1)}, f32[64,384]{1,0:T(8,128)S(1)}, u32[]{:S(2)}, u32[]{:S(2)}) collective-permute-start(f32[64,384]{1,0:T(8,128)S(1)} %get-tuple-element.99), channel_id=1, source_target_pairs={{0,4},{1,5},{2,6},{3,7},{4,0},{5,1},{6,2},{7,3},{8,12},{9,13},{10,... | collective-permute-start | bytes 294920 | tf_op jit(solution)/shard_map/ppermute | solution.py:375
  119.3 5.6 %collective-permute-start.29 = (f32[64,384]{1,0:T(8,128)S(1)}, f32[64,384]{1,0:T(8,128)S(1)}, u32[]{:S(2)}, u32[]{:S(2)}) collective-permute-start(f32[64,384]{1,0:T(8,128)S(1)} %get-tuple-element.98), channel_id=1, source_target_pairs={{0,2},{1,3},{2,0},{3,1},{4,6},{5,7},{6,4},{7,5},{8,10},{9,11},{10,... | collective-permute-start | bytes 294920 | tf_op jit(solution)/shard_map/ppermute | solution.py:375
  123.7 4.7 %collective-permute-start.32 = (f32[64,384]{1,0:T(8,128)S(1)}, f32[64,384]{1,0:T(8,128)S(1)}, u32[]{:S(2)}, u32[]{:S(2)}) collective-permute-start(f32[64,384]{1,0:T(8,128)S(1)} %add.34), channel_id=1, source_target_pairs={{0,2},{1,3},{2,0},{3,1},{4,6},{5,7},{6,4},{7,5},{8,10},{9,11},{10,... | collective-permute-start | bytes 294920 | tf_op jit(solution)/shard_map/ppermute | solution.py:375
  125.0 4.7 %collective-permute-start.30 = (f32[64,384]{1,0:T(8,128)S(1)}, f32[64,384]{1,0:T(8,128)S(1)}, u32[]{:S(2)}, u32[]{:S(2)}) collective-permute-start(f32[64,384]{1,0:T(8,128)S(1)} %add.32), channel_id=1, source_target_pairs={{0,4},{1,5},{2,6},{3,7},{4,0},{5,1},{6,2},{7,3},{8,12},{9,13},{10,... | collective-permute-start | bytes 294920 | tf_op jit(solution)/shard_map/ppermute | solution.py:375
  (9 other events, 86.6 us)

commit v10 on v9

--- a/solution.py
+++ b/solution.py
@@ -13,6 +13,7 @@
 LARGE_LIMIT = 58 * 1024 * 1024
 COLUMNS = 512
 QUEUES = 2
+ARRIVED = (4, 0)
 SPLITS = 2
 
 
@@ -57,8 +58,8 @@
     return pltpu.with_memory_space_constraint(x, pltpu.HBM)
 
 
-def pack(x, n_wide):
-    rows, order = x.shape
+def pack(x, base, rows, n_wide):
+    order = x.shape[1]
     ncols = order // n_wide
     step = 16 if rows % 16 == 0 else rows
     n_copies = n_wide * rows // step
@@ -68,7 +69,7 @@
         for first in range(0, rows, step):
             for k in range(n_wide):
                 i, at = len(into), pl.ds(first, step)
-                source = x_ref.at[at, pl.ds(k * ncols, ncols)]
+                source = x_ref.at[pl.ds(base + first, step), pl.ds(k * ncols, ncols)]
                 into.append(pltpu.make_async_copy(source, held.at[k, at], in_sems.at[i]))
                 out_of.append(pltpu.make_async_copy(held.at[k, at], out_ref.at[k, at], out_sems.at[i]))
         for i, copy in enumerate(into):
@@ -104,12 +105,11 @@
     return roots, slot, ranks, counts
 
 
-def feed(here, place, stack, evens, odds, n_rows, part, cols):
+def feed(here, place, stack, turn, turns, last, store, n_rows, part, cols):
     slots, width, _ = stack.shape
-    turn = len(evens)
 
     def kernel(here_ref, place_ref, stack_ref, *refs):
-        arrived, (out_even, out_odd, sems) = refs[:-3], refs[-3:]
+        last_refs, (out_even, out_odd, *store_refs, sems) = refs[:len(last)], refs[len(last) + (store is not None):]
         roots, slot, ranks, _ = plan(place_ref, slots, n_rows)
         me = here_ref[0]
         mine = [r == me for r in roots]
@@ -123,38 +123,59 @@
                 pltpu.make_async_copy(stored, out, sems.at[side]).start()
 
             for i in range(turn):
+                source = last_refs[1 - side] if i == turn - 1 else store_refs[0].at[1 - side, i]
+
                 @pl.when((older == i) & (count <= turn))
                 def _():
-                    pltpu.make_async_copy(arrived[(1 - side) * turn + i], out, sems.at[side]).start()
+                    pltpu.make_async_copy(source, out, sems.at[side]).start()
+        keeps = [
+            pltpu.make_async_copy(ref, store_refs[0].at[side, turn - 1], sems.at[2 + side]) for side, ref in enumerate(last_refs)
+        ]
+        for keep in keeps:
+            keep.start()
         for side, out in ((0, out_even), (1, out_odd)):
             pltpu.make_async_copy(stored, out, sems.at[side]).wait()
-
-    return pl.pallas_call(
-        kernel,
-        out_shape=[jax.ShapeDtypeStruct((width, cols), jnp.float32)] * 2,
-        in_specs=[SMEM, SMEM, ANY] + [ANY] * (2 * turn),
-        out_specs=[VMEM] * 2,
-        scratch_shapes=[pltpu.SemaphoreType.DMA((2,))],
+        for keep in keeps:
+            keep.wait()
+
+    out_shape = [jax.ShapeDtypeStruct((width, cols), jnp.float32)] * 2
+    out_specs = [VMEM] * 2
+    operands = [here, place, stack, *last]
+    aliases = {}
+    if turn > 0:
+        out_shape.append(pltpu.HBM((2, turns, width, cols), jnp.float32))
+        out_specs.append(ANY)
+    if store is not None:
+        aliases = {len(operands): 2}
+        operands.append(store)
+    results = pl.pallas_call(
+        kernel,
+        out_shape=out_shape,
+        in_specs=[SMEM, SMEM] + [ANY] * (len(operands) - 2),
+        out_specs=out_specs,
+        scratch_shapes=[pltpu.SemaphoreType.DMA((4,))],
+        input_output_aliases=aliases,
         compiler_params=params(limit=SMALL_LIMIT),
         cost_estimate=cost(0, 16 * width * cols),
         name="feed",
-    )(here, place, stack, *evens, *odds)
+    )(*operands)
+    return results[0], results[1], (results[2] if turn > 0 else None)
 
 
 def packed_width(steps, width):
     return -(-(width * steps * (steps - 1) // 2) // 128) * 128
 
 
-def assemble(here, place, offsets, stack, evens, odds, n_rows):
+def assemble(here, place, offsets, stack, stores, lasts, n_rows):
     slots, width, ncols = stack.shape
     steps = place.shape[0]
     height = steps * width
-    turns, splits = len(evens), len(evens[0])
+    turns, splits = stores[0].shape[1], len(stores)
     cols = ncols // splits
 
     def kernel(here_ref, place_ref, offset_ref, stack_ref, *refs):
         arrived, (high_ref, low_ref, both_t_ref, gram_ref, held, sems) = refs[:-6], refs[-6:]
-        even, odd = arrived[:turns * splits], arrived[turns * splits:]
+        kept, latest = arrived[:splits], arrived[splits:]
         roots, slot, ranks, counts = plan(place_ref, slots, n_rows)
         me = here_ref[0]
         me_odd = lax.rem(me, 2) == 1
@@ -170,13 +191,14 @@
             def _():
                 pltpu.make_async_copy(stack_ref.at[slot[s]], target, sems.at[s]).start()
 
-            for side, came in (((below & me_odd) | (above & ~me_odd), even), ((below & ~me_odd) | (above & me_odd), odd)):
+            for side, came in ((0, (below & me_odd) | (above & ~me_odd)), (1, (below & ~me_odd) | (above & me_odd))):
                 for i in range(turns):
-                    @pl.when(side & (turn == i))
+                    @pl.when(came & (turn == i))
                     def _():
                         for p in range(splits):
                             piece = held.at[pl.ds(s * width, width), pl.ds(p * cols, cols)]
-                            pltpu.make_async_copy(came[i * splits + p], piece, sems.at[s]).start()
+                            source = latest[2 * p + side] if i == turns - 1 else kept[p].at[side, i]
+                            pltpu.make_async_copy(source, piece, sems.at[s]).start()
         columns = here_ref[1] * ncols + lax.broadcasted_iota(jnp.int32, (width, ncols), 1)
         for s in range(steps):
             rows = pl.ds(s * width, width)
@@ -204,13 +226,13 @@
             pltpu.HBM((ncols, 2 * height), jnp.bfloat16),
             jax.ShapeDtypeStruct((width, packed_width(steps, width)), jnp.float32),
         ],
-        in_specs=[SMEM, SMEM, SMEM, ANY] + [ANY] * (2 * turns * splits),
+        in_specs=[SMEM, SMEM, SMEM, ANY] + [ANY] * (3 * splits),
         out_specs=[VMEM] * 4,
         scratch_shapes=[pltpu.VMEM((height, ncols), jnp.float32), pltpu.SemaphoreType.DMA((steps,))],
         compiler_params=params(limit=SMALL_LIMIT),
         cost_estimate=cost(12 * height * height * ncols, 8 * height * ncols),
         name="assemble",
-    )(here, place, offsets, stack, *[p for turn in evens for p in turn], *[p for turn in odds for p in turn])
+    )(here, place, offsets, stack, *[in_hbm(store) for store in stores], *[array for last in lasts for array in last])
 
 
 def merge(cross, factors, vecs):
@@ -286,7 +308,7 @@
     )(in_hbm(x))
 
 
-def inner_products(here, x, vecs_t):
+def inner_products(here, x, vecs_t, hold):
     rows, ncols = x.shape
     height = vecs_t.shape[1] // 2
     half = rows // 2
@@ -316,59 +338,78 @@
 
     return pl.pallas_call(
         kernel,
-        out_shape=[jax.ShapeDtypeStruct((half // 2, 2 * height), jnp.float32)] * 2 + [pltpu.VMEM(x.shape, jnp.float32)],
+        out_shape=[jax.ShapeDtypeStruct((half // 2, 2 * height), jnp.float32)] * 2
+        + [pltpu.VMEM(x.shape, jnp.float32)] * hold,
         in_specs=[SMEM, ANY, VMEM],
-        out_specs=[VMEM] * 3,
-        scratch_shapes=[pltpu.VMEM((rows, height), jnp.float32), pltpu.SemaphoreType.DMA((n_copies,))],
+        out_specs=[VMEM] * (2 + hold),
+        scratch_shapes=[pltpu.VMEM(x.shape, jnp.float32)] * (1 - hold)
+        + [pltpu.VMEM((rows, height), jnp.float32), pltpu.SemaphoreType.DMA((n_copies,))],
         compiler_params=params(),
         cost_estimate=cost(6 * rows * ncols * height, 4 * rows * ncols),
         name="inner_products",
     )(here, in_hbm(x), vecs_t)
 
 
-def update(here, x, sums, changes, out, other):
-    rows, ncols = x.shape
-    half = rows // 2
+def update(here, early, late, mine, theirs, changes):
+    chunks = early + [late]
+    lead, rows, ncols = late.shape
+    height = changes.shape[0] // 3
+    size = lead * rows
+    half = size // 2
     blocks = column_blocks(ncols)
     depth = min(4, len(blocks))
 
-    def kernel(here_ref, sum_ref, x_ref, p_ref, *refs):
-        out_ref, held, sems = refs[-3:]
+    def kernel(here_ref, mine_ref, theirs_ref, p_ref, *refs):
+        x_refs, (out_ref, w_ref, fetched, held, in_sems, out_sems) = refs[:len(chunks)], refs[len(chunks):]
+        fetches = [
+            [pltpu.make_async_copy(x_refs[c].at[:, :, at], fetched.at[c, :, :, at], in_sems.at[c, i]) for c in range(len(early))]
+            for i, at in enumerate(blocks)
+        ]
+        for fetch in fetches:
+            for copy in fetch:
+                copy.start(priority=1)
         core = lax.rem(here_ref[1], 2)
-        mine = pl.ds(pl.multiple_of((1 - core if other else core) * half, 8), half)
-        high, low = halves(unfold(sum_ref[...]))
+        for c in range(len(chunks)):
+            folded = slice(c * half // 2, (c + 1) * half // 2)
+            w_ref[pl.ds(pl.multiple_of(c * size + core * half, 8), half), :] = unfold(mine_ref[folded, :])
+            w_ref[pl.ds(pl.multiple_of(c * size + (1 - core) * half, 8), half), :] = unfold(theirs_ref[folded, :])
+        high, low = halves(w_ref[...])
         w = jnp.concatenate([high, low, high], axis=1)
-        copies = [pltpu.make_async_copy(held.at[i % depth], out_ref.at[mine, at], sems.at[i]) for i, at in enumerate(blocks)]
+        stores = [
+            [
+                pltpu.make_async_copy(held.at[i % depth, c], out_ref.at[:, pl.ds(c * rows, rows), at], out_sems.at[c, i])
+                for c in range(len(chunks))
+            ]
+            for i, at in enumerate(blocks)
+        ]
         for i, at in enumerate(blocks):
             change = jnp.dot(w, p_ref[:, at], preferred_element_type=jnp.float32)
-            if i >= depth:
-                copies[i - depth].wait()
-            held[i % depth] = x_ref[mine, at] - change
-            copies[i].start(priority=i % QUEUES)
-        for copy in copies[-depth:]:
-            copy.wait()
-
-    operands = [here, sums, x, changes]
-    in_specs = [SMEM] + [VMEM] * 3
-    aliases = {}
-    if out is not None:
-        aliases = {len(operands): 0}
-        operands.append(out)
-        in_specs.append(ANY)
+            for copy in fetches[i] + (stores[i - depth] if i >= depth else []):
+                copy.wait()
+            for c in range(len(chunks)):
+                x = x_refs[c][:, :, at] if c == len(early) else fetched[c, :, :, at]
+                held[i % depth, c] = x - change[c * size:(c + 1) * size].reshape(lead, rows, at.size)
+                stores[i][c].start(priority=0)
+        for store in stores[-depth:]:
+            for copy in store:
+                copy.wait()
+
     return pl.pallas_call(
         kernel,
-        out_shape=jax.ShapeDtypeStruct(x.shape, jnp.float32),
-        in_specs=in_specs,
+        out_shape=jax.ShapeDtypeStruct((lead, len(chunks) * rows, ncols), jnp.float32),
+        in_specs=[SMEM] + [VMEM] * 3 + [ANY] * len(early) + [VMEM],
         out_specs=ANY,
         scratch_shapes=[
-            pltpu.VMEM((depth, half, blocks[0].size), jnp.float32),
-            pltpu.SemaphoreType.DMA((len(blocks),)),
+            pltpu.VMEM((len(chunks) * size, height), jnp.float32),
+            pltpu.VMEM((max(len(early), 1), lead, rows, ncols), jnp.float32),
+            pltpu.VMEM((depth, len(chunks), lead, rows, blocks[0].size), jnp.float32),
+            pltpu.SemaphoreType.DMA((max(len(early), 1), len(blocks))),
+            pltpu.SemaphoreType.DMA((len(chunks), len(blocks))),
         ],
-        input_output_aliases=aliases,
         compiler_params=params(),
-        cost_estimate=cost(3 * rows * ncols * changes.shape[0], 4 * rows * ncols),
+        cost_estimate=cost(6 * len(chunks) * size * ncols * height, 8 * len(chunks) * size * ncols),
         name="update",
-    )(*operands)
+    )(here, mine, theirs, changes, *[in_hbm(x) for x in early], late)
 
 
 def swap(array, k, size):
@@ -379,10 +420,8 @@
     return [pair] + [swap(pair, k, size) for k in range(2, size, 2)]
 
 
-def chips_sum(pair, size, token):
+def chips_sum(upper, lower, size, token):
     shifts = [k for k in (1 << i for i in range(1, size.bit_length())) if k < size]
-    half = pair.shape[0] // 2
-    upper, lower = pair[:half], pair[half:]
     for i, (first, second) in enumerate(zip(shifts, reversed(shifts))):
         come_upper, come_lower = swap(upper, first, size), swap(lower, second, size)
         if i == 0:
@@ -400,7 +439,7 @@
 
     turns = max(z + min(steps - 1, slots * (n_row - 1 - z)) for z in range(n_row - 1))
     cols = ncols // SPLITS
-    streams = [([], []) for _ in range(SPLITS)]
+    streams = [((), None)] * SPLITS
 
     def exchange(array, odd):
         pairs = []
@@ -411,35 +450,53 @@
                 pairs.append((z * n_wide + w, target))
         return lax.ppermute(array, ("row", "wide"), pairs)
 
-    whole = rows % 8 == 0
-    if whole:
-        piece = pack(eigvec_t, n_wide)
-        x = lax.all_to_all(piece, "wide", split_axis=0, concat_axis=0, tiled=True)
-        tokens = [piece]
+    chunks = 2 if rows % 16 == 0 else 1
+    size = rows // chunks
+    if chunks > 1:
+        pieces = [pack(eigvec_t, i * size, size, n_wide) for i in range(chunks)]
+        parts = [lax.all_to_all(pieces[0], "wide", split_axis=0, concat_axis=0, tiled=True)]
+        tokens = [pieces[0]]
     else:
-        x = lax.all_to_all(eigvec_t, "wide", split_axis=1, concat_axis=0, tiled=True)[None]
+        parts = [lax.all_to_all(eigvec_t, "wide", split_axis=1, concat_axis=0, tiled=True)[None]]
         tokens = []
     for turn in range(turns):
         for part in range(SPLITS):
-            evens, odds = streams[part]
-            to_even, to_odd = feed(after(here, *tokens), block_place, householder, evens, odds, n_row, part, cols)
+            last, store = streams[part]
+            to_even, to_odd, store = feed(
+                after(here, *tokens), block_place, householder, turn, turns, last, store, n_row, part, cols
+            )
             tokens = [to_odd]
-            streams[part] = (evens + [exchange(to_even, 0)], odds + [exchange(to_odd, 1)])
-    evens = list(zip(*[stream[0] for stream in streams]))
-    odds = list(zip(*[stream[1] for stream in streams]))
-    high, low, both_t, gram = assemble(here, block_place, offsets, householder, evens, odds, n_row)
+            streams[part] = ((exchange(to_even, 0), exchange(to_odd, 1)), store)
+            if chunks > 1 and (turn, part) == (0, 1):
+                tokens.append(pieces[1])
+            if chunks > 1 and (turn, part) == ARRIVED:
+                piece = after(pieces[1], parts[0], to_odd)
+                parts.append(lax.all_to_all(piece, "wide", split_axis=0, concat_axis=0, tiled=True))
+                tokens.append(piece)
+    stores, lasts = [store for _, store in streams], [last for last, _ in streams]
+    high, low, both_t, gram = assemble(here, block_place, offsets, householder, stores, lasts, n_row)
     cross = spread(gram + swap(gram, 1, n_wide), n_wide)
-    x = x.reshape(n_wide * rows, ncols)
-    both_t = lift(after(both_t, x))
-    cross[0] = after(cross[0], both_t)
+
+    def flat(x):
+        return x.reshape(-1, ncols)
+
+    pairs = []
+    for x in parts[:-1]:
+        mine, theirs = inner_products(here, flat(x), lift(both_t), 0)
+        pairs.append(mine + swap(theirs, 1, n_wide))
+    late_t = lift(after(both_t, parts[-1], *pairs))
+    cross[0] = after(cross[0], late_t)
     cross = functools.reduce(jnp.add, cross)
     changes = merge([cross], wy_factor, (high, low))
-
-    mine, theirs, x = inner_products(after(here, cross), x, both_t)
-    mine = chips_sum(mine + swap(theirs, 1, n_wide), n_wide, changes)
+    mine, theirs, late = inner_products(after(here, cross), flat(parts[-1]), late_t, 1)
+    pairs.append(mine + swap(theirs, 1, n_wide))
+    if chunks == 1:
+        middle = pairs[0].shape[0] // 2
+        pairs = [pairs[0][:middle], pairs[0][middle:]]
+    mine = chips_sum(pairs[0], pairs[1], n_wide, changes)
     theirs = swap(mine, 1, n_wide)
-    out = update(here, x, mine, changes, None, False)
-    return update(here, x, theirs, changes, out, True)
+    out = update(here, parts[:-1], late.reshape(parts[-1].shape), mine, theirs, changes)
+    return out.reshape(n_wide * rows, ncols)
 
 
 def solution(mesh):

time: 138 us -> 146 us (1.058)
  Pallas kernels: 42.1 us -> 60.9 us
  waiting for transfers between devices: 42.3 us -> 30.4 us
    pallas_call x14 -> x13, Pallas kernels: 15.9 us -> 26.8 us  [the longest x12 19.1 us: feed(): pl.pallas_call(kernel, out_shape=out_shape, in_specs=[SMEM, SMEM] + [ANY]...]
    all_to_all x1 -> x2, waiting for transfers between devices: 11.9 us -> 3.11 us  [the longest x1 3.11 us: body(): lax.all_to_all(pieces[0], 'wide', split_axis=0, concat_axis=0, tiled=True)]
    ppermute x24, waiting for transfers between devices: 24.4 us -> 19.4 us  [exchange(): return lax.ppermute(array, ('row', 'wide'), pairs)]
    all_to_all x1 -> x2, starting transfers between devices: 5.31 us -> 9.87 us  [the longest x1 5.31 us: body(): lax.all_to_all(pieces[0], 'wide', split_axis=0, concat_axis=0, tiled=True)]
    pallas_call x1 -> x2, Pallas kernels: 8.32 us -> 12.4 us  [inner_products(): pl.pallas_call(kernel, out_shape=[jax.ShapeDtypeStruct((half // 2, 2 * he...]
    ppermute x24, starting transfers between devices: 39.6 us -> 35.5 us  [exchange(): return lax.ppermute(array, ('row', 'wide'), pairs)]
    ppermute x10 -> x11, waiting for transfers between devices: 5.99 us -> 7.91 us  [swap(): return lax.ppermute(array, 'wide', [(i, i ^ k) for i in range(size)])]
    pallas_call x1 -> x2, Pallas kernels: 2.03 us -> 3.76 us  [lift(): pl.pallas_call(kernel, out_shape=pltpu.VMEM(x.shape, x.dtype), in_specs=[...]
  transfers between devices with their start and end apart: 35 -> 37, of which waited for: 17 -> 16; matrix products, arithmetic and copies ran while one was open for 0% -> 0% of each run, Pallas kernels for 17% -> 30%
where the time goes in v10:
time: 146 us
  Pallas kernels  60.9 us (42%)
  starting transfers between devices  53.7 us (37%)
  waiting for transfers between devices  30.4 us (21%)
    ppermute x24, starting transfers between devices, exchange(): return lax.ppermute(array, ('row', 'wide'), pairs)  35.5 us
    ppermute x24, waiting for transfers between devices, exchange(): return lax.ppermute(array, ('row', 'wide'), pairs)  19.4 us
    pallas_call x12, Pallas kernels, feed(): pl.pallas_call(kernel, out_shape=out_shape, in_specs=[SMEM, SMEM] + [ANY]...  19.1 us
    pallas_call x2, Pallas kernels, inner_products(): pl.pallas_call(kernel, out_shape=[jax.ShapeDtypeStruct((half // 2, 2 * he...  12.4 us
    ppermute x11, starting transfers between devices, swap(): return lax.ppermute(array, 'wide', [(i, i ^ k) for i in range(size)])  8.26 us
    ppermute x11, waiting for transfers between devices, swap(): return lax.ppermute(array, 'wide', [(i, i ^ k) for i in range(size)])  7.91 us
    pallas_call x1, Pallas kernels, update(): pl.pallas_call(kernel, out_shape=jax.ShapeDtypeStruct((lead, len(chunks)...  7.64 us
    pallas_call x2, Pallas kernels, pack(): pl.pallas_call(kernel, out_shape=jax.ShapeDtypeStruct((n_wide, rows, ncol...  7.55 us
  transfers between devices with their start and end apart: 37, of which 16 were waited for; matrix products, arithmetic and copies ran while one was open for 0% of the time, Pallas kernels for 30%

profile of v10, /device:TPU:0, one launch (start us, length us, event | category | flops | bytes accessed | tf_op | source)
XLA Modules:
  0.0 145.8 jit_solution(8602057031707425112)
XLA Ops:
  0.0 3.8 %pack.2 = f32[8,32,4096]{2,1,0:T(8,128)} custom-call(f32[64,32768]{1,0:T(8,128)} %x_ref.3), custom_call_target="tpu_custom_call" | custom-call | bytes 8388608 | tf_op jit(solution)/shard_map/pack/pallas_call | solution.py:83
  3.8 5.3 %all-to-all-start = ((f32[8,32,4096]{2,1,0:T(8,128)}), f32[8,32,4096]{2,1,0:T(8,128)}, u32[]{:S(2)}, u32[]{:S(2)}) async-start(f32[8,32,4096]{2,1,0:T(8,128)} %pack.2), calls=%async_computation | async-start | bytes 8388608 | tf_op jit(solution)/shard_map/all_to_all | solution.py:457
  9.9 2.5 %collective-permute-start = (f32[32,2048]{1,0:T(8,128)S(1)}, f32[32,2048]{1,0:T(8,128)S(1)}, u32[]{:S(2)}, u32[]{:S(2)}) collective-permute-start(f32[32,2048]{1,0:T(8,128)S(1)} %get-tuple-element.71), channel_id=1, source_target_pairs={{0,8},{1,9},{2,10},{3,11},{4,12},{5,13},{6,14},{7,15},{8,0},{9,1},... | collective-permute-start | bytes 786440 | tf_op jit(solution)/shard_map/ppermute | solution.py:451
  13.1 3.1 %collective-permute-start.2 = (f32[32,2048]{1,0:T(8,128)S(1)}, f32[32,2048]{1,0:T(8,128)S(1)}, u32[]{:S(2)}, u32[]{:S(2)}) collective-permute-start(f32[32,2048]{1,0:T(8,128)S(1)} %get-tuple-element.74), channel_id=1, source_target_pairs={{0,8},{1,9},{2,10},{3,11},{4,12},{5,13},{6,14},{7,15},{8,0},{9,1},... | collective-permute-start | bytes 786440 | tf_op jit(solution)/shard_map/ppermute | solution.py:451
  16.3 3.8 %pack.3 = f32[8,32,4096]{2,1,0:T(8,128)} custom-call(f32[64,32768]{1,0:T(8,128)} %x_ref.3), custom_call_target="tpu_custom_call" | custom-call | bytes 8388608 | tf_op jit(solution)/shard_map/pack/pallas_call | solution.py:83
  21.6 2.6 %collective-permute-start.4 = (f32[32,2048]{1,0:T(8,128)S(1)}, f32[32,2048]{1,0:T(8,128)S(1)}, u32[]{:S(2)}, u32[]{:S(2)}) collective-permute-start(f32[32,2048]{1,0:T(8,128)S(1)} %get-tuple-element.77), channel_id=1, source_target_pairs={{0,8},{1,9},{2,10},{3,11},{4,12},{5,13},{6,14},{7,15},{8,0},{9,1},... | collective-permute-start | bytes 786440 | tf_op jit(solution)/shard_map/ppermute | solution.py:451
  26.4 3.4 %collective-permute-start.6 = (f32[32,2048]{1,0:T(8,128)S(1)}, f32[32,2048]{1,0:T(8,128)S(1)}, u32[]{:S(2)}, u32[]{:S(2)}) collective-permute-start(f32[32,2048]{1,0:T(8,128)S(1)} %get-tuple-element.81), channel_id=1, source_target_pairs={{0,8},{1,9},{2,10},{3,11},{4,12},{5,13},{6,14},{7,15},{8,0},{9,1},... | collective-permute-start | bytes 786440 | tf_op jit(solution)/shard_map/ppermute | solution.py:451
  32.9 2.5 %collective-permute-start.8 = (f32[32,2048]{1,0:T(8,128)S(1)}, f32[32,2048]{1,0:T(8,128)S(1)}, u32[]{:S(2)}, u32[]{:S(2)}) collective-permute-start(f32[32,2048]{1,0:T(8,128)S(1)} %get-tuple-element.85), channel_id=1, source_target_pairs={{0,8},{1,9},{2,10},{3,11},{4,12},{5,13},{6,14},{7,15},{8,0},{9,1},... | collective-permute-start | bytes 786440 | tf_op jit(solution)/shard_map/ppermute | solution.py:451
  38.6 4.5 %collective-permute-start.10 = (f32[32,2048]{1,0:T(8,128)S(1)}, f32[32,2048]{1,0:T(8,128)S(1)}, u32[]{:S(2)}, u32[]{:S(2)}) collective-permute-start(f32[32,2048]{1,0:T(8,128)S(1)} %get-tuple-element.89), channel_id=1, source_target_pairs={{0,8},{1,9},{2,10},{3,11},{4,12},{5,13},{6,14},{7,15},{8,0},{9,1},... | collective-permute-start | bytes 786440 | tf_op jit(solution)/shard_map/ppermute | solution.py:451
  43.1 1.9 %feed.18 = (f32[32,2048]{1,0:T(8,128)S(1)}, f32[32,2048]{1,0:T(8,128)S(1)}, f32[2,6,32,2048]{3,2,1,0:T(8,128)}) custom-call(s32[2]{0:T(128)S(1)} %pad_add_fusion.here_ref, s32[6]{0:T(128)S(1)} %copy-done.4, f32[4,32,4096]{2,1,0:T(8,128)S(1)} %copy-done, f32[32,2048]{1,0:T(8,128)S(1)} %collective-permute-done.8.refs_0_, ...), custom_call_target="tpu_custom_call", output_to_operand_aliasing={{2}: (5, {})} | custom-call | bytes 1048576 | tf_op jit(solution)/shard_map/feed/pallas_call | solution.py:151
  46.7 2.2 %collective-permute-done.10.refs_0_ = f32[32,2048]{1,0:T(8,128)S(1)} collective-permute-done((f32[32,2048]{1,0:T(8,128)S(1)}, f32[32,2048]{1,0:T(8,128)S(1)}, u32[]{:S(2)}, u32[]{:S(2)}) %collective-permute-start.10) | collective-permute-done | bytes 262176 | tf_op jit(solution)/shard_map/ppermute | solution.py:451
  50.7 2.7 %collective-permute-done.12.refs_0_ = f32[32,2048]{1,0:T(8,128)S(1)} collective-permute-done((f32[32,2048]{1,0:T(8,128)S(1)}, f32[32,2048]{1,0:T(8,128)S(1)}, u32[]{:S(2)}, u32[]{:S(2)}) %collective-permute-start.12) | collective-permute-done | bytes 262176 | tf_op jit(solution)/shard_map/ppermute | solution.py:451
  53.4 1.9 %feed.20 = (f32[32,2048]{1,0:T(8,128)S(1)}, f32[32,2048]{1,0:T(8,128)S(1)}, f32[2,6,32,2048]{3,2,1,0:T(8,128)}) custom-call(s32[2]{0:T(128)S(1)} %pad_add_fusion.here_ref, s32[6]{0:T(128)S(1)} %copy-done.4, f32[4,32,4096]{2,1,0:T(8,128)S(1)} %copy-done, f32[32,2048]{1,0:T(8,128)S(1)} %collective-permute-done.12.refs_0_, ...), custom_call_target="tpu_custom_call", output_to_operand_aliasing={{2}: (5, {})} | custom-call | bytes 1048576 | tf_op jit(solution)/shard_map/feed/pallas_call | solution.py:151
  55.2 3.1 %all-to-all-done.refs_0_ = f32[8,32,4096]{2,1,0:T(8,128)} async-done(((f32[8,32,4096]{2,1,0:T(8,128)}), f32[8,32,4096]{2,1,0:T(8,128)}, u32[]{:S(2)}, u32[]{:S(2)}) %all-to-all-start) | async-done | bytes 4194336 | tf_op jit(solution)/shard_map/all_to_all | solution.py:457
  58.4 4.6 %all-to-all-start.1 = ((f32[8,32,4096]{2,1,0:T(8,128)}), f32[8,32,4096]{2,1,0:T(8,128)}, u32[]{:S(2)}, u32[]{:S(2)}) async-start(f32[8,32,4096]{2,1,0:T(8,128)} %pack.3), calls=%async_computation.1 | async-start | bytes 8388608 | tf_op jit(solution)/shard_map/all_to_all | solution.py:474
  62.9 2.4 %collective-permute-start.14 = (f32[32,2048]{1,0:T(8,128)S(1)}, f32[32,2048]{1,0:T(8,128)S(1)}, u32[]{:S(2)}, u32[]{:S(2)}) collective-permute-start(f32[32,2048]{1,0:T(8,128)S(1)} %get-tuple-element.98), channel_id=1, source_target_pairs={{0,8},{1,9},{2,10},{3,11},{4,12},{5,13},{6,14},{7,15},{8,0},{9,1},... | collective-permute-start | bytes 786440 | tf_op jit(solution)/shard_map/ppermute | solution.py:451
  65.3 3.1 %collective-permute-start.16 = (f32[32,2048]{1,0:T(8,128)S(1)}, f32[32,2048]{1,0:T(8,128)S(1)}, u32[]{:S(2)}, u32[]{:S(2)}) collective-permute-start(f32[32,2048]{1,0:T(8,128)S(1)} %get-tuple-element.102), channel_id=1, source_target_pairs={{0,8},{1,9},{2,10},{3,11},{4,12},{5,13},{6,14},{7,15},{8,0},{9,1},... | collective-permute-start | bytes 786440 | tf_op jit(solution)/shard_map/ppermute | solution.py:451
  68.5 3.9 %collective-permute-done.14.refs_0_ = f32[32,2048]{1,0:T(8,128)S(1)} collective-permute-done((f32[32,2048]{1,0:T(8,128)S(1)}, f32[32,2048]{1,0:T(8,128)S(1)}, u32[]{:S(2)}, u32[]{:S(2)}) %collective-permute-start.14) | collective-permute-done | bytes 262176 | tf_op jit(solution)/shard_map/ppermute | solution.py:451
  74.2 2.9 %collective-permute-start.18 = (f32[32,2048]{1,0:T(8,128)S(1)}, f32[32,2048]{1,0:T(8,128)S(1)}, u32[]{:S(2)}, u32[]{:S(2)}) collective-permute-start(f32[32,2048]{1,0:T(8,128)S(1)} %get-tuple-element.107), channel_id=1, source_target_pairs={{0,8},{1,9},{2,10},{3,11},{4,12},{5,13},{6,14},{7,15},{8,0},{9,1},... | collective-permute-start | bytes 786440 | tf_op jit(solution)/shard_map/ppermute | solution.py:451
  78.0 1.9 %feed.22 = (f32[32,2048]{1,0:T(8,128)S(1)}, f32[32,2048]{1,0:T(8,128)S(1)}, f32[2,6,32,2048]{3,2,1,0:T(8,128)}) custom-call(s32[2]{0:T(128)S(1)} %pad_add_fusion.here_ref, s32[6]{0:T(128)S(1)} %copy-done.4, f32[4,32,4096]{2,1,0:T(8,128)S(1)} %copy-done, f32[32,2048]{1,0:T(8,128)S(1)} %collective-permute-done.16.refs_0_, ...), custom_call_target="tpu_custom_call", output_to_operand_aliasing={{2}: (5, {})} | custom-call | bytes 1048576 | tf_op jit(solution)/shard_map/feed/pallas_call | solution.py:151
  80.0 4.9 %collective-permute-start.20 = (f32[32,2048]{1,0:T(8,128)S(1)}, f32[32,2048]{1,0:T(8,128)S(1)}, u32[]{:S(2)}, u32[]{:S(2)}) collective-permute-start(f32[32,2048]{1,0:T(8,128)S(1)} %get-tuple-element.110), channel_id=1, source_target_pairs={{0,8},{1,9},{2,10},{3,11},{4,12},{5,13},{6,14},{7,15},{8,0},{9,1},... | collective-permute-start | bytes 786440 | tf_op jit(solution)/shard_map/ppermute | solution.py:451
  88.4 1.9 %collective-permute-done.20.refs_2_ = f32[32,2048]{1,0:T(8,128)S(1)} collective-permute-done((f32[32,2048]{1,0:T(8,128)S(1)}, f32[32,2048]{1,0:T(8,128)S(1)}, u32[]{:S(2)}, u32[]{:S(2)}) %collective-permute-start.20) | collective-permute-done | bytes 262176 | tf_op jit(solution)/shard_map/ppermute | solution.py:451
  90.3 4.6 %collective-permute-done.22.refs_4_ = f32[32,2048]{1,0:T(8,128)S(1)} collective-permute-done((f32[32,2048]{1,0:T(8,128)S(1)}, f32[32,2048]{1,0:T(8,128)S(1)}, u32[]{:S(2)}, u32[]{:S(2)}) %collective-permute-start.22) | collective-permute-done | bytes 262176 | tf_op jit(solution)/shard_map/ppermute | solution.py:451
  94.9 7.0 %assemble.1 = (bf16[192,4096]{1,0:T(8,128)(2,1)}, bf16[192,4096]{1,0:T(8,128)(2,1)}, bf16[4096,384]{1,0:T(8,128)(2,1)}, f32[32,512]{1,0:T(8,128)S(1)}) custom-call(s32[2]{0:T(128)S(1)} %pad_add_fusion.here_ref, s32[6]{0:T(128)S(1)} %copy-done.4, s32[6]{0:T(128)S(1)} %copy-done.5, f32[4,32,4096]{2,1,0:T(8,128)S(1)} %copy-done, ...), custom_call_target="tpu_custom_call" | custom-call | flops 1811939328 | bytes 6291456 | tf_op jit(solution)/shard_map/assemble/pallas_call | solution.py:221
  101.9 1.9 %lift.2.vecs_ref = bf16[4096,384]{1,0:T(8,128)(2,1)S(1)} custom-call(bf16[4096,384]{1,0:T(8,128)(2,1)} %get-tuple-element.117.x_ref), custom_call_target="tpu_custom_call" | custom-call | bytes 3145728 | tf_op jit(solution)/shard_map/lift/pallas_call | solution.py:299
  103.8 6.1 %inner_products.2 = (f32[64,384]{1,0:T(8,128)S(1)}, f32[64,384]{1,0:T(8,128)S(1)}) custom-call(s32[2]{0:T(128)S(1)} %pad_add_fusion.here_ref, f32[256,4096]{1,0:T(8,128)} %bitcast.2.x_ref, bf16[4096,384]{1,0:T(8,128)(2,1)S(1)} %lift.2.vecs_ref), custom_call_target="tpu_custom_call" | custom-call | flops 1207959552 | bytes 4194304 | tf_op jit(solution)/shard_map/inner_products/pallas_call | solution.py:339
  110.5 2.8 %collective-permute-start.28 = (f32[32,512]{1,0:T(8,128)S(1)}, f32[32,512]{1,0:T(8,128)S(1)}, u32[]{:S(2)}, u32[]{:S(2)}) collective-permute-start(f32[32,512]{1,0:T(8,128)S(1)} %add.31), channel_id=1, source_target_pairs={{0,6},{1,7},{2,4},{3,5},{4,2},{5,3},{6,0},{7,1},{8,14},{9,15},{10,... | collective-permute-start | bytes 196616 | tf_op jit(solution)/shard_map/ppermute | solution.py:416
  114.1 1.9 %lift.3.vecs_ref = bf16[4096,384]{1,0:T(8,128)(2,1)S(1)} custom-call(bf16[4096,384]{1,0:T(8,128)(2,1)} %get-tuple-element.117.x_ref), custom_call_target="tpu_custom_call" | custom-call | bytes 3145728 | tf_op jit(solution)/shard_map/lift/pallas_call | solution.py:299
  118.1 6.3 %inner_products.3 = (f32[64,384]{1,0:T(8,128)S(1)}, f32[64,384]{1,0:T(8,128)S(1)}, f32[256,4096]{1,0:T(8,128)S(1)}) custom-call(s32[2]{0:T(128)S(1)} %pad_add_fusion.here_ref, f32[256,4096]{1,0:T(8,128)} %bitcast.3.x_ref, bf16[4096,384]{1,0:T(8,128)(2,1)S(1)} %lift.3.vecs_ref), custom_call_target="tpu_custom_call" | custom-call | flops 1207959552 | bytes 4194304 | tf_op jit(solution)/shard_map/inner_products/pallas_call | solution.py:339
  127.4 3.5 %merge.1.p_ref = bf16[576,4096]{1,0:T(8,128)(2,1)S(1)} custom-call(f32[32,512]{1,0:T(8,128)S(1)} %add_add_fusion.refs_0_, f32[6,32,32]{2,1,0:T(8,128)S(1)} %copy-done.3, bf16[192,4096]{1,0:T(8,128)(2,1)S(1)} %copy-done.1, bf16[192,4096]{1,0:T(8,128)(2,1)S(1)} %copy-done.2), custom_call_target="tpu_custom_call" | custom-call | flops 905969664 | bytes 6291456 | tf_op jit(solution)/shard_map/merge/pallas_call | solution.py:258
  132.6 3.0 %collective-permute-done.31 = f32[64,384]{1,0:T(8,128)S(1)} collective-permute-done((f32[64,384]{1,0:T(8,128)S(1)}, f32[64,384]{1,0:T(8,128)S(1)}, u32[]{:S(2)}, u32[]{:S(2)}) %collective-permute-start.31) | collective-permute-done | bytes 98336 | tf_op jit(solution)/shard_map/ppermute | solution.py:416
  138.0 7.6 %update.1 = f32[8,64,4096]{2,1,0:T(8,128)} custom-call(s32[2]{0:T(128)S(1)} %pad_add_fusion.here_ref, f32[128,384]{1,0:T(8,128)S(1)} %pad_maximum_fusion.mine_ref, f32[128,384]{1,0:T(8,128)S(1)} %collective-permute-done.34.theirs_ref, bf16[576,4096]{1,0:T(8,128)(2,1)S(1)} %merge.1.p_ref, f32[8,32,4096]{2,1,0:T(8,128)} %all-to-all-done.refs_0_, ...), custom_call_target="tpu_custom_call" | custom-call | flops 2415919104 | bytes 16777216 | tf_op jit(solution)/shard_map/update/pallas_call | solution.py:397
  (85 shorter events, 32.0 us)
Async XLA Ops:
  3.8 54.5 %all-to-all-start = ((f32[8,32,4096]{2,1,0:T(8,128)}), f32[8,32,4096]{2,1,0:T(8,128)}, u32[]{:S(2)}, u32[]{:S(2)}) async-start(f32[8,32,4096]{2,1,0:T(8,128)} %pack.2), calls=%async_computation | async-start | bytes 8388608 | tf_op jit(solution)/shard_map/all_to_all | solution.py:457
  9.9 10.2 %collective-permute-start = (f32[32,2048]{1,0:T(8,128)S(1)}, f32[32,2048]{1,0:T(8,128)S(1)}, u32[]{:S(2)}, u32[]{:S(2)}) collective-permute-start(f32[32,2048]{1,0:T(8,128)S(1)} %get-tuple-element.71), channel_id=1, source_target_pairs={{0,8},{1,9},{2,10},{3,11},{4,12},{5,13},{6,14},{7,15},{8,0},{9,1},... | collective-permute-start | bytes 786440 | tf_op jit(solution)/shard_map/ppermute | solution.py:451
  12.4 7.7 %collective-permute-start.1 = (f32[32,2048]{1,0:T(8,128)S(1)}, f32[32,2048]{1,0:T(8,128)S(1)}, u32[]{:S(2)}, u32[]{:S(2)}) collective-permute-start(f32[32,2048]{1,0:T(8,128)S(1)} %get-tuple-element.67), channel_id=1, source_target_pairs={{0,1},{1,0},{2,3},{3,2},{4,5},{5,4},{6,7},{7,6},{8,16},{9,17},{10,... | collective-permute-start | bytes 786440 | tf_op jit(solution)/shard_map/ppermute | solution.py:451
  13.1 11.7 %collective-permute-start.2 = (f32[32,2048]{1,0:T(8,128)S(1)}, f32[32,2048]{1,0:T(8,128)S(1)}, u32[]{:S(2)}, u32[]{:S(2)}) collective-permute-start(f32[32,2048]{1,0:T(8,128)S(1)} %get-tuple-element.74), channel_id=1, source_target_pairs={{0,8},{1,9},{2,10},{3,11},{4,12},{5,13},{6,14},{7,15},{8,0},{9,1},... | collective-permute-start | bytes 786440 | tf_op jit(solution)/shard_map/ppermute | solution.py:451
  16.3 8.6 %collective-permute-start.3 = (f32[32,2048]{1,0:T(8,128)S(1)}, f32[32,2048]{1,0:T(8,128)S(1)}, u32[]{:S(2)}, u32[]{:S(2)}) collective-permute-start(f32[32,2048]{1,0:T(8,128)S(1)} %get-tuple-element.69), channel_id=1, source_target_pairs={{0,1},{1,0},{2,3},{3,2},{4,5},{5,4},{6,7},{7,6},{8,16},{9,17},{10,... | collective-permute-start | bytes 786440 | tf_op jit(solution)/shard_map/ppermute | solution.py:451
  21.6 9.5 %collective-permute-start.4 = (f32[32,2048]{1,0:T(8,128)S(1)}, f32[32,2048]{1,0:T(8,128)S(1)}, u32[]{:S(2)}, u32[]{:S(2)}) collective-permute-start(f32[32,2048]{1,0:T(8,128)S(1)} %get-tuple-element.77), channel_id=1, source_target_pairs={{0,8},{1,9},{2,10},{3,11},{4,12},{5,13},{6,14},{7,15},{8,0},{9,1},... | collective-permute-start | bytes 786440 | tf_op jit(solution)/shard_map/ppermute | solution.py:451
  24.2 6.9 %collective-permute-start.5 = (f32[32,2048]{1,0:T(8,128)S(1)}, f32[32,2048]{1,0:T(8,128)S(1)}, u32[]{:S(2)}, u32[]{:S(2)}) collective-permute-start(f32[32,2048]{1,0:T(8,128)S(1)} %get-tuple-element.72), channel_id=1, source_target_pairs={{0,1},{1,0},{2,3},{3,2},{4,5},{5,4},{6,7},{7,6},{8,16},{9,17},{10,... | collective-permute-start | bytes 786440 | tf_op jit(solution)/shard_map/ppermute | solution.py:451
  26.4 10.3 %collective-permute-start.6 = (f32[32,2048]{1,0:T(8,128)S(1)}, f32[32,2048]{1,0:T(8,128)S(1)}, u32[]{:S(2)}, u32[]{:S(2)}) collective-permute-start(f32[32,2048]{1,0:T(8,128)S(1)} %get-tuple-element.81), channel_id=1, source_target_pairs={{0,8},{1,9},{2,10},{3,11},{4,12},{5,13},{6,14},{7,15},{8,0},{9,1},... | collective-permute-start | bytes 786440 | tf_op jit(solution)/shard_map/ppermute | solution.py:451
  29.8 6.9 %collective-permute-start.7 = (f32[32,2048]{1,0:T(8,128)S(1)}, f32[32,2048]{1,0:T(8,128)S(1)}, u32[]{:S(2)}, u32[]{:S(2)}) collective-permute-start(f32[32,2048]{1,0:T(8,128)S(1)} %get-tuple-element.75), channel_id=1, source_target_pairs={{0,1},{1,0},{2,3},{3,2},{4,5},{5,4},{6,7},{7,6},{8,16},{9,17},{10,... | collective-permute-start | bytes 786440 | tf_op jit(solution)/shard_map/ppermute | solution.py:451
  32.9 10.2 %collective-permute-start.8 = (f32[32,2048]{1,0:T(8,128)S(1)}, f32[32,2048]{1,0:T(8,128)S(1)}, u32[]{:S(2)}, u32[]{:S(2)}) collective-permute-start(f32[32,2048]{1,0:T(8,128)S(1)} %get-tuple-element.85), channel_id=1, source_target_pairs={{0,8},{1,9},{2,10},{3,11},{4,12},{5,13},{6,14},{7,15},{8,0},{9,1},... | collective-permute-start | bytes 786440 | tf_op jit(solution)/shard_map/ppermute | solution.py:451
  35.4 7.7 %collective-permute-start.9 = (f32[32,2048]{1,0:T(8,128)S(1)}, f32[32,2048]{1,0:T(8,128)S(1)}, u32[]{:S(2)}, u32[]{:S(2)}) collective-permute-start(f32[32,2048]{1,0:T(8,128)S(1)} %get-tuple-element.79), channel_id=1, source_target_pairs={{0,1},{1,0},{2,3},{3,2},{4,5},{5,4},{6,7},{7,6},{8,16},{9,17},{10,... | collective-permute-start | bytes 786440 | tf_op jit(solution)/shard_map/ppermute | solution.py:451
  38.6 10.3 %collective-permute-start.11 = (f32[32,2048]{1,0:T(8,128)S(1)}, f32[32,2048]{1,0:T(8,128)S(1)}, u32[]{:S(2)}, u32[]{:S(2)}) collective-permute-start(f32[32,2048]{1,0:T(8,128)S(1)} %get-tuple-element.83), channel_id=1, source_target_pairs={{0,1},{1,0},{2,3},{3,2},{4,5},{5,4},{6,7},{7,6},{8,16},{9,17},{10,... | collective-permute-start | bytes 786440 | tf_op jit(solution)/shard_map/ppermute | solution.py:451
  38.6 10.2 %collective-permute-start.10 = (f32[32,2048]{1,0:T(8,128)S(1)}, f32[32,2048]{1,0:T(8,128)S(1)}, u32[]{:S(2)}, u32[]{:S(2)}) collective-permute-start(f32[32,2048]{1,0:T(8,128)S(1)} %get-tuple-element.89), channel_id=1, source_target_pairs={{0,8},{1,9},{2,10},{3,11},{4,12},{5,13},{6,14},{7,15},{8,0},{9,1},... | collective-permute-start | bytes 786440 | tf_op jit(solution)/shard_map/ppermute | solution.py:451
  45.0 8.4 %collective-permute-start.12 = (f32[32,2048]{1,0:T(8,128)S(1)}, f32[32,2048]{1,0:T(8,128)S(1)}, u32[]{:S(2)}, u32[]{:S(2)}) collective-permute-start(f32[32,2048]{1,0:T(8,128)S(1)} %get-tuple-element.93), channel_id=1, source_target_pairs={{0,8},{1,9},{2,10},{3,11},{4,12},{5,13},{6,14},{7,15},{8,0},{9,1},... | collective-permute-start | bytes 786440 | tf_op jit(solution)/shard_map/ppermute | solution.py:451
  46.7 6.7 %collective-permute-start.13 = (f32[32,2048]{1,0:T(8,128)S(1)}, f32[32,2048]{1,0:T(8,128)S(1)}, u32[]{:S(2)}, u32[]{:S(2)}) collective-permute-start(f32[32,2048]{1,0:T(8,128)S(1)} %get-tuple-element.87), channel_id=1, source_target_pairs={{0,1},{1,0},{2,3},{3,2},{4,5},{5,4},{6,7},{7,6},{8,16},{9,17},{10,... | collective-permute-start | bytes 786440 | tf_op jit(solution)/shard_map/ppermute | solution.py:451
  58.4 55.7 %all-to-all-start.1 = ((f32[8,32,4096]{2,1,0:T(8,128)}), f32[8,32,4096]{2,1,0:T(8,128)}, u32[]{:S(2)}, u32[]{:S(2)}) async-start(f32[8,32,4096]{2,1,0:T(8,128)} %pack.3), calls=%async_computation.1 | async-start | bytes 8388608 | tf_op jit(solution)/shard_map/all_to_all | solution.py:474
  62.9 9.5 %collective-permute-start.14 = (f32[32,2048]{1,0:T(8,128)S(1)}, f32[32,2048]{1,0:T(8,128)S(1)}, u32[]{:S(2)}, u32[]{:S(2)}) collective-permute-start(f32[32,2048]{1,0:T(8,128)S(1)} %get-tuple-element.98), channel_id=1, source_target_pairs={{0,8},{1,9},{2,10},{3,11},{4,12},{5,13},{6,14},{7,15},{8,0},{9,1},... | collective-permute-start | bytes 786440 | tf_op jit(solution)/shard_map/ppermute | solution.py:451
  65.3 7.1 %collective-permute-start.15 = (f32[32,2048]{1,0:T(8,128)S(1)}, f32[32,2048]{1,0:T(8,128)S(1)}, u32[]{:S(2)}, u32[]{:S(2)}) collective-permute-start(f32[32,2048]{1,0:T(8,128)S(1)} %get-tuple-element.91), channel_id=1, source_target_pairs={{0,1},{1,0},{2,3},{3,2},{4,5},{5,4},{6,7},{7,6},{8,16},{9,17},{10,... | collective-permute-start | bytes 786440 | tf_op jit(solution)/shard_map/ppermute | solution.py:451
  65.3 12.7 %collective-permute-start.16 = (f32[32,2048]{1,0:T(8,128)S(1)}, f32[32,2048]{1,0:T(8,128)S(1)}, u32[]{:S(2)}, u32[]{:S(2)}) collective-permute-start(f32[32,2048]{1,0:T(8,128)S(1)} %get-tuple-element.102), channel_id=1, source_target_pairs={{0,8},{1,9},{2,10},{3,11},{4,12},{5,13},{6,14},{7,15},{8,0},{9,1},... | collective-permute-start | bytes 786440 | tf_op jit(solution)/shard_map/ppermute | solution.py:451
  68.5 9.5 %collective-permute-start.17 = (f32[32,2048]{1,0:T(8,128)S(1)}, f32[32,2048]{1,0:T(8,128)S(1)}, u32[]{:S(2)}, u32[]{:S(2)}) collective-permute-start(f32[32,2048]{1,0:T(8,128)S(1)} %get-tuple-element.95), channel_id=1, source_target_pairs={{0,1},{1,0},{2,3},{3,2},{4,5},{5,4},{6,7},{7,6},{8,16},{9,17},{10,... | collective-permute-start | bytes 786440 | tf_op jit(solution)/shard_map/ppermute | solution.py:451
  74.2 10.6 %collective-permute-start.18 = (f32[32,2048]{1,0:T(8,128)S(1)}, f32[32,2048]{1,0:T(8,128)S(1)}, u32[]{:S(2)}, u32[]{:S(2)}) collective-permute-start(f32[32,2048]{1,0:T(8,128)S(1)} %get-tuple-element.107), channel_id=1, source_target_pairs={{0,8},{1,9},{2,10},{3,11},{4,12},{5,13},{6,14},{7,15},{8,0},{9,1},... | collective-permute-start | bytes 786440 | tf_op jit(solution)/shard_map/ppermute | solution.py:451
  77.1 7.7 %collective-permute-start.19 = (f32[32,2048]{1,0:T(8,128)S(1)}, f32[32,2048]{1,0:T(8,128)S(1)}, u32[]{:S(2)}, u32[]{:S(2)}) collective-permute-start(f32[32,2048]{1,0:T(8,128)S(1)} %get-tuple-element.100), channel_id=1, source_target_pairs={{0,1},{1,0},{2,3},{3,2},{4,5},{5,4},{6,7},{7,6},{8,16},{9,17},{10,... | collective-permute-start | bytes 786440 | tf_op jit(solution)/shard_map/ppermute | solution.py:451
  79.9 10.4 %collective-permute-start.21 = (f32[32,2048]{1,0:T(8,128)S(1)}, f32[32,2048]{1,0:T(8,128)S(1)}, u32[]{:S(2)}, u32[]{:S(2)}) collective-permute-start(f32[32,2048]{1,0:T(8,128)S(1)} %get-tuple-element.105), channel_id=1, source_target_pairs={{0,1},{1,0},{2,3},{3,2},{4,5},{5,4},{6,7},{7,6},{8,16},{9,17},{10,... | collective-permute-start | bytes 786440 | tf_op jit(solution)/shard_map/ppermute | solution.py:451
  80.0 10.3 %collective-permute-start.20 = (f32[32,2048]{1,0:T(8,128)S(1)}, f32[32,2048]{1,0:T(8,128)S(1)}, u32[]{:S(2)}, u32[]{:S(2)}) collective-permute-start(f32[32,2048]{1,0:T(8,128)S(1)} %get-tuple-element.110), channel_id=1, source_target_pairs={{0,8},{1,9},{2,10},{3,11},{4,12},{5,13},{6,14},{7,15},{8,0},{9,1},... | collective-permute-start | bytes 786440 | tf_op jit(solution)/shard_map/ppermute | solution.py:451
  86.7 8.2 %collective-permute-start.22 = (f32[32,2048]{1,0:T(8,128)S(1)}, f32[32,2048]{1,0:T(8,128)S(1)}, u32[]{:S(2)}, u32[]{:S(2)}) collective-permute-start(f32[32,2048]{1,0:T(8,128)S(1)} %get-tuple-element.111), channel_id=1, source_target_pairs={{0,8},{1,9},{2,10},{3,11},{4,12},{5,13},{6,14},{7,15},{8,0},{9,1},... | collective-permute-start | bytes 786440 | tf_op jit(solution)/shard_map/ppermute | solution.py:451
  88.4 6.5 %collective-permute-start.23 = (f32[32,2048]{1,0:T(8,128)S(1)}, f32[32,2048]{1,0:T(8,128)S(1)}, u32[]{:S(2)}, u32[]{:S(2)}) collective-permute-start(f32[32,2048]{1,0:T(8,128)S(1)} %get-tuple-element.112), channel_id=1, source_target_pairs={{0,1},{1,0},{2,3},{3,2},{4,5},{5,4},{6,7},{7,6},{8,16},{9,17},{10,... | collective-permute-start | bytes 786440 | tf_op jit(solution)/shard_map/ppermute | solution.py:451
  101.9 8.6 %collective-permute-start.25 = (f32[32,512]{1,0:T(8,128)S(1)}, f32[32,512]{1,0:T(8,128)S(1)}, u32[]{:S(2)}, u32[]{:S(2)}) collective-permute-start(f32[32,512]{1,0:T(8,128)S(1)} %get-tuple-element.116), channel_id=1, source_target_pairs={{0,1},{1,0},{2,3},{3,2},{4,5},{5,4},{6,7},{7,6},{8,9},{9,8},{10,11... | collective-permute-start | bytes 196616 | tf_op jit(solution)/shard_map/ppermute | solution.py:416
  110.5 5.5 %collective-permute-start.28 = (f32[32,512]{1,0:T(8,128)S(1)}, f32[32,512]{1,0:T(8,128)S(1)}, u32[]{:S(2)}, u32[]{:S(2)}) collective-permute-start(f32[32,512]{1,0:T(8,128)S(1)} %add.31), channel_id=1, source_target_pairs={{0,6},{1,7},{2,4},{3,5},{4,2},{5,3},{6,0},{7,1},{8,14},{9,15},{10,... | collective-permute-start | bytes 196616 | tf_op jit(solution)/shard_map/ppermute | solution.py:416
  124.5 6.4 %collective-permute-start.30 = (f32[64,384]{1,0:T(8,128)S(1)}, f32[64,384]{1,0:T(8,128)S(1)}, u32[]{:S(2)}, u32[]{:S(2)}) collective-permute-start(f32[64,384]{1,0:T(8,128)S(1)} %add.30), channel_id=1, source_target_pairs={{0,2},{1,3},{2,0},{3,1},{4,6},{5,7},{6,4},{7,5},{8,10},{9,11},{10,... | collective-permute-start | bytes 294920 | tf_op jit(solution)/shard_map/ppermute | solution.py:416
  125.8 5.7 %collective-permute-start.32 = (f32[64,384]{1,0:T(8,128)S(1)}, f32[64,384]{1,0:T(8,128)S(1)}, u32[]{:S(2)}, u32[]{:S(2)}) collective-permute-start(f32[64,384]{1,0:T(8,128)S(1)} %add.35), channel_id=1, source_target_pairs={{0,4},{1,5},{2,6},{3,7},{4,0},{5,1},{6,2},{7,3},{8,12},{9,13},{10,... | collective-permute-start | bytes 294920 | tf_op jit(solution)/shard_map/ppermute | solution.py:416
  130.9 4.7 %collective-permute-start.31 = (f32[64,384]{1,0:T(8,128)S(1)}, f32[64,384]{1,0:T(8,128)S(1)}, u32[]{:S(2)}, u32[]{:S(2)}) collective-permute-start(f32[64,384]{1,0:T(8,128)S(1)} %add.36), channel_id=1, source_target_pairs={{0,4},{1,5},{2,6},{3,7},{4,0},{5,1},{6,2},{7,3},{8,12},{9,13},{10,... | collective-permute-start | bytes 294920 | tf_op jit(solution)/shard_map/ppermute | solution.py:416
  131.5 4.9 %collective-permute-start.33 = (f32[64,384]{1,0:T(8,128)S(1)}, f32[64,384]{1,0:T(8,128)S(1)}, u32[]{:S(2)}, u32[]{:S(2)}) collective-permute-start(f32[64,384]{1,0:T(8,128)S(1)} %add.38), channel_id=1, source_target_pairs={{0,2},{1,3},{2,0},{3,1},{4,6},{5,7},{6,4},{7,5},{8,10},{9,11},{10,... | collective-permute-start | bytes 294920 | tf_op jit(solution)/shard_map/ppermute | solution.py:416
  (11 other events, 69.1 us)

commit v11 on v8

--- a/solution.py
+++ b/solution.py
@@ -153,7 +153,7 @@
     cols = ncols // splits
 
     def kernel(here_ref, place_ref, offset_ref, stack_ref, *refs):
-        arrived, (high_ref, low_ref, both_t_ref, gram_ref, held, sems) = refs[:-6], refs[-6:]
+        arrived, (high_ref, low_ref, high_t_ref, low_t_ref, gram_ref, held, sems) = refs[:-7], refs[-7:]
         even, odd = arrived[:turns * splits], arrived[turns * splits:]
         roots, slot, ranks, counts = plan(place_ref, slots, n_rows)
         me = here_ref[0]
@@ -187,8 +187,7 @@
             high_ref[rows, :] = high
             low_ref[rows, :] = low
         for at in column_blocks(ncols):
-            high, low = halves(held[:, at].T)
-            both_t_ref[at, :] = jnp.concatenate([high, low], axis=1)
+            high_t_ref[at, :], low_t_ref[at, :] = halves(held[:, at].T)
         gram = dot_t(held[...], held[...])
         gram_ref[...] = jnp.zeros_like(gram_ref)
         first = 0
@@ -201,11 +200,12 @@
         out_shape=[
             pltpu.HBM((height, ncols), jnp.bfloat16),
             pltpu.HBM((height, ncols), jnp.bfloat16),
-            pltpu.HBM((ncols, 2 * height), jnp.bfloat16),
+            pltpu.HBM((ncols, height), jnp.bfloat16),
+            pltpu.HBM((ncols, height), jnp.bfloat16),
             jax.ShapeDtypeStruct((width, packed_width(steps, width)), jnp.float32),
         ],
         in_specs=[SMEM, SMEM, SMEM, ANY] + [ANY] * (2 * turns * splits),
-        out_specs=[VMEM] * 4,
+        out_specs=[VMEM] * 5,
         scratch_shapes=[pltpu.VMEM((height, ncols), jnp.float32), pltpu.SemaphoreType.DMA((steps,))],
         compiler_params=params(limit=SMALL_LIMIT),
         cost_estimate=cost(12 * height * height * ncols, 8 * height * ncols),
@@ -260,24 +260,54 @@
     return [pl.ds(start, cols) for start in range(0, ncols, cols)]
 
 
+def lift(arrays):
+    n, rows = len(arrays), arrays[0].shape[0]
+    step = rows // 4 if rows % 64 == 0 else rows
+
+    def kernel(*refs):
+        sems = refs[-1]
+        copies = []
+        for source, out in zip(refs[:n], refs[n:2 * n]):
+            for start in range(0, rows, step):
+                at = pl.ds(start, step)
+                copies.append(pltpu.make_async_copy(source.at[at], out.at[at], sems.at[len(copies)]))
+        for i, copy in enumerate(copies):
+            copy.start(priority=i % QUEUES)
+        for copy in copies:
+            copy.wait()
+
+    return pl.pallas_call(
+        kernel,
+        out_shape=[pltpu.VMEM(x.shape, x.dtype) for x in arrays],
+        in_specs=[ANY] * n,
+        out_specs=[VMEM] * n,
+        scratch_shapes=[pltpu.SemaphoreType.DMA((n * rows // step,))],
+        compiler_params=params(),
+        cost_estimate=cost(0, 2 * n * arrays[0].size),
+        name="lift",
+    )(*[in_hbm(x) for x in arrays])
+
+
 def inner_products(here, x, vecs_t):
-    lead, rows, ncols = x.shape
-    height = vecs_t.shape[1] // 2
-    half = lead * rows // 2
-    lanes = min(-(-height // 128) * 128, 2 * height)
-    cuts = sorted({0, lead // 4, lead * 5 // 8, lead})
-
-    def kernel(here_ref, x_ref, vecs_ref, mine_ref, theirs_ref, held, total, sems):
-        copies = [pltpu.make_async_copy(x_ref.at[i], held.at[i], sems.at[i]) for i in range(lead)]
+    rows, ncols = x.shape
+    height = vecs_t[0].shape[1]
+    half = rows // 2
+    step = rows // 8 if rows % 64 == 0 else rows
+    n_copies = rows // step
+    cuts = sorted({0, n_copies // 4, n_copies})
+
+    def kernel(here_ref, x_ref, high_ref, low_ref, mine_ref, theirs_ref, held, total, sems):
+        copies = []
+        for i in range(n_copies):
+            at = pl.ds(i * step, step)
+            copies.append(pltpu.make_async_copy(x_ref.at[at], held.at[at], sems.at[i]))
         for i, copy in enumerate(copies):
             copy.start(priority=i % QUEUES)
         for start, end in zip(cuts[:-1], cuts[1:]):
             for copy in copies[start:end]:
                 copy.wait()
-            high, low = halves(held[start:end].reshape((end - start) * rows, ncols))
-            by_high = jnp.dot(high, vecs_ref[...], preferred_element_type=jnp.float32)
-            by_low = jnp.dot(low, vecs_ref[:, :lanes], preferred_element_type=jnp.float32)
-            total[start * rows:end * rows, :] = by_high[:, :height] + (by_high[:, height:] + by_low[:, :height])
+            at = pl.ds(start * step, (end - start) * step)
+            total[at, :] = dot3(halves(held[at, :]), (high_ref[...], low_ref[...]), ((1,), (0,)))
         core = lax.rem(here_ref[1], 2)
         mine_ref[...] = fold(total[pl.ds(pl.multiple_of(core * half, 8), half), :])
         theirs_ref[...] = fold(total[pl.ds(pl.multiple_of((1 - core) * half, 8), half), :])
@@ -285,22 +315,19 @@
     return pl.pallas_call(
         kernel,
         out_shape=[jax.ShapeDtypeStruct((half // 2, 2 * height), jnp.float32)] * 2 + [pltpu.VMEM(x.shape, jnp.float32)],
-        in_specs=[SMEM, ANY, VMEM],
+        in_specs=[SMEM, ANY, VMEM, VMEM],
         out_specs=[VMEM] * 3,
-        scratch_shapes=[
-            pltpu.VMEM((lead * rows, height), jnp.float32),
-            pltpu.SemaphoreType.DMA((lead,)),
-        ],
+        scratch_shapes=[pltpu.VMEM((rows, height), jnp.float32), pltpu.SemaphoreType.DMA((n_copies,))],
         compiler_params=params(),
-        cost_estimate=cost(6 * lead * rows * ncols * height, 4 * lead * rows * ncols),
+        cost_estimate=cost(6 * rows * ncols * height, 4 * rows * ncols),
         name="inner_products",
-    )(here, in_hbm(x), vecs_t)
+    )(here, in_hbm(x), *vecs_t)
 
 
 def update(here, x, mine, theirs, changes):
-    lead, rows, ncols = x.shape
+    rows, ncols = x.shape
     height = changes.shape[0] // 3
-    half = lead * rows // 2
+    half = rows // 2
     blocks = column_blocks(ncols)
     depth = min(4, len(blocks))
 
@@ -310,12 +337,12 @@
         w_ref[pl.ds(pl.multiple_of((1 - core) * half, 8), half), :] = unfold(theirs_ref[...])
         high, low = halves(w_ref[...])
         w = jnp.concatenate([high, low, high], axis=1)
-        copies = [pltpu.make_async_copy(held.at[i % depth], out_ref.at[:, :, at], sems.at[i]) for i, at in enumerate(blocks)]
+        copies = [pltpu.make_async_copy(held.at[i % depth], out_ref.at[:, at], sems.at[i]) for i, at in enumerate(blocks)]
         for i, at in enumerate(blocks):
             change = lax.dot_general(w, p_ref[:, at], (((1,), (0,)), ((), ())), preferred_element_type=jnp.float32)
             if i >= depth:
                 copies[i - depth].wait()
-            held[i % depth] = x_ref[:, :, at] - change.reshape(lead, rows, at.size)
+            held[i % depth] = x_ref[:, at] - change
             copies[i].start(priority=i % QUEUES)
         for copy in copies[-depth:]:
             copy.wait()
@@ -326,12 +353,12 @@
         in_specs=[SMEM] + [VMEM] * 4,
         out_specs=ANY,
         scratch_shapes=[
-            pltpu.VMEM((lead * rows, height), jnp.float32),
-            pltpu.VMEM((depth, lead, rows, blocks[0].size), jnp.float32),
+            pltpu.VMEM((rows, height), jnp.float32),
+            pltpu.VMEM((depth, rows, blocks[0].size), jnp.float32),
             pltpu.SemaphoreType.DMA((len(blocks),)),
         ],
         compiler_params=params(),
-        cost_estimate=cost(6 * lead * rows * ncols * height, 8 * lead * rows * ncols),
+        cost_estimate=cost(6 * rows * ncols * height, 8 * rows * ncols),
         name="update",
     )(here, mine, theirs, x, changes)
 
@@ -392,15 +419,15 @@
             streams[part] = (evens + [exchange(to_even, 0)], odds + [exchange(to_odd, 1)])
     evens = list(zip(*[stream[0] for stream in streams]))
     odds = list(zip(*[stream[1] for stream in streams]))
-    high, low, both_t, gram = assemble(here, block_place, offsets, householder, evens, odds, n_row)
-    cross = spread(gram + swap(gram, 1, n_wide), n_wide)
-    cross[0] = after(cross[0], x)
-    cross = functools.reduce(jnp.add, cross)
+    high, low, high_t, low_t, gram = assemble(here, block_place, offsets, householder, evens, odds, n_row)
+    x = x.reshape(n_wide * rows, ncols)
+    vecs_t = lift([high_t, low_t])
+    cross = functools.reduce(jnp.add, spread(after(gram + swap(gram, 1, n_wide), *vecs_t), n_wide))
     changes = merge([cross], wy_factor, (high, low))
 
-    mine, theirs, x = inner_products(after(here, cross), x, both_t)
-    mine = chips_sum(mine + swap(theirs, 1, n_wide), n_wide, changes)
-    return update(here, x, mine, swap(mine, 1, n_wide), changes).reshape(n_wide * rows, ncols)
+    mine, theirs, x = inner_products(here, x, vecs_t)
+    mine = chips_sum(mine + swap(after(theirs, cross), 1, n_wide), n_wide, changes)
+    return update(here, x, mine, swap(mine, 1, n_wide), changes)
 
 
 def solution(mesh):

time: 140 us -> 140 us (level)
  waiting for transfers between devices: 45.7 us -> 40.9 us
  Pallas kernels: 38.7 us -> 42.5 us
    all_to_all x1, waiting for transfers between devices: 11.8 us -> 0.01 us  [body(): x = lax.all_to_all(piece, 'wide', split_axis=0, concat_axis=0, tiled=True)]
    ppermute x10, waiting for transfers between devices: 9.43 us -> 16.4 us  [swap(): return lax.ppermute(array, 'wide', [(i, i ^ k) for i in range(size)])]
    pallas_call x0 -> x1, Pallas kernels: none -> 2.22 us  [lift(): pl.pallas_call(kernel, out_shape=[pltpu.VMEM(x.shape, x.dtype) for x in a...]
    unnamed x14 -> x16, local copies, waits for them, and re-layouts: 1.91 us -> 2.92 us
  transfers between devices with their start and end apart: 35 -> 35, of which waited for: 20 -> 18; matrix products, arithmetic and copies ran while one was open for 0% -> 0% of each run, Pallas kernels for 13% -> 15%
where the time goes in v11:
time: 140 us
  starting transfers between devices  52.7 us (38%)
  Pallas kernels  42.5 us (30%)
  waiting for transfers between devices  40.9 us (29%)
  local copies, waits for them, and re-layouts  2.94 us (2%)
    ppermute x24, starting transfers between devices, exchange(): return lax.ppermute(array, ('row', 'wide'), pairs)  39.6 us
    ppermute x24, waiting for transfers between devices, exchange(): return lax.ppermute(array, ('row', 'wide'), pairs)  24.4 us
    ppermute x10, waiting for transfers between devices, swap(): return lax.ppermute(array, 'wide', [(i, i ^ k) for i in range(size)])  16.4 us
    pallas_call x1, Pallas kernels, inner_products(): pl.pallas_call(kernel, out_shape=[jax.ShapeDtypeStruct((half // 2, 2 * he...  8.83 us
    pallas_call x12, Pallas kernels, feed(): pl.pallas_call(kernel, out_shape=[jax.ShapeDtypeStruct((width, cols), jnp...  8.07 us
    ppermute x10, starting transfers between devices, swap(): return lax.ppermute(array, 'wide', [(i, i ^ k) for i in range(size)])  7.8 us
    pallas_call x1, Pallas kernels, assemble(): pl.pallas_call(kernel, out_shape=[pltpu.HBM((height, ncols), jnp.bfloat16...  7.64 us
    pallas_call x1, Pallas kernels, update(): pl.pallas_call(kernel, out_shape=jax.ShapeDtypeStruct(x.shape, jnp.float3...  6.21 us
  transfers between devices with their start and end apart: 35, of which 18 were waited for; matrix products, arithmetic and copies ran while one was open for 0% of the time, Pallas kernels for 15%

profile of v11, /device:TPU:0, one launch (start us, length us, event | category | flops | bytes accessed | tf_op | source)
XLA Modules:
  0.0 139.6 jit_solution(17568982979020684362)
XLA Ops:
  0.0 6.0 %pack.1 = f32[8,64,4096]{2,1,0:T(8,128)} custom-call(f32[64,32768]{1,0:T(8,128)} %x_ref.1), custom_call_target="tpu_custom_call" | custom-call | bytes 16777216 | tf_op jit(solution)/shard_map/pack/pallas_call | solution.py:82
  6.1 5.3 %all-to-all-start = ((f32[8,64,4096]{2,1,0:T(8,128)}), f32[8,64,4096]{2,1,0:T(8,128)}, u32[]{:S(2)}, u32[]{:S(2)}) async-start(f32[8,64,4096]{2,1,0:T(8,128)} %pack.1), calls=%async_computation | async-start | bytes 16777216 | tf_op jit(solution)/shard_map/all_to_all | solution.py:409
  12.1 2.9 %collective-permute-start = (f32[32,2048]{1,0:T(8,128)S(1)}, f32[32,2048]{1,0:T(8,128)S(1)}, u32[]{:S(2)}, u32[]{:S(2)}) collective-permute-start(f32[32,2048]{1,0:T(8,128)S(1)} %get-tuple-element.56), channel_id=1, source_target_pairs={{0,8},{1,9},{2,10},{3,11},{4,12},{5,13},{6,14},{7,15},{8,0},{9,1},... | collective-permute-start | bytes 786440 | tf_op jit(solution)/shard_map/ppermute | solution.py:404
  15.8 3.1 %collective-permute-start.1 = (f32[32,2048]{1,0:T(8,128)S(1)}, f32[32,2048]{1,0:T(8,128)S(1)}, u32[]{:S(2)}, u32[]{:S(2)}) collective-permute-start(f32[32,2048]{1,0:T(8,128)S(1)} %get-tuple-element.59), channel_id=1, source_target_pairs={{0,8},{1,9},{2,10},{3,11},{4,12},{5,13},{6,14},{7,15},{8,0},{9,1},... | collective-permute-start | bytes 786440 | tf_op jit(solution)/shard_map/ppermute | solution.py:404
  18.9 3.3 %collective-permute-done.refs_0_ = f32[32,2048]{1,0:T(8,128)S(1)} collective-permute-done((f32[32,2048]{1,0:T(8,128)S(1)}, f32[32,2048]{1,0:T(8,128)S(1)}, u32[]{:S(2)}, u32[]{:S(2)}) %collective-permute-start) | collective-permute-done | bytes 262176 | tf_op jit(solution)/shard_map/ppermute | solution.py:404
  22.9 3.2 %collective-permute-start.3 = (f32[32,2048]{1,0:T(8,128)S(1)}, f32[32,2048]{1,0:T(8,128)S(1)}, u32[]{:S(2)}, u32[]{:S(2)}) collective-permute-start(f32[32,2048]{1,0:T(8,128)S(1)} %get-tuple-element.62), channel_id=1, source_target_pairs={{0,8},{1,9},{2,10},{3,11},{4,12},{5,13},{6,14},{7,15},{8,0},{9,1},... | collective-permute-start | bytes 786440 | tf_op jit(solution)/shard_map/ppermute | solution.py:404
  26.0 1.8 %collective-permute-done.1.refs_0_.refs_1_ = f32[32,2048]{1,0:T(8,128)S(1)} collective-permute-done((f32[32,2048]{1,0:T(8,128)S(1)}, f32[32,2048]{1,0:T(8,128)S(1)}, u32[]{:S(2)}, u32[]{:S(2)}) %collective-permute-start.1) | collective-permute-done | bytes 262176 | tf_op jit(solution)/shard_map/ppermute | solution.py:404
  28.5 3.2 %collective-permute-start.5 = (f32[32,2048]{1,0:T(8,128)S(1)}, f32[32,2048]{1,0:T(8,128)S(1)}, u32[]{:S(2)}, u32[]{:S(2)}) collective-permute-start(f32[32,2048]{1,0:T(8,128)S(1)} %get-tuple-element.65), channel_id=1, source_target_pairs={{0,8},{1,9},{2,10},{3,11},{4,12},{5,13},{6,14},{7,15},{8,0},{9,1},... | collective-permute-start | bytes 786440 | tf_op jit(solution)/shard_map/ppermute | solution.py:404
  31.7 1.8 %collective-permute-done.3.refs_1_.refs_2_ = f32[32,2048]{1,0:T(8,128)S(1)} collective-permute-done((f32[32,2048]{1,0:T(8,128)S(1)}, f32[32,2048]{1,0:T(8,128)S(1)}, u32[]{:S(2)}, u32[]{:S(2)}) %collective-permute-start.3) | collective-permute-done | bytes 262176 | tf_op jit(solution)/shard_map/ppermute | solution.py:404
  34.1 3.2 %collective-permute-start.7 = (f32[32,2048]{1,0:T(8,128)S(1)}, f32[32,2048]{1,0:T(8,128)S(1)}, u32[]{:S(2)}, u32[]{:S(2)}) collective-permute-start(f32[32,2048]{1,0:T(8,128)S(1)} %get-tuple-element.68), channel_id=1, source_target_pairs={{0,8},{1,9},{2,10},{3,11},{4,12},{5,13},{6,14},{7,15},{8,0},{9,1},... | collective-permute-start | bytes 786440 | tf_op jit(solution)/shard_map/ppermute | solution.py:404
  37.3 1.8 %collective-permute-done.5.refs_1_.refs_3_ = f32[32,2048]{1,0:T(8,128)S(1)} collective-permute-done((f32[32,2048]{1,0:T(8,128)S(1)}, f32[32,2048]{1,0:T(8,128)S(1)}, u32[]{:S(2)}, u32[]{:S(2)}) %collective-permute-start.5) | collective-permute-done | bytes 262176 | tf_op jit(solution)/shard_map/ppermute | solution.py:404
  39.7 3.2 %collective-permute-start.9 = (f32[32,2048]{1,0:T(8,128)S(1)}, f32[32,2048]{1,0:T(8,128)S(1)}, u32[]{:S(2)}, u32[]{:S(2)}) collective-permute-start(f32[32,2048]{1,0:T(8,128)S(1)} %get-tuple-element.71), channel_id=1, source_target_pairs={{0,8},{1,9},{2,10},{3,11},{4,12},{5,13},{6,14},{7,15},{8,0},{9,1},... | collective-permute-start | bytes 786440 | tf_op jit(solution)/shard_map/ppermute | solution.py:404
  42.9 1.8 %collective-permute-done.7.refs_2_.refs_4_ = f32[32,2048]{1,0:T(8,128)S(1)} collective-permute-done((f32[32,2048]{1,0:T(8,128)S(1)}, f32[32,2048]{1,0:T(8,128)S(1)}, u32[]{:S(2)}, u32[]{:S(2)}) %collective-permute-start.7) | collective-permute-done | bytes 262176 | tf_op jit(solution)/shard_map/ppermute | solution.py:404
  45.4 3.2 %collective-permute-start.11 = (f32[32,2048]{1,0:T(8,128)S(1)}, f32[32,2048]{1,0:T(8,128)S(1)}, u32[]{:S(2)}, u32[]{:S(2)}) collective-permute-start(f32[32,2048]{1,0:T(8,128)S(1)} %get-tuple-element.74), channel_id=1, source_target_pairs={{0,8},{1,9},{2,10},{3,11},{4,12},{5,13},{6,14},{7,15},{8,0},{9,1},... | collective-permute-start | bytes 786440 | tf_op jit(solution)/shard_map/ppermute | solution.py:404
  48.5 1.8 %collective-permute-done.9.refs_2_.refs_5_ = f32[32,2048]{1,0:T(8,128)S(1)} collective-permute-done((f32[32,2048]{1,0:T(8,128)S(1)}, f32[32,2048]{1,0:T(8,128)S(1)}, u32[]{:S(2)}, u32[]{:S(2)}) %collective-permute-start.9) | collective-permute-done | bytes 262176 | tf_op jit(solution)/shard_map/ppermute | solution.py:404
  51.0 3.2 %collective-permute-start.13 = (f32[32,2048]{1,0:T(8,128)S(1)}, f32[32,2048]{1,0:T(8,128)S(1)}, u32[]{:S(2)}, u32[]{:S(2)}) collective-permute-start(f32[32,2048]{1,0:T(8,128)S(1)} %get-tuple-element.77), channel_id=1, source_target_pairs={{0,8},{1,9},{2,10},{3,11},{4,12},{5,13},{6,14},{7,15},{8,0},{9,1},... | collective-permute-start | bytes 786440 | tf_op jit(solution)/shard_map/ppermute | solution.py:404
  54.2 1.8 %collective-permute-done.11.refs_3_.refs_6_ = f32[32,2048]{1,0:T(8,128)S(1)} collective-permute-done((f32[32,2048]{1,0:T(8,128)S(1)}, f32[32,2048]{1,0:T(8,128)S(1)}, u32[]{:S(2)}, u32[]{:S(2)}) %collective-permute-start.11) | collective-permute-done | bytes 262176 | tf_op jit(solution)/shard_map/ppermute | solution.py:404
  56.6 3.2 %collective-permute-start.15 = (f32[32,2048]{1,0:T(8,128)S(1)}, f32[32,2048]{1,0:T(8,128)S(1)}, u32[]{:S(2)}, u32[]{:S(2)}) collective-permute-start(f32[32,2048]{1,0:T(8,128)S(1)} %get-tuple-element.80), channel_id=1, source_target_pairs={{0,8},{1,9},{2,10},{3,11},{4,12},{5,13},{6,14},{7,15},{8,0},{9,1},... | collective-permute-start | bytes 786440 | tf_op jit(solution)/shard_map/ppermute | solution.py:404
  62.2 3.2 %collective-permute-start.17 = (f32[32,2048]{1,0:T(8,128)S(1)}, f32[32,2048]{1,0:T(8,128)S(1)}, u32[]{:S(2)}, u32[]{:S(2)}) collective-permute-start(f32[32,2048]{1,0:T(8,128)S(1)} %get-tuple-element.83), channel_id=1, source_target_pairs={{0,8},{1,9},{2,10},{3,11},{4,12},{5,13},{6,14},{7,15},{8,0},{9,1},... | collective-permute-start | bytes 786440 | tf_op jit(solution)/shard_map/ppermute | solution.py:404
  65.4 1.7 %collective-permute-done.15.refs_4_.refs_8_ = f32[32,2048]{1,0:T(8,128)S(1)} collective-permute-done((f32[32,2048]{1,0:T(8,128)S(1)}, f32[32,2048]{1,0:T(8,128)S(1)}, u32[]{:S(2)}, u32[]{:S(2)}) %collective-permute-start.15) | collective-permute-done | bytes 262176 | tf_op jit(solution)/shard_map/ppermute | solution.py:404
  67.9 5.1 %collective-permute-start.19 = (f32[32,2048]{1,0:T(8,128)S(1)}, f32[32,2048]{1,0:T(8,128)S(1)}, u32[]{:S(2)}, u32[]{:S(2)}) collective-permute-start(f32[32,2048]{1,0:T(8,128)S(1)} %get-tuple-element.86), channel_id=1, source_target_pairs={{0,8},{1,9},{2,10},{3,11},{4,12},{5,13},{6,14},{7,15},{8,0},{9,1},... | collective-permute-start | bytes 786440 | tf_op jit(solution)/shard_map/ppermute | solution.py:404
  73.8 2.8 %collective-permute-start.21 = (f32[32,2048]{1,0:T(8,128)S(1)}, f32[32,2048]{1,0:T(8,128)S(1)}, u32[]{:S(2)}, u32[]{:S(2)}) collective-permute-start(f32[32,2048]{1,0:T(8,128)S(1)} %get-tuple-element.89), channel_id=1, source_target_pairs={{0,8},{1,9},{2,10},{3,11},{4,12},{5,13},{6,14},{7,15},{8,0},{9,1},... | collective-permute-start | bytes 786440 | tf_op jit(solution)/shard_map/ppermute | solution.py:404
  76.6 2.8 %collective-permute-done.19.refs_10_ = f32[32,2048]{1,0:T(8,128)S(1)} collective-permute-done((f32[32,2048]{1,0:T(8,128)S(1)}, f32[32,2048]{1,0:T(8,128)S(1)}, u32[]{:S(2)}, u32[]{:S(2)}) %collective-permute-start.19) | collective-permute-done | bytes 262176 | tf_op jit(solution)/shard_map/ppermute | solution.py:404
  79.5 4.2 %collective-permute-done.21.refs_11_ = f32[32,2048]{1,0:T(8,128)S(1)} collective-permute-done((f32[32,2048]{1,0:T(8,128)S(1)}, f32[32,2048]{1,0:T(8,128)S(1)}, u32[]{:S(2)}, u32[]{:S(2)}) %collective-permute-start.21) | collective-permute-done | bytes 262176 | tf_op jit(solution)/shard_map/ppermute | solution.py:404
  83.7 7.6 %assemble.1 = (bf16[192,4096]{1,0:T(8,128)(2,1)}, bf16[192,4096]{1,0:T(8,128)(2,1)}, bf16[4096,192]{1,0:T(8,128)(2,1)}, bf16[4096,192]{1,0:T(8,128)(2,1)}, f32[32,512]{1,0:T(8,128)S(1)}) custom-call(s32[2]{0:T(128)S(1)} %pad_add_fusion.here_ref, s32[6]{0:T(128)S(1)} %copy-done.6, s32[6]{0:T(128)S(1)} %copy-done.7, f32[4,32,4096]{2,1,0:T(8,128)S(1)} %copy-done, ...), custom_call_target="tpu_custom_call" | custom-call | flops 1811939328 | bytes 6291456 | tf_op jit(solution)/shard_map/assemble/pallas_call | solution.py:198
  91.4 2.2 %lift.1 = (bf16[4096,192]{1,0:T(8,128)(2,1)S(1)}, bf16[4096,192]{1,0:T(8,128)(2,1)S(1)}) custom-call(bf16[4096,192]{1,0:T(8,128)(2,1)} %get-tuple-element.91.refs_0_, bf16[4096,192]{1,0:T(8,128)(2,1)} %get-tuple-element.92.refs_1_), custom_call_target="tpu_custom_call" | custom-call | bytes 3145728 | tf_op jit(solution)/shard_map/lift/pallas_call | solution.py:279
  95.0 2.7 %collective-permute-start.27 = (f32[32,512]{1,0:T(8,128)S(1)}, f32[32,512]{1,0:T(8,128)S(1)}, u32[]{:S(2)}, u32[]{:S(2)}) collective-permute-start(f32[32,512]{1,0:T(8,128)S(1)} %add.27), channel_id=1, source_target_pairs={{0,6},{1,7},{2,4},{3,5},{4,2},{5,3},{6,0},{7,1},{8,14},{9,15},{10,... | collective-permute-start | bytes 196616 | tf_op jit(solution)/shard_map/ppermute | solution.py:367
  98.5 9.5 %collective-permute-done.27 = f32[32,512]{1,0:T(8,128)S(1)} collective-permute-done((f32[32,512]{1,0:T(8,128)S(1)}, f32[32,512]{1,0:T(8,128)S(1)}, u32[]{:S(2)}, u32[]{:S(2)}) %collective-permute-start.27) | collective-permute-done | bytes 65568 | tf_op jit(solution)/shard_map/ppermute | solution.py:367
  110.3 8.8 %inner_products.1 = (f32[128,384]{1,0:T(8,128)S(1)}, f32[128,384]{1,0:T(8,128)S(1)}, f32[512,4096]{1,0:T(8,128)S(1)}) custom-call(s32[2]{0:T(128)S(1)} %pad_add_fusion.here_ref, f32[512,4096]{1,0:T(8,128)} %bitcast.2.x_ref, bf16[4096,192]{1,0:T(8,128)(2,1)S(1)} %get-tuple-element.93.high_ref, bf16[4096,192]{1,0:T(8,128)(2,1)S(1)} %copy-done.2), custom_call_target="tpu_custom_call" | custom-call | flops 2415919104 | bytes 8388608 | tf_op jit(solution)/shard_map/inner_products/pallas_call | solution.py:315
  121.8 3.5 %merge.1.p_ref = bf16[576,4096]{1,0:T(8,128)(2,1)S(1)} custom-call(f32[32,512]{1,0:T(8,128)S(1)} %add_add_fusion.refs_0_, f32[6,32,32]{2,1,0:T(8,128)S(1)} %copy-done.5, bf16[192,4096]{1,0:T(8,128)(2,1)S(1)} %copy-done.3, bf16[192,4096]{1,0:T(8,128)(2,1)S(1)} %copy-done.4), custom_call_target="tpu_custom_call" | custom-call | flops 905969664 | bytes 6291456 | tf_op jit(solution)/shard_map/merge/pallas_call | solution.py:236
  128.5 1.8 %collective-permute-done.32 = f32[64,384]{1,0:T(8,128)S(1)} collective-permute-done((f32[64,384]{1,0:T(8,128)S(1)}, f32[64,384]{1,0:T(8,128)S(1)}, u32[]{:S(2)}, u32[]{:S(2)}) %collective-permute-start.32) | collective-permute-done | bytes 98336 | tf_op jit(solution)/shard_map/ppermute | solution.py:367
  133.2 6.2 %update.1 = f32[512,4096]{1,0:T(8,128)} custom-call(s32[2]{0:T(128)S(1)} %pad_add_fusion.here_ref, f32[128,384]{1,0:T(8,128)S(1)} %pad_maximum_fusion.mine_ref, f32[128,384]{1,0:T(8,128)S(1)} %collective-permute-done.33.theirs_ref, f32[512,4096]{1,0:T(8,128)S(1)} %get-tuple-element.104.x_ref, bf16[576,4096]{1,0:T(8,128)(2,1)S(1)} %merge.1.p_ref), custom_call_target="tpu_custom_call" | custom-call | flops 2415919104 | bytes 16777216 | tf_op jit(solution)/shard_map/update/pallas_call | solution.py:350
  (82 shorter events, 23.4 us)
Async XLA Ops:
  6.1 102.6 %all-to-all-start = ((f32[8,64,4096]{2,1,0:T(8,128)}), f32[8,64,4096]{2,1,0:T(8,128)}, u32[]{:S(2)}, u32[]{:S(2)}) async-start(f32[8,64,4096]{2,1,0:T(8,128)} %pack.1), calls=%async_computation | async-start | bytes 16777216 | tf_op jit(solution)/shard_map/all_to_all | solution.py:409
  12.1 10.1 %collective-permute-start = (f32[32,2048]{1,0:T(8,128)S(1)}, f32[32,2048]{1,0:T(8,128)S(1)}, u32[]{:S(2)}, u32[]{:S(2)}) collective-permute-start(f32[32,2048]{1,0:T(8,128)S(1)} %get-tuple-element.56), channel_id=1, source_target_pairs={{0,8},{1,9},{2,10},{3,11},{4,12},{5,13},{6,14},{7,15},{8,0},{9,1},... | collective-permute-start | bytes 786440 | tf_op jit(solution)/shard_map/ppermute | solution.py:404
  15.1 7.1 %collective-permute-start.2 = (f32[32,2048]{1,0:T(8,128)S(1)}, f32[32,2048]{1,0:T(8,128)S(1)}, u32[]{:S(2)}, u32[]{:S(2)}) collective-permute-start(f32[32,2048]{1,0:T(8,128)S(1)} %get-tuple-element.57), channel_id=1, source_target_pairs={{0,1},{1,0},{2,3},{3,2},{4,5},{5,4},{6,7},{7,6},{8,16},{9,17},{10,... | collective-permute-start | bytes 786440 | tf_op jit(solution)/shard_map/ppermute | solution.py:404
  15.8 12.0 %collective-permute-start.1 = (f32[32,2048]{1,0:T(8,128)S(1)}, f32[32,2048]{1,0:T(8,128)S(1)}, u32[]{:S(2)}, u32[]{:S(2)}) collective-permute-start(f32[32,2048]{1,0:T(8,128)S(1)} %get-tuple-element.59), channel_id=1, source_target_pairs={{0,8},{1,9},{2,10},{3,11},{4,12},{5,13},{6,14},{7,15},{8,0},{9,1},... | collective-permute-start | bytes 786440 | tf_op jit(solution)/shard_map/ppermute | solution.py:404
  18.9 8.9 %collective-permute-start.4 = (f32[32,2048]{1,0:T(8,128)S(1)}, f32[32,2048]{1,0:T(8,128)S(1)}, u32[]{:S(2)}, u32[]{:S(2)}) collective-permute-start(f32[32,2048]{1,0:T(8,128)S(1)} %get-tuple-element.60), channel_id=1, source_target_pairs={{0,1},{1,0},{2,3},{3,2},{4,5},{5,4},{6,7},{7,6},{8,16},{9,17},{10,... | collective-permute-start | bytes 786440 | tf_op jit(solution)/shard_map/ppermute | solution.py:404
  22.9 10.6 %collective-permute-start.3 = (f32[32,2048]{1,0:T(8,128)S(1)}, f32[32,2048]{1,0:T(8,128)S(1)}, u32[]{:S(2)}, u32[]{:S(2)}) collective-permute-start(f32[32,2048]{1,0:T(8,128)S(1)} %get-tuple-element.62), channel_id=1, source_target_pairs={{0,8},{1,9},{2,10},{3,11},{4,12},{5,13},{6,14},{7,15},{8,0},{9,1},... | collective-permute-start | bytes 786440 | tf_op jit(solution)/shard_map/ppermute | solution.py:404
  26.0 7.4 %collective-permute-start.6 = (f32[32,2048]{1,0:T(8,128)S(1)}, f32[32,2048]{1,0:T(8,128)S(1)}, u32[]{:S(2)}, u32[]{:S(2)}) collective-permute-start(f32[32,2048]{1,0:T(8,128)S(1)} %get-tuple-element.63), channel_id=1, source_target_pairs={{0,1},{1,0},{2,3},{3,2},{4,5},{5,4},{6,7},{7,6},{8,16},{9,17},{10,... | collective-permute-start | bytes 786440 | tf_op jit(solution)/shard_map/ppermute | solution.py:404
  28.5 10.6 %collective-permute-start.5 = (f32[32,2048]{1,0:T(8,128)S(1)}, f32[32,2048]{1,0:T(8,128)S(1)}, u32[]{:S(2)}, u32[]{:S(2)}) collective-permute-start(f32[32,2048]{1,0:T(8,128)S(1)} %get-tuple-element.65), channel_id=1, source_target_pairs={{0,8},{1,9},{2,10},{3,11},{4,12},{5,13},{6,14},{7,15},{8,0},{9,1},... | collective-permute-start | bytes 786440 | tf_op jit(solution)/shard_map/ppermute | solution.py:404
  31.7 7.4 %collective-permute-start.8 = (f32[32,2048]{1,0:T(8,128)S(1)}, f32[32,2048]{1,0:T(8,128)S(1)}, u32[]{:S(2)}, u32[]{:S(2)}) collective-permute-start(f32[32,2048]{1,0:T(8,128)S(1)} %get-tuple-element.66), channel_id=1, source_target_pairs={{0,1},{1,0},{2,3},{3,2},{4,5},{5,4},{6,7},{7,6},{8,16},{9,17},{10,... | collective-permute-start | bytes 786440 | tf_op jit(solution)/shard_map/ppermute | solution.py:404
  34.1 10.6 %collective-permute-start.7 = (f32[32,2048]{1,0:T(8,128)S(1)}, f32[32,2048]{1,0:T(8,128)S(1)}, u32[]{:S(2)}, u32[]{:S(2)}) collective-permute-start(f32[32,2048]{1,0:T(8,128)S(1)} %get-tuple-element.68), channel_id=1, source_target_pairs={{0,8},{1,9},{2,10},{3,11},{4,12},{5,13},{6,14},{7,15},{8,0},{9,1},... | collective-permute-start | bytes 786440 | tf_op jit(solution)/shard_map/ppermute | solution.py:404
  37.3 7.4 %collective-permute-start.10 = (f32[32,2048]{1,0:T(8,128)S(1)}, f32[32,2048]{1,0:T(8,128)S(1)}, u32[]{:S(2)}, u32[]{:S(2)}) collective-permute-start(f32[32,2048]{1,0:T(8,128)S(1)} %get-tuple-element.69), channel_id=1, source_target_pairs={{0,1},{1,0},{2,3},{3,2},{4,5},{5,4},{6,7},{7,6},{8,16},{9,17},{10,... | collective-permute-start | bytes 786440 | tf_op jit(solution)/shard_map/ppermute | solution.py:404
  39.7 10.6 %collective-permute-start.9 = (f32[32,2048]{1,0:T(8,128)S(1)}, f32[32,2048]{1,0:T(8,128)S(1)}, u32[]{:S(2)}, u32[]{:S(2)}) collective-permute-start(f32[32,2048]{1,0:T(8,128)S(1)} %get-tuple-element.71), channel_id=1, source_target_pairs={{0,8},{1,9},{2,10},{3,11},{4,12},{5,13},{6,14},{7,15},{8,0},{9,1},... | collective-permute-start | bytes 786440 | tf_op jit(solution)/shard_map/ppermute | solution.py:404
  42.9 7.4 %collective-permute-start.12 = (f32[32,2048]{1,0:T(8,128)S(1)}, f32[32,2048]{1,0:T(8,128)S(1)}, u32[]{:S(2)}, u32[]{:S(2)}) collective-permute-start(f32[32,2048]{1,0:T(8,128)S(1)} %get-tuple-element.72), channel_id=1, source_target_pairs={{0,1},{1,0},{2,3},{3,2},{4,5},{5,4},{6,7},{7,6},{8,16},{9,17},{10,... | collective-permute-start | bytes 786440 | tf_op jit(solution)/shard_map/ppermute | solution.py:404
  45.4 10.5 %collective-permute-start.11 = (f32[32,2048]{1,0:T(8,128)S(1)}, f32[32,2048]{1,0:T(8,128)S(1)}, u32[]{:S(2)}, u32[]{:S(2)}) collective-permute-start(f32[32,2048]{1,0:T(8,128)S(1)} %get-tuple-element.74), channel_id=1, source_target_pairs={{0,8},{1,9},{2,10},{3,11},{4,12},{5,13},{6,14},{7,15},{8,0},{9,1},... | collective-permute-start | bytes 786440 | tf_op jit(solution)/shard_map/ppermute | solution.py:404
  48.5 7.4 %collective-permute-start.14 = (f32[32,2048]{1,0:T(8,128)S(1)}, f32[32,2048]{1,0:T(8,128)S(1)}, u32[]{:S(2)}, u32[]{:S(2)}) collective-permute-start(f32[32,2048]{1,0:T(8,128)S(1)} %get-tuple-element.75), channel_id=1, source_target_pairs={{0,1},{1,0},{2,3},{3,2},{4,5},{5,4},{6,7},{7,6},{8,16},{9,17},{10,... | collective-permute-start | bytes 786440 | tf_op jit(solution)/shard_map/ppermute | solution.py:404
  51.0 10.5 %collective-permute-start.13 = (f32[32,2048]{1,0:T(8,128)S(1)}, f32[32,2048]{1,0:T(8,128)S(1)}, u32[]{:S(2)}, u32[]{:S(2)}) collective-permute-start(f32[32,2048]{1,0:T(8,128)S(1)} %get-tuple-element.77), channel_id=1, source_target_pairs={{0,8},{1,9},{2,10},{3,11},{4,12},{5,13},{6,14},{7,15},{8,0},{9,1},... | collective-permute-start | bytes 786440 | tf_op jit(solution)/shard_map/ppermute | solution.py:404
  54.1 7.4 %collective-permute-start.16 = (f32[32,2048]{1,0:T(8,128)S(1)}, f32[32,2048]{1,0:T(8,128)S(1)}, u32[]{:S(2)}, u32[]{:S(2)}) collective-permute-start(f32[32,2048]{1,0:T(8,128)S(1)} %get-tuple-element.78), channel_id=1, source_target_pairs={{0,1},{1,0},{2,3},{3,2},{4,5},{5,4},{6,7},{7,6},{8,16},{9,17},{10,... | collective-permute-start | bytes 786440 | tf_op jit(solution)/shard_map/ppermute | solution.py:404
  56.6 10.5 %collective-permute-start.15 = (f32[32,2048]{1,0:T(8,128)S(1)}, f32[32,2048]{1,0:T(8,128)S(1)}, u32[]{:S(2)}, u32[]{:S(2)}) collective-permute-start(f32[32,2048]{1,0:T(8,128)S(1)} %get-tuple-element.80), channel_id=1, source_target_pairs={{0,8},{1,9},{2,10},{3,11},{4,12},{5,13},{6,14},{7,15},{8,0},{9,1},... | collective-permute-start | bytes 786440 | tf_op jit(solution)/shard_map/ppermute | solution.py:404
  59.8 7.4 %collective-permute-start.18 = (f32[32,2048]{1,0:T(8,128)S(1)}, f32[32,2048]{1,0:T(8,128)S(1)}, u32[]{:S(2)}, u32[]{:S(2)}) collective-permute-start(f32[32,2048]{1,0:T(8,128)S(1)} %get-tuple-element.81), channel_id=1, source_target_pairs={{0,1},{1,0},{2,3},{3,2},{4,5},{5,4},{6,7},{7,6},{8,16},{9,17},{10,... | collective-permute-start | bytes 786440 | tf_op jit(solution)/shard_map/ppermute | solution.py:404
  62.2 10.9 %collective-permute-start.17 = (f32[32,2048]{1,0:T(8,128)S(1)}, f32[32,2048]{1,0:T(8,128)S(1)}, u32[]{:S(2)}, u32[]{:S(2)}) collective-permute-start(f32[32,2048]{1,0:T(8,128)S(1)} %get-tuple-element.83), channel_id=1, source_target_pairs={{0,8},{1,9},{2,10},{3,11},{4,12},{5,13},{6,14},{7,15},{8,0},{9,1},... | collective-permute-start | bytes 786440 | tf_op jit(solution)/shard_map/ppermute | solution.py:404
  65.4 7.7 %collective-permute-start.20 = (f32[32,2048]{1,0:T(8,128)S(1)}, f32[32,2048]{1,0:T(8,128)S(1)}, u32[]{:S(2)}, u32[]{:S(2)}) collective-permute-start(f32[32,2048]{1,0:T(8,128)S(1)} %get-tuple-element.84), channel_id=1, source_target_pairs={{0,1},{1,0},{2,3},{3,2},{4,5},{5,4},{6,7},{7,6},{8,16},{9,17},{10,... | collective-permute-start | bytes 786440 | tf_op jit(solution)/shard_map/ppermute | solution.py:404
  67.9 11.6 %collective-permute-start.22 = (f32[32,2048]{1,0:T(8,128)S(1)}, f32[32,2048]{1,0:T(8,128)S(1)}, u32[]{:S(2)}, u32[]{:S(2)}) collective-permute-start(f32[32,2048]{1,0:T(8,128)S(1)} %get-tuple-element.87), channel_id=1, source_target_pairs={{0,1},{1,0},{2,3},{3,2},{4,5},{5,4},{6,7},{7,6},{8,16},{9,17},{10,... | collective-permute-start | bytes 786440 | tf_op jit(solution)/shard_map/ppermute | solution.py:404
  67.9 11.5 %collective-permute-start.19 = (f32[32,2048]{1,0:T(8,128)S(1)}, f32[32,2048]{1,0:T(8,128)S(1)}, u32[]{:S(2)}, u32[]{:S(2)}) collective-permute-start(f32[32,2048]{1,0:T(8,128)S(1)} %get-tuple-element.86), channel_id=1, source_target_pairs={{0,8},{1,9},{2,10},{3,11},{4,12},{5,13},{6,14},{7,15},{8,0},{9,1},... | collective-permute-start | bytes 786440 | tf_op jit(solution)/shard_map/ppermute | solution.py:404
  73.8 9.9 %collective-permute-start.21 = (f32[32,2048]{1,0:T(8,128)S(1)}, f32[32,2048]{1,0:T(8,128)S(1)}, u32[]{:S(2)}, u32[]{:S(2)}) collective-permute-start(f32[32,2048]{1,0:T(8,128)S(1)} %get-tuple-element.89), channel_id=1, source_target_pairs={{0,8},{1,9},{2,10},{3,11},{4,12},{5,13},{6,14},{7,15},{8,0},{9,1},... | collective-permute-start | bytes 786440 | tf_op jit(solution)/shard_map/ppermute | solution.py:404
  76.6 7.0 %collective-permute-start.23 = (f32[32,2048]{1,0:T(8,128)S(1)}, f32[32,2048]{1,0:T(8,128)S(1)}, u32[]{:S(2)}, u32[]{:S(2)}) collective-permute-start(f32[32,2048]{1,0:T(8,128)S(1)} %get-tuple-element.90), channel_id=1, source_target_pairs={{0,1},{1,0},{2,3},{3,2},{4,5},{5,4},{6,7},{7,6},{8,16},{9,17},{10,... | collective-permute-start | bytes 786440 | tf_op jit(solution)/shard_map/ppermute | solution.py:404
  95.0 13.0 %collective-permute-start.27 = (f32[32,512]{1,0:T(8,128)S(1)}, f32[32,512]{1,0:T(8,128)S(1)}, u32[]{:S(2)}, u32[]{:S(2)}) collective-permute-start(f32[32,512]{1,0:T(8,128)S(1)} %add.27), channel_id=1, source_target_pairs={{0,6},{1,7},{2,4},{3,5},{4,2},{5,3},{6,0},{7,1},{8,14},{9,15},{10,... | collective-permute-start | bytes 196616 | tf_op jit(solution)/shard_map/ppermute | solution.py:367
  97.6 11.0 %collective-permute-start.26 = (f32[32,512]{1,0:T(8,128)S(1)}, f32[32,512]{1,0:T(8,128)S(1)}, u32[]{:S(2)}, u32[]{:S(2)}) collective-permute-start(f32[32,512]{1,0:T(8,128)S(1)} %add.27), channel_id=1, source_target_pairs={{0,4},{1,5},{2,6},{3,7},{4,0},{5,1},{6,2},{7,3},{8,12},{9,13},{10,... | collective-permute-start | bytes 196616 | tf_op jit(solution)/shard_map/ppermute | solution.py:367
  98.2 10.5 %collective-permute-start.25 = (f32[32,512]{1,0:T(8,128)S(1)}, f32[32,512]{1,0:T(8,128)S(1)}, u32[]{:S(2)}, u32[]{:S(2)}) collective-permute-start(f32[32,512]{1,0:T(8,128)S(1)} %add.27), channel_id=1, source_target_pairs={{0,2},{1,3},{2,0},{3,1},{4,6},{5,7},{6,4},{7,5},{8,10},{9,11},{10,... | collective-permute-start | bytes 196616 | tf_op jit(solution)/shard_map/ppermute | solution.py:367
  120.7 4.9 %collective-permute-start.31 = (f32[64,384]{1,0:T(8,128)S(1)}, f32[64,384]{1,0:T(8,128)S(1)}, u32[]{:S(2)}, u32[]{:S(2)}) collective-permute-start(f32[64,384]{1,0:T(8,128)S(1)} %get-tuple-element.103), channel_id=1, source_target_pairs={{0,4},{1,5},{2,6},{3,7},{4,0},{5,1},{6,2},{7,3},{8,12},{9,13},{10,... | collective-permute-start | bytes 294920 | tf_op jit(solution)/shard_map/ppermute | solution.py:367
  121.4 5.6 %collective-permute-start.29 = (f32[64,384]{1,0:T(8,128)S(1)}, f32[64,384]{1,0:T(8,128)S(1)}, u32[]{:S(2)}, u32[]{:S(2)}) collective-permute-start(f32[64,384]{1,0:T(8,128)S(1)} %get-tuple-element.102), channel_id=1, source_target_pairs={{0,2},{1,3},{2,0},{3,1},{4,6},{5,7},{6,4},{7,5},{8,10},{9,11},{10,... | collective-permute-start | bytes 294920 | tf_op jit(solution)/shard_map/ppermute | solution.py:367
  125.6 4.7 %collective-permute-start.32 = (f32[64,384]{1,0:T(8,128)S(1)}, f32[64,384]{1,0:T(8,128)S(1)}, u32[]{:S(2)}, u32[]{:S(2)}) collective-permute-start(f32[64,384]{1,0:T(8,128)S(1)} %add.34), channel_id=1, source_target_pairs={{0,2},{1,3},{2,0},{3,1},{4,6},{5,7},{6,4},{7,5},{8,10},{9,11},{10,... | collective-permute-start | bytes 294920 | tf_op jit(solution)/shard_map/ppermute | solution.py:367
  127.0 4.7 %collective-permute-start.30 = (f32[64,384]{1,0:T(8,128)S(1)}, f32[64,384]{1,0:T(8,128)S(1)}, u32[]{:S(2)}, u32[]{:S(2)}) collective-permute-start(f32[64,384]{1,0:T(8,128)S(1)} %add.32), channel_id=1, source_target_pairs={{0,4},{1,5},{2,6},{3,7},{4,0},{5,1},{6,2},{7,3},{8,12},{9,13},{10,... | collective-permute-start | bytes 294920 | tf_op jit(solution)/shard_map/ppermute | solution.py:367
  (11 other events, 70.7 us)

commit v12 on v11

--- a/solution.py
+++ b/solution.py
@@ -71,11 +71,11 @@
                 source = x_ref.at[at, pl.ds(k * ncols, ncols)]
                 into.append(pltpu.make_async_copy(source, held.at[k, at], in_sems.at[i]))
                 out_of.append(pltpu.make_async_copy(held.at[k, at], out_ref.at[k, at], out_sems.at[i]))
-        for i, copy in enumerate(into):
-            copy.start(priority=i % QUEUES)
-        for i, (came, goes) in enumerate(zip(into, out_of)):
+        for copy in into:
+            copy.start()
+        for came, goes in zip(into, out_of):
             came.wait()
-            goes.start(priority=i % QUEUES)
+            goes.start(priority=1)
         for copy in out_of:
             copy.wait()
 
@@ -301,8 +301,8 @@
         for i in range(n_copies):
             at = pl.ds(i * step, step)
             copies.append(pltpu.make_async_copy(x_ref.at[at], held.at[at], sems.at[i]))
-        for i, copy in enumerate(copies):
-            copy.start(priority=i % QUEUES)
+        for copy in copies:
+            copy.start()
         for start, end in zip(cuts[:-1], cuts[1:]):
             for copy in copies[start:end]:
                 copy.wait()
@@ -421,12 +421,14 @@
     odds = list(zip(*[stream[1] for stream in streams]))
     high, low, high_t, low_t, gram = assemble(here, block_place, offsets, householder, evens, odds, n_row)
     x = x.reshape(n_wide * rows, ncols)
-    vecs_t = lift([high_t, low_t])
-    cross = functools.reduce(jnp.add, spread(after(gram + swap(gram, 1, n_wide), *vecs_t), n_wide))
+    vecs_t = lift([after(high_t, x), low_t])
+    cross = spread(gram + swap(gram, 1, n_wide), n_wide)
+    cross[0] = after(cross[0], *vecs_t)
+    cross = functools.reduce(jnp.add, cross)
     changes = merge([cross], wy_factor, (high, low))
 
-    mine, theirs, x = inner_products(here, x, vecs_t)
-    mine = chips_sum(mine + swap(after(theirs, cross), 1, n_wide), n_wide, changes)
+    mine, theirs, x = inner_products(after(here, cross), x, vecs_t)
+    mine = chips_sum(mine + swap(theirs, 1, n_wide), n_wide, changes)
     return update(here, x, mine, swap(mine, 1, n_wide), changes)
 
 

time: 140 us -> 139 us (level)
  local copies, waits for them, and re-layouts: 2.94 us -> 0.05 us
  waiting for transfers between devices: 40.9 us -> 42.4 us
    all_to_all x1, waiting for transfers between devices: 0.01 us -> 10.5 us  [body(): x = lax.all_to_all(piece, 'wide', split_axis=0, concat_axis=0, tiled=True)]
    ppermute x10, waiting for transfers between devices: 16.4 us -> 7.43 us  [swap(): return lax.ppermute(array, 'wide', [(i, i ^ k) for i in range(size)])]
    unnamed x16 -> x12, local copies, waits for them, and re-layouts: 2.92 us -> 0.03 us
where the time goes in v12:
time: 139 us; the launch traced here: 138 us
  starting transfers between devices  52.7 us (38%)
  Pallas kernels  42.5 us (31%)
  waiting for transfers between devices  42.4 us (31%)
    ppermute x24, starting transfers between devices, exchange(): return lax.ppermute(array, ('row', 'wide'), pairs)  39.6 us
    ppermute x24, waiting for transfers between devices, exchange(): return lax.ppermute(array, ('row', 'wide'), pairs)  24.4 us
    all_to_all x1, waiting for transfers between devices, body(): x = lax.all_to_all(piece, 'wide', split_axis=0, concat_axis=0, tiled=True)  10.5 us
    pallas_call x12, Pallas kernels, feed(): pl.pallas_call(kernel, out_shape=[jax.ShapeDtypeStruct((width, cols), jnp...  8.06 us
    pallas_call x1, Pallas kernels, inner_products(): pl.pallas_call(kernel, out_shape=[jax.ShapeDtypeStruct((half // 2, 2 * he...  7.92 us
    ppermute x10, starting transfers between devices, swap(): return lax.ppermute(array, 'wide', [(i, i ^ k) for i in range(size)])  7.77 us
    pallas_call x1, Pallas kernels, assemble(): pl.pallas_call(kernel, out_shape=[pltpu.HBM((height, ncols), jnp.bfloat16...  7.65 us
    ppermute x10, waiting for transfers between devices, swap(): return lax.ppermute(array, 'wide', [(i, i ^ k) for i in range(size)])  7.43 us
  transfers between devices with their start and end apart: 35, of which 18 were waited for; matrix products, arithmetic and copies ran while one was open for 0% of the time, Pallas kernels for 15%

profile of v12, /device:TPU:0, one launch (start us, length us, event | category | flops | bytes accessed | tf_op | source)
XLA Modules:
  0.0 138.3 jit_solution(4924984028164295893)
XLA Ops:
  0.0 7.0 %pack.1 = f32[8,64,4096]{2,1,0:T(8,128)} custom-call(f32[64,32768]{1,0:T(8,128)} %x_ref.1), custom_call_target="tpu_custom_call" | custom-call | bytes 16777216 | tf_op jit(solution)/shard_map/pack/pallas_call | solution.py:82
  7.0 5.3 %all-to-all-start = ((f32[8,64,4096]{2,1,0:T(8,128)}), f32[8,64,4096]{2,1,0:T(8,128)}, u32[]{:S(2)}, u32[]{:S(2)}) async-start(f32[8,64,4096]{2,1,0:T(8,128)} %pack.1), calls=%async_computation | async-start | bytes 16777216 | tf_op jit(solution)/shard_map/all_to_all | solution.py:409
  13.1 2.9 %collective-permute-start = (f32[32,2048]{1,0:T(8,128)S(1)}, f32[32,2048]{1,0:T(8,128)S(1)}, u32[]{:S(2)}, u32[]{:S(2)}) collective-permute-start(f32[32,2048]{1,0:T(8,128)S(1)} %get-tuple-element.57), channel_id=1, source_target_pairs={{0,8},{1,9},{2,10},{3,11},{4,12},{5,13},{6,14},{7,15},{8,0},{9,1},... | collective-permute-start | bytes 786440 | tf_op jit(solution)/shard_map/ppermute | solution.py:404
  16.7 3.1 %collective-permute-start.1 = (f32[32,2048]{1,0:T(8,128)S(1)}, f32[32,2048]{1,0:T(8,128)S(1)}, u32[]{:S(2)}, u32[]{:S(2)}) collective-permute-start(f32[32,2048]{1,0:T(8,128)S(1)} %get-tuple-element.60), channel_id=1, source_target_pairs={{0,8},{1,9},{2,10},{3,11},{4,12},{5,13},{6,14},{7,15},{8,0},{9,1},... | collective-permute-start | bytes 786440 | tf_op jit(solution)/shard_map/ppermute | solution.py:404
  19.9 3.3 %collective-permute-done.refs_0_ = f32[32,2048]{1,0:T(8,128)S(1)} collective-permute-done((f32[32,2048]{1,0:T(8,128)S(1)}, f32[32,2048]{1,0:T(8,128)S(1)}, u32[]{:S(2)}, u32[]{:S(2)}) %collective-permute-start) | collective-permute-done | bytes 262176 | tf_op jit(solution)/shard_map/ppermute | solution.py:404
  23.8 3.2 %collective-permute-start.3 = (f32[32,2048]{1,0:T(8,128)S(1)}, f32[32,2048]{1,0:T(8,128)S(1)}, u32[]{:S(2)}, u32[]{:S(2)}) collective-permute-start(f32[32,2048]{1,0:T(8,128)S(1)} %get-tuple-element.63), channel_id=1, source_target_pairs={{0,8},{1,9},{2,10},{3,11},{4,12},{5,13},{6,14},{7,15},{8,0},{9,1},... | collective-permute-start | bytes 786440 | tf_op jit(solution)/shard_map/ppermute | solution.py:404
  27.0 1.8 %collective-permute-done.1.refs_0_.refs_1_ = f32[32,2048]{1,0:T(8,128)S(1)} collective-permute-done((f32[32,2048]{1,0:T(8,128)S(1)}, f32[32,2048]{1,0:T(8,128)S(1)}, u32[]{:S(2)}, u32[]{:S(2)}) %collective-permute-start.1) | collective-permute-done | bytes 262176 | tf_op jit(solution)/shard_map/ppermute | solution.py:404
  29.5 3.2 %collective-permute-start.5 = (f32[32,2048]{1,0:T(8,128)S(1)}, f32[32,2048]{1,0:T(8,128)S(1)}, u32[]{:S(2)}, u32[]{:S(2)}) collective-permute-start(f32[32,2048]{1,0:T(8,128)S(1)} %get-tuple-element.66), channel_id=1, source_target_pairs={{0,8},{1,9},{2,10},{3,11},{4,12},{5,13},{6,14},{7,15},{8,0},{9,1},... | collective-permute-start | bytes 786440 | tf_op jit(solution)/shard_map/ppermute | solution.py:404
  32.6 1.8 %collective-permute-done.3.refs_1_.refs_2_ = f32[32,2048]{1,0:T(8,128)S(1)} collective-permute-done((f32[32,2048]{1,0:T(8,128)S(1)}, f32[32,2048]{1,0:T(8,128)S(1)}, u32[]{:S(2)}, u32[]{:S(2)}) %collective-permute-start.3) | collective-permute-done | bytes 262176 | tf_op jit(solution)/shard_map/ppermute | solution.py:404
  35.1 3.2 %collective-permute-start.7 = (f32[32,2048]{1,0:T(8,128)S(1)}, f32[32,2048]{1,0:T(8,128)S(1)}, u32[]{:S(2)}, u32[]{:S(2)}) collective-permute-start(f32[32,2048]{1,0:T(8,128)S(1)} %get-tuple-element.69), channel_id=1, source_target_pairs={{0,8},{1,9},{2,10},{3,11},{4,12},{5,13},{6,14},{7,15},{8,0},{9,1},... | collective-permute-start | bytes 786440 | tf_op jit(solution)/shard_map/ppermute | solution.py:404
  38.3 1.8 %collective-permute-done.5.refs_1_.refs_3_ = f32[32,2048]{1,0:T(8,128)S(1)} collective-permute-done((f32[32,2048]{1,0:T(8,128)S(1)}, f32[32,2048]{1,0:T(8,128)S(1)}, u32[]{:S(2)}, u32[]{:S(2)}) %collective-permute-start.5) | collective-permute-done | bytes 262176 | tf_op jit(solution)/shard_map/ppermute | solution.py:404
  40.7 3.2 %collective-permute-start.9 = (f32[32,2048]{1,0:T(8,128)S(1)}, f32[32,2048]{1,0:T(8,128)S(1)}, u32[]{:S(2)}, u32[]{:S(2)}) collective-permute-start(f32[32,2048]{1,0:T(8,128)S(1)} %get-tuple-element.72), channel_id=1, source_target_pairs={{0,8},{1,9},{2,10},{3,11},{4,12},{5,13},{6,14},{7,15},{8,0},{9,1},... | collective-permute-start | bytes 786440 | tf_op jit(solution)/shard_map/ppermute | solution.py:404
  43.9 1.8 %collective-permute-done.7.refs_2_.refs_4_ = f32[32,2048]{1,0:T(8,128)S(1)} collective-permute-done((f32[32,2048]{1,0:T(8,128)S(1)}, f32[32,2048]{1,0:T(8,128)S(1)}, u32[]{:S(2)}, u32[]{:S(2)}) %collective-permute-start.7) | collective-permute-done | bytes 262176 | tf_op jit(solution)/shard_map/ppermute | solution.py:404
  46.3 3.2 %collective-permute-start.11 = (f32[32,2048]{1,0:T(8,128)S(1)}, f32[32,2048]{1,0:T(8,128)S(1)}, u32[]{:S(2)}, u32[]{:S(2)}) collective-permute-start(f32[32,2048]{1,0:T(8,128)S(1)} %get-tuple-element.75), channel_id=1, source_target_pairs={{0,8},{1,9},{2,10},{3,11},{4,12},{5,13},{6,14},{7,15},{8,0},{9,1},... | collective-permute-start | bytes 786440 | tf_op jit(solution)/shard_map/ppermute | solution.py:404
  49.5 1.8 %collective-permute-done.9.refs_2_.refs_5_ = f32[32,2048]{1,0:T(8,128)S(1)} collective-permute-done((f32[32,2048]{1,0:T(8,128)S(1)}, f32[32,2048]{1,0:T(8,128)S(1)}, u32[]{:S(2)}, u32[]{:S(2)}) %collective-permute-start.9) | collective-permute-done | bytes 262176 | tf_op jit(solution)/shard_map/ppermute | solution.py:404
  51.9 3.2 %collective-permute-start.13 = (f32[32,2048]{1,0:T(8,128)S(1)}, f32[32,2048]{1,0:T(8,128)S(1)}, u32[]{:S(2)}, u32[]{:S(2)}) collective-permute-start(f32[32,2048]{1,0:T(8,128)S(1)} %get-tuple-element.78), channel_id=1, source_target_pairs={{0,8},{1,9},{2,10},{3,11},{4,12},{5,13},{6,14},{7,15},{8,0},{9,1},... | collective-permute-start | bytes 786440 | tf_op jit(solution)/shard_map/ppermute | solution.py:404
  55.1 1.8 %collective-permute-done.11.refs_3_.refs_6_ = f32[32,2048]{1,0:T(8,128)S(1)} collective-permute-done((f32[32,2048]{1,0:T(8,128)S(1)}, f32[32,2048]{1,0:T(8,128)S(1)}, u32[]{:S(2)}, u32[]{:S(2)}) %collective-permute-start.11) | collective-permute-done | bytes 262176 | tf_op jit(solution)/shard_map/ppermute | solution.py:404
  57.6 3.2 %collective-permute-start.15 = (f32[32,2048]{1,0:T(8,128)S(1)}, f32[32,2048]{1,0:T(8,128)S(1)}, u32[]{:S(2)}, u32[]{:S(2)}) collective-permute-start(f32[32,2048]{1,0:T(8,128)S(1)} %get-tuple-element.81), channel_id=1, source_target_pairs={{0,8},{1,9},{2,10},{3,11},{4,12},{5,13},{6,14},{7,15},{8,0},{9,1},... | collective-permute-start | bytes 786440 | tf_op jit(solution)/shard_map/ppermute | solution.py:404
  63.2 3.2 %collective-permute-start.17 = (f32[32,2048]{1,0:T(8,128)S(1)}, f32[32,2048]{1,0:T(8,128)S(1)}, u32[]{:S(2)}, u32[]{:S(2)}) collective-permute-start(f32[32,2048]{1,0:T(8,128)S(1)} %get-tuple-element.84), channel_id=1, source_target_pairs={{0,8},{1,9},{2,10},{3,11},{4,12},{5,13},{6,14},{7,15},{8,0},{9,1},... | collective-permute-start | bytes 786440 | tf_op jit(solution)/shard_map/ppermute | solution.py:404
  66.4 1.7 %collective-permute-done.15.refs_4_.refs_8_ = f32[32,2048]{1,0:T(8,128)S(1)} collective-permute-done((f32[32,2048]{1,0:T(8,128)S(1)}, f32[32,2048]{1,0:T(8,128)S(1)}, u32[]{:S(2)}, u32[]{:S(2)}) %collective-permute-start.15) | collective-permute-done | bytes 262176 | tf_op jit(solution)/shard_map/ppermute | solution.py:404
  68.9 5.1 %collective-permute-start.19 = (f32[32,2048]{1,0:T(8,128)S(1)}, f32[32,2048]{1,0:T(8,128)S(1)}, u32[]{:S(2)}, u32[]{:S(2)}) collective-permute-start(f32[32,2048]{1,0:T(8,128)S(1)} %get-tuple-element.87), channel_id=1, source_target_pairs={{0,8},{1,9},{2,10},{3,11},{4,12},{5,13},{6,14},{7,15},{8,0},{9,1},... | collective-permute-start | bytes 786440 | tf_op jit(solution)/shard_map/ppermute | solution.py:404
  74.8 2.8 %collective-permute-start.21 = (f32[32,2048]{1,0:T(8,128)S(1)}, f32[32,2048]{1,0:T(8,128)S(1)}, u32[]{:S(2)}, u32[]{:S(2)}) collective-permute-start(f32[32,2048]{1,0:T(8,128)S(1)} %get-tuple-element.90), channel_id=1, source_target_pairs={{0,8},{1,9},{2,10},{3,11},{4,12},{5,13},{6,14},{7,15},{8,0},{9,1},... | collective-permute-start | bytes 786440 | tf_op jit(solution)/shard_map/ppermute | solution.py:404
  77.6 2.8 %collective-permute-done.19.refs_10_ = f32[32,2048]{1,0:T(8,128)S(1)} collective-permute-done((f32[32,2048]{1,0:T(8,128)S(1)}, f32[32,2048]{1,0:T(8,128)S(1)}, u32[]{:S(2)}, u32[]{:S(2)}) %collective-permute-start.19) | collective-permute-done | bytes 262176 | tf_op jit(solution)/shard_map/ppermute | solution.py:404
  80.4 4.2 %collective-permute-done.21.refs_11_ = f32[32,2048]{1,0:T(8,128)S(1)} collective-permute-done((f32[32,2048]{1,0:T(8,128)S(1)}, f32[32,2048]{1,0:T(8,128)S(1)}, u32[]{:S(2)}, u32[]{:S(2)}) %collective-permute-start.21) | collective-permute-done | bytes 262176 | tf_op jit(solution)/shard_map/ppermute | solution.py:404
  84.6 7.6 %assemble.1 = (bf16[192,4096]{1,0:T(8,128)(2,1)}, bf16[192,4096]{1,0:T(8,128)(2,1)}, bf16[4096,192]{1,0:T(8,128)(2,1)}, bf16[4096,192]{1,0:T(8,128)(2,1)}, f32[32,512]{1,0:T(8,128)S(1)}) custom-call(s32[2]{0:T(128)S(1)} %pad_add_fusion.here_ref, s32[6]{0:T(128)S(1)} %copy-done.4, s32[6]{0:T(128)S(1)} %copy-done.5, f32[4,32,4096]{2,1,0:T(8,128)S(1)} %copy-done, ...), custom_call_target="tpu_custom_call" | custom-call | flops 1811939328 | bytes 6291456 | tf_op jit(solution)/shard_map/assemble/pallas_call | solution.py:198
  93.6 2.7 %collective-permute-start.27 = (f32[32,512]{1,0:T(8,128)S(1)}, f32[32,512]{1,0:T(8,128)S(1)}, u32[]{:S(2)}, u32[]{:S(2)}) collective-permute-start(f32[32,512]{1,0:T(8,128)S(1)} %add.27), channel_id=1, source_target_pairs={{0,6},{1,7},{2,4},{3,5},{4,2},{5,3},{6,0},{7,1},{8,14},{9,15},{10,... | collective-permute-start | bytes 196616 | tf_op jit(solution)/shard_map/ppermute | solution.py:367
  97.2 10.5 %all-to-all-done = f32[8,64,4096]{2,1,0:T(8,128)} async-done(((f32[8,64,4096]{2,1,0:T(8,128)}), f32[8,64,4096]{2,1,0:T(8,128)}, u32[]{:S(2)}, u32[]{:S(2)}) %all-to-all-start) | async-done | bytes 8388640 | tf_op jit(solution)/shard_map/all_to_all | solution.py:409
  107.7 2.2 %lift.1 = (bf16[4096,192]{1,0:T(8,128)(2,1)S(1)}, bf16[4096,192]{1,0:T(8,128)(2,1)S(1)}) custom-call(bf16[4096,192]{1,0:T(8,128)(2,1)} %get-tuple-element.94.refs_0_, bf16[4096,192]{1,0:T(8,128)(2,1)} %get-tuple-element.95.refs_1_), custom_call_target="tpu_custom_call" | custom-call | bytes 3145728 | tf_op jit(solution)/shard_map/lift/pallas_call | solution.py:279
  110.1 7.9 %inner_products.1 = (f32[128,384]{1,0:T(8,128)S(1)}, f32[128,384]{1,0:T(8,128)S(1)}, f32[512,4096]{1,0:T(8,128)S(1)}) custom-call(s32[2]{0:T(128)S(1)} %pad_add_fusion.here_ref, f32[512,4096]{1,0:T(8,128)} %bitcast.2.x_ref, bf16[4096,192]{1,0:T(8,128)(2,1)S(1)} %get-tuple-element.96.high_ref, bf16[4096,192]{1,0:T(8,128)(2,1)S(1)} %get-tuple-element.97.low_ref), custom_call_target="tpu_custom_call" | custom-call | flops 2415919104 | bytes 8388608 | tf_op jit(solution)/shard_map/inner_products/pallas_call | solution.py:315
  120.7 3.5 %merge.1.p_ref = bf16[576,4096]{1,0:T(8,128)(2,1)S(1)} custom-call(f32[32,512]{1,0:T(8,128)S(1)} %add_add_fusion.refs_0_, f32[6,32,32]{2,1,0:T(8,128)S(1)} %copy-done.3, bf16[192,4096]{1,0:T(8,128)(2,1)S(1)} %copy-done.1, bf16[192,4096]{1,0:T(8,128)(2,1)S(1)} %copy-done.2), custom_call_target="tpu_custom_call" | custom-call | flops 905969664 | bytes 6291456 | tf_op jit(solution)/shard_map/merge/pallas_call | solution.py:236
  127.3 1.8 %collective-permute-done.32 = f32[64,384]{1,0:T(8,128)S(1)} collective-permute-done((f32[64,384]{1,0:T(8,128)S(1)}, f32[64,384]{1,0:T(8,128)S(1)}, u32[]{:S(2)}, u32[]{:S(2)}) %collective-permute-start.32) | collective-permute-done | bytes 98336 | tf_op jit(solution)/shard_map/ppermute | solution.py:367
  132.0 6.2 %update.1 = f32[512,4096]{1,0:T(8,128)} custom-call(s32[2]{0:T(128)S(1)} %pad_add_fusion.here_ref, f32[128,384]{1,0:T(8,128)S(1)} %pad_maximum_fusion.mine_ref, f32[128,384]{1,0:T(8,128)S(1)} %collective-permute-done.33.theirs_ref, f32[512,4096]{1,0:T(8,128)S(1)} %get-tuple-element.106.x_ref, bf16[576,4096]{1,0:T(8,128)(2,1)S(1)} %merge.1.p_ref), custom_call_target="tpu_custom_call" | custom-call | flops 2415919104 | bytes 16777216 | tf_op jit(solution)/shard_map/update/pallas_call | solution.py:350
  (78 shorter events, 21.0 us)
Async XLA Ops:
  7.0 100.7 %all-to-all-start = ((f32[8,64,4096]{2,1,0:T(8,128)}), f32[8,64,4096]{2,1,0:T(8,128)}, u32[]{:S(2)}, u32[]{:S(2)}) async-start(f32[8,64,4096]{2,1,0:T(8,128)} %pack.1), calls=%async_computation | async-start | bytes 16777216 | tf_op jit(solution)/shard_map/all_to_all | solution.py:409
  13.1 10.1 %collective-permute-start = (f32[32,2048]{1,0:T(8,128)S(1)}, f32[32,2048]{1,0:T(8,128)S(1)}, u32[]{:S(2)}, u32[]{:S(2)}) collective-permute-start(f32[32,2048]{1,0:T(8,128)S(1)} %get-tuple-element.57), channel_id=1, source_target_pairs={{0,8},{1,9},{2,10},{3,11},{4,12},{5,13},{6,14},{7,15},{8,0},{9,1},... | collective-permute-start | bytes 786440 | tf_op jit(solution)/shard_map/ppermute | solution.py:404
  16.0 7.1 %collective-permute-start.2 = (f32[32,2048]{1,0:T(8,128)S(1)}, f32[32,2048]{1,0:T(8,128)S(1)}, u32[]{:S(2)}, u32[]{:S(2)}) collective-permute-start(f32[32,2048]{1,0:T(8,128)S(1)} %get-tuple-element.58), channel_id=1, source_target_pairs={{0,1},{1,0},{2,3},{3,2},{4,5},{5,4},{6,7},{7,6},{8,16},{9,17},{10,... | collective-permute-start | bytes 786440 | tf_op jit(solution)/shard_map/ppermute | solution.py:404
  16.7 12.0 %collective-permute-start.1 = (f32[32,2048]{1,0:T(8,128)S(1)}, f32[32,2048]{1,0:T(8,128)S(1)}, u32[]{:S(2)}, u32[]{:S(2)}) collective-permute-start(f32[32,2048]{1,0:T(8,128)S(1)} %get-tuple-element.60), channel_id=1, source_target_pairs={{0,8},{1,9},{2,10},{3,11},{4,12},{5,13},{6,14},{7,15},{8,0},{9,1},... | collective-permute-start | bytes 786440 | tf_op jit(solution)/shard_map/ppermute | solution.py:404
  19.9 8.9 %collective-permute-start.4 = (f32[32,2048]{1,0:T(8,128)S(1)}, f32[32,2048]{1,0:T(8,128)S(1)}, u32[]{:S(2)}, u32[]{:S(2)}) collective-permute-start(f32[32,2048]{1,0:T(8,128)S(1)} %get-tuple-element.61), channel_id=1, source_target_pairs={{0,1},{1,0},{2,3},{3,2},{4,5},{5,4},{6,7},{7,6},{8,16},{9,17},{10,... | collective-permute-start | bytes 786440 | tf_op jit(solution)/shard_map/ppermute | solution.py:404
  23.8 10.6 %collective-permute-start.3 = (f32[32,2048]{1,0:T(8,128)S(1)}, f32[32,2048]{1,0:T(8,128)S(1)}, u32[]{:S(2)}, u32[]{:S(2)}) collective-permute-start(f32[32,2048]{1,0:T(8,128)S(1)} %get-tuple-element.63), channel_id=1, source_target_pairs={{0,8},{1,9},{2,10},{3,11},{4,12},{5,13},{6,14},{7,15},{8,0},{9,1},... | collective-permute-start | bytes 786440 | tf_op jit(solution)/shard_map/ppermute | solution.py:404
  27.0 7.4 %collective-permute-start.6 = (f32[32,2048]{1,0:T(8,128)S(1)}, f32[32,2048]{1,0:T(8,128)S(1)}, u32[]{:S(2)}, u32[]{:S(2)}) collective-permute-start(f32[32,2048]{1,0:T(8,128)S(1)} %get-tuple-element.64), channel_id=1, source_target_pairs={{0,1},{1,0},{2,3},{3,2},{4,5},{5,4},{6,7},{7,6},{8,16},{9,17},{10,... | collective-permute-start | bytes 786440 | tf_op jit(solution)/shard_map/ppermute | solution.py:404
  29.5 10.6 %collective-permute-start.5 = (f32[32,2048]{1,0:T(8,128)S(1)}, f32[32,2048]{1,0:T(8,128)S(1)}, u32[]{:S(2)}, u32[]{:S(2)}) collective-permute-start(f32[32,2048]{1,0:T(8,128)S(1)} %get-tuple-element.66), channel_id=1, source_target_pairs={{0,8},{1,9},{2,10},{3,11},{4,12},{5,13},{6,14},{7,15},{8,0},{9,1},... | collective-permute-start | bytes 786440 | tf_op jit(solution)/shard_map/ppermute | solution.py:404
  32.6 7.4 %collective-permute-start.8 = (f32[32,2048]{1,0:T(8,128)S(1)}, f32[32,2048]{1,0:T(8,128)S(1)}, u32[]{:S(2)}, u32[]{:S(2)}) collective-permute-start(f32[32,2048]{1,0:T(8,128)S(1)} %get-tuple-element.67), channel_id=1, source_target_pairs={{0,1},{1,0},{2,3},{3,2},{4,5},{5,4},{6,7},{7,6},{8,16},{9,17},{10,... | collective-permute-start | bytes 786440 | tf_op jit(solution)/shard_map/ppermute | solution.py:404
  35.1 10.6 %collective-permute-start.7 = (f32[32,2048]{1,0:T(8,128)S(1)}, f32[32,2048]{1,0:T(8,128)S(1)}, u32[]{:S(2)}, u32[]{:S(2)}) collective-permute-start(f32[32,2048]{1,0:T(8,128)S(1)} %get-tuple-element.69), channel_id=1, source_target_pairs={{0,8},{1,9},{2,10},{3,11},{4,12},{5,13},{6,14},{7,15},{8,0},{9,1},... | collective-permute-start | bytes 786440 | tf_op jit(solution)/shard_map/ppermute | solution.py:404
  38.2 7.4 %collective-permute-start.10 = (f32[32,2048]{1,0:T(8,128)S(1)}, f32[32,2048]{1,0:T(8,128)S(1)}, u32[]{:S(2)}, u32[]{:S(2)}) collective-permute-start(f32[32,2048]{1,0:T(8,128)S(1)} %get-tuple-element.70), channel_id=1, source_target_pairs={{0,1},{1,0},{2,3},{3,2},{4,5},{5,4},{6,7},{7,6},{8,16},{9,17},{10,... | collective-permute-start | bytes 786440 | tf_op jit(solution)/shard_map/ppermute | solution.py:404
  40.7 10.6 %collective-permute-start.9 = (f32[32,2048]{1,0:T(8,128)S(1)}, f32[32,2048]{1,0:T(8,128)S(1)}, u32[]{:S(2)}, u32[]{:S(2)}) collective-permute-start(f32[32,2048]{1,0:T(8,128)S(1)} %get-tuple-element.72), channel_id=1, source_target_pairs={{0,8},{1,9},{2,10},{3,11},{4,12},{5,13},{6,14},{7,15},{8,0},{9,1},... | collective-permute-start | bytes 786440 | tf_op jit(solution)/shard_map/ppermute | solution.py:404
  43.9 7.4 %collective-permute-start.12 = (f32[32,2048]{1,0:T(8,128)S(1)}, f32[32,2048]{1,0:T(8,128)S(1)}, u32[]{:S(2)}, u32[]{:S(2)}) collective-permute-start(f32[32,2048]{1,0:T(8,128)S(1)} %get-tuple-element.73), channel_id=1, source_target_pairs={{0,1},{1,0},{2,3},{3,2},{4,5},{5,4},{6,7},{7,6},{8,16},{9,17},{10,... | collective-permute-start | bytes 786440 | tf_op jit(solution)/shard_map/ppermute | solution.py:404
  46.3 10.5 %collective-permute-start.11 = (f32[32,2048]{1,0:T(8,128)S(1)}, f32[32,2048]{1,0:T(8,128)S(1)}, u32[]{:S(2)}, u32[]{:S(2)}) collective-permute-start(f32[32,2048]{1,0:T(8,128)S(1)} %get-tuple-element.75), channel_id=1, source_target_pairs={{0,8},{1,9},{2,10},{3,11},{4,12},{5,13},{6,14},{7,15},{8,0},{9,1},... | collective-permute-start | bytes 786440 | tf_op jit(solution)/shard_map/ppermute | solution.py:404
  49.5 7.4 %collective-permute-start.14 = (f32[32,2048]{1,0:T(8,128)S(1)}, f32[32,2048]{1,0:T(8,128)S(1)}, u32[]{:S(2)}, u32[]{:S(2)}) collective-permute-start(f32[32,2048]{1,0:T(8,128)S(1)} %get-tuple-element.76), channel_id=1, source_target_pairs={{0,1},{1,0},{2,3},{3,2},{4,5},{5,4},{6,7},{7,6},{8,16},{9,17},{10,... | collective-permute-start | bytes 786440 | tf_op jit(solution)/shard_map/ppermute | solution.py:404
  51.9 10.5 %collective-permute-start.13 = (f32[32,2048]{1,0:T(8,128)S(1)}, f32[32,2048]{1,0:T(8,128)S(1)}, u32[]{:S(2)}, u32[]{:S(2)}) collective-permute-start(f32[32,2048]{1,0:T(8,128)S(1)} %get-tuple-element.78), channel_id=1, source_target_pairs={{0,8},{1,9},{2,10},{3,11},{4,12},{5,13},{6,14},{7,15},{8,0},{9,1},... | collective-permute-start | bytes 786440 | tf_op jit(solution)/shard_map/ppermute | solution.py:404
  55.1 7.4 %collective-permute-start.16 = (f32[32,2048]{1,0:T(8,128)S(1)}, f32[32,2048]{1,0:T(8,128)S(1)}, u32[]{:S(2)}, u32[]{:S(2)}) collective-permute-start(f32[32,2048]{1,0:T(8,128)S(1)} %get-tuple-element.79), channel_id=1, source_target_pairs={{0,1},{1,0},{2,3},{3,2},{4,5},{5,4},{6,7},{7,6},{8,16},{9,17},{10,... | collective-permute-start | bytes 786440 | tf_op jit(solution)/shard_map/ppermute | solution.py:404
  57.6 10.5 %collective-permute-start.15 = (f32[32,2048]{1,0:T(8,128)S(1)}, f32[32,2048]{1,0:T(8,128)S(1)}, u32[]{:S(2)}, u32[]{:S(2)}) collective-permute-start(f32[32,2048]{1,0:T(8,128)S(1)} %get-tuple-element.81), channel_id=1, source_target_pairs={{0,8},{1,9},{2,10},{3,11},{4,12},{5,13},{6,14},{7,15},{8,0},{9,1},... | collective-permute-start | bytes 786440 | tf_op jit(solution)/shard_map/ppermute | solution.py:404
  60.7 7.4 %collective-permute-start.18 = (f32[32,2048]{1,0:T(8,128)S(1)}, f32[32,2048]{1,0:T(8,128)S(1)}, u32[]{:S(2)}, u32[]{:S(2)}) collective-permute-start(f32[32,2048]{1,0:T(8,128)S(1)} %get-tuple-element.82), channel_id=1, source_target_pairs={{0,1},{1,0},{2,3},{3,2},{4,5},{5,4},{6,7},{7,6},{8,16},{9,17},{10,... | collective-permute-start | bytes 786440 | tf_op jit(solution)/shard_map/ppermute | solution.py:404
  63.2 10.9 %collective-permute-start.17 = (f32[32,2048]{1,0:T(8,128)S(1)}, f32[32,2048]{1,0:T(8,128)S(1)}, u32[]{:S(2)}, u32[]{:S(2)}) collective-permute-start(f32[32,2048]{1,0:T(8,128)S(1)} %get-tuple-element.84), channel_id=1, source_target_pairs={{0,8},{1,9},{2,10},{3,11},{4,12},{5,13},{6,14},{7,15},{8,0},{9,1},... | collective-permute-start | bytes 786440 | tf_op jit(solution)/shard_map/ppermute | solution.py:404
  66.4 7.7 %collective-permute-start.20 = (f32[32,2048]{1,0:T(8,128)S(1)}, f32[32,2048]{1,0:T(8,128)S(1)}, u32[]{:S(2)}, u32[]{:S(2)}) collective-permute-start(f32[32,2048]{1,0:T(8,128)S(1)} %get-tuple-element.85), channel_id=1, source_target_pairs={{0,1},{1,0},{2,3},{3,2},{4,5},{5,4},{6,7},{7,6},{8,16},{9,17},{10,... | collective-permute-start | bytes 786440 | tf_op jit(solution)/shard_map/ppermute | solution.py:404
  68.8 11.6 %collective-permute-start.22 = (f32[32,2048]{1,0:T(8,128)S(1)}, f32[32,2048]{1,0:T(8,128)S(1)}, u32[]{:S(2)}, u32[]{:S(2)}) collective-permute-start(f32[32,2048]{1,0:T(8,128)S(1)} %get-tuple-element.88), channel_id=1, source_target_pairs={{0,1},{1,0},{2,3},{3,2},{4,5},{5,4},{6,7},{7,6},{8,16},{9,17},{10,... | collective-permute-start | bytes 786440 | tf_op jit(solution)/shard_map/ppermute | solution.py:404
  68.9 11.5 %collective-permute-start.19 = (f32[32,2048]{1,0:T(8,128)S(1)}, f32[32,2048]{1,0:T(8,128)S(1)}, u32[]{:S(2)}, u32[]{:S(2)}) collective-permute-start(f32[32,2048]{1,0:T(8,128)S(1)} %get-tuple-element.87), channel_id=1, source_target_pairs={{0,8},{1,9},{2,10},{3,11},{4,12},{5,13},{6,14},{7,15},{8,0},{9,1},... | collective-permute-start | bytes 786440 | tf_op jit(solution)/shard_map/ppermute | solution.py:404
  74.8 9.9 %collective-permute-start.21 = (f32[32,2048]{1,0:T(8,128)S(1)}, f32[32,2048]{1,0:T(8,128)S(1)}, u32[]{:S(2)}, u32[]{:S(2)}) collective-permute-start(f32[32,2048]{1,0:T(8,128)S(1)} %get-tuple-element.90), channel_id=1, source_target_pairs={{0,8},{1,9},{2,10},{3,11},{4,12},{5,13},{6,14},{7,15},{8,0},{9,1},... | collective-permute-start | bytes 786440 | tf_op jit(solution)/shard_map/ppermute | solution.py:404
  77.6 7.0 %collective-permute-start.23 = (f32[32,2048]{1,0:T(8,128)S(1)}, f32[32,2048]{1,0:T(8,128)S(1)}, u32[]{:S(2)}, u32[]{:S(2)}) collective-permute-start(f32[32,2048]{1,0:T(8,128)S(1)} %get-tuple-element.91), channel_id=1, source_target_pairs={{0,1},{1,0},{2,3},{3,2},{4,5},{5,4},{6,7},{7,6},{8,16},{9,17},{10,... | collective-permute-start | bytes 786440 | tf_op jit(solution)/shard_map/ppermute | solution.py:404
  93.6 16.3 %collective-permute-start.27 = (f32[32,512]{1,0:T(8,128)S(1)}, f32[32,512]{1,0:T(8,128)S(1)}, u32[]{:S(2)}, u32[]{:S(2)}) collective-permute-start(f32[32,512]{1,0:T(8,128)S(1)} %add.27), channel_id=1, source_target_pairs={{0,6},{1,7},{2,4},{3,5},{4,2},{5,3},{6,0},{7,1},{8,14},{9,15},{10,... | collective-permute-start | bytes 196616 | tf_op jit(solution)/shard_map/ppermute | solution.py:367
  96.3 13.7 %collective-permute-start.26 = (f32[32,512]{1,0:T(8,128)S(1)}, f32[32,512]{1,0:T(8,128)S(1)}, u32[]{:S(2)}, u32[]{:S(2)}) collective-permute-start(f32[32,512]{1,0:T(8,128)S(1)} %add.27), channel_id=1, source_target_pairs={{0,4},{1,5},{2,6},{3,7},{4,0},{5,1},{6,2},{7,3},{8,12},{9,13},{10,... | collective-permute-start | bytes 196616 | tf_op jit(solution)/shard_map/ppermute | solution.py:367
  96.8 13.1 %collective-permute-start.25 = (f32[32,512]{1,0:T(8,128)S(1)}, f32[32,512]{1,0:T(8,128)S(1)}, u32[]{:S(2)}, u32[]{:S(2)}) collective-permute-start(f32[32,512]{1,0:T(8,128)S(1)} %add.27), channel_id=1, source_target_pairs={{0,2},{1,3},{2,0},{3,1},{4,6},{5,7},{6,4},{7,5},{8,10},{9,11},{10,... | collective-permute-start | bytes 196616 | tf_op jit(solution)/shard_map/ppermute | solution.py:367
  119.5 4.9 %collective-permute-start.31 = (f32[64,384]{1,0:T(8,128)S(1)}, f32[64,384]{1,0:T(8,128)S(1)}, u32[]{:S(2)}, u32[]{:S(2)}) collective-permute-start(f32[64,384]{1,0:T(8,128)S(1)} %get-tuple-element.105), channel_id=1, source_target_pairs={{0,4},{1,5},{2,6},{3,7},{4,0},{5,1},{6,2},{7,3},{8,12},{9,13},{10,... | collective-permute-start | bytes 294920 | tf_op jit(solution)/shard_map/ppermute | solution.py:367
  120.1 5.6 %collective-permute-start.29 = (f32[64,384]{1,0:T(8,128)S(1)}, f32[64,384]{1,0:T(8,128)S(1)}, u32[]{:S(2)}, u32[]{:S(2)}) collective-permute-start(f32[64,384]{1,0:T(8,128)S(1)} %get-tuple-element.104), channel_id=1, source_target_pairs={{0,2},{1,3},{2,0},{3,1},{4,6},{5,7},{6,4},{7,5},{8,10},{9,11},{10,... | collective-permute-start | bytes 294920 | tf_op jit(solution)/shard_map/ppermute | solution.py:367
  124.5 4.7 %collective-permute-start.32 = (f32[64,384]{1,0:T(8,128)S(1)}, f32[64,384]{1,0:T(8,128)S(1)}, u32[]{:S(2)}, u32[]{:S(2)}) collective-permute-start(f32[64,384]{1,0:T(8,128)S(1)} %add.34), channel_id=1, source_target_pairs={{0,2},{1,3},{2,0},{3,1},{4,6},{5,7},{6,4},{7,5},{8,10},{9,11},{10,... | collective-permute-start | bytes 294920 | tf_op jit(solution)/shard_map/ppermute | solution.py:367
  125.7 4.7 %collective-permute-start.30 = (f32[64,384]{1,0:T(8,128)S(1)}, f32[64,384]{1,0:T(8,128)S(1)}, u32[]{:S(2)}, u32[]{:S(2)}) collective-permute-start(f32[64,384]{1,0:T(8,128)S(1)} %add.32), channel_id=1, source_target_pairs={{0,4},{1,5},{2,6},{3,7},{4,0},{5,1},{6,2},{7,3},{8,12},{9,13},{10,... | collective-permute-start | bytes 294920 | tf_op jit(solution)/shard_map/ppermute | solution.py:367
  (9 other events, 62.9 us)

commit v13 on v12

--- a/solution.py
+++ b/solution.py
@@ -71,11 +71,11 @@
                 source = x_ref.at[at, pl.ds(k * ncols, ncols)]
                 into.append(pltpu.make_async_copy(source, held.at[k, at], in_sems.at[i]))
                 out_of.append(pltpu.make_async_copy(held.at[k, at], out_ref.at[k, at], out_sems.at[i]))
-        for copy in into:
-            copy.start()
-        for came, goes in zip(into, out_of):
+        for i, copy in enumerate(into):
+            copy.start(priority=i % QUEUES)
+        for i, (came, goes) in enumerate(zip(into, out_of)):
             came.wait()
-            goes.start(priority=1)
+            goes.start(priority=i % QUEUES)
         for copy in out_of:
             copy.wait()
 
@@ -294,7 +294,7 @@
     half = rows // 2
     step = rows // 8 if rows % 64 == 0 else rows
     n_copies = rows // step
-    cuts = sorted({0, n_copies // 4, n_copies})
+    cuts = sorted({0, n_copies * 3 // 8, n_copies})
 
     def kernel(here_ref, x_ref, high_ref, low_ref, mine_ref, theirs_ref, held, total, sems):
         copies = []

time: 139 us -> 139 us (level)
  no operation moved by 1% of the time
where the time goes in v13:
time: 139 us; the launch traced here: 138 us
  starting transfers between devices  52.6 us (38%)
  Pallas kernels  42.6 us (31%)
  waiting for transfers between devices  42.4 us (31%)
    ppermute x24, starting transfers between devices, exchange(): return lax.ppermute(array, ('row', 'wide'), pairs)  39.6 us
    ppermute x24, waiting for transfers between devices, exchange(): return lax.ppermute(array, ('row', 'wide'), pairs)  24.4 us
    all_to_all x1, waiting for transfers between devices, body(): x = lax.all_to_all(piece, 'wide', split_axis=0, concat_axis=0, tiled=True)  10.5 us
    pallas_call x1, Pallas kernels, inner_products(): pl.pallas_call(kernel, out_shape=[jax.ShapeDtypeStruct((half // 2, 2 * he...  8.96 us
    pallas_call x12, Pallas kernels, feed(): pl.pallas_call(kernel, out_shape=[jax.ShapeDtypeStruct((width, cols), jnp...  8.07 us
    ppermute x10, starting transfers between devices, swap(): return lax.ppermute(array, 'wide', [(i, i ^ k) for i in range(size)])  7.77 us
    pallas_call x1, Pallas kernels, assemble(): pl.pallas_call(kernel, out_shape=[pltpu.HBM((height, ncols), jnp.bfloat16...  7.65 us
    ppermute x10, waiting for transfers between devices, swap(): return lax.ppermute(array, 'wide', [(i, i ^ k) for i in range(size)])  7.43 us
  transfers between devices with their start and end apart: 35, of which 18 were waited for; matrix products, arithmetic and copies ran while one was open for 0% of the time, Pallas kernels for 15%

profile of v13, /device:TPU:0, one launch (start us, length us, event | category | flops | bytes accessed | tf_op | source)
XLA Modules:
  0.0 138.4 jit_solution(932415678956938387)
XLA Ops:
  0.0 6.0 %pack.1 = f32[8,64,4096]{2,1,0:T(8,128)} custom-call(f32[64,32768]{1,0:T(8,128)} %x_ref.1), custom_call_target="tpu_custom_call" | custom-call | bytes 16777216 | tf_op jit(solution)/shard_map/pack/pallas_call | solution.py:82
  6.1 5.3 %all-to-all-start = ((f32[8,64,4096]{2,1,0:T(8,128)}), f32[8,64,4096]{2,1,0:T(8,128)}, u32[]{:S(2)}, u32[]{:S(2)}) async-start(f32[8,64,4096]{2,1,0:T(8,128)} %pack.1), calls=%async_computation | async-start | bytes 16777216 | tf_op jit(solution)/shard_map/all_to_all | solution.py:409
  12.1 2.9 %collective-permute-start = (f32[32,2048]{1,0:T(8,128)S(1)}, f32[32,2048]{1,0:T(8,128)S(1)}, u32[]{:S(2)}, u32[]{:S(2)}) collective-permute-start(f32[32,2048]{1,0:T(8,128)S(1)} %get-tuple-element.57), channel_id=1, source_target_pairs={{0,8},{1,9},{2,10},{3,11},{4,12},{5,13},{6,14},{7,15},{8,0},{9,1},... | collective-permute-start | bytes 786440 | tf_op jit(solution)/shard_map/ppermute | solution.py:404
  15.8 3.1 %collective-permute-start.1 = (f32[32,2048]{1,0:T(8,128)S(1)}, f32[32,2048]{1,0:T(8,128)S(1)}, u32[]{:S(2)}, u32[]{:S(2)}) collective-permute-start(f32[32,2048]{1,0:T(8,128)S(1)} %get-tuple-element.60), channel_id=1, source_target_pairs={{0,8},{1,9},{2,10},{3,11},{4,12},{5,13},{6,14},{7,15},{8,0},{9,1},... | collective-permute-start | bytes 786440 | tf_op jit(solution)/shard_map/ppermute | solution.py:404
  18.9 3.3 %collective-permute-done.refs_0_ = f32[32,2048]{1,0:T(8,128)S(1)} collective-permute-done((f32[32,2048]{1,0:T(8,128)S(1)}, f32[32,2048]{1,0:T(8,128)S(1)}, u32[]{:S(2)}, u32[]{:S(2)}) %collective-permute-start) | collective-permute-done | bytes 262176 | tf_op jit(solution)/shard_map/ppermute | solution.py:404
  22.9 3.2 %collective-permute-start.3 = (f32[32,2048]{1,0:T(8,128)S(1)}, f32[32,2048]{1,0:T(8,128)S(1)}, u32[]{:S(2)}, u32[]{:S(2)}) collective-permute-start(f32[32,2048]{1,0:T(8,128)S(1)} %get-tuple-element.63), channel_id=1, source_target_pairs={{0,8},{1,9},{2,10},{3,11},{4,12},{5,13},{6,14},{7,15},{8,0},{9,1},... | collective-permute-start | bytes 786440 | tf_op jit(solution)/shard_map/ppermute | solution.py:404
  26.0 1.8 %collective-permute-done.1.refs_0_.refs_1_ = f32[32,2048]{1,0:T(8,128)S(1)} collective-permute-done((f32[32,2048]{1,0:T(8,128)S(1)}, f32[32,2048]{1,0:T(8,128)S(1)}, u32[]{:S(2)}, u32[]{:S(2)}) %collective-permute-start.1) | collective-permute-done | bytes 262176 | tf_op jit(solution)/shard_map/ppermute | solution.py:404
  28.5 3.2 %collective-permute-start.5 = (f32[32,2048]{1,0:T(8,128)S(1)}, f32[32,2048]{1,0:T(8,128)S(1)}, u32[]{:S(2)}, u32[]{:S(2)}) collective-permute-start(f32[32,2048]{1,0:T(8,128)S(1)} %get-tuple-element.66), channel_id=1, source_target_pairs={{0,8},{1,9},{2,10},{3,11},{4,12},{5,13},{6,14},{7,15},{8,0},{9,1},... | collective-permute-start | bytes 786440 | tf_op jit(solution)/shard_map/ppermute | solution.py:404
  31.7 1.8 %collective-permute-done.3.refs_1_.refs_2_ = f32[32,2048]{1,0:T(8,128)S(1)} collective-permute-done((f32[32,2048]{1,0:T(8,128)S(1)}, f32[32,2048]{1,0:T(8,128)S(1)}, u32[]{:S(2)}, u32[]{:S(2)}) %collective-permute-start.3) | collective-permute-done | bytes 262176 | tf_op jit(solution)/shard_map/ppermute | solution.py:404
  34.1 3.2 %collective-permute-start.7 = (f32[32,2048]{1,0:T(8,128)S(1)}, f32[32,2048]{1,0:T(8,128)S(1)}, u32[]{:S(2)}, u32[]{:S(2)}) collective-permute-start(f32[32,2048]{1,0:T(8,128)S(1)} %get-tuple-element.69), channel_id=1, source_target_pairs={{0,8},{1,9},{2,10},{3,11},{4,12},{5,13},{6,14},{7,15},{8,0},{9,1},... | collective-permute-start | bytes 786440 | tf_op jit(solution)/shard_map/ppermute | solution.py:404
  37.3 1.8 %collective-permute-done.5.refs_1_.refs_3_ = f32[32,2048]{1,0:T(8,128)S(1)} collective-permute-done((f32[32,2048]{1,0:T(8,128)S(1)}, f32[32,2048]{1,0:T(8,128)S(1)}, u32[]{:S(2)}, u32[]{:S(2)}) %collective-permute-start.5) | collective-permute-done | bytes 262176 | tf_op jit(solution)/shard_map/ppermute | solution.py:404
  39.7 3.2 %collective-permute-start.9 = (f32[32,2048]{1,0:T(8,128)S(1)}, f32[32,2048]{1,0:T(8,128)S(1)}, u32[]{:S(2)}, u32[]{:S(2)}) collective-permute-start(f32[32,2048]{1,0:T(8,128)S(1)} %get-tuple-element.72), channel_id=1, source_target_pairs={{0,8},{1,9},{2,10},{3,11},{4,12},{5,13},{6,14},{7,15},{8,0},{9,1},... | collective-permute-start | bytes 786440 | tf_op jit(solution)/shard_map/ppermute | solution.py:404
  42.9 1.8 %collective-permute-done.7.refs_2_.refs_4_ = f32[32,2048]{1,0:T(8,128)S(1)} collective-permute-done((f32[32,2048]{1,0:T(8,128)S(1)}, f32[32,2048]{1,0:T(8,128)S(1)}, u32[]{:S(2)}, u32[]{:S(2)}) %collective-permute-start.7) | collective-permute-done | bytes 262176 | tf_op jit(solution)/shard_map/ppermute | solution.py:404
  45.4 3.2 %collective-permute-start.11 = (f32[32,2048]{1,0:T(8,128)S(1)}, f32[32,2048]{1,0:T(8,128)S(1)}, u32[]{:S(2)}, u32[]{:S(2)}) collective-permute-start(f32[32,2048]{1,0:T(8,128)S(1)} %get-tuple-element.75), channel_id=1, source_target_pairs={{0,8},{1,9},{2,10},{3,11},{4,12},{5,13},{6,14},{7,15},{8,0},{9,1},... | collective-permute-start | bytes 786440 | tf_op jit(solution)/shard_map/ppermute | solution.py:404
  48.5 1.8 %collective-permute-done.9.refs_2_.refs_5_ = f32[32,2048]{1,0:T(8,128)S(1)} collective-permute-done((f32[32,2048]{1,0:T(8,128)S(1)}, f32[32,2048]{1,0:T(8,128)S(1)}, u32[]{:S(2)}, u32[]{:S(2)}) %collective-permute-start.9) | collective-permute-done | bytes 262176 | tf_op jit(solution)/shard_map/ppermute | solution.py:404
  51.0 3.2 %collective-permute-start.13 = (f32[32,2048]{1,0:T(8,128)S(1)}, f32[32,2048]{1,0:T(8,128)S(1)}, u32[]{:S(2)}, u32[]{:S(2)}) collective-permute-start(f32[32,2048]{1,0:T(8,128)S(1)} %get-tuple-element.78), channel_id=1, source_target_pairs={{0,8},{1,9},{2,10},{3,11},{4,12},{5,13},{6,14},{7,15},{8,0},{9,1},... | collective-permute-start | bytes 786440 | tf_op jit(solution)/shard_map/ppermute | solution.py:404
  54.1 1.8 %collective-permute-done.11.refs_3_.refs_6_ = f32[32,2048]{1,0:T(8,128)S(1)} collective-permute-done((f32[32,2048]{1,0:T(8,128)S(1)}, f32[32,2048]{1,0:T(8,128)S(1)}, u32[]{:S(2)}, u32[]{:S(2)}) %collective-permute-start.11) | collective-permute-done | bytes 262176 | tf_op jit(solution)/shard_map/ppermute | solution.py:404
  56.6 3.2 %collective-permute-start.15 = (f32[32,2048]{1,0:T(8,128)S(1)}, f32[32,2048]{1,0:T(8,128)S(1)}, u32[]{:S(2)}, u32[]{:S(2)}) collective-permute-start(f32[32,2048]{1,0:T(8,128)S(1)} %get-tuple-element.81), channel_id=1, source_target_pairs={{0,8},{1,9},{2,10},{3,11},{4,12},{5,13},{6,14},{7,15},{8,0},{9,1},... | collective-permute-start | bytes 786440 | tf_op jit(solution)/shard_map/ppermute | solution.py:404
  62.2 3.2 %collective-permute-start.17 = (f32[32,2048]{1,0:T(8,128)S(1)}, f32[32,2048]{1,0:T(8,128)S(1)}, u32[]{:S(2)}, u32[]{:S(2)}) collective-permute-start(f32[32,2048]{1,0:T(8,128)S(1)} %get-tuple-element.84), channel_id=1, source_target_pairs={{0,8},{1,9},{2,10},{3,11},{4,12},{5,13},{6,14},{7,15},{8,0},{9,1},... | collective-permute-start | bytes 786440 | tf_op jit(solution)/shard_map/ppermute | solution.py:404
  65.4 1.7 %collective-permute-done.15.refs_4_.refs_8_ = f32[32,2048]{1,0:T(8,128)S(1)} collective-permute-done((f32[32,2048]{1,0:T(8,128)S(1)}, f32[32,2048]{1,0:T(8,128)S(1)}, u32[]{:S(2)}, u32[]{:S(2)}) %collective-permute-start.15) | collective-permute-done | bytes 262176 | tf_op jit(solution)/shard_map/ppermute | solution.py:404
  67.9 5.1 %collective-permute-start.19 = (f32[32,2048]{1,0:T(8,128)S(1)}, f32[32,2048]{1,0:T(8,128)S(1)}, u32[]{:S(2)}, u32[]{:S(2)}) collective-permute-start(f32[32,2048]{1,0:T(8,128)S(1)} %get-tuple-element.87), channel_id=1, source_target_pairs={{0,8},{1,9},{2,10},{3,11},{4,12},{5,13},{6,14},{7,15},{8,0},{9,1},... | collective-permute-start | bytes 786440 | tf_op jit(solution)/shard_map/ppermute | solution.py:404
  73.8 2.8 %collective-permute-start.21 = (f32[32,2048]{1,0:T(8,128)S(1)}, f32[32,2048]{1,0:T(8,128)S(1)}, u32[]{:S(2)}, u32[]{:S(2)}) collective-permute-start(f32[32,2048]{1,0:T(8,128)S(1)} %get-tuple-element.90), channel_id=1, source_target_pairs={{0,8},{1,9},{2,10},{3,11},{4,12},{5,13},{6,14},{7,15},{8,0},{9,1},... | collective-permute-start | bytes 786440 | tf_op jit(solution)/shard_map/ppermute | solution.py:404
  76.6 2.8 %collective-permute-done.19.refs_10_ = f32[32,2048]{1,0:T(8,128)S(1)} collective-permute-done((f32[32,2048]{1,0:T(8,128)S(1)}, f32[32,2048]{1,0:T(8,128)S(1)}, u32[]{:S(2)}, u32[]{:S(2)}) %collective-permute-start.19) | collective-permute-done | bytes 262176 | tf_op jit(solution)/shard_map/ppermute | solution.py:404
  79.5 4.2 %collective-permute-done.21.refs_11_ = f32[32,2048]{1,0:T(8,128)S(1)} collective-permute-done((f32[32,2048]{1,0:T(8,128)S(1)}, f32[32,2048]{1,0:T(8,128)S(1)}, u32[]{:S(2)}, u32[]{:S(2)}) %collective-permute-start.21) | collective-permute-done | bytes 262176 | tf_op jit(solution)/shard_map/ppermute | solution.py:404
  83.7 7.6 %assemble.1 = (bf16[192,4096]{1,0:T(8,128)(2,1)}, bf16[192,4096]{1,0:T(8,128)(2,1)}, bf16[4096,192]{1,0:T(8,128)(2,1)}, bf16[4096,192]{1,0:T(8,128)(2,1)}, f32[32,512]{1,0:T(8,128)S(1)}) custom-call(s32[2]{0:T(128)S(1)} %pad_add_fusion.here_ref, s32[6]{0:T(128)S(1)} %copy-done.4, s32[6]{0:T(128)S(1)} %copy-done.5, f32[4,32,4096]{2,1,0:T(8,128)S(1)} %copy-done, ...), custom_call_target="tpu_custom_call" | custom-call | flops 1811939328 | bytes 6291456 | tf_op jit(solution)/shard_map/assemble/pallas_call | solution.py:198
  92.7 2.7 %collective-permute-start.27 = (f32[32,512]{1,0:T(8,128)S(1)}, f32[32,512]{1,0:T(8,128)S(1)}, u32[]{:S(2)}, u32[]{:S(2)}) collective-permute-start(f32[32,512]{1,0:T(8,128)S(1)} %add.27), channel_id=1, source_target_pairs={{0,6},{1,7},{2,4},{3,5},{4,2},{5,3},{6,0},{7,1},{8,14},{9,15},{10,... | collective-permute-start | bytes 196616 | tf_op jit(solution)/shard_map/ppermute | solution.py:367
  96.2 10.5 %all-to-all-done = f32[8,64,4096]{2,1,0:T(8,128)} async-done(((f32[8,64,4096]{2,1,0:T(8,128)}), f32[8,64,4096]{2,1,0:T(8,128)}, u32[]{:S(2)}, u32[]{:S(2)}) %all-to-all-start) | async-done | bytes 8388640 | tf_op jit(solution)/shard_map/all_to_all | solution.py:409
  106.8 2.2 %lift.1 = (bf16[4096,192]{1,0:T(8,128)(2,1)S(1)}, bf16[4096,192]{1,0:T(8,128)(2,1)S(1)}) custom-call(bf16[4096,192]{1,0:T(8,128)(2,1)} %get-tuple-element.94.refs_0_, bf16[4096,192]{1,0:T(8,128)(2,1)} %get-tuple-element.95.refs_1_), custom_call_target="tpu_custom_call" | custom-call | bytes 3145728 | tf_op jit(solution)/shard_map/lift/pallas_call | solution.py:279
  109.1 9.0 %inner_products.1 = (f32[128,384]{1,0:T(8,128)S(1)}, f32[128,384]{1,0:T(8,128)S(1)}, f32[512,4096]{1,0:T(8,128)S(1)}) custom-call(s32[2]{0:T(128)S(1)} %pad_add_fusion.here_ref, f32[512,4096]{1,0:T(8,128)} %bitcast.2.x_ref, bf16[4096,192]{1,0:T(8,128)(2,1)S(1)} %get-tuple-element.96.high_ref, bf16[4096,192]{1,0:T(8,128)(2,1)S(1)} %get-tuple-element.97.low_ref), custom_call_target="tpu_custom_call" | custom-call | flops 2415919104 | bytes 8388608 | tf_op jit(solution)/shard_map/inner_products/pallas_call | solution.py:315
  120.8 3.5 %merge.1.p_ref = bf16[576,4096]{1,0:T(8,128)(2,1)S(1)} custom-call(f32[32,512]{1,0:T(8,128)S(1)} %add_add_fusion.refs_0_, f32[6,32,32]{2,1,0:T(8,128)S(1)} %copy-done.3, bf16[192,4096]{1,0:T(8,128)(2,1)S(1)} %copy-done.1, bf16[192,4096]{1,0:T(8,128)(2,1)S(1)} %copy-done.2), custom_call_target="tpu_custom_call" | custom-call | flops 905969664 | bytes 6291456 | tf_op jit(solution)/shard_map/merge/pallas_call | solution.py:236
  127.4 1.8 %collective-permute-done.32 = f32[64,384]{1,0:T(8,128)S(1)} collective-permute-done((f32[64,384]{1,0:T(8,128)S(1)}, f32[64,384]{1,0:T(8,128)S(1)}, u32[]{:S(2)}, u32[]{:S(2)}) %collective-permute-start.32) | collective-permute-done | bytes 98336 | tf_op jit(solution)/shard_map/ppermute | solution.py:367
  132.0 6.2 %update.1 = f32[512,4096]{1,0:T(8,128)} custom-call(s32[2]{0:T(128)S(1)} %pad_add_fusion.here_ref, f32[128,384]{1,0:T(8,128)S(1)} %pad_maximum_fusion.mine_ref, f32[128,384]{1,0:T(8,128)S(1)} %collective-permute-done.33.theirs_ref, f32[512,4096]{1,0:T(8,128)S(1)} %get-tuple-element.106.x_ref, bf16[576,4096]{1,0:T(8,128)(2,1)S(1)} %merge.1.p_ref), custom_call_target="tpu_custom_call" | custom-call | flops 2415919104 | bytes 16777216 | tf_op jit(solution)/shard_map/update/pallas_call | solution.py:350
  (78 shorter events, 21.0 us)
Async XLA Ops:
  6.1 100.7 %all-to-all-start = ((f32[8,64,4096]{2,1,0:T(8,128)}), f32[8,64,4096]{2,1,0:T(8,128)}, u32[]{:S(2)}, u32[]{:S(2)}) async-start(f32[8,64,4096]{2,1,0:T(8,128)} %pack.1), calls=%async_computation | async-start | bytes 16777216 | tf_op jit(solution)/shard_map/all_to_all | solution.py:409
  12.1 10.1 %collective-permute-start = (f32[32,2048]{1,0:T(8,128)S(1)}, f32[32,2048]{1,0:T(8,128)S(1)}, u32[]{:S(2)}, u32[]{:S(2)}) collective-permute-start(f32[32,2048]{1,0:T(8,128)S(1)} %get-tuple-element.57), channel_id=1, source_target_pairs={{0,8},{1,9},{2,10},{3,11},{4,12},{5,13},{6,14},{7,15},{8,0},{9,1},... | collective-permute-start | bytes 786440 | tf_op jit(solution)/shard_map/ppermute | solution.py:404
  15.1 7.1 %collective-permute-start.2 = (f32[32,2048]{1,0:T(8,128)S(1)}, f32[32,2048]{1,0:T(8,128)S(1)}, u32[]{:S(2)}, u32[]{:S(2)}) collective-permute-start(f32[32,2048]{1,0:T(8,128)S(1)} %get-tuple-element.58), channel_id=1, source_target_pairs={{0,1},{1,0},{2,3},{3,2},{4,5},{5,4},{6,7},{7,6},{8,16},{9,17},{10,... | collective-permute-start | bytes 786440 | tf_op jit(solution)/shard_map/ppermute | solution.py:404
  15.8 12.0 %collective-permute-start.1 = (f32[32,2048]{1,0:T(8,128)S(1)}, f32[32,2048]{1,0:T(8,128)S(1)}, u32[]{:S(2)}, u32[]{:S(2)}) collective-permute-start(f32[32,2048]{1,0:T(8,128)S(1)} %get-tuple-element.60), channel_id=1, source_target_pairs={{0,8},{1,9},{2,10},{3,11},{4,12},{5,13},{6,14},{7,15},{8,0},{9,1},... | collective-permute-start | bytes 786440 | tf_op jit(solution)/shard_map/ppermute | solution.py:404
  18.9 8.9 %collective-permute-start.4 = (f32[32,2048]{1,0:T(8,128)S(1)}, f32[32,2048]{1,0:T(8,128)S(1)}, u32[]{:S(2)}, u32[]{:S(2)}) collective-permute-start(f32[32,2048]{1,0:T(8,128)S(1)} %get-tuple-element.61), channel_id=1, source_target_pairs={{0,1},{1,0},{2,3},{3,2},{4,5},{5,4},{6,7},{7,6},{8,16},{9,17},{10,... | collective-permute-start | bytes 786440 | tf_op jit(solution)/shard_map/ppermute | solution.py:404
  22.9 10.6 %collective-permute-start.3 = (f32[32,2048]{1,0:T(8,128)S(1)}, f32[32,2048]{1,0:T(8,128)S(1)}, u32[]{:S(2)}, u32[]{:S(2)}) collective-permute-start(f32[32,2048]{1,0:T(8,128)S(1)} %get-tuple-element.63), channel_id=1, source_target_pairs={{0,8},{1,9},{2,10},{3,11},{4,12},{5,13},{6,14},{7,15},{8,0},{9,1},... | collective-permute-start | bytes 786440 | tf_op jit(solution)/shard_map/ppermute | solution.py:404
  26.0 7.4 %collective-permute-start.6 = (f32[32,2048]{1,0:T(8,128)S(1)}, f32[32,2048]{1,0:T(8,128)S(1)}, u32[]{:S(2)}, u32[]{:S(2)}) collective-permute-start(f32[32,2048]{1,0:T(8,128)S(1)} %get-tuple-element.64), channel_id=1, source_target_pairs={{0,1},{1,0},{2,3},{3,2},{4,5},{5,4},{6,7},{7,6},{8,16},{9,17},{10,... | collective-permute-start | bytes 786440 | tf_op jit(solution)/shard_map/ppermute | solution.py:404
  28.5 10.6 %collective-permute-start.5 = (f32[32,2048]{1,0:T(8,128)S(1)}, f32[32,2048]{1,0:T(8,128)S(1)}, u32[]{:S(2)}, u32[]{:S(2)}) collective-permute-start(f32[32,2048]{1,0:T(8,128)S(1)} %get-tuple-element.66), channel_id=1, source_target_pairs={{0,8},{1,9},{2,10},{3,11},{4,12},{5,13},{6,14},{7,15},{8,0},{9,1},... | collective-permute-start | bytes 786440 | tf_op jit(solution)/shard_map/ppermute | solution.py:404
  31.7 7.4 %collective-permute-start.8 = (f32[32,2048]{1,0:T(8,128)S(1)}, f32[32,2048]{1,0:T(8,128)S(1)}, u32[]{:S(2)}, u32[]{:S(2)}) collective-permute-start(f32[32,2048]{1,0:T(8,128)S(1)} %get-tuple-element.67), channel_id=1, source_target_pairs={{0,1},{1,0},{2,3},{3,2},{4,5},{5,4},{6,7},{7,6},{8,16},{9,17},{10,... | collective-permute-start | bytes 786440 | tf_op jit(solution)/shard_map/ppermute | solution.py:404
  34.1 10.6 %collective-permute-start.7 = (f32[32,2048]{1,0:T(8,128)S(1)}, f32[32,2048]{1,0:T(8,128)S(1)}, u32[]{:S(2)}, u32[]{:S(2)}) collective-permute-start(f32[32,2048]{1,0:T(8,128)S(1)} %get-tuple-element.69), channel_id=1, source_target_pairs={{0,8},{1,9},{2,10},{3,11},{4,12},{5,13},{6,14},{7,15},{8,0},{9,1},... | collective-permute-start | bytes 786440 | tf_op jit(solution)/shard_map/ppermute | solution.py:404
  37.3 7.4 %collective-permute-start.10 = (f32[32,2048]{1,0:T(8,128)S(1)}, f32[32,2048]{1,0:T(8,128)S(1)}, u32[]{:S(2)}, u32[]{:S(2)}) collective-permute-start(f32[32,2048]{1,0:T(8,128)S(1)} %get-tuple-element.70), channel_id=1, source_target_pairs={{0,1},{1,0},{2,3},{3,2},{4,5},{5,4},{6,7},{7,6},{8,16},{9,17},{10,... | collective-permute-start | bytes 786440 | tf_op jit(solution)/shard_map/ppermute | solution.py:404
  39.7 10.6 %collective-permute-start.9 = (f32[32,2048]{1,0:T(8,128)S(1)}, f32[32,2048]{1,0:T(8,128)S(1)}, u32[]{:S(2)}, u32[]{:S(2)}) collective-permute-start(f32[32,2048]{1,0:T(8,128)S(1)} %get-tuple-element.72), channel_id=1, source_target_pairs={{0,8},{1,9},{2,10},{3,11},{4,12},{5,13},{6,14},{7,15},{8,0},{9,1},... | collective-permute-start | bytes 786440 | tf_op jit(solution)/shard_map/ppermute | solution.py:404
  42.9 7.4 %collective-permute-start.12 = (f32[32,2048]{1,0:T(8,128)S(1)}, f32[32,2048]{1,0:T(8,128)S(1)}, u32[]{:S(2)}, u32[]{:S(2)}) collective-permute-start(f32[32,2048]{1,0:T(8,128)S(1)} %get-tuple-element.73), channel_id=1, source_target_pairs={{0,1},{1,0},{2,3},{3,2},{4,5},{5,4},{6,7},{7,6},{8,16},{9,17},{10,... | collective-permute-start | bytes 786440 | tf_op jit(solution)/shard_map/ppermute | solution.py:404
  45.4 10.5 %collective-permute-start.11 = (f32[32,2048]{1,0:T(8,128)S(1)}, f32[32,2048]{1,0:T(8,128)S(1)}, u32[]{:S(2)}, u32[]{:S(2)}) collective-permute-start(f32[32,2048]{1,0:T(8,128)S(1)} %get-tuple-element.75), channel_id=1, source_target_pairs={{0,8},{1,9},{2,10},{3,11},{4,12},{5,13},{6,14},{7,15},{8,0},{9,1},... | collective-permute-start | bytes 786440 | tf_op jit(solution)/shard_map/ppermute | solution.py:404
  48.5 7.4 %collective-permute-start.14 = (f32[32,2048]{1,0:T(8,128)S(1)}, f32[32,2048]{1,0:T(8,128)S(1)}, u32[]{:S(2)}, u32[]{:S(2)}) collective-permute-start(f32[32,2048]{1,0:T(8,128)S(1)} %get-tuple-element.76), channel_id=1, source_target_pairs={{0,1},{1,0},{2,3},{3,2},{4,5},{5,4},{6,7},{7,6},{8,16},{9,17},{10,... | collective-permute-start | bytes 786440 | tf_op jit(solution)/shard_map/ppermute | solution.py:404
  51.0 10.5 %collective-permute-start.13 = (f32[32,2048]{1,0:T(8,128)S(1)}, f32[32,2048]{1,0:T(8,128)S(1)}, u32[]{:S(2)}, u32[]{:S(2)}) collective-permute-start(f32[32,2048]{1,0:T(8,128)S(1)} %get-tuple-element.78), channel_id=1, source_target_pairs={{0,8},{1,9},{2,10},{3,11},{4,12},{5,13},{6,14},{7,15},{8,0},{9,1},... | collective-permute-start | bytes 786440 | tf_op jit(solution)/shard_map/ppermute | solution.py:404
  54.1 7.4 %collective-permute-start.16 = (f32[32,2048]{1,0:T(8,128)S(1)}, f32[32,2048]{1,0:T(8,128)S(1)}, u32[]{:S(2)}, u32[]{:S(2)}) collective-permute-start(f32[32,2048]{1,0:T(8,128)S(1)} %get-tuple-element.79), channel_id=1, source_target_pairs={{0,1},{1,0},{2,3},{3,2},{4,5},{5,4},{6,7},{7,6},{8,16},{9,17},{10,... | collective-permute-start | bytes 786440 | tf_op jit(solution)/shard_map/ppermute | solution.py:404
  56.6 10.5 %collective-permute-start.15 = (f32[32,2048]{1,0:T(8,128)S(1)}, f32[32,2048]{1,0:T(8,128)S(1)}, u32[]{:S(2)}, u32[]{:S(2)}) collective-permute-start(f32[32,2048]{1,0:T(8,128)S(1)} %get-tuple-element.81), channel_id=1, source_target_pairs={{0,8},{1,9},{2,10},{3,11},{4,12},{5,13},{6,14},{7,15},{8,0},{9,1},... | collective-permute-start | bytes 786440 | tf_op jit(solution)/shard_map/ppermute | solution.py:404
  59.8 7.4 %collective-permute-start.18 = (f32[32,2048]{1,0:T(8,128)S(1)}, f32[32,2048]{1,0:T(8,128)S(1)}, u32[]{:S(2)}, u32[]{:S(2)}) collective-permute-start(f32[32,2048]{1,0:T(8,128)S(1)} %get-tuple-element.82), channel_id=1, source_target_pairs={{0,1},{1,0},{2,3},{3,2},{4,5},{5,4},{6,7},{7,6},{8,16},{9,17},{10,... | collective-permute-start | bytes 786440 | tf_op jit(solution)/shard_map/ppermute | solution.py:404
  62.2 10.9 %collective-permute-start.17 = (f32[32,2048]{1,0:T(8,128)S(1)}, f32[32,2048]{1,0:T(8,128)S(1)}, u32[]{:S(2)}, u32[]{:S(2)}) collective-permute-start(f32[32,2048]{1,0:T(8,128)S(1)} %get-tuple-element.84), channel_id=1, source_target_pairs={{0,8},{1,9},{2,10},{3,11},{4,12},{5,13},{6,14},{7,15},{8,0},{9,1},... | collective-permute-start | bytes 786440 | tf_op jit(solution)/shard_map/ppermute | solution.py:404
  65.4 7.7 %collective-permute-start.20 = (f32[32,2048]{1,0:T(8,128)S(1)}, f32[32,2048]{1,0:T(8,128)S(1)}, u32[]{:S(2)}, u32[]{:S(2)}) collective-permute-start(f32[32,2048]{1,0:T(8,128)S(1)} %get-tuple-element.85), channel_id=1, source_target_pairs={{0,1},{1,0},{2,3},{3,2},{4,5},{5,4},{6,7},{7,6},{8,16},{9,17},{10,... | collective-permute-start | bytes 786440 | tf_op jit(solution)/shard_map/ppermute | solution.py:404
  67.8 11.6 %collective-permute-start.22 = (f32[32,2048]{1,0:T(8,128)S(1)}, f32[32,2048]{1,0:T(8,128)S(1)}, u32[]{:S(2)}, u32[]{:S(2)}) collective-permute-start(f32[32,2048]{1,0:T(8,128)S(1)} %get-tuple-element.88), channel_id=1, source_target_pairs={{0,1},{1,0},{2,3},{3,2},{4,5},{5,4},{6,7},{7,6},{8,16},{9,17},{10,... | collective-permute-start | bytes 786440 | tf_op jit(solution)/shard_map/ppermute | solution.py:404
  67.9 11.5 %collective-permute-start.19 = (f32[32,2048]{1,0:T(8,128)S(1)}, f32[32,2048]{1,0:T(8,128)S(1)}, u32[]{:S(2)}, u32[]{:S(2)}) collective-permute-start(f32[32,2048]{1,0:T(8,128)S(1)} %get-tuple-element.87), channel_id=1, source_target_pairs={{0,8},{1,9},{2,10},{3,11},{4,12},{5,13},{6,14},{7,15},{8,0},{9,1},... | collective-permute-start | bytes 786440 | tf_op jit(solution)/shard_map/ppermute | solution.py:404
  73.8 9.9 %collective-permute-start.21 = (f32[32,2048]{1,0:T(8,128)S(1)}, f32[32,2048]{1,0:T(8,128)S(1)}, u32[]{:S(2)}, u32[]{:S(2)}) collective-permute-start(f32[32,2048]{1,0:T(8,128)S(1)} %get-tuple-element.90), channel_id=1, source_target_pairs={{0,8},{1,9},{2,10},{3,11},{4,12},{5,13},{6,14},{7,15},{8,0},{9,1},... | collective-permute-start | bytes 786440 | tf_op jit(solution)/shard_map/ppermute | solution.py:404
  76.6 7.0 %collective-permute-start.23 = (f32[32,2048]{1,0:T(8,128)S(1)}, f32[32,2048]{1,0:T(8,128)S(1)}, u32[]{:S(2)}, u32[]{:S(2)}) collective-permute-start(f32[32,2048]{1,0:T(8,128)S(1)} %get-tuple-element.91), channel_id=1, source_target_pairs={{0,1},{1,0},{2,3},{3,2},{4,5},{5,4},{6,7},{7,6},{8,16},{9,17},{10,... | collective-permute-start | bytes 786440 | tf_op jit(solution)/shard_map/ppermute | solution.py:404
  92.7 16.3 %collective-permute-start.27 = (f32[32,512]{1,0:T(8,128)S(1)}, f32[32,512]{1,0:T(8,128)S(1)}, u32[]{:S(2)}, u32[]{:S(2)}) collective-permute-start(f32[32,512]{1,0:T(8,128)S(1)} %add.27), channel_id=1, source_target_pairs={{0,6},{1,7},{2,4},{3,5},{4,2},{5,3},{6,0},{7,1},{8,14},{9,15},{10,... | collective-permute-start | bytes 196616 | tf_op jit(solution)/shard_map/ppermute | solution.py:367
  95.3 13.7 %collective-permute-start.26 = (f32[32,512]{1,0:T(8,128)S(1)}, f32[32,512]{1,0:T(8,128)S(1)}, u32[]{:S(2)}, u32[]{:S(2)}) collective-permute-start(f32[32,512]{1,0:T(8,128)S(1)} %add.27), channel_id=1, source_target_pairs={{0,4},{1,5},{2,6},{3,7},{4,0},{5,1},{6,2},{7,3},{8,12},{9,13},{10,... | collective-permute-start | bytes 196616 | tf_op jit(solution)/shard_map/ppermute | solution.py:367
  95.9 13.1 %collective-permute-start.25 = (f32[32,512]{1,0:T(8,128)S(1)}, f32[32,512]{1,0:T(8,128)S(1)}, u32[]{:S(2)}, u32[]{:S(2)}) collective-permute-start(f32[32,512]{1,0:T(8,128)S(1)} %add.27), channel_id=1, source_target_pairs={{0,2},{1,3},{2,0},{3,1},{4,6},{5,7},{6,4},{7,5},{8,10},{9,11},{10,... | collective-permute-start | bytes 196616 | tf_op jit(solution)/shard_map/ppermute | solution.py:367
  119.6 4.9 %collective-permute-start.31 = (f32[64,384]{1,0:T(8,128)S(1)}, f32[64,384]{1,0:T(8,128)S(1)}, u32[]{:S(2)}, u32[]{:S(2)}) collective-permute-start(f32[64,384]{1,0:T(8,128)S(1)} %get-tuple-element.105), channel_id=1, source_target_pairs={{0,4},{1,5},{2,6},{3,7},{4,0},{5,1},{6,2},{7,3},{8,12},{9,13},{10,... | collective-permute-start | bytes 294920 | tf_op jit(solution)/shard_map/ppermute | solution.py:367
  120.2 5.6 %collective-permute-start.29 = (f32[64,384]{1,0:T(8,128)S(1)}, f32[64,384]{1,0:T(8,128)S(1)}, u32[]{:S(2)}, u32[]{:S(2)}) collective-permute-start(f32[64,384]{1,0:T(8,128)S(1)} %get-tuple-element.104), channel_id=1, source_target_pairs={{0,2},{1,3},{2,0},{3,1},{4,6},{5,7},{6,4},{7,5},{8,10},{9,11},{10,... | collective-permute-start | bytes 294920 | tf_op jit(solution)/shard_map/ppermute | solution.py:367
  124.5 4.7 %collective-permute-start.32 = (f32[64,384]{1,0:T(8,128)S(1)}, f32[64,384]{1,0:T(8,128)S(1)}, u32[]{:S(2)}, u32[]{:S(2)}) collective-permute-start(f32[64,384]{1,0:T(8,128)S(1)} %add.34), channel_id=1, source_target_pairs={{0,2},{1,3},{2,0},{3,1},{4,6},{5,7},{6,4},{7,5},{8,10},{9,11},{10,... | collective-permute-start | bytes 294920 | tf_op jit(solution)/shard_map/ppermute | solution.py:367
  125.8 4.7 %collective-permute-start.30 = (f32[64,384]{1,0:T(8,128)S(1)}, f32[64,384]{1,0:T(8,128)S(1)}, u32[]{:S(2)}, u32[]{:S(2)}) collective-permute-start(f32[64,384]{1,0:T(8,128)S(1)} %add.32), channel_id=1, source_target_pairs={{0,4},{1,5},{2,6},{3,7},{4,0},{5,1},{6,2},{7,3},{8,12},{9,13},{10,... | collective-permute-start | bytes 294920 | tf_op jit(solution)/shard_map/ppermute | solution.py:367
  (9 other events, 66.0 us)

commit v14 on v13

--- a/solution.py
+++ b/solution.py
@@ -294,7 +294,7 @@
     half = rows // 2
     step = rows // 8 if rows % 64 == 0 else rows
     n_copies = rows // step
-    cuts = sorted({0, n_copies * 3 // 8, n_copies})
+    cuts = sorted({0, n_copies // 2, n_copies})
 
     def kernel(here_ref, x_ref, high_ref, low_ref, mine_ref, theirs_ref, held, total, sems):
         copies = []

time: 139 us -> 140 us (level)
  no operation moved by 1% of the time
where the time goes in v14:
time: 140 us; the launch traced here: 139 us
  starting transfers between devices  52.6 us (38%)
  Pallas kernels  43.7 us (31%)
  waiting for transfers between devices  42.4 us (30%)
    ppermute x24, starting transfers between devices, exchange(): return lax.ppermute(array, ('row', 'wide'), pairs)  39.6 us
    ppermute x24, waiting for transfers between devices, exchange(): return lax.ppermute(array, ('row', 'wide'), pairs)  24.4 us
    all_to_all x1, waiting for transfers between devices, body(): x = lax.all_to_all(piece, 'wide', split_axis=0, concat_axis=0, tiled=True)  10.5 us
    pallas_call x1, Pallas kernels, inner_products(): pl.pallas_call(kernel, out_shape=[jax.ShapeDtypeStruct((half // 2, 2 * he...  10 us
    pallas_call x12, Pallas kernels, feed(): pl.pallas_call(kernel, out_shape=[jax.ShapeDtypeStruct((width, cols), jnp...  8.07 us
    ppermute x10, starting transfers between devices, swap(): return lax.ppermute(array, 'wide', [(i, i ^ k) for i in range(size)])  7.77 us
    pallas_call x1, Pallas kernels, assemble(): pl.pallas_call(kernel, out_shape=[pltpu.HBM((height, ncols), jnp.bfloat16...  7.65 us
    ppermute x10, waiting for transfers between devices, swap(): return lax.ppermute(array, 'wide', [(i, i ^ k) for i in range(size)])  7.43 us
  transfers between devices with their start and end apart: 35, of which 18 were waited for; matrix products, arithmetic and copies ran while one was open for 0% of the time, Pallas kernels for 15%

profile of v14, /device:TPU:0, one launch (start us, length us, event | category | flops | bytes accessed | tf_op | source)
XLA Modules:
  0.0 139.5 jit_solution(14324279593451502681)
XLA Ops:
  0.0 6.0 %pack.1 = f32[8,64,4096]{2,1,0:T(8,128)} custom-call(f32[64,32768]{1,0:T(8,128)} %x_ref.1), custom_call_target="tpu_custom_call" | custom-call | bytes 16777216 | tf_op jit(solution)/shard_map/pack/pallas_call | solution.py:82
  6.1 5.3 %all-to-all-start = ((f32[8,64,4096]{2,1,0:T(8,128)}), f32[8,64,4096]{2,1,0:T(8,128)}, u32[]{:S(2)}, u32[]{:S(2)}) async-start(f32[8,64,4096]{2,1,0:T(8,128)} %pack.1), calls=%async_computation | async-start | bytes 16777216 | tf_op jit(solution)/shard_map/all_to_all | solution.py:409
  12.1 2.9 %collective-permute-start = (f32[32,2048]{1,0:T(8,128)S(1)}, f32[32,2048]{1,0:T(8,128)S(1)}, u32[]{:S(2)}, u32[]{:S(2)}) collective-permute-start(f32[32,2048]{1,0:T(8,128)S(1)} %get-tuple-element.57), channel_id=1, source_target_pairs={{0,8},{1,9},{2,10},{3,11},{4,12},{5,13},{6,14},{7,15},{8,0},{9,1},... | collective-permute-start | bytes 786440 | tf_op jit(solution)/shard_map/ppermute | solution.py:404
  15.8 3.1 %collective-permute-start.1 = (f32[32,2048]{1,0:T(8,128)S(1)}, f32[32,2048]{1,0:T(8,128)S(1)}, u32[]{:S(2)}, u32[]{:S(2)}) collective-permute-start(f32[32,2048]{1,0:T(8,128)S(1)} %get-tuple-element.60), channel_id=1, source_target_pairs={{0,8},{1,9},{2,10},{3,11},{4,12},{5,13},{6,14},{7,15},{8,0},{9,1},... | collective-permute-start | bytes 786440 | tf_op jit(solution)/shard_map/ppermute | solution.py:404
  18.9 3.3 %collective-permute-done.refs_0_ = f32[32,2048]{1,0:T(8,128)S(1)} collective-permute-done((f32[32,2048]{1,0:T(8,128)S(1)}, f32[32,2048]{1,0:T(8,128)S(1)}, u32[]{:S(2)}, u32[]{:S(2)}) %collective-permute-start) | collective-permute-done | bytes 262176 | tf_op jit(solution)/shard_map/ppermute | solution.py:404
  22.9 3.2 %collective-permute-start.3 = (f32[32,2048]{1,0:T(8,128)S(1)}, f32[32,2048]{1,0:T(8,128)S(1)}, u32[]{:S(2)}, u32[]{:S(2)}) collective-permute-start(f32[32,2048]{1,0:T(8,128)S(1)} %get-tuple-element.63), channel_id=1, source_target_pairs={{0,8},{1,9},{2,10},{3,11},{4,12},{5,13},{6,14},{7,15},{8,0},{9,1},... | collective-permute-start | bytes 786440 | tf_op jit(solution)/shard_map/ppermute | solution.py:404
  26.0 1.8 %collective-permute-done.1.refs_0_.refs_1_ = f32[32,2048]{1,0:T(8,128)S(1)} collective-permute-done((f32[32,2048]{1,0:T(8,128)S(1)}, f32[32,2048]{1,0:T(8,128)S(1)}, u32[]{:S(2)}, u32[]{:S(2)}) %collective-permute-start.1) | collective-permute-done | bytes 262176 | tf_op jit(solution)/shard_map/ppermute | solution.py:404
  28.5 3.2 %collective-permute-start.5 = (f32[32,2048]{1,0:T(8,128)S(1)}, f32[32,2048]{1,0:T(8,128)S(1)}, u32[]{:S(2)}, u32[]{:S(2)}) collective-permute-start(f32[32,2048]{1,0:T(8,128)S(1)} %get-tuple-element.66), channel_id=1, source_target_pairs={{0,8},{1,9},{2,10},{3,11},{4,12},{5,13},{6,14},{7,15},{8,0},{9,1},... | collective-permute-start | bytes 786440 | tf_op jit(solution)/shard_map/ppermute | solution.py:404
  31.7 1.8 %collective-permute-done.3.refs_1_.refs_2_ = f32[32,2048]{1,0:T(8,128)S(1)} collective-permute-done((f32[32,2048]{1,0:T(8,128)S(1)}, f32[32,2048]{1,0:T(8,128)S(1)}, u32[]{:S(2)}, u32[]{:S(2)}) %collective-permute-start.3) | collective-permute-done | bytes 262176 | tf_op jit(solution)/shard_map/ppermute | solution.py:404
  34.1 3.2 %collective-permute-start.7 = (f32[32,2048]{1,0:T(8,128)S(1)}, f32[32,2048]{1,0:T(8,128)S(1)}, u32[]{:S(2)}, u32[]{:S(2)}) collective-permute-start(f32[32,2048]{1,0:T(8,128)S(1)} %get-tuple-element.69), channel_id=1, source_target_pairs={{0,8},{1,9},{2,10},{3,11},{4,12},{5,13},{6,14},{7,15},{8,0},{9,1},... | collective-permute-start | bytes 786440 | tf_op jit(solution)/shard_map/ppermute | solution.py:404
  37.3 1.8 %collective-permute-done.5.refs_1_.refs_3_ = f32[32,2048]{1,0:T(8,128)S(1)} collective-permute-done((f32[32,2048]{1,0:T(8,128)S(1)}, f32[32,2048]{1,0:T(8,128)S(1)}, u32[]{:S(2)}, u32[]{:S(2)}) %collective-permute-start.5) | collective-permute-done | bytes 262176 | tf_op jit(solution)/shard_map/ppermute | solution.py:404
  39.7 3.2 %collective-permute-start.9 = (f32[32,2048]{1,0:T(8,128)S(1)}, f32[32,2048]{1,0:T(8,128)S(1)}, u32[]{:S(2)}, u32[]{:S(2)}) collective-permute-start(f32[32,2048]{1,0:T(8,128)S(1)} %get-tuple-element.72), channel_id=1, source_target_pairs={{0,8},{1,9},{2,10},{3,11},{4,12},{5,13},{6,14},{7,15},{8,0},{9,1},... | collective-permute-start | bytes 786440 | tf_op jit(solution)/shard_map/ppermute | solution.py:404
  42.9 1.8 %collective-permute-done.7.refs_2_.refs_4_ = f32[32,2048]{1,0:T(8,128)S(1)} collective-permute-done((f32[32,2048]{1,0:T(8,128)S(1)}, f32[32,2048]{1,0:T(8,128)S(1)}, u32[]{:S(2)}, u32[]{:S(2)}) %collective-permute-start.7) | collective-permute-done | bytes 262176 | tf_op jit(solution)/shard_map/ppermute | solution.py:404
  45.4 3.2 %collective-permute-start.11 = (f32[32,2048]{1,0:T(8,128)S(1)}, f32[32,2048]{1,0:T(8,128)S(1)}, u32[]{:S(2)}, u32[]{:S(2)}) collective-permute-start(f32[32,2048]{1,0:T(8,128)S(1)} %get-tuple-element.75), channel_id=1, source_target_pairs={{0,8},{1,9},{2,10},{3,11},{4,12},{5,13},{6,14},{7,15},{8,0},{9,1},... | collective-permute-start | bytes 786440 | tf_op jit(solution)/shard_map/ppermute | solution.py:404
  48.5 1.8 %collective-permute-done.9.refs_2_.refs_5_ = f32[32,2048]{1,0:T(8,128)S(1)} collective-permute-done((f32[32,2048]{1,0:T(8,128)S(1)}, f32[32,2048]{1,0:T(8,128)S(1)}, u32[]{:S(2)}, u32[]{:S(2)}) %collective-permute-start.9) | collective-permute-done | bytes 262176 | tf_op jit(solution)/shard_map/ppermute | solution.py:404
  51.0 3.2 %collective-permute-start.13 = (f32[32,2048]{1,0:T(8,128)S(1)}, f32[32,2048]{1,0:T(8,128)S(1)}, u32[]{:S(2)}, u32[]{:S(2)}) collective-permute-start(f32[32,2048]{1,0:T(8,128)S(1)} %get-tuple-element.78), channel_id=1, source_target_pairs={{0,8},{1,9},{2,10},{3,11},{4,12},{5,13},{6,14},{7,15},{8,0},{9,1},... | collective-permute-start | bytes 786440 | tf_op jit(solution)/shard_map/ppermute | solution.py:404
  54.1 1.8 %collective-permute-done.11.refs_3_.refs_6_ = f32[32,2048]{1,0:T(8,128)S(1)} collective-permute-done((f32[32,2048]{1,0:T(8,128)S(1)}, f32[32,2048]{1,0:T(8,128)S(1)}, u32[]{:S(2)}, u32[]{:S(2)}) %collective-permute-start.11) | collective-permute-done | bytes 262176 | tf_op jit(solution)/shard_map/ppermute | solution.py:404
  56.6 3.2 %collective-permute-start.15 = (f32[32,2048]{1,0:T(8,128)S(1)}, f32[32,2048]{1,0:T(8,128)S(1)}, u32[]{:S(2)}, u32[]{:S(2)}) collective-permute-start(f32[32,2048]{1,0:T(8,128)S(1)} %get-tuple-element.81), channel_id=1, source_target_pairs={{0,8},{1,9},{2,10},{3,11},{4,12},{5,13},{6,14},{7,15},{8,0},{9,1},... | collective-permute-start | bytes 786440 | tf_op jit(solution)/shard_map/ppermute | solution.py:404
  62.2 3.2 %collective-permute-start.17 = (f32[32,2048]{1,0:T(8,128)S(1)}, f32[32,2048]{1,0:T(8,128)S(1)}, u32[]{:S(2)}, u32[]{:S(2)}) collective-permute-start(f32[32,2048]{1,0:T(8,128)S(1)} %get-tuple-element.84), channel_id=1, source_target_pairs={{0,8},{1,9},{2,10},{3,11},{4,12},{5,13},{6,14},{7,15},{8,0},{9,1},... | collective-permute-start | bytes 786440 | tf_op jit(solution)/shard_map/ppermute | solution.py:404
  65.4 1.7 %collective-permute-done.15.refs_4_.refs_8_ = f32[32,2048]{1,0:T(8,128)S(1)} collective-permute-done((f32[32,2048]{1,0:T(8,128)S(1)}, f32[32,2048]{1,0:T(8,128)S(1)}, u32[]{:S(2)}, u32[]{:S(2)}) %collective-permute-start.15) | collective-permute-done | bytes 262176 | tf_op jit(solution)/shard_map/ppermute | solution.py:404
  67.9 5.1 %collective-permute-start.19 = (f32[32,2048]{1,0:T(8,128)S(1)}, f32[32,2048]{1,0:T(8,128)S(1)}, u32[]{:S(2)}, u32[]{:S(2)}) collective-permute-start(f32[32,2048]{1,0:T(8,128)S(1)} %get-tuple-element.87), channel_id=1, source_target_pairs={{0,8},{1,9},{2,10},{3,11},{4,12},{5,13},{6,14},{7,15},{8,0},{9,1},... | collective-permute-start | bytes 786440 | tf_op jit(solution)/shard_map/ppermute | solution.py:404
  73.8 2.8 %collective-permute-start.21 = (f32[32,2048]{1,0:T(8,128)S(1)}, f32[32,2048]{1,0:T(8,128)S(1)}, u32[]{:S(2)}, u32[]{:S(2)}) collective-permute-start(f32[32,2048]{1,0:T(8,128)S(1)} %get-tuple-element.90), channel_id=1, source_target_pairs={{0,8},{1,9},{2,10},{3,11},{4,12},{5,13},{6,14},{7,15},{8,0},{9,1},... | collective-permute-start | bytes 786440 | tf_op jit(solution)/shard_map/ppermute | solution.py:404
  76.6 2.8 %collective-permute-done.19.refs_10_ = f32[32,2048]{1,0:T(8,128)S(1)} collective-permute-done((f32[32,2048]{1,0:T(8,128)S(1)}, f32[32,2048]{1,0:T(8,128)S(1)}, u32[]{:S(2)}, u32[]{:S(2)}) %collective-permute-start.19) | collective-permute-done | bytes 262176 | tf_op jit(solution)/shard_map/ppermute | solution.py:404
  79.5 4.2 %collective-permute-done.21.refs_11_ = f32[32,2048]{1,0:T(8,128)S(1)} collective-permute-done((f32[32,2048]{1,0:T(8,128)S(1)}, f32[32,2048]{1,0:T(8,128)S(1)}, u32[]{:S(2)}, u32[]{:S(2)}) %collective-permute-start.21) | collective-permute-done | bytes 262176 | tf_op jit(solution)/shard_map/ppermute | solution.py:404
  83.7 7.6 %assemble.1 = (bf16[192,4096]{1,0:T(8,128)(2,1)}, bf16[192,4096]{1,0:T(8,128)(2,1)}, bf16[4096,192]{1,0:T(8,128)(2,1)}, bf16[4096,192]{1,0:T(8,128)(2,1)}, f32[32,512]{1,0:T(8,128)S(1)}) custom-call(s32[2]{0:T(128)S(1)} %pad_add_fusion.here_ref, s32[6]{0:T(128)S(1)} %copy-done.4, s32[6]{0:T(128)S(1)} %copy-done.5, f32[4,32,4096]{2,1,0:T(8,128)S(1)} %copy-done, ...), custom_call_target="tpu_custom_call" | custom-call | flops 1811939328 | bytes 6291456 | tf_op jit(solution)/shard_map/assemble/pallas_call | solution.py:198
  92.7 2.7 %collective-permute-start.27 = (f32[32,512]{1,0:T(8,128)S(1)}, f32[32,512]{1,0:T(8,128)S(1)}, u32[]{:S(2)}, u32[]{:S(2)}) collective-permute-start(f32[32,512]{1,0:T(8,128)S(1)} %add.27), channel_id=1, source_target_pairs={{0,6},{1,7},{2,4},{3,5},{4,2},{5,3},{6,0},{7,1},{8,14},{9,15},{10,... | collective-permute-start | bytes 196616 | tf_op jit(solution)/shard_map/ppermute | solution.py:367
  96.2 10.5 %all-to-all-done = f32[8,64,4096]{2,1,0:T(8,128)} async-done(((f32[8,64,4096]{2,1,0:T(8,128)}), f32[8,64,4096]{2,1,0:T(8,128)}, u32[]{:S(2)}, u32[]{:S(2)}) %all-to-all-start) | async-done | bytes 8388640 | tf_op jit(solution)/shard_map/all_to_all | solution.py:409
  106.8 2.2 %lift.1 = (bf16[4096,192]{1,0:T(8,128)(2,1)S(1)}, bf16[4096,192]{1,0:T(8,128)(2,1)S(1)}) custom-call(bf16[4096,192]{1,0:T(8,128)(2,1)} %get-tuple-element.94.refs_0_, bf16[4096,192]{1,0:T(8,128)(2,1)} %get-tuple-element.95.refs_1_), custom_call_target="tpu_custom_call" | custom-call | bytes 3145728 | tf_op jit(solution)/shard_map/lift/pallas_call | solution.py:279
  109.1 10.0 %inner_products.1 = (f32[128,384]{1,0:T(8,128)S(1)}, f32[128,384]{1,0:T(8,128)S(1)}, f32[512,4096]{1,0:T(8,128)S(1)}) custom-call(s32[2]{0:T(128)S(1)} %pad_add_fusion.here_ref, f32[512,4096]{1,0:T(8,128)} %bitcast.2.x_ref, bf16[4096,192]{1,0:T(8,128)(2,1)S(1)} %get-tuple-element.96.high_ref, bf16[4096,192]{1,0:T(8,128)(2,1)S(1)} %get-tuple-element.97.low_ref), custom_call_target="tpu_custom_call" | custom-call | flops 2415919104 | bytes 8388608 | tf_op jit(solution)/shard_map/inner_products/pallas_call | solution.py:315
  121.8 3.5 %merge.1.p_ref = bf16[576,4096]{1,0:T(8,128)(2,1)S(1)} custom-call(f32[32,512]{1,0:T(8,128)S(1)} %add_add_fusion.refs_0_, f32[6,32,32]{2,1,0:T(8,128)S(1)} %copy-done.3, bf16[192,4096]{1,0:T(8,128)(2,1)S(1)} %copy-done.1, bf16[192,4096]{1,0:T(8,128)(2,1)S(1)} %copy-done.2), custom_call_target="tpu_custom_call" | custom-call | flops 905969664 | bytes 6291456 | tf_op jit(solution)/shard_map/merge/pallas_call | solution.py:236
  128.5 1.8 %collective-permute-done.32 = f32[64,384]{1,0:T(8,128)S(1)} collective-permute-done((f32[64,384]{1,0:T(8,128)S(1)}, f32[64,384]{1,0:T(8,128)S(1)}, u32[]{:S(2)}, u32[]{:S(2)}) %collective-permute-start.32) | collective-permute-done | bytes 98336 | tf_op jit(solution)/shard_map/ppermute | solution.py:367
  133.1 6.2 %update.1 = f32[512,4096]{1,0:T(8,128)} custom-call(s32[2]{0:T(128)S(1)} %pad_add_fusion.here_ref, f32[128,384]{1,0:T(8,128)S(1)} %pad_maximum_fusion.mine_ref, f32[128,384]{1,0:T(8,128)S(1)} %collective-permute-done.33.theirs_ref, f32[512,4096]{1,0:T(8,128)S(1)} %get-tuple-element.106.x_ref, bf16[576,4096]{1,0:T(8,128)(2,1)S(1)} %merge.1.p_ref), custom_call_target="tpu_custom_call" | custom-call | flops 2415919104 | bytes 16777216 | tf_op jit(solution)/shard_map/update/pallas_call | solution.py:350
  (78 shorter events, 21.0 us)
Async XLA Ops:
  6.1 100.7 %all-to-all-start = ((f32[8,64,4096]{2,1,0:T(8,128)}), f32[8,64,4096]{2,1,0:T(8,128)}, u32[]{:S(2)}, u32[]{:S(2)}) async-start(f32[8,64,4096]{2,1,0:T(8,128)} %pack.1), calls=%async_computation | async-start | bytes 16777216 | tf_op jit(solution)/shard_map/all_to_all | solution.py:409
  12.1 10.1 %collective-permute-start = (f32[32,2048]{1,0:T(8,128)S(1)}, f32[32,2048]{1,0:T(8,128)S(1)}, u32[]{:S(2)}, u32[]{:S(2)}) collective-permute-start(f32[32,2048]{1,0:T(8,128)S(1)} %get-tuple-element.57), channel_id=1, source_target_pairs={{0,8},{1,9},{2,10},{3,11},{4,12},{5,13},{6,14},{7,15},{8,0},{9,1},... | collective-permute-start | bytes 786440 | tf_op jit(solution)/shard_map/ppermute | solution.py:404
  15.1 7.1 %collective-permute-start.2 = (f32[32,2048]{1,0:T(8,128)S(1)}, f32[32,2048]{1,0:T(8,128)S(1)}, u32[]{:S(2)}, u32[]{:S(2)}) collective-permute-start(f32[32,2048]{1,0:T(8,128)S(1)} %get-tuple-element.58), channel_id=1, source_target_pairs={{0,1},{1,0},{2,3},{3,2},{4,5},{5,4},{6,7},{7,6},{8,16},{9,17},{10,... | collective-permute-start | bytes 786440 | tf_op jit(solution)/shard_map/ppermute | solution.py:404
  15.8 12.0 %collective-permute-start.1 = (f32[32,2048]{1,0:T(8,128)S(1)}, f32[32,2048]{1,0:T(8,128)S(1)}, u32[]{:S(2)}, u32[]{:S(2)}) collective-permute-start(f32[32,2048]{1,0:T(8,128)S(1)} %get-tuple-element.60), channel_id=1, source_target_pairs={{0,8},{1,9},{2,10},{3,11},{4,12},{5,13},{6,14},{7,15},{8,0},{9,1},... | collective-permute-start | bytes 786440 | tf_op jit(solution)/shard_map/ppermute | solution.py:404
  18.9 8.9 %collective-permute-start.4 = (f32[32,2048]{1,0:T(8,128)S(1)}, f32[32,2048]{1,0:T(8,128)S(1)}, u32[]{:S(2)}, u32[]{:S(2)}) collective-permute-start(f32[32,2048]{1,0:T(8,128)S(1)} %get-tuple-element.61), channel_id=1, source_target_pairs={{0,1},{1,0},{2,3},{3,2},{4,5},{5,4},{6,7},{7,6},{8,16},{9,17},{10,... | collective-permute-start | bytes 786440 | tf_op jit(solution)/shard_map/ppermute | solution.py:404
  22.9 10.6 %collective-permute-start.3 = (f32[32,2048]{1,0:T(8,128)S(1)}, f32[32,2048]{1,0:T(8,128)S(1)}, u32[]{:S(2)}, u32[]{:S(2)}) collective-permute-start(f32[32,2048]{1,0:T(8,128)S(1)} %get-tuple-element.63), channel_id=1, source_target_pairs={{0,8},{1,9},{2,10},{3,11},{4,12},{5,13},{6,14},{7,15},{8,0},{9,1},... | collective-permute-start | bytes 786440 | tf_op jit(solution)/shard_map/ppermute | solution.py:404
  26.0 7.4 %collective-permute-start.6 = (f32[32,2048]{1,0:T(8,128)S(1)}, f32[32,2048]{1,0:T(8,128)S(1)}, u32[]{:S(2)}, u32[]{:S(2)}) collective-permute-start(f32[32,2048]{1,0:T(8,128)S(1)} %get-tuple-element.64), channel_id=1, source_target_pairs={{0,1},{1,0},{2,3},{3,2},{4,5},{5,4},{6,7},{7,6},{8,16},{9,17},{10,... | collective-permute-start | bytes 786440 | tf_op jit(solution)/shard_map/ppermute | solution.py:404
  28.5 10.6 %collective-permute-start.5 = (f32[32,2048]{1,0:T(8,128)S(1)}, f32[32,2048]{1,0:T(8,128)S(1)}, u32[]{:S(2)}, u32[]{:S(2)}) collective-permute-start(f32[32,2048]{1,0:T(8,128)S(1)} %get-tuple-element.66), channel_id=1, source_target_pairs={{0,8},{1,9},{2,10},{3,11},{4,12},{5,13},{6,14},{7,15},{8,0},{9,1},... | collective-permute-start | bytes 786440 | tf_op jit(solution)/shard_map/ppermute | solution.py:404
  31.7 7.4 %collective-permute-start.8 = (f32[32,2048]{1,0:T(8,128)S(1)}, f32[32,2048]{1,0:T(8,128)S(1)}, u32[]{:S(2)}, u32[]{:S(2)}) collective-permute-start(f32[32,2048]{1,0:T(8,128)S(1)} %get-tuple-element.67), channel_id=1, source_target_pairs={{0,1},{1,0},{2,3},{3,2},{4,5},{5,4},{6,7},{7,6},{8,16},{9,17},{10,... | collective-permute-start | bytes 786440 | tf_op jit(solution)/shard_map/ppermute | solution.py:404
  34.1 10.6 %collective-permute-start.7 = (f32[32,2048]{1,0:T(8,128)S(1)}, f32[32,2048]{1,0:T(8,128)S(1)}, u32[]{:S(2)}, u32[]{:S(2)}) collective-permute-start(f32[32,2048]{1,0:T(8,128)S(1)} %get-tuple-element.69), channel_id=1, source_target_pairs={{0,8},{1,9},{2,10},{3,11},{4,12},{5,13},{6,14},{7,15},{8,0},{9,1},... | collective-permute-start | bytes 786440 | tf_op jit(solution)/shard_map/ppermute | solution.py:404
  37.3 7.4 %collective-permute-start.10 = (f32[32,2048]{1,0:T(8,128)S(1)}, f32[32,2048]{1,0:T(8,128)S(1)}, u32[]{:S(2)}, u32[]{:S(2)}) collective-permute-start(f32[32,2048]{1,0:T(8,128)S(1)} %get-tuple-element.70), channel_id=1, source_target_pairs={{0,1},{1,0},{2,3},{3,2},{4,5},{5,4},{6,7},{7,6},{8,16},{9,17},{10,... | collective-permute-start | bytes 786440 | tf_op jit(solution)/shard_map/ppermute | solution.py:404
  39.7 10.6 %collective-permute-start.9 = (f32[32,2048]{1,0:T(8,128)S(1)}, f32[32,2048]{1,0:T(8,128)S(1)}, u32[]{:S(2)}, u32[]{:S(2)}) collective-permute-start(f32[32,2048]{1,0:T(8,128)S(1)} %get-tuple-element.72), channel_id=1, source_target_pairs={{0,8},{1,9},{2,10},{3,11},{4,12},{5,13},{6,14},{7,15},{8,0},{9,1},... | collective-permute-start | bytes 786440 | tf_op jit(solution)/shard_map/ppermute | solution.py:404
  42.9 7.4 %collective-permute-start.12 = (f32[32,2048]{1,0:T(8,128)S(1)}, f32[32,2048]{1,0:T(8,128)S(1)}, u32[]{:S(2)}, u32[]{:S(2)}) collective-permute-start(f32[32,2048]{1,0:T(8,128)S(1)} %get-tuple-element.73), channel_id=1, source_target_pairs={{0,1},{1,0},{2,3},{3,2},{4,5},{5,4},{6,7},{7,6},{8,16},{9,17},{10,... | collective-permute-start | bytes 786440 | tf_op jit(solution)/shard_map/ppermute | solution.py:404
  45.4 10.5 %collective-permute-start.11 = (f32[32,2048]{1,0:T(8,128)S(1)}, f32[32,2048]{1,0:T(8,128)S(1)}, u32[]{:S(2)}, u32[]{:S(2)}) collective-permute-start(f32[32,2048]{1,0:T(8,128)S(1)} %get-tuple-element.75), channel_id=1, source_target_pairs={{0,8},{1,9},{2,10},{3,11},{4,12},{5,13},{6,14},{7,15},{8,0},{9,1},... | collective-permute-start | bytes 786440 | tf_op jit(solution)/shard_map/ppermute | solution.py:404
  48.5 7.4 %collective-permute-start.14 = (f32[32,2048]{1,0:T(8,128)S(1)}, f32[32,2048]{1,0:T(8,128)S(1)}, u32[]{:S(2)}, u32[]{:S(2)}) collective-permute-start(f32[32,2048]{1,0:T(8,128)S(1)} %get-tuple-element.76), channel_id=1, source_target_pairs={{0,1},{1,0},{2,3},{3,2},{4,5},{5,4},{6,7},{7,6},{8,16},{9,17},{10,... | collective-permute-start | bytes 786440 | tf_op jit(solution)/shard_map/ppermute | solution.py:404
  51.0 10.5 %collective-permute-start.13 = (f32[32,2048]{1,0:T(8,128)S(1)}, f32[32,2048]{1,0:T(8,128)S(1)}, u32[]{:S(2)}, u32[]{:S(2)}) collective-permute-start(f32[32,2048]{1,0:T(8,128)S(1)} %get-tuple-element.78), channel_id=1, source_target_pairs={{0,8},{1,9},{2,10},{3,11},{4,12},{5,13},{6,14},{7,15},{8,0},{9,1},... | collective-permute-start | bytes 786440 | tf_op jit(solution)/shard_map/ppermute | solution.py:404
  54.1 7.4 %collective-permute-start.16 = (f32[32,2048]{1,0:T(8,128)S(1)}, f32[32,2048]{1,0:T(8,128)S(1)}, u32[]{:S(2)}, u32[]{:S(2)}) collective-permute-start(f32[32,2048]{1,0:T(8,128)S(1)} %get-tuple-element.79), channel_id=1, source_target_pairs={{0,1},{1,0},{2,3},{3,2},{4,5},{5,4},{6,7},{7,6},{8,16},{9,17},{10,... | collective-permute-start | bytes 786440 | tf_op jit(solution)/shard_map/ppermute | solution.py:404
  56.6 10.5 %collective-permute-start.15 = (f32[32,2048]{1,0:T(8,128)S(1)}, f32[32,2048]{1,0:T(8,128)S(1)}, u32[]{:S(2)}, u32[]{:S(2)}) collective-permute-start(f32[32,2048]{1,0:T(8,128)S(1)} %get-tuple-element.81), channel_id=1, source_target_pairs={{0,8},{1,9},{2,10},{3,11},{4,12},{5,13},{6,14},{7,15},{8,0},{9,1},... | collective-permute-start | bytes 786440 | tf_op jit(solution)/shard_map/ppermute | solution.py:404
  59.8 7.4 %collective-permute-start.18 = (f32[32,2048]{1,0:T(8,128)S(1)}, f32[32,2048]{1,0:T(8,128)S(1)}, u32[]{:S(2)}, u32[]{:S(2)}) collective-permute-start(f32[32,2048]{1,0:T(8,128)S(1)} %get-tuple-element.82), channel_id=1, source_target_pairs={{0,1},{1,0},{2,3},{3,2},{4,5},{5,4},{6,7},{7,6},{8,16},{9,17},{10,... | collective-permute-start | bytes 786440 | tf_op jit(solution)/shard_map/ppermute | solution.py:404
  62.2 10.9 %collective-permute-start.17 = (f32[32,2048]{1,0:T(8,128)S(1)}, f32[32,2048]{1,0:T(8,128)S(1)}, u32[]{:S(2)}, u32[]{:S(2)}) collective-permute-start(f32[32,2048]{1,0:T(8,128)S(1)} %get-tuple-element.84), channel_id=1, source_target_pairs={{0,8},{1,9},{2,10},{3,11},{4,12},{5,13},{6,14},{7,15},{8,0},{9,1},... | collective-permute-start | bytes 786440 | tf_op jit(solution)/shard_map/ppermute | solution.py:404
  65.4 7.7 %collective-permute-start.20 = (f32[32,2048]{1,0:T(8,128)S(1)}, f32[32,2048]{1,0:T(8,128)S(1)}, u32[]{:S(2)}, u32[]{:S(2)}) collective-permute-start(f32[32,2048]{1,0:T(8,128)S(1)} %get-tuple-element.85), channel_id=1, source_target_pairs={{0,1},{1,0},{2,3},{3,2},{4,5},{5,4},{6,7},{7,6},{8,16},{9,17},{10,... | collective-permute-start | bytes 786440 | tf_op jit(solution)/shard_map/ppermute | solution.py:404
  67.8 11.6 %collective-permute-start.22 = (f32[32,2048]{1,0:T(8,128)S(1)}, f32[32,2048]{1,0:T(8,128)S(1)}, u32[]{:S(2)}, u32[]{:S(2)}) collective-permute-start(f32[32,2048]{1,0:T(8,128)S(1)} %get-tuple-element.88), channel_id=1, source_target_pairs={{0,1},{1,0},{2,3},{3,2},{4,5},{5,4},{6,7},{7,6},{8,16},{9,17},{10,... | collective-permute-start | bytes 786440 | tf_op jit(solution)/shard_map/ppermute | solution.py:404
  67.9 11.5 %collective-permute-start.19 = (f32[32,2048]{1,0:T(8,128)S(1)}, f32[32,2048]{1,0:T(8,128)S(1)}, u32[]{:S(2)}, u32[]{:S(2)}) collective-permute-start(f32[32,2048]{1,0:T(8,128)S(1)} %get-tuple-element.87), channel_id=1, source_target_pairs={{0,8},{1,9},{2,10},{3,11},{4,12},{5,13},{6,14},{7,15},{8,0},{9,1},... | collective-permute-start | bytes 786440 | tf_op jit(solution)/shard_map/ppermute | solution.py:404
  73.8 9.9 %collective-permute-start.21 = (f32[32,2048]{1,0:T(8,128)S(1)}, f32[32,2048]{1,0:T(8,128)S(1)}, u32[]{:S(2)}, u32[]{:S(2)}) collective-permute-start(f32[32,2048]{1,0:T(8,128)S(1)} %get-tuple-element.90), channel_id=1, source_target_pairs={{0,8},{1,9},{2,10},{3,11},{4,12},{5,13},{6,14},{7,15},{8,0},{9,1},... | collective-permute-start | bytes 786440 | tf_op jit(solution)/shard_map/ppermute | solution.py:404
  76.6 7.0 %collective-permute-start.23 = (f32[32,2048]{1,0:T(8,128)S(1)}, f32[32,2048]{1,0:T(8,128)S(1)}, u32[]{:S(2)}, u32[]{:S(2)}) collective-permute-start(f32[32,2048]{1,0:T(8,128)S(1)} %get-tuple-element.91), channel_id=1, source_target_pairs={{0,1},{1,0},{2,3},{3,2},{4,5},{5,4},{6,7},{7,6},{8,16},{9,17},{10,... | collective-permute-start | bytes 786440 | tf_op jit(solution)/shard_map/ppermute | solution.py:404
  92.7 16.3 %collective-permute-start.27 = (f32[32,512]{1,0:T(8,128)S(1)}, f32[32,512]{1,0:T(8,128)S(1)}, u32[]{:S(2)}, u32[]{:S(2)}) collective-permute-start(f32[32,512]{1,0:T(8,128)S(1)} %add.27), channel_id=1, source_target_pairs={{0,6},{1,7},{2,4},{3,5},{4,2},{5,3},{6,0},{7,1},{8,14},{9,15},{10,... | collective-permute-start | bytes 196616 | tf_op jit(solution)/shard_map/ppermute | solution.py:367
  95.3 13.7 %collective-permute-start.26 = (f32[32,512]{1,0:T(8,128)S(1)}, f32[32,512]{1,0:T(8,128)S(1)}, u32[]{:S(2)}, u32[]{:S(2)}) collective-permute-start(f32[32,512]{1,0:T(8,128)S(1)} %add.27), channel_id=1, source_target_pairs={{0,4},{1,5},{2,6},{3,7},{4,0},{5,1},{6,2},{7,3},{8,12},{9,13},{10,... | collective-permute-start | bytes 196616 | tf_op jit(solution)/shard_map/ppermute | solution.py:367
  95.9 13.1 %collective-permute-start.25 = (f32[32,512]{1,0:T(8,128)S(1)}, f32[32,512]{1,0:T(8,128)S(1)}, u32[]{:S(2)}, u32[]{:S(2)}) collective-permute-start(f32[32,512]{1,0:T(8,128)S(1)} %add.27), channel_id=1, source_target_pairs={{0,2},{1,3},{2,0},{3,1},{4,6},{5,7},{6,4},{7,5},{8,10},{9,11},{10,... | collective-permute-start | bytes 196616 | tf_op jit(solution)/shard_map/ppermute | solution.py:367
  120.7 4.9 %collective-permute-start.31 = (f32[64,384]{1,0:T(8,128)S(1)}, f32[64,384]{1,0:T(8,128)S(1)}, u32[]{:S(2)}, u32[]{:S(2)}) collective-permute-start(f32[64,384]{1,0:T(8,128)S(1)} %get-tuple-element.105), channel_id=1, source_target_pairs={{0,4},{1,5},{2,6},{3,7},{4,0},{5,1},{6,2},{7,3},{8,12},{9,13},{10,... | collective-permute-start | bytes 294920 | tf_op jit(solution)/shard_map/ppermute | solution.py:367
  121.2 5.6 %collective-permute-start.29 = (f32[64,384]{1,0:T(8,128)S(1)}, f32[64,384]{1,0:T(8,128)S(1)}, u32[]{:S(2)}, u32[]{:S(2)}) collective-permute-start(f32[64,384]{1,0:T(8,128)S(1)} %get-tuple-element.104), channel_id=1, source_target_pairs={{0,2},{1,3},{2,0},{3,1},{4,6},{5,7},{6,4},{7,5},{8,10},{9,11},{10,... | collective-permute-start | bytes 294920 | tf_op jit(solution)/shard_map/ppermute | solution.py:367
  125.6 4.7 %collective-permute-start.32 = (f32[64,384]{1,0:T(8,128)S(1)}, f32[64,384]{1,0:T(8,128)S(1)}, u32[]{:S(2)}, u32[]{:S(2)}) collective-permute-start(f32[64,384]{1,0:T(8,128)S(1)} %add.34), channel_id=1, source_target_pairs={{0,2},{1,3},{2,0},{3,1},{4,6},{5,7},{6,4},{7,5},{8,10},{9,11},{10,... | collective-permute-start | bytes 294920 | tf_op jit(solution)/shard_map/ppermute | solution.py:367
  126.9 4.7 %collective-permute-start.30 = (f32[64,384]{1,0:T(8,128)S(1)}, f32[64,384]{1,0:T(8,128)S(1)}, u32[]{:S(2)}, u32[]{:S(2)}) collective-permute-start(f32[64,384]{1,0:T(8,128)S(1)} %add.32), channel_id=1, source_target_pairs={{0,4},{1,5},{2,6},{3,7},{4,0},{5,1},{6,2},{7,3},{8,12},{9,13},{10,... | collective-permute-start | bytes 294920 | tf_op jit(solution)/shard_map/ppermute | solution.py:367
  (9 other events, 69.2 us)

commit v15 on v14

--- a/solution.py
+++ b/solution.py
@@ -294,7 +294,7 @@
     half = rows // 2
     step = rows // 8 if rows % 64 == 0 else rows
     n_copies = rows // step
-    cuts = sorted({0, n_copies // 2, n_copies})
+    cuts = sorted({0, n_copies // 8, n_copies})
 
     def kernel(here_ref, x_ref, high_ref, low_ref, mine_ref, theirs_ref, held, total, sems):
         copies = []

time: 140 us -> 138 us (0.986)
  Pallas kernels: 43.7 us -> 41.7 us
    pallas_call x1, Pallas kernels: 10 us -> 8.07 us  [inner_products(): pl.pallas_call(kernel, out_shape=[jax.ShapeDtypeStruct((half // 2, 2 * he...]
  transfers between devices with their start and end apart: 35 -> 35, of which waited for: 18 -> 18; matrix products, arithmetic and copies ran while one was open for 0% -> 0% of each run, Pallas kernels for 15% -> 16%
where the time goes in v15:
time: 138 us
  starting transfers between devices  52.6 us (38%)
  waiting for transfers between devices  42.4 us (31%)
  Pallas kernels  41.7 us (30%)
    ppermute x24, starting transfers between devices, exchange(): return lax.ppermute(array, ('row', 'wide'), pairs)  39.6 us
    ppermute x24, waiting for transfers between devices, exchange(): return lax.ppermute(array, ('row', 'wide'), pairs)  24.4 us
    all_to_all x1, waiting for transfers between devices, body(): x = lax.all_to_all(piece, 'wide', split_axis=0, concat_axis=0, tiled=True)  10.5 us
    pallas_call x1, Pallas kernels, inner_products(): pl.pallas_call(kernel, out_shape=[jax.ShapeDtypeStruct((half // 2, 2 * he...  8.07 us
    pallas_call x12, Pallas kernels, feed(): pl.pallas_call(kernel, out_shape=[jax.ShapeDtypeStruct((width, cols), jnp...  8.07 us
    ppermute x10, starting transfers between devices, swap(): return lax.ppermute(array, 'wide', [(i, i ^ k) for i in range(size)])  7.77 us
    pallas_call x1, Pallas kernels, assemble(): pl.pallas_call(kernel, out_shape=[pltpu.HBM((height, ncols), jnp.bfloat16...  7.65 us
    ppermute x10, waiting for transfers between devices, swap(): return lax.ppermute(array, 'wide', [(i, i ^ k) for i in range(size)])  7.43 us
  transfers between devices with their start and end apart: 35, of which 18 were waited for; matrix products, arithmetic and copies ran while one was open for 0% of the time, Pallas kernels for 16%

profile of v15, /device:TPU:0, one launch (start us, length us, event | category | flops | bytes accessed | tf_op | source)
XLA Modules:
  0.0 137.5 jit_solution(5533392616224562007)
XLA Ops:
  0.0 6.0 %pack.1 = f32[8,64,4096]{2,1,0:T(8,128)} custom-call(f32[64,32768]{1,0:T(8,128)} %x_ref.1), custom_call_target="tpu_custom_call" | custom-call | bytes 16777216 | tf_op jit(solution)/shard_map/pack/pallas_call | solution.py:82
  6.1 5.3 %all-to-all-start = ((f32[8,64,4096]{2,1,0:T(8,128)}), f32[8,64,4096]{2,1,0:T(8,128)}, u32[]{:S(2)}, u32[]{:S(2)}) async-start(f32[8,64,4096]{2,1,0:T(8,128)} %pack.1), calls=%async_computation | async-start | bytes 16777216 | tf_op jit(solution)/shard_map/all_to_all | solution.py:409
  12.1 2.9 %collective-permute-start = (f32[32,2048]{1,0:T(8,128)S(1)}, f32[32,2048]{1,0:T(8,128)S(1)}, u32[]{:S(2)}, u32[]{:S(2)}) collective-permute-start(f32[32,2048]{1,0:T(8,128)S(1)} %get-tuple-element.57), channel_id=1, source_target_pairs={{0,8},{1,9},{2,10},{3,11},{4,12},{5,13},{6,14},{7,15},{8,0},{9,1},... | collective-permute-start | bytes 786440 | tf_op jit(solution)/shard_map/ppermute | solution.py:404
  15.8 3.1 %collective-permute-start.1 = (f32[32,2048]{1,0:T(8,128)S(1)}, f32[32,2048]{1,0:T(8,128)S(1)}, u32[]{:S(2)}, u32[]{:S(2)}) collective-permute-start(f32[32,2048]{1,0:T(8,128)S(1)} %get-tuple-element.60), channel_id=1, source_target_pairs={{0,8},{1,9},{2,10},{3,11},{4,12},{5,13},{6,14},{7,15},{8,0},{9,1},... | collective-permute-start | bytes 786440 | tf_op jit(solution)/shard_map/ppermute | solution.py:404
  18.9 3.3 %collective-permute-done.refs_0_ = f32[32,2048]{1,0:T(8,128)S(1)} collective-permute-done((f32[32,2048]{1,0:T(8,128)S(1)}, f32[32,2048]{1,0:T(8,128)S(1)}, u32[]{:S(2)}, u32[]{:S(2)}) %collective-permute-start) | collective-permute-done | bytes 262176 | tf_op jit(solution)/shard_map/ppermute | solution.py:404
  22.9 3.2 %collective-permute-start.3 = (f32[32,2048]{1,0:T(8,128)S(1)}, f32[32,2048]{1,0:T(8,128)S(1)}, u32[]{:S(2)}, u32[]{:S(2)}) collective-permute-start(f32[32,2048]{1,0:T(8,128)S(1)} %get-tuple-element.63), channel_id=1, source_target_pairs={{0,8},{1,9},{2,10},{3,11},{4,12},{5,13},{6,14},{7,15},{8,0},{9,1},... | collective-permute-start | bytes 786440 | tf_op jit(solution)/shard_map/ppermute | solution.py:404
  26.0 1.8 %collective-permute-done.1.refs_0_.refs_1_ = f32[32,2048]{1,0:T(8,128)S(1)} collective-permute-done((f32[32,2048]{1,0:T(8,128)S(1)}, f32[32,2048]{1,0:T(8,128)S(1)}, u32[]{:S(2)}, u32[]{:S(2)}) %collective-permute-start.1) | collective-permute-done | bytes 262176 | tf_op jit(solution)/shard_map/ppermute | solution.py:404
  28.5 3.2 %collective-permute-start.5 = (f32[32,2048]{1,0:T(8,128)S(1)}, f32[32,2048]{1,0:T(8,128)S(1)}, u32[]{:S(2)}, u32[]{:S(2)}) collective-permute-start(f32[32,2048]{1,0:T(8,128)S(1)} %get-tuple-element.66), channel_id=1, source_target_pairs={{0,8},{1,9},{2,10},{3,11},{4,12},{5,13},{6,14},{7,15},{8,0},{9,1},... | collective-permute-start | bytes 786440 | tf_op jit(solution)/shard_map/ppermute | solution.py:404
  31.7 1.8 %collective-permute-done.3.refs_1_.refs_2_ = f32[32,2048]{1,0:T(8,128)S(1)} collective-permute-done((f32[32,2048]{1,0:T(8,128)S(1)}, f32[32,2048]{1,0:T(8,128)S(1)}, u32[]{:S(2)}, u32[]{:S(2)}) %collective-permute-start.3) | collective-permute-done | bytes 262176 | tf_op jit(solution)/shard_map/ppermute | solution.py:404
  34.1 3.2 %collective-permute-start.7 = (f32[32,2048]{1,0:T(8,128)S(1)}, f32[32,2048]{1,0:T(8,128)S(1)}, u32[]{:S(2)}, u32[]{:S(2)}) collective-permute-start(f32[32,2048]{1,0:T(8,128)S(1)} %get-tuple-element.69), channel_id=1, source_target_pairs={{0,8},{1,9},{2,10},{3,11},{4,12},{5,13},{6,14},{7,15},{8,0},{9,1},... | collective-permute-start | bytes 786440 | tf_op jit(solution)/shard_map/ppermute | solution.py:404
  37.3 1.8 %collective-permute-done.5.refs_1_.refs_3_ = f32[32,2048]{1,0:T(8,128)S(1)} collective-permute-done((f32[32,2048]{1,0:T(8,128)S(1)}, f32[32,2048]{1,0:T(8,128)S(1)}, u32[]{:S(2)}, u32[]{:S(2)}) %collective-permute-start.5) | collective-permute-done | bytes 262176 | tf_op jit(solution)/shard_map/ppermute | solution.py:404
  39.7 3.2 %collective-permute-start.9 = (f32[32,2048]{1,0:T(8,128)S(1)}, f32[32,2048]{1,0:T(8,128)S(1)}, u32[]{:S(2)}, u32[]{:S(2)}) collective-permute-start(f32[32,2048]{1,0:T(8,128)S(1)} %get-tuple-element.72), channel_id=1, source_target_pairs={{0,8},{1,9},{2,10},{3,11},{4,12},{5,13},{6,14},{7,15},{8,0},{9,1},... | collective-permute-start | bytes 786440 | tf_op jit(solution)/shard_map/ppermute | solution.py:404
  42.9 1.8 %collective-permute-done.7.refs_2_.refs_4_ = f32[32,2048]{1,0:T(8,128)S(1)} collective-permute-done((f32[32,2048]{1,0:T(8,128)S(1)}, f32[32,2048]{1,0:T(8,128)S(1)}, u32[]{:S(2)}, u32[]{:S(2)}) %collective-permute-start.7) | collective-permute-done | bytes 262176 | tf_op jit(solution)/shard_map/ppermute | solution.py:404
  45.4 3.2 %collective-permute-start.11 = (f32[32,2048]{1,0:T(8,128)S(1)}, f32[32,2048]{1,0:T(8,128)S(1)}, u32[]{:S(2)}, u32[]{:S(2)}) collective-permute-start(f32[32,2048]{1,0:T(8,128)S(1)} %get-tuple-element.75), channel_id=1, source_target_pairs={{0,8},{1,9},{2,10},{3,11},{4,12},{5,13},{6,14},{7,15},{8,0},{9,1},... | collective-permute-start | bytes 786440 | tf_op jit(solution)/shard_map/ppermute | solution.py:404
  48.5 1.8 %collective-permute-done.9.refs_2_.refs_5_ = f32[32,2048]{1,0:T(8,128)S(1)} collective-permute-done((f32[32,2048]{1,0:T(8,128)S(1)}, f32[32,2048]{1,0:T(8,128)S(1)}, u32[]{:S(2)}, u32[]{:S(2)}) %collective-permute-start.9) | collective-permute-done | bytes 262176 | tf_op jit(solution)/shard_map/ppermute | solution.py:404
  51.0 3.2 %collective-permute-start.13 = (f32[32,2048]{1,0:T(8,128)S(1)}, f32[32,2048]{1,0:T(8,128)S(1)}, u32[]{:S(2)}, u32[]{:S(2)}) collective-permute-start(f32[32,2048]{1,0:T(8,128)S(1)} %get-tuple-element.78), channel_id=1, source_target_pairs={{0,8},{1,9},{2,10},{3,11},{4,12},{5,13},{6,14},{7,15},{8,0},{9,1},... | collective-permute-start | bytes 786440 | tf_op jit(solution)/shard_map/ppermute | solution.py:404
  54.1 1.8 %collective-permute-done.11.refs_3_.refs_6_ = f32[32,2048]{1,0:T(8,128)S(1)} collective-permute-done((f32[32,2048]{1,0:T(8,128)S(1)}, f32[32,2048]{1,0:T(8,128)S(1)}, u32[]{:S(2)}, u32[]{:S(2)}) %collective-permute-start.11) | collective-permute-done | bytes 262176 | tf_op jit(solution)/shard_map/ppermute | solution.py:404
  56.6 3.2 %collective-permute-start.15 = (f32[32,2048]{1,0:T(8,128)S(1)}, f32[32,2048]{1,0:T(8,128)S(1)}, u32[]{:S(2)}, u32[]{:S(2)}) collective-permute-start(f32[32,2048]{1,0:T(8,128)S(1)} %get-tuple-element.81), channel_id=1, source_target_pairs={{0,8},{1,9},{2,10},{3,11},{4,12},{5,13},{6,14},{7,15},{8,0},{9,1},... | collective-permute-start | bytes 786440 | tf_op jit(solution)/shard_map/ppermute | solution.py:404
  62.2 3.2 %collective-permute-start.17 = (f32[32,2048]{1,0:T(8,128)S(1)}, f32[32,2048]{1,0:T(8,128)S(1)}, u32[]{:S(2)}, u32[]{:S(2)}) collective-permute-start(f32[32,2048]{1,0:T(8,128)S(1)} %get-tuple-element.84), channel_id=1, source_target_pairs={{0,8},{1,9},{2,10},{3,11},{4,12},{5,13},{6,14},{7,15},{8,0},{9,1},... | collective-permute-start | bytes 786440 | tf_op jit(solution)/shard_map/ppermute | solution.py:404
  65.4 1.7 %collective-permute-done.15.refs_4_.refs_8_ = f32[32,2048]{1,0:T(8,128)S(1)} collective-permute-done((f32[32,2048]{1,0:T(8,128)S(1)}, f32[32,2048]{1,0:T(8,128)S(1)}, u32[]{:S(2)}, u32[]{:S(2)}) %collective-permute-start.15) | collective-permute-done | bytes 262176 | tf_op jit(solution)/shard_map/ppermute | solution.py:404
  67.9 5.1 %collective-permute-start.19 = (f32[32,2048]{1,0:T(8,128)S(1)}, f32[32,2048]{1,0:T(8,128)S(1)}, u32[]{:S(2)}, u32[]{:S(2)}) collective-permute-start(f32[32,2048]{1,0:T(8,128)S(1)} %get-tuple-element.87), channel_id=1, source_target_pairs={{0,8},{1,9},{2,10},{3,11},{4,12},{5,13},{6,14},{7,15},{8,0},{9,1},... | collective-permute-start | bytes 786440 | tf_op jit(solution)/shard_map/ppermute | solution.py:404
  73.8 2.8 %collective-permute-start.21 = (f32[32,2048]{1,0:T(8,128)S(1)}, f32[32,2048]{1,0:T(8,128)S(1)}, u32[]{:S(2)}, u32[]{:S(2)}) collective-permute-start(f32[32,2048]{1,0:T(8,128)S(1)} %get-tuple-element.90), channel_id=1, source_target_pairs={{0,8},{1,9},{2,10},{3,11},{4,12},{5,13},{6,14},{7,15},{8,0},{9,1},... | collective-permute-start | bytes 786440 | tf_op jit(solution)/shard_map/ppermute | solution.py:404
  76.6 2.8 %collective-permute-done.19.refs_10_ = f32[32,2048]{1,0:T(8,128)S(1)} collective-permute-done((f32[32,2048]{1,0:T(8,128)S(1)}, f32[32,2048]{1,0:T(8,128)S(1)}, u32[]{:S(2)}, u32[]{:S(2)}) %collective-permute-start.19) | collective-permute-done | bytes 262176 | tf_op jit(solution)/shard_map/ppermute | solution.py:404
  79.5 4.2 %collective-permute-done.21.refs_11_ = f32[32,2048]{1,0:T(8,128)S(1)} collective-permute-done((f32[32,2048]{1,0:T(8,128)S(1)}, f32[32,2048]{1,0:T(8,128)S(1)}, u32[]{:S(2)}, u32[]{:S(2)}) %collective-permute-start.21) | collective-permute-done | bytes 262176 | tf_op jit(solution)/shard_map/ppermute | solution.py:404
  83.7 7.6 %assemble.1 = (bf16[192,4096]{1,0:T(8,128)(2,1)}, bf16[192,4096]{1,0:T(8,128)(2,1)}, bf16[4096,192]{1,0:T(8,128)(2,1)}, bf16[4096,192]{1,0:T(8,128)(2,1)}, f32[32,512]{1,0:T(8,128)S(1)}) custom-call(s32[2]{0:T(128)S(1)} %pad_add_fusion.here_ref, s32[6]{0:T(128)S(1)} %copy-done.4, s32[6]{0:T(128)S(1)} %copy-done.5, f32[4,32,4096]{2,1,0:T(8,128)S(1)} %copy-done, ...), custom_call_target="tpu_custom_call" | custom-call | flops 1811939328 | bytes 6291456 | tf_op jit(solution)/shard_map/assemble/pallas_call | solution.py:198
  92.7 2.7 %collective-permute-start.27 = (f32[32,512]{1,0:T(8,128)S(1)}, f32[32,512]{1,0:T(8,128)S(1)}, u32[]{:S(2)}, u32[]{:S(2)}) collective-permute-start(f32[32,512]{1,0:T(8,128)S(1)} %add.27), channel_id=1, source_target_pairs={{0,6},{1,7},{2,4},{3,5},{4,2},{5,3},{6,0},{7,1},{8,14},{9,15},{10,... | collective-permute-start | bytes 196616 | tf_op jit(solution)/shard_map/ppermute | solution.py:367
  96.2 10.5 %all-to-all-done = f32[8,64,4096]{2,1,0:T(8,128)} async-done(((f32[8,64,4096]{2,1,0:T(8,128)}), f32[8,64,4096]{2,1,0:T(8,128)}, u32[]{:S(2)}, u32[]{:S(2)}) %all-to-all-start) | async-done | bytes 8388640 | tf_op jit(solution)/shard_map/all_to_all | solution.py:409
  106.8 2.2 %lift.1 = (bf16[4096,192]{1,0:T(8,128)(2,1)S(1)}, bf16[4096,192]{1,0:T(8,128)(2,1)S(1)}) custom-call(bf16[4096,192]{1,0:T(8,128)(2,1)} %get-tuple-element.94.refs_0_, bf16[4096,192]{1,0:T(8,128)(2,1)} %get-tuple-element.95.refs_1_), custom_call_target="tpu_custom_call" | custom-call | bytes 3145728 | tf_op jit(solution)/shard_map/lift/pallas_call | solution.py:279
  109.1 8.1 %inner_products.1 = (f32[128,384]{1,0:T(8,128)S(1)}, f32[128,384]{1,0:T(8,128)S(1)}, f32[512,4096]{1,0:T(8,128)S(1)}) custom-call(s32[2]{0:T(128)S(1)} %pad_add_fusion.here_ref, f32[512,4096]{1,0:T(8,128)} %bitcast.2.x_ref, bf16[4096,192]{1,0:T(8,128)(2,1)S(1)} %get-tuple-element.96.high_ref, bf16[4096,192]{1,0:T(8,128)(2,1)S(1)} %get-tuple-element.97.low_ref), custom_call_target="tpu_custom_call" | custom-call | flops 2415919104 | bytes 8388608 | tf_op jit(solution)/shard_map/inner_products/pallas_call | solution.py:315
  119.9 3.5 %merge.1.p_ref = bf16[576,4096]{1,0:T(8,128)(2,1)S(1)} custom-call(f32[32,512]{1,0:T(8,128)S(1)} %add_add_fusion.refs_0_, f32[6,32,32]{2,1,0:T(8,128)S(1)} %copy-done.3, bf16[192,4096]{1,0:T(8,128)(2,1)S(1)} %copy-done.1, bf16[192,4096]{1,0:T(8,128)(2,1)S(1)} %copy-done.2), custom_call_target="tpu_custom_call" | custom-call | flops 905969664 | bytes 6291456 | tf_op jit(solution)/shard_map/merge/pallas_call | solution.py:236
  126.5 1.8 %collective-permute-done.32 = f32[64,384]{1,0:T(8,128)S(1)} collective-permute-done((f32[64,384]{1,0:T(8,128)S(1)}, f32[64,384]{1,0:T(8,128)S(1)}, u32[]{:S(2)}, u32[]{:S(2)}) %collective-permute-start.32) | collective-permute-done | bytes 98336 | tf_op jit(solution)/shard_map/ppermute | solution.py:367
  131.2 6.2 %update.1 = f32[512,4096]{1,0:T(8,128)} custom-call(s32[2]{0:T(128)S(1)} %pad_add_fusion.here_ref, f32[128,384]{1,0:T(8,128)S(1)} %pad_maximum_fusion.mine_ref, f32[128,384]{1,0:T(8,128)S(1)} %collective-permute-done.33.theirs_ref, f32[512,4096]{1,0:T(8,128)S(1)} %get-tuple-element.106.x_ref, bf16[576,4096]{1,0:T(8,128)(2,1)S(1)} %merge.1.p_ref), custom_call_target="tpu_custom_call" | custom-call | flops 2415919104 | bytes 16777216 | tf_op jit(solution)/shard_map/update/pallas_call | solution.py:350
  (78 shorter events, 21.0 us)
Async XLA Ops:
  6.1 100.7 %all-to-all-start = ((f32[8,64,4096]{2,1,0:T(8,128)}), f32[8,64,4096]{2,1,0:T(8,128)}, u32[]{:S(2)}, u32[]{:S(2)}) async-start(f32[8,64,4096]{2,1,0:T(8,128)} %pack.1), calls=%async_computation | async-start | bytes 16777216 | tf_op jit(solution)/shard_map/all_to_all | solution.py:409
  12.1 10.1 %collective-permute-start = (f32[32,2048]{1,0:T(8,128)S(1)}, f32[32,2048]{1,0:T(8,128)S(1)}, u32[]{:S(2)}, u32[]{:S(2)}) collective-permute-start(f32[32,2048]{1,0:T(8,128)S(1)} %get-tuple-element.57), channel_id=1, source_target_pairs={{0,8},{1,9},{2,10},{3,11},{4,12},{5,13},{6,14},{7,15},{8,0},{9,1},... | collective-permute-start | bytes 786440 | tf_op jit(solution)/shard_map/ppermute | solution.py:404
  15.1 7.1 %collective-permute-start.2 = (f32[32,2048]{1,0:T(8,128)S(1)}, f32[32,2048]{1,0:T(8,128)S(1)}, u32[]{:S(2)}, u32[]{:S(2)}) collective-permute-start(f32[32,2048]{1,0:T(8,128)S(1)} %get-tuple-element.58), channel_id=1, source_target_pairs={{0,1},{1,0},{2,3},{3,2},{4,5},{5,4},{6,7},{7,6},{8,16},{9,17},{10,... | collective-permute-start | bytes 786440 | tf_op jit(solution)/shard_map/ppermute | solution.py:404
  15.8 12.0 %collective-permute-start.1 = (f32[32,2048]{1,0:T(8,128)S(1)}, f32[32,2048]{1,0:T(8,128)S(1)}, u32[]{:S(2)}, u32[]{:S(2)}) collective-permute-start(f32[32,2048]{1,0:T(8,128)S(1)} %get-tuple-element.60), channel_id=1, source_target_pairs={{0,8},{1,9},{2,10},{3,11},{4,12},{5,13},{6,14},{7,15},{8,0},{9,1},... | collective-permute-start | bytes 786440 | tf_op jit(solution)/shard_map/ppermute | solution.py:404
  18.9 8.9 %collective-permute-start.4 = (f32[32,2048]{1,0:T(8,128)S(1)}, f32[32,2048]{1,0:T(8,128)S(1)}, u32[]{:S(2)}, u32[]{:S(2)}) collective-permute-start(f32[32,2048]{1,0:T(8,128)S(1)} %get-tuple-element.61), channel_id=1, source_target_pairs={{0,1},{1,0},{2,3},{3,2},{4,5},{5,4},{6,7},{7,6},{8,16},{9,17},{10,... | collective-permute-start | bytes 786440 | tf_op jit(solution)/shard_map/ppermute | solution.py:404
  22.9 10.6 %collective-permute-start.3 = (f32[32,2048]{1,0:T(8,128)S(1)}, f32[32,2048]{1,0:T(8,128)S(1)}, u32[]{:S(2)}, u32[]{:S(2)}) collective-permute-start(f32[32,2048]{1,0:T(8,128)S(1)} %get-tuple-element.63), channel_id=1, source_target_pairs={{0,8},{1,9},{2,10},{3,11},{4,12},{5,13},{6,14},{7,15},{8,0},{9,1},... | collective-permute-start | bytes 786440 | tf_op jit(solution)/shard_map/ppermute | solution.py:404
  26.0 7.4 %collective-permute-start.6 = (f32[32,2048]{1,0:T(8,128)S(1)}, f32[32,2048]{1,0:T(8,128)S(1)}, u32[]{:S(2)}, u32[]{:S(2)}) collective-permute-start(f32[32,2048]{1,0:T(8,128)S(1)} %get-tuple-element.64), channel_id=1, source_target_pairs={{0,1},{1,0},{2,3},{3,2},{4,5},{5,4},{6,7},{7,6},{8,16},{9,17},{10,... | collective-permute-start | bytes 786440 | tf_op jit(solution)/shard_map/ppermute | solution.py:404
  28.5 10.6 %collective-permute-start.5 = (f32[32,2048]{1,0:T(8,128)S(1)}, f32[32,2048]{1,0:T(8,128)S(1)}, u32[]{:S(2)}, u32[]{:S(2)}) collective-permute-start(f32[32,2048]{1,0:T(8,128)S(1)} %get-tuple-element.66), channel_id=1, source_target_pairs={{0,8},{1,9},{2,10},{3,11},{4,12},{5,13},{6,14},{7,15},{8,0},{9,1},... | collective-permute-start | bytes 786440 | tf_op jit(solution)/shard_map/ppermute | solution.py:404
  31.7 7.4 %collective-permute-start.8 = (f32[32,2048]{1,0:T(8,128)S(1)}, f32[32,2048]{1,0:T(8,128)S(1)}, u32[]{:S(2)}, u32[]{:S(2)}) collective-permute-start(f32[32,2048]{1,0:T(8,128)S(1)} %get-tuple-element.67), channel_id=1, source_target_pairs={{0,1},{1,0},{2,3},{3,2},{4,5},{5,4},{6,7},{7,6},{8,16},{9,17},{10,... | collective-permute-start | bytes 786440 | tf_op jit(solution)/shard_map/ppermute | solution.py:404
  34.1 10.6 %collective-permute-start.7 = (f32[32,2048]{1,0:T(8,128)S(1)}, f32[32,2048]{1,0:T(8,128)S(1)}, u32[]{:S(2)}, u32[]{:S(2)}) collective-permute-start(f32[32,2048]{1,0:T(8,128)S(1)} %get-tuple-element.69), channel_id=1, source_target_pairs={{0,8},{1,9},{2,10},{3,11},{4,12},{5,13},{6,14},{7,15},{8,0},{9,1},... | collective-permute-start | bytes 786440 | tf_op jit(solution)/shard_map/ppermute | solution.py:404
  37.3 7.4 %collective-permute-start.10 = (f32[32,2048]{1,0:T(8,128)S(1)}, f32[32,2048]{1,0:T(8,128)S(1)}, u32[]{:S(2)}, u32[]{:S(2)}) collective-permute-start(f32[32,2048]{1,0:T(8,128)S(1)} %get-tuple-element.70), channel_id=1, source_target_pairs={{0,1},{1,0},{2,3},{3,2},{4,5},{5,4},{6,7},{7,6},{8,16},{9,17},{10,... | collective-permute-start | bytes 786440 | tf_op jit(solution)/shard_map/ppermute | solution.py:404
  39.7 10.6 %collective-permute-start.9 = (f32[32,2048]{1,0:T(8,128)S(1)}, f32[32,2048]{1,0:T(8,128)S(1)}, u32[]{:S(2)}, u32[]{:S(2)}) collective-permute-start(f32[32,2048]{1,0:T(8,128)S(1)} %get-tuple-element.72), channel_id=1, source_target_pairs={{0,8},{1,9},{2,10},{3,11},{4,12},{5,13},{6,14},{7,15},{8,0},{9,1},... | collective-permute-start | bytes 786440 | tf_op jit(solution)/shard_map/ppermute | solution.py:404
  42.9 7.4 %collective-permute-start.12 = (f32[32,2048]{1,0:T(8,128)S(1)}, f32[32,2048]{1,0:T(8,128)S(1)}, u32[]{:S(2)}, u32[]{:S(2)}) collective-permute-start(f32[32,2048]{1,0:T(8,128)S(1)} %get-tuple-element.73), channel_id=1, source_target_pairs={{0,1},{1,0},{2,3},{3,2},{4,5},{5,4},{6,7},{7,6},{8,16},{9,17},{10,... | collective-permute-start | bytes 786440 | tf_op jit(solution)/shard_map/ppermute | solution.py:404
  45.4 10.5 %collective-permute-start.11 = (f32[32,2048]{1,0:T(8,128)S(1)}, f32[32,2048]{1,0:T(8,128)S(1)}, u32[]{:S(2)}, u32[]{:S(2)}) collective-permute-start(f32[32,2048]{1,0:T(8,128)S(1)} %get-tuple-element.75), channel_id=1, source_target_pairs={{0,8},{1,9},{2,10},{3,11},{4,12},{5,13},{6,14},{7,15},{8,0},{9,1},... | collective-permute-start | bytes 786440 | tf_op jit(solution)/shard_map/ppermute | solution.py:404
  48.5 7.4 %collective-permute-start.14 = (f32[32,2048]{1,0:T(8,128)S(1)}, f32[32,2048]{1,0:T(8,128)S(1)}, u32[]{:S(2)}, u32[]{:S(2)}) collective-permute-start(f32[32,2048]{1,0:T(8,128)S(1)} %get-tuple-element.76), channel_id=1, source_target_pairs={{0,1},{1,0},{2,3},{3,2},{4,5},{5,4},{6,7},{7,6},{8,16},{9,17},{10,... | collective-permute-start | bytes 786440 | tf_op jit(solution)/shard_map/ppermute | solution.py:404
  51.0 10.5 %collective-permute-start.13 = (f32[32,2048]{1,0:T(8,128)S(1)}, f32[32,2048]{1,0:T(8,128)S(1)}, u32[]{:S(2)}, u32[]{:S(2)}) collective-permute-start(f32[32,2048]{1,0:T(8,128)S(1)} %get-tuple-element.78), channel_id=1, source_target_pairs={{0,8},{1,9},{2,10},{3,11},{4,12},{5,13},{6,14},{7,15},{8,0},{9,1},... | collective-permute-start | bytes 786440 | tf_op jit(solution)/shard_map/ppermute | solution.py:404
  54.1 7.4 %collective-permute-start.16 = (f32[32,2048]{1,0:T(8,128)S(1)}, f32[32,2048]{1,0:T(8,128)S(1)}, u32[]{:S(2)}, u32[]{:S(2)}) collective-permute-start(f32[32,2048]{1,0:T(8,128)S(1)} %get-tuple-element.79), channel_id=1, source_target_pairs={{0,1},{1,0},{2,3},{3,2},{4,5},{5,4},{6,7},{7,6},{8,16},{9,17},{10,... | collective-permute-start | bytes 786440 | tf_op jit(solution)/shard_map/ppermute | solution.py:404
  56.6 10.5 %collective-permute-start.15 = (f32[32,2048]{1,0:T(8,128)S(1)}, f32[32,2048]{1,0:T(8,128)S(1)}, u32[]{:S(2)}, u32[]{:S(2)}) collective-permute-start(f32[32,2048]{1,0:T(8,128)S(1)} %get-tuple-element.81), channel_id=1, source_target_pairs={{0,8},{1,9},{2,10},{3,11},{4,12},{5,13},{6,14},{7,15},{8,0},{9,1},... | collective-permute-start | bytes 786440 | tf_op jit(solution)/shard_map/ppermute | solution.py:404
  59.8 7.4 %collective-permute-start.18 = (f32[32,2048]{1,0:T(8,128)S(1)}, f32[32,2048]{1,0:T(8,128)S(1)}, u32[]{:S(2)}, u32[]{:S(2)}) collective-permute-start(f32[32,2048]{1,0:T(8,128)S(1)} %get-tuple-element.82), channel_id=1, source_target_pairs={{0,1},{1,0},{2,3},{3,2},{4,5},{5,4},{6,7},{7,6},{8,16},{9,17},{10,... | collective-permute-start | bytes 786440 | tf_op jit(solution)/shard_map/ppermute | solution.py:404
  62.2 10.9 %collective-permute-start.17 = (f32[32,2048]{1,0:T(8,128)S(1)}, f32[32,2048]{1,0:T(8,128)S(1)}, u32[]{:S(2)}, u32[]{:S(2)}) collective-permute-start(f32[32,2048]{1,0:T(8,128)S(1)} %get-tuple-element.84), channel_id=1, source_target_pairs={{0,8},{1,9},{2,10},{3,11},{4,12},{5,13},{6,14},{7,15},{8,0},{9,1},... | collective-permute-start | bytes 786440 | tf_op jit(solution)/shard_map/ppermute | solution.py:404
  65.4 7.7 %collective-permute-start.20 = (f32[32,2048]{1,0:T(8,128)S(1)}, f32[32,2048]{1,0:T(8,128)S(1)}, u32[]{:S(2)}, u32[]{:S(2)}) collective-permute-start(f32[32,2048]{1,0:T(8,128)S(1)} %get-tuple-element.85), channel_id=1, source_target_pairs={{0,1},{1,0},{2,3},{3,2},{4,5},{5,4},{6,7},{7,6},{8,16},{9,17},{10,... | collective-permute-start | bytes 786440 | tf_op jit(solution)/shard_map/ppermute | solution.py:404
  67.8 11.6 %collective-permute-start.22 = (f32[32,2048]{1,0:T(8,128)S(1)}, f32[32,2048]{1,0:T(8,128)S(1)}, u32[]{:S(2)}, u32[]{:S(2)}) collective-permute-start(f32[32,2048]{1,0:T(8,128)S(1)} %get-tuple-element.88), channel_id=1, source_target_pairs={{0,1},{1,0},{2,3},{3,2},{4,5},{5,4},{6,7},{7,6},{8,16},{9,17},{10,... | collective-permute-start | bytes 786440 | tf_op jit(solution)/shard_map/ppermute | solution.py:404
  67.9 11.5 %collective-permute-start.19 = (f32[32,2048]{1,0:T(8,128)S(1)}, f32[32,2048]{1,0:T(8,128)S(1)}, u32[]{:S(2)}, u32[]{:S(2)}) collective-permute-start(f32[32,2048]{1,0:T(8,128)S(1)} %get-tuple-element.87), channel_id=1, source_target_pairs={{0,8},{1,9},{2,10},{3,11},{4,12},{5,13},{6,14},{7,15},{8,0},{9,1},... | collective-permute-start | bytes 786440 | tf_op jit(solution)/shard_map/ppermute | solution.py:404
  73.8 9.9 %collective-permute-start.21 = (f32[32,2048]{1,0:T(8,128)S(1)}, f32[32,2048]{1,0:T(8,128)S(1)}, u32[]{:S(2)}, u32[]{:S(2)}) collective-permute-start(f32[32,2048]{1,0:T(8,128)S(1)} %get-tuple-element.90), channel_id=1, source_target_pairs={{0,8},{1,9},{2,10},{3,11},{4,12},{5,13},{6,14},{7,15},{8,0},{9,1},... | collective-permute-start | bytes 786440 | tf_op jit(solution)/shard_map/ppermute | solution.py:404
  76.6 7.0 %collective-permute-start.23 = (f32[32,2048]{1,0:T(8,128)S(1)}, f32[32,2048]{1,0:T(8,128)S(1)}, u32[]{:S(2)}, u32[]{:S(2)}) collective-permute-start(f32[32,2048]{1,0:T(8,128)S(1)} %get-tuple-element.91), channel_id=1, source_target_pairs={{0,1},{1,0},{2,3},{3,2},{4,5},{5,4},{6,7},{7,6},{8,16},{9,17},{10,... | collective-permute-start | bytes 786440 | tf_op jit(solution)/shard_map/ppermute | solution.py:404
  92.7 16.3 %collective-permute-start.27 = (f32[32,512]{1,0:T(8,128)S(1)}, f32[32,512]{1,0:T(8,128)S(1)}, u32[]{:S(2)}, u32[]{:S(2)}) collective-permute-start(f32[32,512]{1,0:T(8,128)S(1)} %add.27), channel_id=1, source_target_pairs={{0,6},{1,7},{2,4},{3,5},{4,2},{5,3},{6,0},{7,1},{8,14},{9,15},{10,... | collective-permute-start | bytes 196616 | tf_op jit(solution)/shard_map/ppermute | solution.py:367
  95.3 13.7 %collective-permute-start.26 = (f32[32,512]{1,0:T(8,128)S(1)}, f32[32,512]{1,0:T(8,128)S(1)}, u32[]{:S(2)}, u32[]{:S(2)}) collective-permute-start(f32[32,512]{1,0:T(8,128)S(1)} %add.27), channel_id=1, source_target_pairs={{0,4},{1,5},{2,6},{3,7},{4,0},{5,1},{6,2},{7,3},{8,12},{9,13},{10,... | collective-permute-start | bytes 196616 | tf_op jit(solution)/shard_map/ppermute | solution.py:367
  95.9 13.1 %collective-permute-start.25 = (f32[32,512]{1,0:T(8,128)S(1)}, f32[32,512]{1,0:T(8,128)S(1)}, u32[]{:S(2)}, u32[]{:S(2)}) collective-permute-start(f32[32,512]{1,0:T(8,128)S(1)} %add.27), channel_id=1, source_target_pairs={{0,2},{1,3},{2,0},{3,1},{4,6},{5,7},{6,4},{7,5},{8,10},{9,11},{10,... | collective-permute-start | bytes 196616 | tf_op jit(solution)/shard_map/ppermute | solution.py:367
  118.7 4.9 %collective-permute-start.31 = (f32[64,384]{1,0:T(8,128)S(1)}, f32[64,384]{1,0:T(8,128)S(1)}, u32[]{:S(2)}, u32[]{:S(2)}) collective-permute-start(f32[64,384]{1,0:T(8,128)S(1)} %get-tuple-element.105), channel_id=1, source_target_pairs={{0,4},{1,5},{2,6},{3,7},{4,0},{5,1},{6,2},{7,3},{8,12},{9,13},{10,... | collective-permute-start | bytes 294920 | tf_op jit(solution)/shard_map/ppermute | solution.py:367
  119.3 5.6 %collective-permute-start.29 = (f32[64,384]{1,0:T(8,128)S(1)}, f32[64,384]{1,0:T(8,128)S(1)}, u32[]{:S(2)}, u32[]{:S(2)}) collective-permute-start(f32[64,384]{1,0:T(8,128)S(1)} %get-tuple-element.104), channel_id=1, source_target_pairs={{0,2},{1,3},{2,0},{3,1},{4,6},{5,7},{6,4},{7,5},{8,10},{9,11},{10,... | collective-permute-start | bytes 294920 | tf_op jit(solution)/shard_map/ppermute | solution.py:367
  123.6 4.7 %collective-permute-start.32 = (f32[64,384]{1,0:T(8,128)S(1)}, f32[64,384]{1,0:T(8,128)S(1)}, u32[]{:S(2)}, u32[]{:S(2)}) collective-permute-start(f32[64,384]{1,0:T(8,128)S(1)} %add.34), channel_id=1, source_target_pairs={{0,2},{1,3},{2,0},{3,1},{4,6},{5,7},{6,4},{7,5},{8,10},{9,11},{10,... | collective-permute-start | bytes 294920 | tf_op jit(solution)/shard_map/ppermute | solution.py:367
  124.9 4.7 %collective-permute-start.30 = (f32[64,384]{1,0:T(8,128)S(1)}, f32[64,384]{1,0:T(8,128)S(1)}, u32[]{:S(2)}, u32[]{:S(2)}) collective-permute-start(f32[64,384]{1,0:T(8,128)S(1)} %add.32), channel_id=1, source_target_pairs={{0,4},{1,5},{2,6},{3,7},{4,0},{5,1},{6,2},{7,3},{8,12},{9,13},{10,... | collective-permute-start | bytes 294920 | tf_op jit(solution)/shard_map/ppermute | solution.py:367
  (9 other events, 63.4 us)
